TPU v7x, 32 devices: a whole 2x2x4 slice. The times are simulated.
32 devices in a mesh: ctx: 8 (over y, x, core), exp: 4 (over z).
Axes of the slice: x: 2, y: 2, z: 4, core: 2. Of those that a mesh axis runs over, the one named last changes fastest.
Arguments:
- mixer_in: bfloat16 [1024, 16384], P('ctx', 'exp'), may hold values from -6 to 6
- gate_in: bfloat16 [1024, 16384], P('ctx', 'exp'), may hold values from -6 to 6
- delta_in: bfloat16 [1024, 16384], P('ctx', 'exp'), may hold values from -3 to 3
- b_proj: float32 [16, 1024], P(None, 'ctx'), may hold values from -0.6 to 0.6
- c_proj: float32 [16, 1024], P(None, 'ctx'), may hold values from -1.8 to 1.8
- conv_kernel: float32 [4, 16384], P(None, 'exp'), may hold values from -3 to 3
- conv_bias: float32 [16384], P('exp'), may hold values from -0.5 to 0.5
- delta_bias: float32 [16384], P('exp'), may hold values from -1 to 0
- decay_log: float32 [16, 16384], P(None, 'exp'), may hold values from -12 to -2
- skip_gain: float32 [16384], P('exp'), may hold values from 0.5 to 1.5
- prefix_state: float32 [16, 16384], P(None, 'exp'), may hold values from -6 to 6
- prefix_tail: bfloat16 [3, 16384], P(None, 'exp'), may hold values from -6 to 6
- out_proj: bfloat16 [16384, 8192], P('exp', 'ctx'), may hold values from -0.046875 to 0.046875
- residual: bfloat16 [1024, 8192], P('exp', 'ctx'), may hold values from -40 to 40
- norm_gain: float32 [8192], P('ctx'), may hold values from 0.1 to 1.9
- expert_gate: bfloat16 [4, 8192, 3072], P('exp', None, 'ctx'), may hold values from -0.0625 to 0.0625
- expert_up: bfloat16 [4, 8192, 3072], P('exp', None, 'ctx'), may hold values from -0.0625 to 0.0625
- expert_down: bfloat16 [4, 3072, 8192], P('exp', 'ctx'), may hold values from -0.15625 to 0.15625
- expert_ids: int32 [1024, 2], P('exp'), may hold values from 0 to 3, all different within a row; in each aligned block of 256 rows (0 to 255, 256 to 511, ...) at most 192 rows name the same one
- route_gates: float32 [1024, 2], P('exp'), may hold values from 0.2 to 1
Outputs:
- mixer_out: bfloat16 [1024, 8192], P('exp', 'ctx')
- block_out: bfloat16 [1024, 8192], P('exp', 'ctx')
Inputs may be any that keep to these rules, and one draw needn't show every extreme that they name: `expert_ids`: each row names 2 different experts. Within each aligned block of 256 rows (the rows of one index of exp) no expert is named more than 192 times, and in every draw some expert is named exactly 192 times in some block.
All inputs are finite; a program needn't handle non-finite values.
Results may differ from a plain program's by a relative error of at most 0.015.
Values may be sent and summed in bfloat16 or wider, within the bound.
No kernel may reach another device: no remote copies, remote signals or barrier semaphores. Data moves between devices by JAX's collectives and lax.ppermute only.
A program may use at most 128 MiB of HBM per device.

v0:
```python
import jax
import jax.numpy as jnp
from jax import lax
from jax.sharding import PartitionSpec as P

D = 8192


def from_behind(array, axis, by):
    length = lax.axis_size(axis)
    pairs = [(i, i + by) for i in range(length) if 0 <= i + by < length]
    return lax.ppermute(array, axis, pairs)


def shards(
    mixer_in,
    gate_in,
    delta_in,
    b_proj,
    c_proj,
    conv_kernel,
    conv_bias,
    delta_bias,
    decay_log,
    skip_gain,
    prefix_state,
    prefix_tail,
    out_proj,
    residual,
    norm_gain,
    expert_gate,
    expert_up,
    expert_down,
    expert_ids,
    route_gates,
):
    tokens = mixer_in.shape[0]
    width = prefix_tail.shape[0]
    leading = lax.axis_index("ctx") == 0
    rim_rows = from_behind(mixer_in[tokens - width :], "ctx", 1)
    rim_rows = jnp.where(leading, prefix_tail, rim_rows)
    padded = jnp.concatenate([rim_rows, mixer_in], axis=0).astype(jnp.float32)
    convolved = conv_bias[None, :] + sum(
        (
            conv_kernel[tap_index][None, :] * padded[tap_index : tap_index + tokens]
            for tap_index in range(width + 1)
        )
    )
    conv_act = jax.nn.silu(convolved)
    step_size = jax.nn.softplus(delta_in.astype(jnp.float32) + delta_bias[None, :])
    decay_rate = -jnp.exp(decay_log)
    driving = step_size * conv_act
    b_rows = b_proj.T
    c_rows = c_proj.T
    group_len = 8
    group_count = tokens // group_len

    def advance(carry_state, inputs):
        step_group, drive_group, b_group, c_group = inputs
        outputs = []
        for offset in range(group_len):
            carry_state = (
                jnp.exp(step_group[offset][None, :] * decay_rate) * carry_state
                + b_group[offset][:, None] * drive_group[offset][None, :]
            )
            outputs.append(jnp.sum(c_group[offset][:, None] * carry_state, axis=0))
        return (carry_state, jnp.stack(outputs))

    local_end, local_out = lax.scan(
        advance,
        jnp.zeros_like(prefix_state),
        (
            step_size.reshape(group_count, group_len, -1),
            driving.reshape(group_count, group_len, -1),
            b_rows.reshape(group_count, group_len, -1),
            c_rows.reshape(group_count, group_len, -1),
        ),
    )
    local_out = local_out.reshape(tokens, -1)
    elapsed = jnp.cumsum(step_size, axis=0)
    through = jnp.exp(decay_rate * elapsed[tokens - 1][None, :])

    def relay_step(step_number, entry_state):
        passed = from_behind(
            (through * entry_state + local_end).astype(jnp.bfloat16), "ctx", 1
        ).astype(jnp.float32)
        return jnp.where(leading, prefix_state, passed)

    entry_state = lax.fori_loop(0, lax.axis_size("ctx") - 1, relay_step, prefix_state)
    carried = jnp.exp(decay_rate[None, :, :] * elapsed[:, None, :]) * entry_state[None, :, :]
    mixed_out = (
        local_out + jnp.sum(c_rows[:, :, None] * carried, axis=1) + skip_gain[None, :] * conv_act
    )
    gated_rows = (mixed_out * jax.nn.silu(gate_in.astype(jnp.float32))).astype(jnp.bfloat16)
    gathered = lax.all_gather(gated_rows, "ctx", axis=0, tiled=True)
    block_rows = residual.shape[0]
    projected = lax.psum_scatter(
        jnp.dot(
            lax.slice_in_dim(gathered, 0, lax.axis_size("exp") * block_rows, axis=0),
            out_proj,
            preferred_element_type=jnp.float32,
        ).astype(jnp.bfloat16),
        "exp",
        scatter_dimension=0,
        tiled=True,
    ).astype(jnp.float32)
    mixer_out = (residual.astype(jnp.float32) + projected).astype(jnp.bfloat16)
    mixer_wide = mixer_out.astype(jnp.float32)
    squares = lax.psum(jnp.sum(mixer_wide * mixer_wide, axis=1), "ctx")
    norm_scale = lax.rsqrt(squares / D + 1e-05)
    normed = (mixer_wide * norm_scale[:, None] * norm_gain[None, :]).astype(jnp.bfloat16)
    experts = expert_gate.shape[0] * lax.axis_size("exp")
    top_count = expert_ids.shape[1]
    capacity = 3 * block_rows * top_count // (2 * experts)
    flat_choice = expert_ids.reshape(-1)
    owner_hot = (flat_choice[:, None] == jnp.arange(experts, dtype=jnp.int32)[None, :]).astype(
        jnp.int32
    )
    earlier_count = jnp.cumsum(owner_hot, axis=0) - owner_hot
    slot_index = jnp.sum(earlier_count * owner_hot, axis=1)
    matches = (
        flat_choice[:, None, None] == jnp.arange(experts, dtype=jnp.int32)[None, :, None]
    ) & (slot_index[:, None, None] == jnp.arange(capacity, dtype=jnp.int32)[None, None, :])
    picks = matches.reshape(block_rows, top_count, experts, capacity)
    selector = jnp.any(picks, axis=1).astype(jnp.bfloat16)
    weights = jnp.sum(picks.astype(jnp.float32) * route_gates[:, :, None, None], axis=1)
    slot_total = experts * capacity
    outgoing = jnp.einsum(
        "tec,td->ecd", selector, normed, preferred_element_type=jnp.float32
    ).astype(jnp.bfloat16)
    received = lax.all_to_all(outgoing, "exp", split_axis=0, concat_axis=0, tiled=True)
    arrived = received.reshape(slot_total, -1)
    piece_rows = lax.all_gather(arrived, "ctx", axis=1, tiled=True)
    feature_count = piece_rows.shape[1]
    gate_rows = lax.slice_in_dim(expert_gate[0], 0, feature_count, axis=0)
    up_rows = lax.slice_in_dim(expert_up[0], 0, feature_count, axis=0)
    gate_act = jnp.dot(piece_rows, gate_rows, preferred_element_type=jnp.float32)
    up_act = jnp.dot(piece_rows, up_rows, preferred_element_type=jnp.float32)
    hidden = (jax.nn.silu(gate_act) * up_act).astype(jnp.bfloat16)
    partial_value = jnp.dot(hidden, expert_down[0], preferred_element_type=jnp.float32)
    summed = lax.psum_scatter(
        partial_value.astype(jnp.bfloat16), "ctx", scatter_dimension=1, tiled=True
    )
    answer = summed.reshape(experts, capacity, -1)
    returned = lax.all_to_all(answer, "exp", split_axis=0, concat_axis=0, tiled=True)
    expert_mix = jnp.einsum(
        "tec,ecd->td", weights, returned.astype(jnp.float32), preferred_element_type=jnp.float32
    )
    block_out = (mixer_wide + expert_mix).astype(jnp.bfloat16)
    return (mixer_out, block_out)


def solution(mesh):
    placed = (
        P("ctx", "exp"),
        P("ctx", "exp"),
        P("ctx", "exp"),
        P(None, "ctx"),
        P(None, "ctx"),
        P(None, "exp"),
        P("exp"),
        P("exp"),
        P(None, "exp"),
        P("exp"),
        P(None, "exp"),
        P(None, "exp"),
        P("exp", "ctx"),
        P("exp", "ctx"),
        P("ctx"),
        P("exp", None, "ctx"),
        P("exp", None, "ctx"),
        P("exp", "ctx", None),
        P("exp", None),
        P("exp", None),
    )
    return jax.shard_map(
        shards,
        mesh=mesh,
        in_specs=placed,
        out_specs=(P("exp", "ctx"), P("exp", "ctx")),
        check_vma=False,
    )
```

profile of v0, /device:TPU:8, one launch (start us, length us, event | category | flops | bytes accessed | tf_op | source)
XLA Modules:
  0.0 575.1 jit_solution(102791389886618395)
XLA Ops:
  7.2 0.9 slice.165
  8.1 1.7 collective-permute-start.1
  9.8 1.1 fusion.36
  10.9 0.8 copy.35
  11.7 0.8 copy.34
  12.5 1.0 copy.53
  13.5 0.8 broadcast_select_fusion
  14.3 1.5 maximum_convert_fusion
  15.8 6.0 %multiply_bitcast_fusion = (f32[16,8,4096]{2,1,0:T(8,128)}, f32[128,4096]{1,0:T(8,128)}, f32[16,8,4096]{2,1,0:T(8,128)}, f32[128,4096]{1,0:T(8,128)S(1)}) fusion(f32[4096]{0:T(1024)S(1)} %copy-done.8, bf16[128,4096]{1,0:T(8,128)(2,1)} %param.26, f32[131,4096]{1,0:T(8,128)S(1)} %maximum_convert_fusion, f32[4096]{0:T(1024)S(1)} %bitcast.226, ...), kind=kLoop, calls=%fused_computation.78 | loop fusion | flops 11010048 | bytes 17924096 | tf_op jit(solution)/shard_map/reshape | solution.py:74
  21.8 3.0 reduce_window_sum.26
  24.9 0.9 slice.212
  25.9 73.2 %while.24 = (s32[]{:T(128)}, f32[16,4096]{1,0:T(8,128)S(1)}, f32[16,8,4096]{2,1,0:T(8,128)}, f32[16,8,4096]{2,1,0:T(8,128)}, f32[16,4096]{1,0:T(8,128)S(1)}, /*i...) while((s32[]{:T(128)}, f32[16,4096]{1,0:T(8,128)S(1)}, ...), condition=%wide.region_9.10_spmd.clone, body=%wide.region_0.9_spmd.clone.sunk | while | flops 4554762 | bytes 4757600 | solution.py:69
  25.9 2.1 constant_dynamic-slice_fusion.21
  30.2 2.3 constant_dynamic-slice_fusion.21
  34.6 2.6 constant_dynamic-slice_fusion.21
  39.4 2.6 constant_dynamic-slice_fusion.21
  44.1 2.4 constant_dynamic-slice_fusion.21
  48.6 2.4 constant_dynamic-slice_fusion.21
  53.1 2.6 constant_dynamic-slice_fusion.21
  57.2 0.7 bitcast_dynamic-update-slice_fusion.2
  57.9 2.5 constant_dynamic-slice_fusion.21
  61.9 0.7 bitcast_dynamic-update-slice_fusion.2
  62.6 2.6 constant_dynamic-slice_fusion.21
  67.4 2.3 constant_dynamic-slice_fusion.21
  71.9 2.3 constant_dynamic-slice_fusion.21
  76.3 2.6 constant_dynamic-slice_fusion.21
  81.0 2.1 constant_dynamic-slice_fusion.21
  85.3 2.6 constant_dynamic-slice_fusion.21
  90.0 2.3 constant_dynamic-slice_fusion.21
  94.5 2.4 constant_dynamic-slice_fusion.21
  98.4 0.7 bitcast_dynamic-update-slice_fusion.2
  99.1 39.8 %while.23 = (s32[]{:T(128)}, f32[16,4096]{1,0:T(8,128)S(1)}, pred[]{:T(512)}, f32[16,4096]{1,0:T(8,128)S(1)}, f32[16,4096]{1,0:T(8,128)S(1)}, /*index=5*/f32[16,4096]{1,0:T(8,128)S(1)}, s32[]{:T(128)}) while((s32[]{:T(128)}, f32[16,4096]{1,0:T(8,128)S(1)}, pred[]{:T(512)}, f32[16,4096]{1,0:T(8,128)S(1)}, f32[16,4096]{1,0:T(8,128)S(1)}, ...), condition=%wide.region_12.13_spmd, body=%wide.region_11.12_spmd.sunk | while | flops 327682 | bytes 2097270 | solution.py:89
  99.1 2.9 collective-permute-start
  102.1 1.0 collective-permute-done
  103.1 2.9 collective-permute-start
  106.0 1.0 collective-permute-done
  107.1 5.3 collective-permute-start
  112.4 1.0 collective-permute-done
  113.4 5.3 collective-permute-start
  118.8 1.0 collective-permute-done
  119.8 5.3 collective-permute-start
  125.1 1.0 collective-permute-done
  126.2 5.3 collective-permute-start
  131.5 1.0 collective-permute-done
  132.6 5.3 collective-permute-start
  137.9 1.0 collective-permute-done
  138.9 11.7 %multiply_reduce_fusion.8 = f32[128,4096]{1,0:T(8,128)S(1)} fusion(f32[16,4096]{1,0:T(8,128)S(1)} %get-tuple-element.79, f32[128,4096]{1,0:T(8,128)} %reduce_window_sum.26, f32[16,4096]{1,0:T(8,128)S(1)} %get-tuple-element.452, f32[128,16]{1,0:T(8,128)S(1)} %bitcast.221), kind=kLoop, calls=%fused_computation.54 | loop fusion | flops 33030144 | bytes 4726784 | tf_op jit(solution)/shard_map/reduce_sum | solution.py:92
  150.6 1.9 fusion.15
  152.6 65.8 %all-gather.3.cloned.1.call-done = bf16[1024,4096]{1,0:T(8,128)(2,1)} async-done(((bf16[128,4096]{1,0:T(8,128)(2,1)}), bf16[1024,4096]{1,0:T(8,128)(2,1)}) %all-gather.3.cloned.1.call-update) | async-done | bytes 8388624 | tf_op jit(solution)/shard_map/all_gather | solution.py:95
  218.4 14.7 %convolution_convert_fusion.1 = bf16[1024,1024]{1,0:T(8,128)(2,1)} fusion(bf16[1024,4096]{1,0:T(8,128)(2,1)} %all-gather.3.cloned.1.call-done, bf16[4096,1024]{1,0:T(8,128)(2,1)} %param.36), kind=kOutput, calls=%fused_computation.83 | convolution fusion | flops 8590983168 | bytes 18874368 | tf_op jit(solution)/shard_map/dot_general | solution.py:98
  234.2 1.2 reduce-window.6
  236.4 38.5 %reduce-scatter.3.cloned.1.call-done = bf16[256,1024]{1,0:T(8,128)(2,1)} async-done(((bf16[1024,1024]{1,0:T(8,128)(2,1)}), bf16[256,1024]{1,0:T(8,128)(2,1)}) %reduce-scatter.3.cloned.1.call-update) | async-done | bytes 524304 | tf_op jit(solution)/shard_map/reduce_scatter | solution.py:97
  274.9 1.3 fusion.24
  276.2 13.5 %psum.7 = f32[256]{0:T(256)S(1)} all-reduce(f32[256]{0:T(256)S(1)} %get-tuple-element.146), channel_id=1, replica_groups=mesh['ctx'=8,'exp'=4] {'ctx'}, use_global_device_ids=true, to_apply=%region_21.22 | all-reduce | flops 256 | bytes 2048 | tf_op jit(solution)/shard_map/psum | solution.py:109
  289.7 0.7 convolution_convert_fusion.2
  290.4 39.8 %all_to_all.10 = bf16[4,192,1024]{2,1,0:T(8,128)(2,1)} all-to-all(bf16[4,192,1024]{2,1,0:T(8,128)(2,1)S(1)} %convolution_convert_fusion.2), channel_id=1, replica_groups=mesh['ctx'=8,'exp'=4] {'exp'}, dimensions={0} | all-to-all | bytes 3145728 | tf_op jit(solution)/shard_map/all_to_all | solution.py:131
  330.3 71.8 %all-gather.5.cloned.1.call-done = bf16[768,8192]{1,0:T(8,128)(2,1)} async-done(((bf16[768,1024]{1,0:T(8,128)(2,1)}), bf16[768,8192]{1,0:T(8,128)(2,1)}) %all-gather.5.cloned.1.call-update) | async-done | bytes 12582928 | tf_op jit(solution)/shard_map/all_gather | solution.py:133
  402.1 12.0 %fusion.4 = f32[768,384]{1,0:T(8,128)S(1)} fusion(bf16[768,8192]{1,0:T(8,128)(2,1)} %all-gather.5.cloned.1.call-done, bf16[1,8192,384]{2,1,0:T(8,128)(2,1)} %param.39), kind=kOutput, calls=%fused_computation.59 | convolution fusion | flops 4831838208 | bytes 20054016 | tf_op jit(solution)/shard_map/dot_general | solution.py:137
  414.1 9.2 %fusion.20 = bf16[768,384]{1,0:T(8,128)(2,1)S(1)} fusion(bf16[768,8192]{1,0:T(8,128)(2,1)S(1)} %copy-done.13, bf16[1,8192,384]{2,1,0:T(8,128)(2,1)} %param.40, f32[768,384]{1,0:T(8,128)S(1)} %fusion.4), kind=kOutput, calls=%fused_computation.91 | convolution fusion | flops 4833607680 | bytes 20643840 | tf_op jit(solution)/shard_map/dot_general | solution.py:138
  423.3 12.5 %convolution_convert_fusion = bf16[768,8192]{1,0:T(8,128)(2,1)} fusion(bf16[768,384]{1,0:T(8,128)(2,1)S(1)} %fusion.20, bf16[1,384,8192]{2,1,0:T(8,128)(2,1)} %param.41), kind=kOutput, calls=%fused_computation.55 | convolution fusion | flops 4838129664 | bytes 19464192 | tf_op jit(solution)/shard_map/dot_general | solution.py:140
  435.8 92.5 %reduce-scatter.5.cloned.1.call-done = bf16[768,1024]{1,0:T(8,128)(2,1)} async-done(((bf16[768,8192]{1,0:T(8,128)(2,1)}), bf16[768,1024]{1,0:T(8,128)(2,1)}) %reduce-scatter.5.cloned.1.call-update) | async-done | bytes 1572880 | tf_op jit(solution)/shard_map/reduce_scatter | solution.py:141
  528.4 5.1 all-to-all-start.1
  533.7 33.5 %all-to-all-done.1 = bf16[4,192,1024]{2,1,0:T(8,128)(2,1)S(1)} async-done(((bf16[4,192,1024]{2,1,0:T(8,128)(2,1)}), bf16[4,192,1024]{2,1,0:T(8,128)(2,1)S(1)}, u32[]{:S(2)}, u32[]{:S(2)}) %all-to-all-start.1) | async-done | bytes 1572896 | tf_op jit(solution)/shard_map/all_to_all | solution.py:145
  567.2 1.4 fusion.23
  (210 shorter events, 34.1 us)
Async XLA Ops:
  7.2 211.3 %all-gather.3.cloned.1.call-start = ((), (), s32[]{:S(2)}) async-start(), calls=%async_computation.4 | async-start | bytes 9437184 | tf_op jit(solution)/shard_map/all_gather | solution.py:95
  8.1 7.7 %copy-start.8 = (f32[4096]{0:T(1024)S(1)}, f32[4096]{0:T(1024)}, u32[]{:S(2)}) copy-start(f32[4096]{0:T(1024)} %param.31) | copy-start | bytes 49156
  8.1 7.7 %copy-start.9 = (f32[4096]{0:T(1024)S(1)}, f32[4096]{0:T(1024)}, u32[]{:S(2)}) copy-start(f32[4096]{0:T(1024)} %param.30) | copy-start | bytes 49156
  8.1 5.4 collective-permute-start.1
  21.8 3.9 copy-start.6
  25.9 73.2 %copy-start = (f32[16,4096]{1,0:T(8,128)S(1)}, f32[16,4096]{1,0:T(8,128)}, u32[]{:S(2)}) copy-start(f32[16,4096]{1,0:T(8,128)} %param.34) | copy-start | bytes 786436
  99.1 3.9 collective-permute-start
  103.1 3.9 collective-permute-start
  107.1 6.3 %collective-permute-start = (bf16[16,4096]{1,0:T(8,128)(2,1)S(1)}, bf16[16,4096]{1,0:T(8,128)(2,1)S(1)}, u32[]{:S(2)}, u32[]{:S(2)}) collective-permute-start(bf16[16,4096]{1,0:T(8,128)(2,1)S(1)} %add_convert_fusion.4), channel_id=1, source_target_pairs={{0,4},{4,8},{8,12},{12,16},{16,20},{20,24},{24,28},{1,5},{5,9},{9,... | collective-permute-start | bytes 393224 | tf_op jit(solution)/shard_map/while/body/eval_jaxpr/ppermute | solution.py:12
  113.4 6.3 %collective-permute-start = (bf16[16,4096]{1,0:T(8,128)(2,1)S(1)}, bf16[16,4096]{1,0:T(8,128)(2,1)S(1)}, u32[]{:S(2)}, u32[]{:S(2)}) collective-permute-start(bf16[16,4096]{1,0:T(8,128)(2,1)S(1)} %add_convert_fusion.4), channel_id=1, source_target_pairs={{0,4},{4,8},{8,12},{12,16},{16,20},{20,24},{24,28},{1,5},{5,9},{9,... | collective-permute-start | bytes 393224 | tf_op jit(solution)/shard_map/while/body/eval_jaxpr/ppermute | solution.py:12
  119.8 6.3 %collective-permute-start = (bf16[16,4096]{1,0:T(8,128)(2,1)S(1)}, bf16[16,4096]{1,0:T(8,128)(2,1)S(1)}, u32[]{:S(2)}, u32[]{:S(2)}) collective-permute-start(bf16[16,4096]{1,0:T(8,128)(2,1)S(1)} %add_convert_fusion.4), channel_id=1, source_target_pairs={{0,4},{4,8},{8,12},{12,16},{16,20},{20,24},{24,28},{1,5},{5,9},{9,... | collective-permute-start | bytes 393224 | tf_op jit(solution)/shard_map/while/body/eval_jaxpr/ppermute | solution.py:12
  126.2 6.3 %collective-permute-start = (bf16[16,4096]{1,0:T(8,128)(2,1)S(1)}, bf16[16,4096]{1,0:T(8,128)(2,1)S(1)}, u32[]{:S(2)}, u32[]{:S(2)}) collective-permute-start(bf16[16,4096]{1,0:T(8,128)(2,1)S(1)} %add_convert_fusion.4), channel_id=1, source_target_pairs={{0,4},{4,8},{8,12},{12,16},{16,20},{20,24},{24,28},{1,5},{5,9},{9,... | collective-permute-start | bytes 393224 | tf_op jit(solution)/shard_map/while/body/eval_jaxpr/ppermute | solution.py:12
  132.6 6.3 %collective-permute-start = (bf16[16,4096]{1,0:T(8,128)(2,1)S(1)}, bf16[16,4096]{1,0:T(8,128)(2,1)S(1)}, u32[]{:S(2)}, u32[]{:S(2)}) collective-permute-start(bf16[16,4096]{1,0:T(8,128)(2,1)S(1)} %add_convert_fusion.4), channel_id=1, source_target_pairs={{0,4},{4,8},{8,12},{12,16},{16,20},{20,24},{24,28},{1,5},{5,9},{9,... | collective-permute-start | bytes 393224 | tf_op jit(solution)/shard_map/while/body/eval_jaxpr/ppermute | solution.py:12
  138.9 11.7 %copy-start.1 = (f32[128,4096]{1,0:T(8,128)S(1)}, f32[128,4096]{1,0:T(8,128)}, u32[]{:S(2)}) copy-start(f32[128,4096]{1,0:T(8,128)} %get-tuple-element.149) | copy-start | bytes 6291460
  138.9 11.7 %copy-start.2 = (f32[16,8,4096]{2,1,0:T(8,128)S(1)}, f32[16,8,4096]{2,1,0:T(8,128)}, u32[]{:S(2)}) copy-start(f32[16,8,4096]{2,1,0:T(8,128)} %get-tuple-element.77) | copy-start | bytes 6291460
  138.9 11.7 %copy-start.4 = (bf16[128,4096]{1,0:T(8,128)(2,1)S(1)}, bf16[128,4096]{1,0:T(8,128)(2,1)}, u32[]{:S(2)}) copy-start(bf16[128,4096]{1,0:T(8,128)(2,1)} %param.25) | copy-start | bytes 3145732
  138.9 11.7 %copy-start.7 = (f32[4096]{0:T(1024)S(1)}, f32[4096]{0:T(1024)}, u32[]{:S(2)}) copy-start(f32[4096]{0:T(1024)} %param.33) | copy-start | bytes 49156
  152.5 122.3 %reduce-scatter.3.cloned.1.call-start = ((), (), s32[]{:S(2)}) async-start(), calls=%async_computation.5 | async-start | bytes 2621440 | tf_op jit(solution)/shard_map/reduce_scatter | solution.py:97
  233.1 0.7 copy-start.10
  233.1 41.8 %copy-start.5 = (bf16[256,1024]{1,0:T(8,128)(2,1)S(1)}, bf16[256,1024]{1,0:T(8,128)(2,1)}, u32[]{:S(2)}) copy-start(bf16[256,1024]{1,0:T(8,128)(2,1)} %param.37) | copy-start | bytes 1572868
  233.1 56.6 %copy-start.11 = (f32[1024]{0:T(1024)S(1)}, f32[1024]{0:T(1024)}, u32[]{:S(2)}) copy-start(f32[1024]{0:T(1024)} %param.38) | copy-start | bytes 12292
  233.1 169.0 %all-gather.5.cloned.1.call-start = ((), (), s32[]{:S(2)}) async-start(), calls=%async_computation.6 | async-start | bytes 14155776 | tf_op jit(solution)/shard_map/all_gather | solution.py:133
  276.2 291.0 %copy-start.3 = (bf16[256,1024]{1,0:T(8,128)(2,1)}, bf16[256,1024]{1,0:T(8,128)(2,1)S(1)}, u32[]{:S(2)}) copy-start(bf16[256,1024]{1,0:T(8,128)(2,1)S(1)} %get-tuple-element.147) | copy-start | bytes 1572868
  330.2 198.2 %reduce-scatter.5.cloned.1.call-start = ((), (), s32[]{:S(2)}) async-start(), calls=%async_computation.7 | async-start | bytes 14155776 | tf_op jit(solution)/shard_map/reduce_scatter | solution.py:141
  402.1 12.0 %copy-start.13 = (bf16[768,8192]{1,0:T(8,128)(2,1)S(1)}, bf16[768,8192]{1,0:T(8,128)(2,1)}, u32[]{:S(2)}) copy-start(bf16[768,8192]{1,0:T(8,128)(2,1)} %all-gather.5.cloned.1.call-done) | copy-start | bytes 37748740
  435.8 97.7 %copy-start.12 = (f32[256,2]{0,1:T(2,128)S(1)}, f32[256,2]{0,1:T(2,128)}, u32[]{:S(2)}) copy-start(f32[256,2]{0,1:T(2,128)} %param.43) | copy-start | bytes 6148
  528.4 38.8 %all-to-all-start.1 = ((bf16[4,192,1024]{2,1,0:T(8,128)(2,1)}), bf16[4,192,1024]{2,1,0:T(8,128)(2,1)S(1)}, u32[]{:S(2)}, u32[]{:S(2)}) async-start(bf16[4,192,1024]{2,1,0:T(8,128)(2,1)} %bitcast.219), calls=%async_computation.3 | async-start | bytes 3145728 | tf_op jit(solution)/shard_map/all_to_all | solution.py:145
Sparse Core Ops, SparseCore 0:
  152.7 65.7 all-gather.2
  233.2 41.6 reduce-scatter.2
  330.3 71.6 all-gather.4
  435.9 92.3 reduce-scatter.4
where the time goes:
time: 581 us; the launch traced here: 575 us
  waiting for transfers between devices  309 us (53%)
  local copies, waits for them, and re-layouts  60 us (10%)
  blocking collectives  53.3 us (9%)
  matrix products  50.4 us (9%)
  other arithmetic  47.2 us (8%)
  starting transfers between devices  39.6 us (7%)
  between operations  14.1 us (2%)
    reduce_scatter x1, waiting for transfers between devices, shards(): lax.psum_scatter(partial_value.astype(jnp.bfloat16), 'ctx', scatter_dimen...  92.5 us
    all_gather x1, waiting for transfers between devices, shards(): piece_rows = lax.all_gather(arrived, 'ctx', axis=1, tiled=True)  71.8 us
    all_gather x1, waiting for transfers between devices, shards(): gathered = lax.all_gather(gated_rows, 'ctx', axis=0, tiled=True)  65.8 us
    all_to_all x1, blocking collectives, shards(): lax.all_to_all(outgoing, 'exp', split_axis=0, concat_axis=0, tiled=True)  39.8 us
    slice x16, local copies, waits for them, and re-layouts, advance(): drive_group[offset][None, :]  38.8 us
    reduce_scatter x1, waiting for transfers between devices, shards(): lax.psum_scatter(jnp.dot(lax.slice_in_dim(gathered, 0, lax.axis_size('exp...  38.5 us
    ppermute x8, starting transfers between devices, from_behind(): return lax.ppermute(array, axis, pairs)  34.1 us
    all_to_all x1, waiting for transfers between devices, shards(): lax.all_to_all(answer, 'exp', split_axis=0, concat_axis=0, tiled=True)  33.5 us
  transfers between devices with their start and end apart: 13, of which 12 were waited for; matrix products, arithmetic and copies ran while one was open for 1% of the time, Pallas kernels for 0%

commit v1 on v0

v1 whole, which is shorter than its diff:
```python
import functools

import jax
import jax.numpy as jnp
from jax import lax
from jax.experimental import pallas as pl
from jax.experimental.pallas import tpu as pltpu
from jax.sharding import PartitionSpec as P

D = 8192
LOG2E = 1.4426950408889634
LANES = 128
MIB = 1 << 20


def from_behind(array, axis, by):
    length = lax.axis_size(axis)
    pairs = [(i, i + by) for i in range(length) if 0 <= i + by < length]
    return lax.ppermute(array, axis, pairs)


def swap(array, axis, mask):
    return lax.ppermute(array, axis, [(i, i ^ mask) for i in range(lax.axis_size(axis))])


def halves_kernel(split_dim, first, second, low, high):
    half = low.shape[split_dim]
    if split_dim == 0:
        low[...] = first[0:half, :]
        high[...] = second[half:, :]
    else:
        low[...] = first[:, 0:half]
        high[...] = second[:, half:]


def halves(first, second, split_dim, after=()):
    shape = list(first.shape)
    shape[split_dim] //= 2
    whole = pl.BlockSpec(first.shape, lambda j: (0, 0))
    part = pl.BlockSpec(tuple(shape), lambda j: (0, 0))
    return launch(
        functools.partial(halves_kernel, split_dim),
        [],
        [first, second],
        [whole, whole],
        [part, part],
        [jax.ShapeDtypeStruct(tuple(shape), first.dtype)] * 2,
        after=after,
        limit=16,
        cost_estimate=cost(0, 6 * first.size),
        name="halves",
    )


def gather_parts(array, split_dim=None, after=()):
    count = lax.axis_size("ctx")
    if count != 8:
        return [(0, None, array)] + [(m, None, swap(array, "ctx", m)) for m in range(1, count)]
    over_a = swap(array, "ctx", 2)
    over_b = swap(array, "ctx", 4)
    if split_dim is None:
        crossed = [(6, None, swap(array, "ctx", 6))]
    else:
        low, high = halves(over_a, over_b, split_dim, after)
        crossed = [(6, 0, swap(low, "ctx", 4)), (6, 1, swap(high, "ctx", 2))]
    parts = []
    for mask, which, part in [(0, None, array), (2, None, over_a), (4, None, over_b)] + crossed:
        parts.append((mask, which, part))
        parts.append((mask + 1, which, swap(part, "ctx", 1)))
    return parts


def silu(value):
    return value / (1.0 + jnp.exp(-value))


def cost(flops, moved, transcendentals=0):
    return pl.CostEstimate(
        flops=int(flops), bytes_accessed=int(moved), transcendentals=int(transcendentals)
    )


ANY = pl.BlockSpec(memory_space=pl.ANY)


def launch(
    kernel, scalars, operands, in_specs, out_specs, out_shape, after=(), grid=(1,), scratch=(),
    limit=56, **rest
):
    taken = len(scalars) + len(operands)

    def body(*refs):
        kernel(*refs[:taken], *refs[taken + len(after) :])

    return pl.pallas_call(
        body,
        grid_spec=pltpu.PrefetchScalarGridSpec(
            num_scalar_prefetch=len(scalars),
            grid=grid,
            in_specs=list(in_specs) + [ANY] * len(after),
            out_specs=out_specs,
            scratch_shapes=list(scratch),
        ),
        out_shape=out_shape,
        compiler_params=pltpu.CompilerParams(vmem_limit_bytes=limit * MIB),
        **rest,
    )(*scalars, *operands, *after)


def cut_kernel(count, *refs):
    for source, out in zip(refs[-2 * count : -count], refs[-count:]):
        out[...] = source[...]


def cut_columns(me, rows, width, masks, after=()):
    step = rows.shape[0] // 3

    def block(mask):
        return pl.BlockSpec((step, width), lambda i, me: (i, me[0] ^ mask))

    return launch(
        functools.partial(cut_kernel, len(masks)),
        [me],
        [rows] * len(masks),
        [block(mask) for mask in masks],
        [pl.BlockSpec((step, width), lambda i, me: (i, 0))] * len(masks),
        [jax.ShapeDtypeStruct((rows.shape[0], width), rows.dtype)] * len(masks),
        after=after,
        grid=(3,),
        cost_estimate=cost(0, 4 * rows.shape[0] * width * len(masks)),
        name="cut_columns",
    )


def join_kernel(count, *refs):
    pieces, out, sems = refs[:count], refs[count], refs[count + 1]
    copies, row = [], 0
    for place, piece in enumerate(pieces):
        copies.append(
            pltpu.make_async_copy(piece, out.at[pl.ds(row, piece.shape[0]), :], sems.at[place])
        )
        row += piece.shape[0]
    for copy in copies:
        copy.start()
    for copy in copies:
        copy.wait()


def join(pieces, after=()):
    rows = sum(piece.shape[0] for piece in pieces)
    columns = pieces[0].shape[1]
    return launch(
        functools.partial(join_kernel, len(pieces)),
        [],
        list(pieces),
        [ANY] * len(pieces),
        pl.BlockSpec((rows, columns), lambda j: (0, 0)),
        jax.ShapeDtypeStruct((rows, columns), pieces[0].dtype),
        after=after,
        scratch=[pltpu.SemaphoreType.DMA((len(pieces),))],
        limit=16,
        cost_estimate=cost(0, 4 * rows * columns),
        name="join",
    )


BLOCK = 512


def by_blocks(kernel, split, *refs):
    width = next(ref for ref, cut in zip(refs, split) if cut).shape[1]

    def one(index, _):
        lanes = pl.ds(pl.multiple_of(index * BLOCK, BLOCK), BLOCK)
        kernel(*[ref.at[:, lanes] if cut else ref for ref, cut in zip(refs, split)])
        return 0

    lax.fori_loop(0, width // BLOCK, one, 0)


GROUP = 16
STATE_ROWS = 32


def state_kernel(
    mixer, rim, delta, kernel, bias, delta_bias, decay_log, extra, b_wide, step_out, conv_out,
    end_out, padded,
):
    tokens, width = mixer.shape
    blocks = width // LANES
    padded[0:8, :] = rim[...]
    padded[8:, :] = mixer[...].astype(jnp.float32)
    rate = [
        -jnp.exp(decay_log[:, k * LANES : (k + 1) * LANES]) * LOG2E for k in range(blocks)
    ]
    taps = kernel.shape[0]

    def group(index, carry):
        states, total = carry
        base = pl.multiple_of(index * GROUP, GROUP)
        window = padded[pl.ds(base, GROUP + 8), :]
        convolved = bias[...] + sum(
            kernel[k : k + 1, :] * window[9 - taps + k : 9 - taps + k + GROUP, :]
            for k in range(taps)
        )
        conv_act = silu(convolved)
        step = jnp.log(
            1.0 + jnp.exp(delta[pl.ds(base, GROUP), :].astype(jnp.float32) + delta_bias[...])
        )
        step_out[pl.ds(base, GROUP), :] = step
        conv_out[pl.ds(base, GROUP), :] = conv_act
        drive = step * conv_act
        states = list(states)
        for i in range(GROUP):
            b_tile = b_wide[pl.ds(pl.multiple_of((base + i) * 16, 16), 16), :]
            for k in range(blocks):
                lanes = slice(k * LANES, (k + 1) * LANES)
                states[k] = (
                    jnp.exp2(step[i : i + 1, lanes] * rate[k]) * states[k]
                    + b_tile * drive[i : i + 1, lanes]
                )
        return tuple(states), total + step[0:8, :] + step[8:16, :]

    start = tuple(jnp.zeros((16, LANES), jnp.float32) for _ in range(blocks))
    states, total = lax.fori_loop(
        0, tokens // GROUP, group, (start, jnp.zeros((8, width), jnp.float32))
    )
    for k in range(blocks):
        end_out[0:16, k * LANES : (k + 1) * LANES] = states[k].astype(end_out.dtype)
    total = jnp.sum(total, axis=0, keepdims=True)
    place = lax.broadcasted_iota(jnp.int32, (16, width), 0)
    pieces = jnp.where(place == 3, extra[...], 0.0)
    for row in range(3):
        piece = total.astype(jnp.bfloat16).astype(jnp.float32)
        pieces = jnp.where(place == row, piece, pieces)
        total = total - piece
    end_out[16:32, :] = pieces.astype(end_out.dtype)


def local_states(mixer_in, rim8, delta_in, kernel, bias, delta_bias, decay_log, extra, b_wide):
    tokens, channels = mixer_in.shape
    width = 1024
    rows = lambda n: pl.BlockSpec((n, width), lambda j: (0, j))
    return launch(
        functools.partial(by_blocks, state_kernel, [1] * 8 + [0] + [1] * 3 + [0]),
        [],
        [mixer_in, rim8, delta_in, kernel, bias, delta_bias, decay_log, extra, b_wide],
        [
            rows(tokens),
            rows(8),
            rows(tokens),
            rows(kernel.shape[0]),
            rows(1),
            rows(1),
            rows(16),
            rows(1),
            pl.BlockSpec((tokens * 16, LANES), lambda j: (0, 0)),
        ],
        [rows(tokens), rows(tokens), rows(STATE_ROWS)],
        [
            jax.ShapeDtypeStruct((tokens, channels), jnp.float32),
            jax.ShapeDtypeStruct((tokens, channels), jnp.float32),
            jax.ShapeDtypeStruct((STATE_ROWS, channels), jnp.bfloat16),
        ],
        grid=(channels // width,),
        scratch=[pltpu.VMEM((tokens + 8, BLOCK), jnp.float32)],
        cost_estimate=cost(
            tokens * channels * 16 * 5, tokens * channels * 12, tokens * channels * 18
        ),
        name="local_states",
    )


def gains_kernel(masks, me, *refs):
    parts, out = refs[: len(masks)], refs[-1]
    width = out.shape[2]
    for mask, part in zip(masks, parts):
        row = part[...].astype(jnp.float32)[3:4, :]
        gain = row[:, 0:width] + row[:, width : 2 * width] + row[:, 2 * width : 3 * width]
        out[me[0] ^ mask] = 1.0 / gain


def inverse_gains(me, ends, width):
    return launch(
        functools.partial(gains_kernel, [mask for mask, _, _ in ends]),
        [me],
        [end for _, _, end in ends],
        [pl.BlockSpec((16, 3 * width), lambda j, me: (1, 0))] * len(ends),
        pl.BlockSpec((len(ends), 1, width), lambda j, me: (0, 0, 0)),
        jax.ShapeDtypeStruct((len(ends), 1, width), jnp.float32),
        limit=16,
        name="inverse_gains",
    )


def fold_rows(tiles):
    place = lax.broadcasted_iota(jnp.int32, (8, LANES), 0)
    for shift in (1, 2, 4):
        first = (place & shift) == 0
        tiles = [
            jnp.where(first, a, b) + pltpu.roll(jnp.where(first, b, a), shift, 0)
            for a, b in zip(tiles[0::2], tiles[1::2])
        ]
    return tiles[0]


def readout_kernel(
    masks, me, step_in, conv_in, gate_in, decay_log, skip, b_wide, c_wide, entering, *refs
):
    ends = refs[: len(masks)]
    gated, leaving, scanned = refs[len(masks) : len(masks) + 3]
    tokens, width = step_in.shape
    blocks = width // LANES
    rate = [
        -jnp.exp(decay_log[:, k * LANES : (k + 1) * LANES]) * LOG2E for k in range(blocks)
    ]
    start = [entering[:, k * LANES : (k + 1) * LANES] for k in range(blocks)]
    if masks:
        held = refs[-1]
        for mask, end in zip(masks, ends):
            held[mask] = end[...].astype(jnp.float32)
        for owner in range(len(masks) - 1):
            end = held[me[0] ^ owner]
            total = end[16:17, :] + end[17:18, :] + end[18:19, :]
            for k in range(blocks):
                lanes = slice(k * LANES, (k + 1) * LANES)
                later = jnp.exp2(total[:, lanes] * rate[k]) * start[k] + end[0:16, lanes]
                start[k] = jnp.where(owner < me[0], later, start[k])

    def group(index, states):
        base = pl.multiple_of(index * GROUP, GROUP)
        step = step_in[pl.ds(base, GROUP), :]
        conv_act = conv_in[pl.ds(base, GROUP), :]
        drive = step * conv_act
        states = list(states)
        for half in range(GROUP // 8):
            tiles = [[] for _ in range(blocks)]
            for i in range(half * 8, half * 8 + 8):
                spot = pl.ds(pl.multiple_of((base + i) * 16, 16), 16)
                b_tile = b_wide[spot, :]
                c_tile = c_wide[spot, :]
                for k in range(blocks):
                    lanes = slice(k * LANES, (k + 1) * LANES)
                    states[k] = (
                        jnp.exp2(step[i : i + 1, lanes] * rate[k]) * states[k]
                        + b_tile * drive[i : i + 1, lanes]
                    )
                    read = c_tile * states[k]
                    tiles[k].append(read[0:8] + read[8:16])
            for k in range(blocks):
                scanned[
                    pl.ds(pl.multiple_of(base + half * 8, 8), 8), k * LANES : (k + 1) * LANES
                ] = fold_rows(tiles[k])
        gate = gate_in[pl.ds(base, GROUP), :].astype(jnp.float32)
        mixed = scanned[pl.ds(base, GROUP), :] + skip[...] * conv_act
        gated[pl.ds(base, GROUP), :] = (mixed * silu(gate)).astype(gated.dtype)
        return tuple(states)

    states = lax.fori_loop(0, tokens // GROUP, group, tuple(start))
    for k in range(blocks):
        leaving[:, k * LANES : (k + 1) * LANES] = states[k]


def read_out(
    me, chunk, chunks, step, conv_act, gate_in, decay_log, skip, b_wide, c_wide, entering, ends,
    after=(),
):
    tokens, channels = step.shape
    tokens = tokens // chunks
    width = 1024
    some = pl.BlockSpec((tokens, width), lambda j, me: (chunk, j))
    rows = lambda n: pl.BlockSpec((n, width), lambda j, me: (0, j))
    wide = pl.BlockSpec((tokens * 16, LANES), lambda j, me: (chunk, 0))
    masks = [mask for mask, _, _ in ends]
    scratch = [pltpu.VMEM((tokens, BLOCK), jnp.float32)]
    if ends:
        scratch.append(pltpu.VMEM((len(ends), STATE_ROWS, BLOCK), jnp.float32))
    split = [0] + [1] * 5 + [0, 0, 1] + [1] * len(ends) + [1, 1] + [0] * len(scratch)
    return launch(
        functools.partial(by_blocks, functools.partial(readout_kernel, masks), split),
        [me],
        [step, conv_act, gate_in, decay_log, skip, b_wide, c_wide, entering]
        + [end for _, _, end in ends],
        [some, some, some, rows(16), rows(1), wide, wide, rows(16)]
        + [rows(STATE_ROWS)] * len(ends),
        [rows(tokens), rows(16)],
        [
            jax.ShapeDtypeStruct((tokens, channels), jnp.bfloat16),
            jax.ShapeDtypeStruct((16, channels), jnp.float32),
        ],
        after=after,
        grid=(channels // width,),
        scratch=scratch,
        cost_estimate=cost(
            tokens * channels * 16 * 7, tokens * channels * 12, tokens * channels * 18
        ),
        name="read_out",
    )


def project_kernel(layout, me, weight, *refs):
    parts, (out, held, sems) = refs[: len(layout)], refs[len(layout) :]
    rows = held.shape[0] // (1 + max(mask for mask, _ in layout))

    @pl.when(pl.program_id(0) == 0)
    def _():
        copies = []
        for place, (mask, column) in enumerate(layout):
            part = parts[place]
            owner = me[0] ^ mask
            copies.append(
                pltpu.make_async_copy(
                    part,
                    held.at[
                        pl.ds(pl.multiple_of(owner * rows, rows), rows),
                        pl.ds(column, part.shape[1]),
                    ],
                    sems.at[place],
                )
            )
        for copy in copies:
            copy.start()
        for copy in copies:
            copy.wait()

    out[...] = jnp.dot(held[...], weight[...], preferred_element_type=jnp.float32).astype(
        out.dtype
    )


def project(me, parts, weight, after=()):
    depth, columns = weight.shape
    rows = parts[0][2].shape[0]
    total = rows * lax.axis_size("ctx")
    layout = [(mask, (which or 0) * depth // 2) for mask, which, _ in parts]
    tile = min(256, columns)
    return launch(
        functools.partial(project_kernel, layout),
        [me],
        [weight] + [part for _, _, part in parts],
        [pl.BlockSpec((depth, tile), lambda j, me: (0, j))] + [ANY] * len(parts),
        pl.BlockSpec((total, tile), lambda j, me: (0, j)),
        jax.ShapeDtypeStruct((total, columns), jnp.bfloat16),
        after=after,
        grid=(columns // tile,),
        scratch=[
            pltpu.VMEM((total, depth), jnp.bfloat16),
            pltpu.SemaphoreType.DMA((len(parts),)),
        ],
        limit=40,
        cost_estimate=cost(
            2 * total * depth * columns, 2 * (total * depth + depth * columns + total * columns)
        ),
        name="project",
    )


def hidden_kernel(layout, me, gain, gate_rows, up_rows, *refs):
    parts, (out, held, total, squares, sems) = refs[: len(layout)], refs[len(layout) :]
    turn = pl.program_id(0)

    def copy_of(place):
        mask, row = layout[place]
        part = parts[place]
        column = ((me[0] ^ mask) & 1) * part.shape[1]
        return pltpu.make_async_copy(
            part,
            held.at[
                mask // 2,
                pl.ds(row, part.shape[0]),
                pl.ds(pl.multiple_of(column, LANES), part.shape[1]),
            ],
            sems.at[place],
        )

    @pl.when(turn == 0)
    def _():
        for place in range(len(layout)):
            copy_of(place).start()
        total[...] = jnp.zeros_like(total)
        squares[...] = jnp.zeros_like(squares)

    for place, (mask, _) in enumerate(layout):

        @pl.when(turn == mask // 2)
        def _():
            copy_of(place).wait()

    width = out.shape[1]
    both = jnp.concatenate([gate_rows[...], up_rows[...]], axis=1)
    total[...] += jnp.dot(held[turn], both, preferred_element_type=jnp.float32)
    slots = out.shape[0]
    for row in range(0, slots, 64):
        mixer_square = squares[row : row + 64, :]
        for lane in range(0, held.shape[2], LANES):
            value = held[turn, row : row + 64, lane : lane + LANES].astype(jnp.float32)
            spot = lane % gain.shape[2]
            value = value * gain[lane // gain.shape[2], :, spot : spot + LANES]
            mixer_square += value * value
        squares[row : row + 64, :] = mixer_square

    @pl.when(turn == pl.num_programs(0) - 1)
    def _():
        def finish(index, _):
            spot = pl.ds(pl.multiple_of(index * 64, 64), 64)
            mean = jnp.sum(squares[spot, :], axis=1, keepdims=True) / D
            factor = lax.rsqrt(mean + 1e-05)
            gate_act = total[spot, 0:width] * factor
            up_act = total[spot, width:] * factor
            out[spot, :] = (silu(gate_act) * up_act).astype(out.dtype)
            return 0

        lax.fori_loop(0, out.shape[0] // 64, finish, 0)


def hidden_units(me, parts, one_over_gain, gate, up, after=()):
    slots, depth = parts[0][2].shape
    count = lax.axis_size("ctx")
    width = gate.shape[1]
    layout = [(mask, (which or 0) * slots // 2) for mask, which, _ in parts]
    block = pl.BlockSpec((2 * depth, width), lambda k, me: ((me[0] // 2) ^ k, 0))
    return launch(
        functools.partial(hidden_kernel, layout),
        [me],
        [one_over_gain, gate, up] + [part for _, _, part in parts],
        [
            pl.BlockSpec((2, 1, depth), lambda k, me: ((me[0] // 2) ^ k, 0, 0)),
            block,
            block,
        ] + [ANY] * len(parts),
        pl.BlockSpec((slots, width), lambda k, me: (0, 0)),
        jax.ShapeDtypeStruct((slots, width), jnp.bfloat16),
        after=after,
        grid=(count // 2,),
        scratch=[
            pltpu.VMEM((count // 2, slots, 2 * depth), jnp.bfloat16),
            pltpu.VMEM((slots, 2 * width), jnp.float32),
            pltpu.VMEM((slots, LANES), jnp.float32),
            pltpu.SemaphoreType.DMA((len(parts),)),
        ],
        limit=40,
        cost_estimate=cost(
            4 * slots * depth * count * width, 2 * count * depth * (slots + 2 * width)
        ),
        name="hidden_units",
    )


def down_kernel(count, *refs):
    units, weights, (out, held, sems) = refs[:count], refs[count : 2 * count], refs[2 * count :]
    width = weights[0].shape[0]

    @pl.when(pl.program_id(0) == 0)
    def _():
        copies = [
            pltpu.make_async_copy(
                unit, held.at[:, pl.ds(place * width, width)], sems.at[place]
            )
            for place, unit in enumerate(units)
        ]
        for copy in copies:
            copy.start()
        for copy in copies:
            copy.wait()

    tall = jnp.concatenate([weight[...] for weight in weights], axis=0)
    out[...] = jnp.dot(held[...], tall, preferred_element_type=jnp.float32).astype(out.dtype)


def down(units, weights, after=()):
    slots, width = units[0].shape
    columns = weights[0].shape[1]
    depth = width * len(weights)
    tile = min(256, columns)
    return launch(
        functools.partial(down_kernel, len(units)),
        [],
        list(units) + list(weights),
        [ANY] * len(units) + [pl.BlockSpec((width, tile), lambda j: (0, j))] * len(weights),
        pl.BlockSpec((slots, tile), lambda j: (0, j)),
        jax.ShapeDtypeStruct((slots, columns), jnp.bfloat16),
        after=after,
        grid=(columns // tile,),
        scratch=[
            pltpu.VMEM((slots, depth), jnp.bfloat16),
            pltpu.SemaphoreType.DMA((len(units),)),
        ],
        limit=40,
        cost_estimate=cost(
            2 * slots * depth * columns, 2 * (slots * depth + depth * columns + slots * columns)
        ),
        name="down",
    )


def pick_kernel(count, rows, *refs):
    for picks, out in zip(refs[:count], refs[count:]):
        out[...] = lax.dot_general(
            picks[...], rows[...], (((0,), (0,)), ((), ())), preferred_element_type=jnp.float32
        ).astype(out.dtype)


def pick_rows(picks, rows, after=()):
    shape = (picks[0].shape[1], rows.shape[1])
    whole = lambda shape: pl.BlockSpec(shape, lambda j: (0, 0))
    return launch(
        functools.partial(pick_kernel, len(picks)),
        [],
        [rows] + list(picks),
        [whole(rows.shape)] + [whole(pick.shape) for pick in picks],
        [whole(shape)] * len(picks),
        [jax.ShapeDtypeStruct(shape, rows.dtype)] * len(picks),
        after=after,
        limit=24,
        cost_estimate=cost(2 * rows.size * shape[0] * len(picks), 4 * rows.size),
        name="pick_rows",
    )


def combine_kernel(mixer, picks, gates, *refs):
    answers, out = refs[:-1], refs[-1]
    total = mixer[...].astype(jnp.float32)
    for place, answer in enumerate(answers):
        total += gates[place] * jnp.dot(
            picks[place], answer[...], preferred_element_type=jnp.float32
        )
    out[...] = total.astype(out.dtype)


def combine(mixer_out, picks, gates, answers):
    return pl.pallas_call(
        combine_kernel,
        out_shape=jax.ShapeDtypeStruct(mixer_out.shape, jnp.bfloat16),
        compiler_params=pltpu.CompilerParams(vmem_limit_bytes=24 * MIB),
        cost_estimate=cost(
            2 * mixer_out.size * answers[0].shape[0] * len(answers), 4 * mixer_out.size
        ),
        name="combine",
    )(mixer_out, picks, gates, *answers)


def shards(
    mixer_in,
    gate_in,
    delta_in,
    b_proj,
    c_proj,
    conv_kernel,
    conv_bias,
    delta_bias,
    decay_log,
    skip_gain,
    prefix_state,
    prefix_tail,
    out_proj,
    residual,
    norm_gain,
    expert_gate,
    expert_up,
    expert_down,
    expert_ids,
    route_gates,
):
    tokens = mixer_in.shape[0]
    rim = prefix_tail.shape[0]
    ctx_count = lax.axis_size("ctx")
    exp_count = lax.axis_size("exp")
    ctx_me = lax.axis_index("ctx")
    exp_me = lax.axis_index("exp")
    me = ctx_me.astype(jnp.int32).reshape(1)

    rim_rows = from_behind(mixer_in[tokens - rim :], "ctx", 1)
    rim_rows = jnp.where(ctx_me == 0, prefix_tail, rim_rows).astype(jnp.float32)
    rim8 = jnp.pad(rim_rows, ((8 - rim, 0), (0, 0)))

    width = out_proj.shape[1]
    down_rows = expert_down[0]
    down_parts = {}

    def send_columns(masks, after=()):
        for mask, cut in zip(masks, cut_columns(me, down_rows, width, masks, after)):
            down_parts[mask] = cut if mask == 0 else swap(cut, "ctx", mask)
        return tuple(down_parts[mask] for mask in masks)

    first = send_columns([2, 4])

    extra, left = [], norm_gain
    for _ in range(3):
        extra.append(lax.reduce_precision(left, 8, 7))
        left = left - extra[-1]
    extra = jnp.concatenate(extra)
    extra = jnp.pad(extra, (0, mixer_in.shape[1] - extra.shape[0]))[None, :]

    wide = lambda proj: jnp.broadcast_to(proj.T[:, :, None], (tokens, 16, LANES)).reshape(
        tokens * 16, LANES
    )
    b_wide, c_wide = wide(b_proj), wide(c_proj)
    step, conv_act, end = local_states(
        mixer_in,
        rim8,
        delta_in,
        conv_kernel,
        conv_bias[None, :],
        delta_bias[None, :],
        decay_log,
        extra,
        b_wide,
    )
    chunks = 2
    state, ends = prefix_state, gather_parts(join([end], first))
    one_over_gain = inverse_gains(me, ends, width)
    gated = []
    for chunk in range(chunks):
        rows, state = read_out(
            me,
            chunk,
            chunks,
            step,
            conv_act,
            gate_in,
            decay_log,
            skip_gain[None, :],
            b_wide,
            c_wide,
            state,
            ends,
        )
        ends = []
        gated.append(rows)
    gathered, projected, after, order = [], [], gated[-1:], gated[-1:]
    for rows in gated:
        parts = gather_parts(rows, 1, after)
        after = [part for mask, which, part in parts if which is not None and mask % 2 == 0]
        gathered.append(parts)
        partial = project(me, parts, out_proj, order)
        order = [partial]
        projected.append(
            lax.psum_scatter(partial, "exp", scatter_dimension=0, tiled=True)
        )
    last_seen = [part for mask, _, part in gathered[-1] if mask in (2, 4)]
    rest = send_columns([3, 5, 6, 7, 0, 1] + list(range(8, ctx_count)), last_seen)

    block_rows = residual.shape[0]
    owners = block_rows // tokens
    projected = jnp.stack(
        [piece.reshape(owners, tokens // chunks, width) for piece in projected], axis=1
    ).reshape(block_rows, width)
    mixer_out = (residual.astype(jnp.float32) + projected.astype(jnp.float32)).astype(
        jnp.bfloat16
    )
    mixer_wide = mixer_out.astype(jnp.float32)
    scaled = (mixer_wide * norm_gain[None, :]).astype(jnp.bfloat16)
    experts = expert_gate.shape[0] * exp_count
    capacity = 3 * block_rows * expert_ids.shape[1] // (2 * experts)
    spots = jnp.arange(capacity, dtype=jnp.int32)
    picks, gates = [], []
    for mask in range(exp_count):
        named = expert_ids == (exp_me ^ mask)
        here = jnp.any(named, axis=1)
        place = jnp.cumsum(here.astype(jnp.int32)) - 1
        picks.append(here[:, None] & (place[:, None] == spots[None, :]))
        gates.append(jnp.sum(jnp.where(named, route_gates, 0.0), axis=1, keepdims=True))
    picked = [pick.astype(jnp.bfloat16) for pick in picks]

    groups = [[0, 2], [1, 3]] if exp_count == 4 else [list(range(exp_count))]
    last = groups[-1][-1] if len(groups) > 1 else None
    masks = [mask for mask in range(exp_count) if mask != last][::-1]
    rows = dict(zip(masks, pick_rows([picked[mask] for mask in masks], scaled, rest[:3])))
    pieces = {mask: swap(rows[mask], "exp", mask) for mask in masks if mask != 0}
    pieces[0] = rows[0]
    if last is not None:
        (sent,) = pick_rows([picked[last]], scaled, (pieces[groups[0][-1]],))
        pieces[last] = swap(sent, "exp", last)
    hiddens, after = [], rest[3:]
    for group in groups:
        parts = gather_parts(join([pieces[mask] for mask in group], after), 0)
        after = tuple(part for mask, _, part in parts if mask in (2, 4))
        hiddens.append(hidden_units(me, parts, one_over_gain, expert_gate[0], expert_up[0]))
    parts = {mask: part for mask, _, part in gather_parts(join(hiddens))}
    answer = down(
        [parts[mask] for mask in range(ctx_count)],
        [down_parts[mask] for mask in range(ctx_count)],
    )
    answers = {}
    for place, mask in enumerate(mask for group in groups for mask in group):
        piece = lax.slice_in_dim(answer, place * capacity, (place + 1) * capacity, axis=0)
        answers[mask] = piece if mask == 0 else swap(piece, "exp", mask)
    block_out = combine(
        mixer_out,
        jnp.stack(picked),
        jnp.stack(gates),
        [answers[mask] for mask in range(exp_count)],
    )
    return (mixer_out, block_out)


def solution(mesh):
    placed = (
        P("ctx", "exp"),
        P("ctx", "exp"),
        P("ctx", "exp"),
        P(None, "ctx"),
        P(None, "ctx"),
        P(None, "exp"),
        P("exp"),
        P("exp"),
        P(None, "exp"),
        P("exp"),
        P(None, "exp"),
        P(None, "exp"),
        P("exp", "ctx"),
        P("exp", "ctx"),
        P("ctx"),
        P("exp", None, "ctx"),
        P("exp", None, "ctx"),
        P("exp", "ctx", None),
        P("exp", None),
        P("exp", None),
    )
    return jax.shard_map(
        shards,
        mesh=mesh,
        in_specs=placed,
        out_specs=(P("exp", "ctx"), P("exp", "ctx")),
        check_vma=False,
    )
```

time: 581 us -> 403 us (0.69)
  waiting for transfers between devices: 309 us -> 187 us
  Pallas kernels: 0 us -> 90.9 us
  blocking collectives: 53.3 us -> 0 us
  matrix products: 50.4 us -> 0 us
  other arithmetic: 47.2 us -> 12.8 us
  local copies, waits for them, and re-layouts: 60 us -> 26.3 us
  starting transfers between devices: 39.6 us -> 69.7 us
    ppermute x0 -> x63, waiting for transfers between devices: none -> 174 us  [swap(): lax.ppermute(array, axis, [(i, i ^ mask) for i in range(lax.axis_size(axi...]
    all_gather x2 -> x0, waiting for transfers between devices: 138 us -> none  [the longest x1 71.8 us: shards(): piece_rows = lax.all_gather(arrived, 'ctx', axis=1, tiled=True)]
    reduce_scatter x2, waiting for transfers between devices: 131 us -> 12.9 us  [shards(): lax.psum_scatter(partial, 'exp', scatter_dimension=0, tiled=True)]
    pallas_call x0 -> x22, Pallas kernels: none -> 90.9 us  [the longest x21 89.3 us: launch(): pl.pallas_call(body, grid_spec=pltpu.PrefetchScalarGridSpec(num_scalar_pr...]
    ppermute x0 -> x63, starting transfers between devices: none -> 67.7 us  [swap(): lax.ppermute(array, axis, [(i, i ^ mask) for i in range(lax.axis_size(axi...]
    dot_general x6 -> x0, matrix products: 50.4 us -> none  [the longest x1 14.7 us: shards(): jnp.dot(lax.slice_in_dim(gathered, 0, lax.axis_size('exp') * block_rows,...]
    slice x20 -> x3, local copies, waits for them, and re-layouts: 41.8 us -> 1.09 us  [the longest x1 0.86 us: shards(): rim_rows = from_behind(mixer_in[tokens - rim:], 'ctx', 1)]
    all_to_all x1 -> x0, blocking collectives: 39.8 us -> none  [shards(): lax.all_to_all(outgoing, 'exp', split_axis=0, concat_axis=0, tiled=True)]
  transfers between devices with their start and end apart: 13 -> 66, of which waited for: 12 -> 35; matrix products, arithmetic and copies ran while one was open for 1% -> 5% of each run, Pallas kernels for 0% -> 13%
where the time goes in v1:
time: 403 us; the launch traced here: 401 us
  waiting for transfers between devices  187 us (46%)
  Pallas kernels  90.9 us (23%)
  starting transfers between devices  69.7 us (17%)
  local copies, waits for them, and re-layouts  26.3 us (7%)
  between operations  14.8 us (4%)
  other arithmetic  12.8 us (3%)
    ppermute x63, waiting for transfers between devices, swap(): lax.ppermute(array, axis, [(i, i ^ mask) for i in range(lax.axis_size(axi...  174 us
    pallas_call x21, Pallas kernels, launch(): pl.pallas_call(body, grid_spec=pltpu.PrefetchScalarGridSpec(num_scalar_pr...  89.3 us
    ppermute x63, starting transfers between devices, swap(): lax.ppermute(array, axis, [(i, i ^ mask) for i in range(lax.axis_size(axi...  67.7 us
    unnamed x110, local copies, waits for them, and re-layouts  16.4 us
    reduce_scatter x2, waiting for transfers between devices, shards(): lax.psum_scatter(partial, 'exp', scatter_dimension=0, tiled=True)  12.9 us
  transfers between devices with their start and end apart: 66, of which 35 were waited for; matrix products, arithmetic and copies ran while one was open for 5% of the time, Pallas kernels for 13%

profile of v1, /device:TPU:8, one launch (start us, length us, event | category | flops | bytes accessed | tf_op | source)
XLA Modules:
  0.0 401.5 jit_solution(15349802042352751177)
XLA Ops:
  8.1 1.7 collective-permute-start
  9.9 3.4 cut_columns.2
  13.2 1.7 collective-permute-start.1
  14.9 1.5 collective-permute-start.2
  18.0 1.3 broadcast_in_dim.27.refs_8_.refs_6_
  19.3 13.8 %local_states.1 = (f32[128,4096]{1,0:T(8,128)}, f32[128,4096]{1,0:T(8,128)}, bf16[32,4096]{1,0:T(8,128)(2,1)}) custom-call(bf16[128,4096]{1,0:T(8,128)(2,1)} %refs_0_.1, f32[8,4096]{1,0:T(8,128)} %pad_convert_fusion.refs_1_, bf16[128,4096]{1,0:T(8,128)(2,1)} %refs_2_.1, f32[4,4096]{1,0:T(4,128)} %refs_3_.3, f32[1,4096]{1,0:T(1,128)} %bitcast.65, ...), custom_call_target="tpu_custom_call" | custom-call | flops 41943040 | bytes 6291456 | tf_op jit(solution)/shard_map/local_states/pallas_call | solution.py:95
  33.2 2.0 collective-permute-done.2.refs_2_.refs_12_
  37.4 1.8 collective-permute-start.6
  39.2 1.4 collective-permute-start.8
  40.6 5.7 %collective-permute-done.4.refs_11_.refs_3_ = bf16[32,4096]{1,0:T(8,128)(2,1)S(1)} collective-permute-done((bf16[32,4096]{1,0:T(8,128)(2,1)S(1)}, bf16[32,4096]{1,0:T(8,128)(2,1)S(1)}, u32[]{:S(2)}, u32[]{:S(2)}) %collective-permute-start.4) | collective-permute-done | bytes 262176 | tf_op jit(solution)/shard_map/ppermute | solution.py:23
  46.3 5.1 %collective-permute-done.6.refs_13_.refs_5_ = bf16[32,4096]{1,0:T(8,128)(2,1)S(1)} collective-permute-done((bf16[32,4096]{1,0:T(8,128)(2,1)S(1)}, bf16[32,4096]{1,0:T(8,128)(2,1)S(1)}, u32[]{:S(2)}, u32[]{:S(2)}) %collective-permute-start.6) | collective-permute-done | bytes 262176 | tf_op jit(solution)/shard_map/ppermute | solution.py:23
  53.3 1.3 broadcast_in_dim.56.refs_7_
  54.7 9.1 %read_out.2 = (bf16[64,4096]{1,0:T(8,128)(2,1)}, f32[16,4096]{1,0:T(8,128)}) custom-call(s32[1]{0:T(128)} %bitcast.refs_0_, f32[128,4096]{1,0:T(8,128)} %get-tuple-element.27.refs_1_, f32[128,4096]{1,0:T(8,128)} %get-tuple-element.28.refs_2_, bf16[128,4096]{1,0:T(8,128)(2,1)} %refs_3_.5, f32[16,4096]{1,0:T(8,128)} %refs_4_.3, f32[1,4096]{1,0:T(1,128)} %bitcast.56, ...), custom_call_target="tpu_custom_call" | custom-call | flops 29360128 | bytes 3145728 | tf_op jit(solution)/shard_map/read_out/pallas_call | solution.py:95
  63.8 1.6 collective-permute-start.11
  65.9 8.3 %read_out.3 = (bf16[64,4096]{1,0:T(8,128)(2,1)}, f32[16,4096]{1,0:T(8,128)}) custom-call(s32[1]{0:T(128)} %bitcast.refs_0_, f32[128,4096]{1,0:T(8,128)} %get-tuple-element.27.refs_1_, f32[128,4096]{1,0:T(8,128)} %get-tuple-element.28.refs_2_, bf16[128,4096]{1,0:T(8,128)(2,1)} %refs_3_.5, f32[16,4096]{1,0:T(8,128)} %refs_4_.3, f32[1,4096]{1,0:T(1,128)} %bitcast.57, ...), custom_call_target="tpu_custom_call" | custom-call | flops 29360128 | bytes 3145728 | tf_op jit(solution)/shard_map/read_out/pallas_call | solution.py:95
  74.2 3.8 collective-permute-done.11.refs_0_.refs_4_
  78.1 1.2 collective-permute-done.13.refs_1_.refs_6_
  81.0 1.5 collective-permute-start.17
  83.0 4.6 %collective-permute-done.15.refs_8_.refs_2_ = bf16[64,2048]{1,0:T(8,128)(2,1)S(1)} collective-permute-done((bf16[64,2048]{1,0:T(8,128)(2,1)S(1)}, bf16[64,2048]{1,0:T(8,128)(2,1)S(1)}, u32[]{:S(2)}, u32[]{:S(2)}) %collective-permute-start.15) | collective-permute-done | bytes 262176 | tf_op jit(solution)/shard_map/ppermute | solution.py:23
  90.6 3.4 copy-done.35
  94.0 7.4 %project.2.refs_12_ = bf16[512,1024]{1,0:T(8,128)(2,1)} custom-call(s32[1]{0:T(128)} %bitcast.refs_0_, bf16[4096,1024]{1,0:T(8,128)(2,1)S(1)} %copy-done.35, bf16[64,4096]{1,0:T(8,128)(2,1)S(1)} %copy-done.36, bf16[64,4096]{1,0:T(8,128)(2,1)S(1)} %collective-permute-done.10.refs_3_, bf16[64,4096]{1,0:T(8,128)(2,1)S(1)} %collective-permute-done.11.refs_0_.refs_4_, ...), custom_call_target="tpu_custom_call" | custom-call | flops 4294967296 | bytes 13631488 | tf_op jit(solution)/shard_map/project/pallas_call | solution.py:95
  101.7 1.5 collective-permute-start.20
  103.8 11.9 %collective-permute-done.20.refs_0_.refs_4_.refs_7_ = bf16[64,4096]{1,0:T(8,128)(2,1)S(1)} collective-permute-done((bf16[64,4096]{1,0:T(8,128)(2,1)S(1)}, bf16[64,4096]{1,0:T(8,128)(2,1)S(1)}, u32[]{:S(2)}, u32[]{:S(2)}) %collective-permute-start.20) | collective-permute-done | bytes 524320 | tf_op jit(solution)/shard_map/ppermute | solution.py:23
  115.7 1.1 collective-permute-done.22.refs_1_.refs_6_.refs_8_
  117.7 1.2 collective-permute-start.26
  118.9 6.7 %collective-permute-done.24.refs_8_ = bf16[64,2048]{1,0:T(8,128)(2,1)S(1)} collective-permute-done((bf16[64,2048]{1,0:T(8,128)(2,1)S(1)}, bf16[64,2048]{1,0:T(8,128)(2,1)S(1)}, u32[]{:S(2)}, u32[]{:S(2)}) %collective-permute-start.24) | collective-permute-done | bytes 262176 | tf_op jit(solution)/shard_map/ppermute | solution.py:23
  127.7 9.4 %project.3 = bf16[512,1024]{1,0:T(8,128)(2,1)} custom-call(s32[1]{0:T(128)} %bitcast.refs_0_, bf16[4096,1024]{1,0:T(8,128)(2,1)} %refs_1_.3, bf16[64,4096]{1,0:T(8,128)(2,1)S(1)} %copy-done.31, bf16[64,4096]{1,0:T(8,128)(2,1)S(1)} %collective-permute-done.19.refs_3_, bf16[64,4096]{1,0:T(8,128)(2,1)S(1)} %collective-permute-done.20.refs_0_.refs_4_.refs_7_, ...), custom_call_target="tpu_custom_call" | custom-call | flops 4294967296 | bytes 13631488 | tf_op jit(solution)/shard_map/project/pallas_call | solution.py:95
  139.1 5.4 %cut_columns.3 = (bf16[384,1024]{1,0:T(8,128)(2,1)}, bf16[384,1024]{1,0:T(8,128)(2,1)}, bf16[384,1024]{1,0:T(8,128)(2,1)}, bf16[384,1024]{1,0:T(8,128)(2,1)}, bf...) custom-call(s32[1]{0:T(128)} %bitcast.refs_0_, bf16[384,8192]{1,0:T(8,128)(2,1)} %bitcast.46, ...), custom_call_target="tpu_custom_call" | custom-call | bytes 9437184 | tf_op jit(solution)/shard_map/cut_columns/pallas_call | solution.py:95
  144.5 1.1 collective-permute-start.28
  146.3 1.5 collective-permute-start.30
  149.7 12.9 %reduce-scatter.5.cloned.1.call-done = bf16[128,1024]{1,0:T(8,128)(2,1)} async-done(((bf16[512,1024]{1,0:T(8,128)(2,1)}), bf16[128,1024]{1,0:T(8,128)(2,1)}) %reduce-scatter.5.cloned.1.call-update) | async-done | bytes 262160 | tf_op jit(solution)/shard_map/reduce_scatter | solution.py:738
  162.5 1.1 pad_maximum_fusion
  163.6 1.3 multiply_convert_fusion
  165.3 17.5 %collective-permute-done.30.refs_6_.refs_14_ = bf16[384,1024]{1,0:T(8,128)(2,1)} collective-permute-done((bf16[384,1024]{1,0:T(8,128)(2,1)}, bf16[384,1024]{1,0:T(8,128)(2,1)}, u32[]{:S(2)}, u32[]{:S(2)}) %collective-permute-start.30) | collective-permute-done | bytes 786464 | tf_op jit(solution)/shard_map/ppermute | solution.py:23
  187.2 2.7 collective-permute-start.31
  189.9 1.3 convert_bitcast_fusion
  192.8 1.3 reduce-window.51
  194.9 4.1 %collective-permute-done.32.refs_2_.refs_15_ = bf16[384,1024]{1,0:T(8,128)(2,1)} collective-permute-done((bf16[384,1024]{1,0:T(8,128)(2,1)}, bf16[384,1024]{1,0:T(8,128)(2,1)}, u32[]{:S(2)}, u32[]{:S(2)}) %collective-permute-start.32) | collective-permute-done | bytes 786464 | tf_op jit(solution)/shard_map/ppermute | solution.py:23
  199.0 1.1 copy-done.27
  201.5 25.3 %collective-permute-start.35 = (bf16[384,1024]{1,0:T(8,128)(2,1)S(1)}, bf16[384,1024]{1,0:T(8,128)(2,1)S(1)}, u32[]{:S(2)}, u32[]{:S(2)}) collective-permute-start(bf16[384,1024]{1,0:T(8,128)(2,1)S(1)} %join.5.refs_4_), channel_id=1, source_target_pairs={{0,8},{4,12},{8,0},{12,4},{16,24},{20,28},{24,16},{28,20},{1,9},{5... | collective-permute-start | bytes 2359304 | tf_op jit(solution)/shard_map/ppermute | solution.py:23
  230.4 3.0 collective-permute-start.44
  233.4 11.2 %collective-permute-done.35.refs_0_.refs_6_.refs_2_ = bf16[384,1024]{1,0:T(8,128)(2,1)S(1)} collective-permute-done((bf16[384,1024]{1,0:T(8,128)(2,1)S(1)}, bf16[384,1024]{1,0:T(8,128)(2,1)S(1)}, u32[]{:S(2)}, u32[]{:S(2)}) %collective-permute-start.35) | collective-permute-done | bytes 786464 | tf_op jit(solution)/shard_map/ppermute | solution.py:23
  244.6 1.5 collective-permute-done.37.refs_1_.refs_8_.refs_3_
  247.4 2.9 collective-permute-done.44.refs_1_
  252.4 5.8 %collective-permute-done.39.refs_10_ = bf16[192,1024]{1,0:T(8,128)(2,1)S(1)} collective-permute-done((bf16[192,1024]{1,0:T(8,128)(2,1)S(1)}, bf16[192,1024]{1,0:T(8,128)(2,1)S(1)}, u32[]{:S(2)}, u32[]{:S(2)}) %collective-permute-start.39) | collective-permute-done | bytes 393248 | tf_op jit(solution)/shard_map/ppermute | solution.py:23
  259.1 14.6 %collective-permute-done.46.refs_0_.refs_6_ = bf16[384,1024]{1,0:T(8,128)(2,1)S(1)} collective-permute-done((bf16[384,1024]{1,0:T(8,128)(2,1)S(1)}, bf16[384,1024]{1,0:T(8,128)(2,1)S(1)}, u32[]{:S(2)}, u32[]{:S(2)}) %collective-permute-start.46) | collective-permute-done | bytes 786464 | tf_op jit(solution)/shard_map/ppermute | solution.py:23
  274.3 1.1 collective-permute-start.50
  276.8 8.6 %collective-permute-done.50.refs_10_ = bf16[192,1024]{1,0:T(8,128)(2,1)S(1)} collective-permute-done((bf16[192,1024]{1,0:T(8,128)(2,1)S(1)}, bf16[192,1024]{1,0:T(8,128)(2,1)S(1)}, u32[]{:S(2)}, u32[]{:S(2)}) %collective-permute-start.50) | collective-permute-done | bytes 393248 | tf_op jit(solution)/shard_map/ppermute | solution.py:23
  286.2 10.2 %hidden_units.2.refs_0_ = bf16[384,384]{1,0:T(8,128)(2,1)S(1)} custom-call(s32[1]{0:T(128)} %bitcast.refs_0_, f32[8,1,1024]{2,1,0:T(1,128)S(1)} %inverse_gains.1.refs_1_, bf16[8192,384]{1,0:T(8,128)(2,1)S(1)} %bitcast.42, bf16[8192,384]{1,0:T(8,128)(2,1)} %bitcast.52, bf16[384,1024]{1,0:T(8,128)(2,1)S(1)} %join.5.refs_4_, ...), custom_call_target="tpu_custom_call" | custom-call | flops 4831838208 | bytes 18874368 | tf_op jit(solution)/shard_map/hidden_units/pallas_call | solution.py:95
  296.5 10.3 %hidden_units.3.refs_1_ = bf16[384,384]{1,0:T(8,128)(2,1)S(1)} custom-call(s32[1]{0:T(128)} %bitcast.refs_0_, f32[8,1,1024]{2,1,0:T(1,128)S(1)} %inverse_gains.1.refs_1_, bf16[8192,384]{1,0:T(8,128)(2,1)S(1)} %bitcast.43, bf16[8192,384]{1,0:T(8,128)(2,1)} %bitcast.53, bf16[384,1024]{1,0:T(8,128)(2,1)S(1)} %join.6.refs_4_, ...), custom_call_target="tpu_custom_call" | custom-call | flops 4831838208 | bytes 18874368 | tf_op jit(solution)/shard_map/hidden_units/pallas_call | solution.py:95
  308.7 1.8 collective-permute-start.59
  310.5 12.6 %collective-permute-done.55.refs_2_ = bf16[768,384]{1,0:T(8,128)(2,1)S(1)} collective-permute-done((bf16[768,384]{1,0:T(8,128)(2,1)S(1)}, bf16[768,384]{1,0:T(8,128)(2,1)S(1)}, u32[]{:S(2)}, u32[]{:S(2)}) %collective-permute-start.55) | collective-permute-done | bytes 589856 | tf_op jit(solution)/shard_map/ppermute | solution.py:23
  323.7 12.2 %collective-permute-done.59.refs_6_ = bf16[768,384]{1,0:T(8,128)(2,1)} collective-permute-done((bf16[768,384]{1,0:T(8,128)(2,1)S(1)}, bf16[768,384]{1,0:T(8,128)(2,1)}, u32[]{:S(2)}, u32[]{:S(2)}) %collective-permute-start.59) | collective-permute-done | bytes 589856 | tf_op jit(solution)/shard_map/ppermute | solution.py:23
  337.5 1.4 copy.46
  338.9 1.5 copy.45
  341.4 1.1 copy-done.24
  342.5 1.1 copy-done.26
  343.6 1.1 copy-done.28
  344.8 9.4 %down.1 = bf16[768,1024]{1,0:T(8,128)(2,1)S(1)} custom-call(bf16[768,384]{1,0:T(8,128)(2,1)S(1)} %join.7.refs_0_, bf16[768,384]{1,0:T(8,128)(2,1)} %collective-permute-done.54.refs_1_, bf16[768,384]{1,0:T(8,128)(2,1)S(1)} %collective-permute-done.55.refs_2_, bf16[768,384]{1,0:T(8,128)(2,1)} %collective-permute-done.56.refs_3_, ...), custom_call_target="tpu_custom_call" | custom-call | flops 4831838208 | bytes 12582912 | tf_op jit(solution)/shard_map/down/pallas_call | solution.py:95
  355.4 2.8 collective-permute-start.62
  359.1 13.2 %collective-permute-done.61.refs_1_ = bf16[192,1024]{1,0:T(8,128)(2,1)S(1)} collective-permute-done((bf16[192,1024]{1,0:T(8,128)(2,1)S(1)}, bf16[192,1024]{1,0:T(8,128)(2,1)S(1)}, u32[]{:S(2)}, u32[]{:S(2)}) %collective-permute-start.61) | collective-permute-done | bytes 393248 | tf_op jit(solution)/shard_map/ppermute | solution.py:23
  372.3 12.3 %collective-permute-done.62.refs_2_ = bf16[192,1024]{1,0:T(8,128)(2,1)S(1)} collective-permute-done((bf16[192,1024]{1,0:T(8,128)(2,1)S(1)}, bf16[192,1024]{1,0:T(8,128)(2,1)S(1)}, u32[]{:S(2)}, u32[]{:S(2)}) %collective-permute-start.62) | collective-permute-done | bytes 393248 | tf_op jit(solution)/shard_map/ppermute | solution.py:23
  384.6 8.4 %collective-permute-done.63.refs_3_ = bf16[192,1024]{1,0:T(8,128)(2,1)S(1)} collective-permute-done((bf16[192,1024]{1,0:T(8,128)(2,1)S(1)}, bf16[192,1024]{1,0:T(8,128)(2,1)S(1)}, u32[]{:S(2)}, u32[]{:S(2)}) %collective-permute-start.63) | collective-permute-done | bytes 393248 | tf_op jit(solution)/shard_map/ppermute | solution.py:23
  393.1 1.6 combine.1
  (254 shorter events, 46.5 us)
Async XLA Ops:
  7.2 142.5 %reduce-scatter.3.cloned.1.call-start = ((), (), s32[]{:S(2)}) async-start(), calls=%async_computation.2 | async-start | bytes 1310720 | tf_op jit(solution)/shard_map/reduce_scatter | solution.py:738
  8.1 9.2 %collective-permute-start = (bf16[3,4096]{1,0:T(4,128)(2,1)S(1)}, bf16[3,4096]{1,0:T(4,128)(2,1)S(1)}, u32[]{:S(2)}, u32[]{:S(2)}) collective-permute-start(bf16[3,4096]{1,0:T(4,128)(2,1)S(1)} %slice.43), channel_id=1, source_target_pairs={{0,4},{4,8},{8,12},{12,16},{16,20},{20,24},{24,28},{1,5},{5,9},{9,... | collective-permute-start | bytes 73736 | tf_op jit(solution)/shard_map/ppermute | solution.py:19
  13.2 19.9 %collective-permute-start.1 = (bf16[384,1024]{1,0:T(8,128)(2,1)}, bf16[384,1024]{1,0:T(8,128)(2,1)S(1)}, u32[]{:S(2)}, u32[]{:S(2)}) collective-permute-start(bf16[384,1024]{1,0:T(8,128)(2,1)} %get-tuple-element.30), channel_id=1, source_target_pairs={{0,8},{4,12},{8,0},{12,4},{16,24},{20,28},{24,16},{28,20},{1,9},{5... | collective-permute-start | bytes 2359304 | tf_op jit(solution)/shard_map/ppermute | solution.py:23
  14.9 20.3 %collective-permute-start.2 = (bf16[384,1024]{1,0:T(8,128)(2,1)}, bf16[384,1024]{1,0:T(8,128)(2,1)S(1)}, u32[]{:S(2)}, u32[]{:S(2)}) collective-permute-start(bf16[384,1024]{1,0:T(8,128)(2,1)} %get-tuple-element.31), channel_id=1, source_target_pairs={{0,16},{4,20},{8,24},{12,28},{16,0},{20,4},{24,8},{28,12},{1,17},{... | collective-permute-start | bytes 2359304 | tf_op jit(solution)/shard_map/ppermute | solution.py:23
  37.1 9.2 %collective-permute-start.4 = (bf16[32,4096]{1,0:T(8,128)(2,1)S(1)}, bf16[32,4096]{1,0:T(8,128)(2,1)S(1)}, u32[]{:S(2)}, u32[]{:S(2)}) collective-permute-start(bf16[32,4096]{1,0:T(8,128)(2,1)S(1)} %join.4.refs_9_.refs_1_), channel_id=1, source_target_pairs={{0,8},{4,12},{8,0},{12,4},{16,24},{20,28},{24,16},{28,20},{1,9},{5... | collective-permute-start | bytes 786440 | tf_op jit(solution)/shard_map/ppermute | solution.py:23
  37.4 14.0 %collective-permute-start.6 = (bf16[32,4096]{1,0:T(8,128)(2,1)S(1)}, bf16[32,4096]{1,0:T(8,128)(2,1)S(1)}, u32[]{:S(2)}, u32[]{:S(2)}) collective-permute-start(bf16[32,4096]{1,0:T(8,128)(2,1)S(1)} %join.4.refs_9_.refs_1_), channel_id=1, source_target_pairs={{0,16},{4,20},{8,24},{12,28},{16,0},{20,4},{24,8},{28,12},{1,17},{... | collective-permute-start | bytes 786440 | tf_op jit(solution)/shard_map/ppermute | solution.py:23
  39.2 12.2 %collective-permute-start.8 = (bf16[32,4096]{1,0:T(8,128)(2,1)S(1)}, bf16[32,4096]{1,0:T(8,128)(2,1)S(1)}, u32[]{:S(2)}, u32[]{:S(2)}) collective-permute-start(bf16[32,4096]{1,0:T(8,128)(2,1)S(1)} %join.4.refs_9_.refs_1_), channel_id=1, source_target_pairs={{0,24},{4,28},{8,16},{12,20},{16,8},{20,12},{24,0},{28,4},{1,25},{... | collective-permute-start | bytes 786440 | tf_op jit(solution)/shard_map/ppermute | solution.py:23
  40.6 11.4 %collective-permute-start.3 = (bf16[32,4096]{1,0:T(8,128)(2,1)S(1)}, bf16[32,4096]{1,0:T(8,128)(2,1)S(1)}, u32[]{:S(2)}, u32[]{:S(2)}) collective-permute-start(bf16[32,4096]{1,0:T(8,128)(2,1)S(1)} %join.4.refs_9_.refs_1_), channel_id=1, source_target_pairs={{0,4},{4,0},{8,12},{12,8},{16,20},{20,16},{24,28},{28,24},{1,5},{5... | collective-permute-start | bytes 786440 | tf_op jit(solution)/shard_map/ppermute | solution.py:23
  46.3 5.8 %collective-permute-start.5 = (bf16[32,4096]{1,0:T(8,128)(2,1)S(1)}, bf16[32,4096]{1,0:T(8,128)(2,1)S(1)}, u32[]{:S(2)}, u32[]{:S(2)}) collective-permute-start(bf16[32,4096]{1,0:T(8,128)(2,1)S(1)} %collective-permute-done.4.refs_11_.refs_3_), channel_id=1, source_target_pairs={{0,4},{4,0},{8,12},{12,8},{16,20},{20,16},{24,28},{28,24},{1,5},{5... | collective-permute-start | bytes 786440 | tf_op jit(solution)/shard_map/ppermute | solution.py:23
  51.4 1.9 collective-permute-start.9
  63.8 14.2 %collective-permute-start.11 = (bf16[64,4096]{1,0:T(8,128)(2,1)}, bf16[64,4096]{1,0:T(8,128)(2,1)S(1)}, u32[]{:S(2)}, u32[]{:S(2)}) collective-permute-start(bf16[64,4096]{1,0:T(8,128)(2,1)} %get-tuple-element.32.refs_2_), channel_id=1, source_target_pairs={{0,8},{4,12},{8,0},{12,4},{16,24},{20,28},{24,16},{28,20},{1,9},{5... | collective-permute-start | bytes 1572872 | tf_op jit(solution)/shard_map/ppermute | solution.py:23
  65.4 13.9 %collective-permute-start.13 = (bf16[64,4096]{1,0:T(8,128)(2,1)}, bf16[64,4096]{1,0:T(8,128)(2,1)S(1)}, u32[]{:S(2)}, u32[]{:S(2)}) collective-permute-start(bf16[64,4096]{1,0:T(8,128)(2,1)} %get-tuple-element.32.refs_2_), channel_id=1, source_target_pairs={{0,16},{4,20},{8,24},{12,28},{16,0},{20,4},{24,8},{28,12},{1,17},{... | collective-permute-start | bytes 1572872 | tf_op jit(solution)/shard_map/ppermute | solution.py:23
  65.9 22.3 %collective-permute-start.10 = (bf16[64,4096]{1,0:T(8,128)(2,1)}, bf16[64,4096]{1,0:T(8,128)(2,1)S(1)}, u32[]{:S(2)}, u32[]{:S(2)}) collective-permute-start(bf16[64,4096]{1,0:T(8,128)(2,1)} %get-tuple-element.32.refs_2_), channel_id=1, source_target_pairs={{0,4},{4,0},{8,12},{12,8},{16,20},{20,16},{24,28},{28,24},{1,5},{5... | collective-permute-start | bytes 1572872 | tf_op jit(solution)/shard_map/ppermute | solution.py:23
  80.4 7.3 %collective-permute-start.15 = (bf16[64,2048]{1,0:T(8,128)(2,1)S(1)}, bf16[64,2048]{1,0:T(8,128)(2,1)S(1)}, u32[]{:S(2)}, u32[]{:S(2)}) collective-permute-start(bf16[64,2048]{1,0:T(8,128)(2,1)S(1)} %get-tuple-element.35), channel_id=1, source_target_pairs={{0,16},{4,20},{8,24},{12,28},{16,0},{20,4},{24,8},{28,12},{1,17},{... | collective-permute-start | bytes 786440 | tf_op jit(solution)/shard_map/ppermute | solution.py:23
  81.0 7.1 %collective-permute-start.17 = (bf16[64,2048]{1,0:T(8,128)(2,1)S(1)}, bf16[64,2048]{1,0:T(8,128)(2,1)S(1)}, u32[]{:S(2)}, u32[]{:S(2)}) collective-permute-start(bf16[64,2048]{1,0:T(8,128)(2,1)S(1)} %get-tuple-element.36), channel_id=1, source_target_pairs={{0,8},{4,12},{8,0},{12,4},{16,24},{20,28},{24,16},{28,20},{1,9},{5... | collective-permute-start | bytes 786440 | tf_op jit(solution)/shard_map/ppermute | solution.py:23
  82.5 7.1 %collective-permute-start.12 = (bf16[64,4096]{1,0:T(8,128)(2,1)S(1)}, bf16[64,4096]{1,0:T(8,128)(2,1)S(1)}, u32[]{:S(2)}, u32[]{:S(2)}) collective-permute-start(bf16[64,4096]{1,0:T(8,128)(2,1)S(1)} %collective-permute-done.11.refs_0_.refs_4_), channel_id=1, source_target_pairs={{0,4},{4,0},{8,12},{12,8},{16,20},{20,16},{24,28},{28,24},{1,5},{5... | collective-permute-start | bytes 1572872 | tf_op jit(solution)/shard_map/ppermute | solution.py:23
  82.5 7.1 %collective-permute-start.14 = (bf16[64,4096]{1,0:T(8,128)(2,1)S(1)}, bf16[64,4096]{1,0:T(8,128)(2,1)S(1)}, u32[]{:S(2)}, u32[]{:S(2)}) collective-permute-start(bf16[64,4096]{1,0:T(8,128)(2,1)S(1)} %collective-permute-done.13.refs_1_.refs_6_), channel_id=1, source_target_pairs={{0,4},{4,0},{8,12},{12,8},{16,20},{20,16},{24,28},{28,24},{1,5},{5... | collective-permute-start | bytes 1572872 | tf_op jit(solution)/shard_map/ppermute | solution.py:23
  87.7 1.5 collective-permute-start.16
  88.0 1.5 collective-permute-start.18
  101.4 61.1 %reduce-scatter.5.cloned.1.call-start = ((), (), s32[]{:S(2)}) async-start(), calls=%async_computation.3 | async-start | bytes 1310720 | tf_op jit(solution)/shard_map/reduce_scatter | solution.py:738
  101.7 14.0 %collective-permute-start.20 = (bf16[64,4096]{1,0:T(8,128)(2,1)S(1)}, bf16[64,4096]{1,0:T(8,128)(2,1)S(1)}, u32[]{:S(2)}, u32[]{:S(2)}) collective-permute-start(bf16[64,4096]{1,0:T(8,128)(2,1)S(1)} %copy-done.31), channel_id=1, source_target_pairs={{0,8},{4,12},{8,0},{12,4},{16,24},{20,28},{24,16},{28,20},{1,9},{5... | collective-permute-start | bytes 1572872 | tf_op jit(solution)/shard_map/ppermute | solution.py:23
  103.1 13.7 %collective-permute-start.22 = (bf16[64,4096]{1,0:T(8,128)(2,1)S(1)}, bf16[64,4096]{1,0:T(8,128)(2,1)S(1)}, u32[]{:S(2)}, u32[]{:S(2)}) collective-permute-start(bf16[64,4096]{1,0:T(8,128)(2,1)S(1)} %copy-done.31), channel_id=1, source_target_pairs={{0,16},{4,20},{8,24},{12,28},{16,0},{20,4},{24,8},{28,12},{1,17},{... | collective-permute-start | bytes 1572872 | tf_op jit(solution)/shard_map/ppermute | solution.py:23
  103.8 23.0 %collective-permute-start.19 = (bf16[64,4096]{1,0:T(8,128)(2,1)S(1)}, bf16[64,4096]{1,0:T(8,128)(2,1)S(1)}, u32[]{:S(2)}, u32[]{:S(2)}) collective-permute-start(bf16[64,4096]{1,0:T(8,128)(2,1)S(1)} %copy-done.31), channel_id=1, source_target_pairs={{0,4},{4,0},{8,12},{12,8},{16,20},{20,16},{24,28},{28,24},{1,5},{5... | collective-permute-start | bytes 1572872 | tf_op jit(solution)/shard_map/ppermute | solution.py:23
  115.7 11.1 %collective-permute-start.21 = (bf16[64,4096]{1,0:T(8,128)(2,1)S(1)}, bf16[64,4096]{1,0:T(8,128)(2,1)S(1)}, u32[]{:S(2)}, u32[]{:S(2)}) collective-permute-start(bf16[64,4096]{1,0:T(8,128)(2,1)S(1)} %collective-permute-done.20.refs_0_.refs_4_.refs_7_), channel_id=1, source_target_pairs={{0,4},{4,0},{8,12},{12,8},{16,20},{20,16},{24,28},{28,24},{1,5},{5... | collective-permute-start | bytes 1572872 | tf_op jit(solution)/shard_map/ppermute | solution.py:23
  116.8 10.0 %collective-permute-start.23 = (bf16[64,4096]{1,0:T(8,128)(2,1)S(1)}, bf16[64,4096]{1,0:T(8,128)(2,1)}, u32[]{:S(2)}, u32[]{:S(2)}) collective-permute-start(bf16[64,4096]{1,0:T(8,128)(2,1)S(1)} %collective-permute-done.22.refs_1_.refs_6_.refs_8_), channel_id=1, source_target_pairs={{0,4},{4,0},{8,12},{12,8},{16,20},{20,16},{24,28},{28,24},{1,5},{5... | collective-permute-start | bytes 1572872 | tf_op jit(solution)/shard_map/ppermute | solution.py:23
  116.9 8.8 %collective-permute-start.24 = (bf16[64,2048]{1,0:T(8,128)(2,1)S(1)}, bf16[64,2048]{1,0:T(8,128)(2,1)S(1)}, u32[]{:S(2)}, u32[]{:S(2)}) collective-permute-start(bf16[64,2048]{1,0:T(8,128)(2,1)S(1)} %get-tuple-element.37), channel_id=1, source_target_pairs={{0,16},{4,20},{8,24},{12,28},{16,0},{20,4},{24,8},{28,12},{1,17},{... | collective-permute-start | bytes 786440 | tf_op jit(solution)/shard_map/ppermute | solution.py:23
  117.7 8.4 %collective-permute-start.26 = (bf16[64,2048]{1,0:T(8,128)(2,1)S(1)}, bf16[64,2048]{1,0:T(8,128)(2,1)S(1)}, u32[]{:S(2)}, u32[]{:S(2)}) collective-permute-start(bf16[64,2048]{1,0:T(8,128)(2,1)S(1)} %get-tuple-element.38), channel_id=1, source_target_pairs={{0,8},{4,12},{8,0},{12,4},{16,24},{20,28},{24,16},{28,20},{1,9},{5... | collective-permute-start | bytes 786440 | tf_op jit(solution)/shard_map/ppermute | solution.py:23
  126.1 1.7 collective-permute-start.27
  144.5 20.4 %collective-permute-start.28 = (bf16[384,1024]{1,0:T(8,128)(2,1)}, bf16[384,1024]{1,0:T(8,128)(2,1)S(1)}, u32[]{:S(2)}, u32[]{:S(2)}) collective-permute-start(bf16[384,1024]{1,0:T(8,128)(2,1)} %get-tuple-element.39), channel_id=1, source_target_pairs={{0,12},{4,8},{8,4},{12,0},{16,28},{20,24},{24,20},{28,16},{1,13},{... | collective-permute-start | bytes 2359304 | tf_op jit(solution)/shard_map/ppermute | solution.py:23
  145.6 19.7 %collective-permute-start.29 = (bf16[384,1024]{1,0:T(8,128)(2,1)}, bf16[384,1024]{1,0:T(8,128)(2,1)S(1)}, u32[]{:S(2)}, u32[]{:S(2)}) collective-permute-start(bf16[384,1024]{1,0:T(8,128)(2,1)} %get-tuple-element.40), channel_id=1, source_target_pairs={{0,20},{4,16},{8,28},{12,24},{16,4},{20,0},{24,12},{28,8},{1,21},{... | collective-permute-start | bytes 2359304 | tf_op jit(solution)/shard_map/ppermute | solution.py:23
  146.3 36.5 %collective-permute-start.30 = (bf16[384,1024]{1,0:T(8,128)(2,1)}, bf16[384,1024]{1,0:T(8,128)(2,1)}, u32[]{:S(2)}, u32[]{:S(2)}) collective-permute-start(bf16[384,1024]{1,0:T(8,128)(2,1)} %get-tuple-element.41), channel_id=1, source_target_pairs={{0,24},{4,28},{8,16},{12,20},{16,8},{20,12},{24,0},{28,4},{1,25},{... | collective-permute-start | bytes 2359304 | tf_op jit(solution)/shard_map/ppermute | solution.py:23
  148.1 50.9 %collective-permute-start.32 = (bf16[384,1024]{1,0:T(8,128)(2,1)}, bf16[384,1024]{1,0:T(8,128)(2,1)}, u32[]{:S(2)}, u32[]{:S(2)}) collective-permute-start(bf16[384,1024]{1,0:T(8,128)(2,1)} %get-tuple-element.44), channel_id=1, source_target_pairs={{0,28},{4,24},{8,20},{12,16},{16,12},{20,8},{24,4},{28,0},{1,29},{... | collective-permute-start | bytes 2359304 | tf_op jit(solution)/shard_map/ppermute | solution.py:23
  149.0 50.0 %collective-permute-start.33 = (bf16[384,1024]{1,0:T(8,128)(2,1)}, bf16[384,1024]{1,0:T(8,128)(2,1)}, u32[]{:S(2)}, u32[]{:S(2)}) collective-permute-start(bf16[384,1024]{1,0:T(8,128)(2,1)} %get-tuple-element.46), channel_id=1, source_target_pairs={{0,4},{4,0},{8,12},{12,8},{16,20},{20,16},{24,28},{28,24},{1,5},{5... | collective-permute-start | bytes 2359304 | tf_op jit(solution)/shard_map/ppermute | solution.py:23
  187.2 11.8 %collective-permute-start.31 = (bf16[192,1024]{1,0:T(8,128)(2,1)}, bf16[192,1024]{1,0:T(8,128)(2,1)S(1)}, u32[]{:S(2)}, u32[]{:S(2)}) collective-permute-start(bf16[192,1024]{1,0:T(8,128)(2,1)} %get-tuple-element.43), channel_id=1, source_target_pairs={{0,2},{1,3},{2,0},{3,1},{4,6},{5,7},{6,4},{7,5},{8,10},{9,11},{10,... | collective-permute-start | bytes 1179656 | tf_op jit(solution)/shard_map/ppermute | solution.py:23
  201.5 43.1 %collective-permute-start.35 = (bf16[384,1024]{1,0:T(8,128)(2,1)S(1)}, bf16[384,1024]{1,0:T(8,128)(2,1)S(1)}, u32[]{:S(2)}, u32[]{:S(2)}) collective-permute-start(bf16[384,1024]{1,0:T(8,128)(2,1)S(1)} %join.5.refs_4_), channel_id=1, source_target_pairs={{0,8},{4,12},{8,0},{12,4},{16,24},{20,28},{24,16},{28,20},{1,9},{5... | collective-permute-start | bytes 2359304 | tf_op jit(solution)/shard_map/ppermute | solution.py:23
  226.8 19.3 %collective-permute-start.37 = (bf16[384,1024]{1,0:T(8,128)(2,1)S(1)}, bf16[384,1024]{1,0:T(8,128)(2,1)S(1)}, u32[]{:S(2)}, u32[]{:S(2)}) collective-permute-start(bf16[384,1024]{1,0:T(8,128)(2,1)S(1)} %join.5.refs_4_), channel_id=1, source_target_pairs={{0,16},{4,20},{8,24},{12,28},{16,0},{20,4},{24,8},{28,12},{1,17},{... | collective-permute-start | bytes 2359304 | tf_op jit(solution)/shard_map/ppermute | solution.py:23
  229.1 18.3 %collective-permute-start.43 = (bf16[192,1024]{1,0:T(8,128)(2,1)}, bf16[192,1024]{1,0:T(8,128)(2,1)S(1)}, u32[]{:S(2)}, u32[]{:S(2)}) collective-permute-start(bf16[192,1024]{1,0:T(8,128)(2,1)} %copy-done.37), channel_id=1, source_target_pairs={{0,1},{1,0},{2,3},{3,2},{4,5},{5,4},{6,7},{7,6},{8,9},{9,8},{10,11... | collective-permute-start | bytes 1179656 | tf_op jit(solution)/shard_map/ppermute | solution.py:23
  230.4 20.0 %collective-permute-start.44 = (bf16[192,1024]{1,0:T(8,128)(2,1)S(1)}, bf16[192,1024]{1,0:T(8,128)(2,1)S(1)}, u32[]{:S(2)}, u32[]{:S(2)}) collective-permute-start(bf16[192,1024]{1,0:T(8,128)(2,1)S(1)} %pick_rows.3), channel_id=1, source_target_pairs={{0,3},{1,2},{2,1},{3,0},{4,7},{5,6},{6,5},{7,4},{8,11},{9,10},{10,... | collective-permute-start | bytes 1179656 | tf_op jit(solution)/shard_map/ppermute | solution.py:23
  246.1 12.1 %collective-permute-start.39 = (bf16[192,1024]{1,0:T(8,128)(2,1)S(1)}, bf16[192,1024]{1,0:T(8,128)(2,1)S(1)}, u32[]{:S(2)}, u32[]{:S(2)}) collective-permute-start(bf16[192,1024]{1,0:T(8,128)(2,1)S(1)} %get-tuple-element.47), channel_id=1, source_target_pairs={{0,16},{4,20},{8,24},{12,28},{16,0},{20,4},{24,8},{28,12},{1,17},{... | collective-permute-start | bytes 1179656 | tf_op jit(solution)/shard_map/ppermute | solution.py:23
  247.1 12.1 %collective-permute-start.41 = (bf16[192,1024]{1,0:T(8,128)(2,1)S(1)}, bf16[192,1024]{1,0:T(8,128)(2,1)S(1)}, u32[]{:S(2)}, u32[]{:S(2)}) collective-permute-start(bf16[192,1024]{1,0:T(8,128)(2,1)S(1)} %get-tuple-element.48), channel_id=1, source_target_pairs={{0,8},{4,12},{8,0},{12,4},{16,24},{20,28},{24,16},{28,20},{1,9},{5... | collective-permute-start | bytes 1179656 | tf_op jit(solution)/shard_map/ppermute | solution.py:23
  250.8 23.0 %collective-permute-start.46 = (bf16[384,1024]{1,0:T(8,128)(2,1)S(1)}, bf16[384,1024]{1,0:T(8,128)(2,1)S(1)}, u32[]{:S(2)}, u32[]{:S(2)}) collective-permute-start(bf16[384,1024]{1,0:T(8,128)(2,1)S(1)} %join.6.refs_4_), channel_id=1, source_target_pairs={{0,8},{4,12},{8,0},{12,4},{16,24},{20,28},{24,16},{28,20},{1,9},{5... | collective-permute-start | bytes 2359304 | tf_op jit(solution)/shard_map/ppermute | solution.py:23
  251.4 22.4 %collective-permute-start.48 = (bf16[384,1024]{1,0:T(8,128)(2,1)S(1)}, bf16[384,1024]{1,0:T(8,128)(2,1)S(1)}, u32[]{:S(2)}, u32[]{:S(2)}) collective-permute-start(bf16[384,1024]{1,0:T(8,128)(2,1)S(1)} %join.6.refs_4_), channel_id=1, source_target_pairs={{0,16},{4,20},{8,24},{12,28},{16,0},{20,4},{24,8},{28,12},{1,17},{... | collective-permute-start | bytes 2359304 | tf_op jit(solution)/shard_map/ppermute | solution.py:23
  252.4 21.9 %collective-permute-start.34 = (bf16[384,1024]{1,0:T(8,128)(2,1)S(1)}, bf16[384,1024]{1,0:T(8,128)(2,1)S(1)}, u32[]{:S(2)}, u32[]{:S(2)}) collective-permute-start(bf16[384,1024]{1,0:T(8,128)(2,1)S(1)} %join.5.refs_4_), channel_id=1, source_target_pairs={{0,4},{4,0},{8,12},{12,8},{16,20},{20,16},{24,28},{28,24},{1,5},{5... | collective-permute-start | bytes 2359304 | tf_op jit(solution)/shard_map/ppermute | solution.py:23
  258.2 17.2 %collective-permute-start.36 = (bf16[384,1024]{1,0:T(8,128)(2,1)S(1)}, bf16[384,1024]{1,0:T(8,128)(2,1)S(1)}, u32[]{:S(2)}, u32[]{:S(2)}) collective-permute-start(bf16[384,1024]{1,0:T(8,128)(2,1)S(1)} %collective-permute-done.35.refs_0_.refs_6_.refs_2_), channel_id=1, source_target_pairs={{0,4},{4,0},{8,12},{12,8},{16,20},{20,16},{24,28},{28,24},{1,5},{5... | collective-permute-start | bytes 2359304 | tf_op jit(solution)/shard_map/ppermute | solution.py:23
  259.1 17.0 %collective-permute-start.38 = (bf16[384,1024]{1,0:T(8,128)(2,1)S(1)}, bf16[384,1024]{1,0:T(8,128)(2,1)S(1)}, u32[]{:S(2)}, u32[]{:S(2)}) collective-permute-start(bf16[384,1024]{1,0:T(8,128)(2,1)S(1)} %collective-permute-done.37.refs_1_.refs_8_.refs_3_), channel_id=1, source_target_pairs={{0,4},{4,0},{8,12},{12,8},{16,20},{20,16},{24,28},{28,24},{1,5},{5... | collective-permute-start | bytes 2359304 | tf_op jit(solution)/shard_map/ppermute | solution.py:23
  273.7 2.4 collective-permute-start.40
  273.7 2.9 collective-permute-start.42
  274.3 11.1 %collective-permute-start.50 = (bf16[192,1024]{1,0:T(8,128)(2,1)S(1)}, bf16[192,1024]{1,0:T(8,128)(2,1)S(1)}, u32[]{:S(2)}, u32[]{:S(2)}) collective-permute-start(bf16[192,1024]{1,0:T(8,128)(2,1)S(1)} %get-tuple-element.50), channel_id=1, source_target_pairs={{0,16},{4,20},{8,24},{12,28},{16,0},{20,4},{24,8},{28,12},{1,17},{... | collective-permute-start | bytes 1179656 | tf_op jit(solution)/shard_map/ppermute | solution.py:23
  275.4 10.7 %collective-permute-start.52 = (bf16[192,1024]{1,0:T(8,128)(2,1)S(1)}, bf16[192,1024]{1,0:T(8,128)(2,1)S(1)}, u32[]{:S(2)}, u32[]{:S(2)}) collective-permute-start(bf16[192,1024]{1,0:T(8,128)(2,1)S(1)} %get-tuple-element.51), channel_id=1, source_target_pairs={{0,8},{4,12},{8,0},{12,4},{16,24},{20,28},{24,16},{28,20},{1,9},{5... | collective-permute-start | bytes 1179656 | tf_op jit(solution)/shard_map/ppermute | solution.py:23
  276.1 20.3 %collective-permute-start.45 = (bf16[384,1024]{1,0:T(8,128)(2,1)S(1)}, bf16[384,1024]{1,0:T(8,128)(2,1)S(1)}, u32[]{:S(2)}, u32[]{:S(2)}) collective-permute-start(bf16[384,1024]{1,0:T(8,128)(2,1)S(1)} %join.6.refs_4_), channel_id=1, source_target_pairs={{0,4},{4,0},{8,12},{12,8},{16,20},{20,16},{24,28},{28,24},{1,5},{5... | collective-permute-start | bytes 2359304 | tf_op jit(solution)/shard_map/ppermute | solution.py:23
  276.1 20.3 %collective-permute-start.47 = (bf16[384,1024]{1,0:T(8,128)(2,1)S(1)}, bf16[384,1024]{1,0:T(8,128)(2,1)S(1)}, u32[]{:S(2)}, u32[]{:S(2)}) collective-permute-start(bf16[384,1024]{1,0:T(8,128)(2,1)S(1)} %collective-permute-done.46.refs_0_.refs_6_), channel_id=1, source_target_pairs={{0,4},{4,0},{8,12},{12,8},{16,20},{20,16},{24,28},{28,24},{1,5},{5... | collective-permute-start | bytes 2359304 | tf_op jit(solution)/shard_map/ppermute | solution.py:23
  276.6 19.8 %collective-permute-start.49 = (bf16[384,1024]{1,0:T(8,128)(2,1)S(1)}, bf16[384,1024]{1,0:T(8,128)(2,1)S(1)}, u32[]{:S(2)}, u32[]{:S(2)}) collective-permute-start(bf16[384,1024]{1,0:T(8,128)(2,1)S(1)} %collective-permute-done.48.refs_1_.refs_8_), channel_id=1, source_target_pairs={{0,4},{4,0},{8,12},{12,8},{16,20},{20,16},{24,28},{28,24},{1,5},{5... | collective-permute-start | bytes 2359304 | tf_op jit(solution)/shard_map/ppermute | solution.py:23
  285.4 11.1 %collective-permute-start.51 = (bf16[192,1024]{1,0:T(8,128)(2,1)S(1)}, bf16[192,1024]{1,0:T(8,128)(2,1)S(1)}, u32[]{:S(2)}, u32[]{:S(2)}) collective-permute-start(bf16[192,1024]{1,0:T(8,128)(2,1)S(1)} %collective-permute-done.50.refs_10_), channel_id=1, source_target_pairs={{0,4},{4,0},{8,12},{12,8},{16,20},{20,16},{24,28},{28,24},{1,5},{5... | collective-permute-start | bytes 1179656 | tf_op jit(solution)/shard_map/ppermute | solution.py:23
  286.2 10.3 %collective-permute-start.53 = (bf16[192,1024]{1,0:T(8,128)(2,1)S(1)}, bf16[192,1024]{1,0:T(8,128)(2,1)S(1)}, u32[]{:S(2)}, u32[]{:S(2)}) collective-permute-start(bf16[192,1024]{1,0:T(8,128)(2,1)S(1)} %collective-permute-done.52.refs_12_), channel_id=1, source_target_pairs={{0,4},{4,0},{8,12},{12,8},{16,20},{20,16},{24,28},{28,24},{1,5},{5... | collective-permute-start | bytes 1179656 | tf_op jit(solution)/shard_map/ppermute | solution.py:23
  306.9 16.2 %collective-permute-start.55 = (bf16[768,384]{1,0:T(8,128)(2,1)S(1)}, bf16[768,384]{1,0:T(8,128)(2,1)S(1)}, u32[]{:S(2)}, u32[]{:S(2)}) collective-permute-start(bf16[768,384]{1,0:T(8,128)(2,1)S(1)} %join.7.refs_0_), channel_id=1, source_target_pairs={{0,8},{4,12},{8,0},{12,4},{16,24},{20,28},{24,16},{28,20},{1,9},{5... | collective-permute-start | bytes 1769480 | tf_op jit(solution)/shard_map/ppermute | solution.py:23
  307.7 15.9 %collective-permute-start.57 = (bf16[768,384]{1,0:T(8,128)(2,1)S(1)}, bf16[768,384]{1,0:T(8,128)(2,1)}, u32[]{:S(2)}, u32[]{:S(2)}) collective-permute-start(bf16[768,384]{1,0:T(8,128)(2,1)S(1)} %join.7.refs_0_), channel_id=1, source_target_pairs={{0,16},{4,20},{8,24},{12,28},{16,0},{20,4},{24,8},{28,12},{1,17},{... | collective-permute-start | bytes 1769480 | tf_op jit(solution)/shard_map/ppermute | solution.py:23
  308.7 27.2 %collective-permute-start.59 = (bf16[768,384]{1,0:T(8,128)(2,1)S(1)}, bf16[768,384]{1,0:T(8,128)(2,1)}, u32[]{:S(2)}, u32[]{:S(2)}) collective-permute-start(bf16[768,384]{1,0:T(8,128)(2,1)S(1)} %join.7.refs_0_), channel_id=1, source_target_pairs={{0,24},{4,28},{8,16},{12,20},{16,8},{20,12},{24,0},{28,4},{1,25},{... | collective-permute-start | bytes 1769480 | tf_op jit(solution)/shard_map/ppermute | solution.py:23
  310.5 30.8 %collective-permute-start.54 = (bf16[768,384]{1,0:T(8,128)(2,1)S(1)}, bf16[768,384]{1,0:T(8,128)(2,1)}, u32[]{:S(2)}, u32[]{:S(2)}) collective-permute-start(bf16[768,384]{1,0:T(8,128)(2,1)S(1)} %join.7.refs_0_), channel_id=1, source_target_pairs={{0,4},{4,0},{8,12},{12,8},{16,20},{20,16},{24,28},{28,24},{1,5},{5... | collective-permute-start | bytes 1769480 | tf_op jit(solution)/shard_map/ppermute | solution.py:23
  323.1 18.2 %collective-permute-start.56 = (bf16[768,384]{1,0:T(8,128)(2,1)S(1)}, bf16[768,384]{1,0:T(8,128)(2,1)}, u32[]{:S(2)}, u32[]{:S(2)}) collective-permute-start(bf16[768,384]{1,0:T(8,128)(2,1)S(1)} %collective-permute-done.55.refs_2_), channel_id=1, source_target_pairs={{0,4},{4,0},{8,12},{12,8},{16,20},{20,16},{24,28},{28,24},{1,5},{5... | collective-permute-start | bytes 1769480 | tf_op jit(solution)/shard_map/ppermute | solution.py:23
  323.6 17.7 %collective-permute-start.58 = (bf16[768,384]{1,0:T(8,128)(2,1)}, bf16[768,384]{1,0:T(8,128)(2,1)}, u32[]{:S(2)}, u32[]{:S(2)}) collective-permute-start(bf16[768,384]{1,0:T(8,128)(2,1)} %collective-permute-done.57.refs_4_), channel_id=1, source_target_pairs={{0,4},{4,0},{8,12},{12,8},{16,20},{20,16},{24,28},{28,24},{1,5},{5... | collective-permute-start | bytes 1769480 | tf_op jit(solution)/shard_map/ppermute | solution.py:23
  335.9 5.4 %collective-permute-start.60 = (bf16[768,384]{1,0:T(8,128)(2,1)}, bf16[768,384]{1,0:T(8,128)(2,1)}, u32[]{:S(2)}, u32[]{:S(2)}) collective-permute-start(bf16[768,384]{1,0:T(8,128)(2,1)} %collective-permute-done.59.refs_6_), channel_id=1, source_target_pairs={{0,4},{4,0},{8,12},{12,8},{16,20},{20,16},{24,28},{28,24},{1,5},{5... | collective-permute-start | bytes 1769480 | tf_op jit(solution)/shard_map/ppermute | solution.py:23
  354.3 18.0 %collective-permute-start.61 = (bf16[192,1024]{1,0:T(8,128)(2,1)S(1)}, bf16[192,1024]{1,0:T(8,128)(2,1)S(1)}, u32[]{:S(2)}, u32[]{:S(2)}) collective-permute-start(bf16[192,1024]{1,0:T(8,128)(2,1)S(1)} %get-tuple-element.64), channel_id=1, source_target_pairs={{0,1},{1,0},{2,3},{3,2},{4,5},{5,4},{6,7},{7,6},{8,9},{9,8},{10,11... | collective-permute-start | bytes 1179656 | tf_op jit(solution)/shard_map/ppermute | solution.py:23
  355.4 29.2 %collective-permute-start.62 = (bf16[192,1024]{1,0:T(8,128)(2,1)S(1)}, bf16[192,1024]{1,0:T(8,128)(2,1)S(1)}, u32[]{:S(2)}, u32[]{:S(2)}) collective-permute-start(bf16[192,1024]{1,0:T(8,128)(2,1)S(1)} %get-tuple-element.63), channel_id=1, source_target_pairs={{0,2},{1,3},{2,0},{3,1},{4,6},{5,7},{6,4},{7,5},{8,10},{9,11},{10,... | collective-permute-start | bytes 1179656 | tf_op jit(solution)/shard_map/ppermute | solution.py:23
  358.2 34.8 %collective-permute-start.63 = (bf16[192,1024]{1,0:T(8,128)(2,1)S(1)}, bf16[192,1024]{1,0:T(8,128)(2,1)S(1)}, u32[]{:S(2)}, u32[]{:S(2)}) collective-permute-start(bf16[192,1024]{1,0:T(8,128)(2,1)S(1)} %get-tuple-element.62), channel_id=1, source_target_pairs={{0,3},{1,2},{2,1},{3,0},{4,7},{5,6},{6,5},{7,4},{8,11},{9,10},{10,... | collective-permute-start | bytes 1179656 | tf_op jit(solution)/shard_map/ppermute | solution.py:23
  (57 other events, 1691.7 us)
Sparse Core Ops, SparseCore 0:
  101.5 25.2 reduce-scatter.2
  137.3 25.1 reduce-scatter.4

commit v2 on v1

--- a/solution.py
+++ b/solution.py
@@ -46,7 +46,7 @@
         [part, part],
         [jax.ShapeDtypeStruct(tuple(shape), first.dtype)] * 2,
         after=after,
-        limit=16,
+        limit=56,
         cost_estimate=cost(0, 6 * first.size),
         name="halves",
     )
@@ -158,7 +158,7 @@
         jax.ShapeDtypeStruct((rows, columns), pieces[0].dtype),
         after=after,
         scratch=[pltpu.SemaphoreType.DMA((len(pieces),))],
-        limit=16,
+        limit=56,
         cost_estimate=cost(0, 4 * rows * columns),
         name="join",
     )
@@ -288,7 +288,7 @@
         [pl.BlockSpec((16, 3 * width), lambda j, me: (1, 0))] * len(ends),
         pl.BlockSpec((len(ends), 1, width), lambda j, me: (0, 0, 0)),
         jax.ShapeDtypeStruct((len(ends), 1, width), jnp.float32),
-        limit=16,
+        limit=56,
         name="inverse_gains",
     )
 
@@ -447,7 +447,7 @@
             pltpu.VMEM((total, depth), jnp.bfloat16),
             pltpu.SemaphoreType.DMA((len(parts),)),
         ],
-        limit=40,
+        limit=56,
         cost_estimate=cost(
             2 * total * depth * columns, 2 * (total * depth + depth * columns + total * columns)
         ),
@@ -538,7 +538,7 @@
             pltpu.VMEM((slots, LANES), jnp.float32),
             pltpu.SemaphoreType.DMA((len(parts),)),
         ],
-        limit=40,
+        limit=56,
         cost_estimate=cost(
             4 * slots * depth * count * width, 2 * count * depth * (slots + 2 * width)
         ),
@@ -546,18 +546,23 @@
     )
 
 
-def down_kernel(count, *refs):
-    units, weights, (out, held, sems) = refs[:count], refs[count : 2 * count], refs[2 * count :]
-    width = weights[0].shape[0]
+def down_kernel(layout, me, *refs):
+    count = len(layout)
+    units, weights, (out, held, sems) = refs[:count], refs[count:-3], refs[-3:]
+    slots, width = held.shape[0], weights[0].shape[0]
+    rows = slots * len(weights) // count
 
     @pl.when(pl.program_id(0) == 0)
     def _():
-        copies = [
-            pltpu.make_async_copy(
-                unit, held.at[:, pl.ds(place * width, width)], sems.at[place]
+        copies = []
+        for place, (mask, begin, row) in enumerate(layout):
+            copies.append(
+                pltpu.make_async_copy(
+                    units[place].at[pl.ds(begin, rows), :],
+                    held.at[pl.ds(row, rows), pl.ds(mask * width, width)],
+                    sems.at[place],
+                )
             )
-            for place, unit in enumerate(units)
-        ]
         for copy in copies:
             copy.start()
         for copy in copies:
@@ -567,25 +572,34 @@
     out[...] = jnp.dot(held[...], tall, preferred_element_type=jnp.float32).astype(out.dtype)
 
 
-def down(units, weights, after=()):
-    slots, width = units[0].shape
-    columns = weights[0].shape[1]
+def down(me, segments, rows, weights, own, after=()):
+    columns = weights[-1].shape[1]
+    width = own.shape[0]
     depth = width * len(weights)
+    slots = rows * len(segments)
     tile = min(256, columns)
-    return launch(
-        functools.partial(down_kernel, len(units)),
-        [],
-        list(units) + list(weights),
-        [ANY] * len(units) + [pl.BlockSpec((width, tile), lambda j: (0, j))] * len(weights),
-        pl.BlockSpec((slots, tile), lambda j: (0, j)),
+    layout, units = [], []
+    for place, (parts, begin) in enumerate(segments):
+        for mask, part in enumerate(parts):
+            layout.append((mask, begin, place * rows))
+            units.append(part)
+    steps = columns // tile
+    return launch(
+        functools.partial(down_kernel, layout),
+        [me],
+        units + [own] + list(weights[1:]),
+        [ANY] * len(units)
+        + [pl.BlockSpec((width, tile), lambda j, me: (0, me[0] * steps + j))]
+        + [pl.BlockSpec((width, tile), lambda j, me: (0, j))] * (len(weights) - 1),
+        pl.BlockSpec((slots, tile), lambda j, me: (0, j)),
         jax.ShapeDtypeStruct((slots, columns), jnp.bfloat16),
         after=after,
-        grid=(columns // tile,),
+        grid=(steps,),
         scratch=[
             pltpu.VMEM((slots, depth), jnp.bfloat16),
             pltpu.SemaphoreType.DMA((len(units),)),
         ],
-        limit=40,
+        limit=56,
         cost_estimate=cost(
             2 * slots * depth * columns, 2 * (slots * depth + depth * columns + slots * columns)
         ),
@@ -611,32 +625,39 @@
         [whole(shape)] * len(picks),
         [jax.ShapeDtypeStruct(shape, rows.dtype)] * len(picks),
         after=after,
-        limit=24,
+        limit=56,
         cost_estimate=cost(2 * rows.size * shape[0] * len(picks), 4 * rows.size),
         name="pick_rows",
     )
 
 
-def combine_kernel(mixer, picks, gates, *refs):
-    answers, out = refs[:-1], refs[-1]
+def combine_kernel(me, mixer, ids, gates, *refs):
+    out = refs[-1]
+    count = len(refs) // 2
     total = mixer[...].astype(jnp.float32)
-    for place, answer in enumerate(answers):
-        total += gates[place] * jnp.dot(
-            picks[place], answer[...], preferred_element_type=jnp.float32
+    for mask in range(count):
+        named = ids[...] == (me[0] ^ mask)
+        gate = jnp.sum(jnp.where(named, gates[...], 0.0), axis=1, keepdims=True)
+        total += gate * jnp.dot(
+            refs[mask][...], refs[count + mask][...], preferred_element_type=jnp.float32
         )
     out[...] = total.astype(out.dtype)
 
 
-def combine(mixer_out, picks, gates, answers):
-    return pl.pallas_call(
+def combine(me, mixer_out, ids, gates, picks, answers):
+    operands = [mixer_out, ids, gates] + list(picks) + list(answers)
+    return launch(
         combine_kernel,
-        out_shape=jax.ShapeDtypeStruct(mixer_out.shape, jnp.bfloat16),
-        compiler_params=pltpu.CompilerParams(vmem_limit_bytes=24 * MIB),
+        [me],
+        operands,
+        [pl.BlockSpec(array.shape, lambda j, me: (0, 0)) for array in operands],
+        pl.BlockSpec(mixer_out.shape, lambda j, me: (0, 0)),
+        jax.ShapeDtypeStruct(mixer_out.shape, jnp.bfloat16),
         cost_estimate=cost(
             2 * mixer_out.size * answers[0].shape[0] * len(answers), 4 * mixer_out.size
         ),
         name="combine",
-    )(mixer_out, picks, gates, *answers)
+    )
 
 
 def shards(
@@ -682,7 +703,7 @@
             down_parts[mask] = cut if mask == 0 else swap(cut, "ctx", mask)
         return tuple(down_parts[mask] for mask in masks)
 
-    first = send_columns([2, 4])
+    early = send_columns([2, 4, 3, 5])
 
     extra, left = [], norm_gain
     for _ in range(3):
@@ -707,7 +728,7 @@
         b_wide,
     )
     chunks = 2
-    state, ends = prefix_state, gather_parts(join([end], first))
+    state, ends = prefix_state, gather_parts(join([end], early[:2]))
     one_over_gain = inverse_gains(me, ends, width)
     gated = []
     for chunk in range(chunks):
@@ -724,21 +745,21 @@
             c_wide,
             state,
             ends,
+            early[2:],
         )
         ends = []
         gated.append(rows)
-    gathered, projected, after, order = [], [], gated[-1:], gated[-1:]
-    for rows in gated:
-        parts = gather_parts(rows, 1, after)
-        after = [part for mask, which, part in parts if which is not None and mask % 2 == 0]
-        gathered.append(parts)
-        partial = project(me, parts, out_proj, order)
-        order = [partial]
-        projected.append(
-            lax.psum_scatter(partial, "exp", scatter_dimension=0, tiled=True)
-        )
-    last_seen = [part for mask, _, part in gathered[-1] if mask in (2, 4)]
-    rest = send_columns([3, 5, 6, 7, 0, 1] + list(range(8, ctx_count)), last_seen)
+    near = lambda parts: [part for mask, _, part in parts if mask in (2, 4)]
+    far = lambda parts: [part for mask, which, part in parts if which is not None][::2]
+    scatter = lambda rows: lax.psum_scatter(rows, "exp", scatter_dimension=0, tiled=True)
+    front = gather_parts(gated[0], 1, gated[1:])
+    back = gather_parts(gated[1], 1, far(front))
+    partial = project(me, front, out_proj, near(back))
+    projected = [scatter(partial)]
+    (middle,) = send_columns([6], far(front))
+    partial = project(me, back, out_proj, [partial, middle])
+    projected.append(scatter(partial))
+    late = send_columns([7, 1] + list(range(8, ctx_count)), [partial])
 
     block_rows = residual.shape[0]
     owners = block_rows // tokens
@@ -753,42 +774,48 @@
     experts = expert_gate.shape[0] * exp_count
     capacity = 3 * block_rows * expert_ids.shape[1] // (2 * experts)
     spots = jnp.arange(capacity, dtype=jnp.int32)
-    picks, gates = [], []
+    picked = []
     for mask in range(exp_count):
-        named = expert_ids == (exp_me ^ mask)
-        here = jnp.any(named, axis=1)
+        here = jnp.any(expert_ids == (exp_me ^ mask), axis=1)
         place = jnp.cumsum(here.astype(jnp.int32)) - 1
-        picks.append(here[:, None] & (place[:, None] == spots[None, :]))
-        gates.append(jnp.sum(jnp.where(named, route_gates, 0.0), axis=1, keepdims=True))
-    picked = [pick.astype(jnp.bfloat16) for pick in picks]
+        pick = here[:, None] & (place[:, None] == spots[None, :])
+        picked.append(pick.astype(jnp.bfloat16))
 
     groups = [[0, 2], [1, 3]] if exp_count == 4 else [list(range(exp_count))]
     last = groups[-1][-1] if len(groups) > 1 else None
     masks = [mask for mask in range(exp_count) if mask != last][::-1]
-    rows = dict(zip(masks, pick_rows([picked[mask] for mask in masks], scaled, rest[:3])))
+    rows = dict(zip(masks, pick_rows([picked[mask] for mask in masks], scaled, late[:1])))
     pieces = {mask: swap(rows[mask], "exp", mask) for mask in masks if mask != 0}
     pieces[0] = rows[0]
     if last is not None:
         (sent,) = pick_rows([picked[last]], scaled, (pieces[groups[0][-1]],))
         pieces[last] = swap(sent, "exp", last)
-    hiddens, after = [], rest[3:]
+    segments, after, order = {}, late[1:], ()
     for group in groups:
-        parts = gather_parts(join([pieces[mask] for mask in group], after), 0)
-        after = tuple(part for mask, _, part in parts if mask in (2, 4))
-        hiddens.append(hidden_units(me, parts, one_over_gain, expert_gate[0], expert_up[0]))
-    parts = {mask: part for mask, _, part in gather_parts(join(hiddens))}
-    answer = down(
-        [parts[mask] for mask in range(ctx_count)],
-        [down_parts[mask] for mask in range(ctx_count)],
-    )
+        parts = gather_parts(join([pieces[mask] for mask in group], after), 0, order)
+        after = near(parts)
+        hidden = hidden_units(me, parts, one_over_gain, expert_gate[0], expert_up[0])
+        order = [hidden]
+        units = {mask: part for mask, _, part in gather_parts(hidden)}
+        for place, mask in enumerate(group):
+            segments[mask] = ([units[m] for m in range(ctx_count)], place * capacity)
     answers = {}
-    for place, mask in enumerate(mask for group in groups for mask in group):
-        piece = lax.slice_in_dim(answer, place * capacity, (place + 1) * capacity, axis=0)
-        answers[mask] = piece if mask == 0 else swap(piece, "exp", mask)
+    weights = [None] + [down_parts[mask] for mask in range(1, ctx_count)]
+    order = ()
+    for group in [list(range(1, exp_count))[::-1], [0]]:
+        answer = down(
+            me, [segments[mask] for mask in group], capacity, weights, down_rows, order
+        )
+        order = [answer]
+        for place, mask in enumerate(group):
+            piece = lax.slice_in_dim(answer, place * capacity, (place + 1) * capacity, axis=0)
+            answers[mask] = piece if mask == 0 else swap(piece, "exp", mask)
     block_out = combine(
+        exp_me.astype(jnp.int32).reshape(1),
         mixer_out,
-        jnp.stack(picked),
-        jnp.stack(gates),
+        expert_ids,
+        route_gates,
+        picked,
         [answers[mask] for mask in range(exp_count)],
     )
     return (mixer_out, block_out)

time: 403 us -> 414 us (1.027)
  Pallas kernels: 90.9 us -> 128 us
  starting transfers between devices: 69.7 us -> 54.1 us
  local copies, waits for them, and re-layouts: 26.3 us -> 19.9 us
  other arithmetic: 12.8 us -> 7.84 us
    pallas_call x21 -> x23, Pallas kernels: 89.3 us -> 128 us  [launch(): pl.pallas_call(body, grid_spec=pltpu.PrefetchScalarGridSpec(num_scalar_pr...]
    ppermute x63 -> x70, starting transfers between devices: 67.7 us -> 52.1 us  [swap(): lax.ppermute(array, axis, [(i, i ^ mask) for i in range(lax.axis_size(axi...]
    another operation x11 -> x7, local copies, waits for them, and re-layouts: 5.76 us -> 0.68 us  [the longest x4 3.83 us: shards(): jnp.stack(gates)]
    unnamed x110 -> x158, local copies, waits for them, and re-layouts: 16.4 us -> 14 us
    ppermute x63 -> x70, waiting for transfers between devices: 174 us -> 172 us  [swap(): lax.ppermute(array, axis, [(i, i ^ mask) for i in range(lax.axis_size(axi...]
  transfers between devices with their start and end apart: 66 -> 73, of which waited for: 35 -> 34; matrix products, arithmetic and copies ran while one was open for 5% -> 3% of each run, Pallas kernels for 13% -> 23%
where the time goes in v2:
time: 414 us; the launch traced here: 413 us
  waiting for transfers between devices  189 us (46%)
  Pallas kernels  128 us (31%)
  starting transfers between devices  54.1 us (13%)
  local copies, waits for them, and re-layouts  19.9 us (5%)
  between operations  14.8 us (4%)
  other arithmetic  7.84 us (2%)
    ppermute x70, waiting for transfers between devices, swap(): lax.ppermute(array, axis, [(i, i ^ mask) for i in range(lax.axis_size(axi...  172 us
    pallas_call x23, Pallas kernels, launch(): pl.pallas_call(body, grid_spec=pltpu.PrefetchScalarGridSpec(num_scalar_pr...  128 us
    ppermute x70, starting transfers between devices, swap(): lax.ppermute(array, axis, [(i, i ^ mask) for i in range(lax.axis_size(axi...  52.1 us
    reduce_scatter x2, waiting for transfers between devices, shards(): lax.psum_scatter(rows, 'exp', scatter_dimension=0, tiled=True)  16.8 us
    unnamed x158, local copies, waits for them, and re-layouts  14 us
  transfers between devices with their start and end apart: 73, of which 34 were waited for; matrix products, arithmetic and copies ran while one was open for 3% of the time, Pallas kernels for 23%

profile of v2, /device:TPU:8, one launch (start us, length us, event | category | flops | bytes accessed | tf_op | source)
XLA Modules:
  0.0 413.1 jit_solution(4759992800610409312)
XLA Ops:
  8.1 1.7 collective-permute-start
  9.9 4.4 %cut_columns.3 = (bf16[384,1024]{1,0:T(8,128)(2,1)}, bf16[384,1024]{1,0:T(8,128)(2,1)}, bf16[384,1024]{1,0:T(8,128)(2,1)}, bf16[384,1024]{1,0:T(8,128)(2,1)}) custom-call(s32[1]{0:T(128)} %bitcast.refs_0_, bf16[384,8192]{1,0:T(8,128)(2,1)} %bitcast.37, bf16[384,8192]{1,0:T(8,128)(2,1)} %bitcast.38, bf16[384,8192]{1,0:T(8,128)(2,1)} %bitcast.39, ...), custom_call_target="tpu_custom_call" | custom-call | bytes 6291456 | tf_op jit(solution)/shard_map/cut_columns/pallas_call | solution.py:95
  14.2 1.7 collective-permute-start.1
  15.9 1.5 collective-permute-start.2
  21.5 13.9 %local_states.1 = (f32[128,4096]{1,0:T(8,128)}, f32[128,4096]{1,0:T(8,128)}, bf16[32,4096]{1,0:T(8,128)(2,1)}) custom-call(bf16[128,4096]{1,0:T(8,128)(2,1)} %refs_0_.1, f32[8,4096]{1,0:T(8,128)} %pad_convert_fusion.refs_1_, bf16[128,4096]{1,0:T(8,128)(2,1)} %refs_2_.2, f32[4,4096]{1,0:T(4,128)} %refs_3_.4, f32[1,4096]{1,0:T(1,128)} %bitcast.57, ...), custom_call_target="tpu_custom_call" | custom-call | flops 41943040 | bytes 6291456 | tf_op jit(solution)/shard_map/local_states/pallas_call | solution.py:95
  37.1 1.7 join.3.refs_9_.refs_1_
  39.4 1.6 collective-permute-start.6
  41.0 1.4 collective-permute-start.8
  42.4 10.1 %collective-permute-done.10.refs_17_.refs_9_.refs_28_.refs_12_ = bf16[384,1024]{1,0:T(8,128)(2,1)S(1)} collective-permute-done((bf16[384,1024]{1,0:T(8,128)(2,1)}, bf16[384,1024]{1,0:T(8,128)(2,1)S(1)}, u32[]{:S(2)}, u32[]{:S(2)}) %collective-permute-start.10) | collective-permute-done | bytes 786464 | tf_op jit(solution)/shard_map/ppermute | solution.py:23
  52.5 4.1 collective-permute-done.4.refs_11_.refs_3_
  56.6 1.7 collective-permute-start.5
  58.2 6.1 %collective-permute-done.6.refs_13_.refs_5_ = bf16[32,4096]{1,0:T(8,128)(2,1)S(1)} collective-permute-done((bf16[32,4096]{1,0:T(8,128)(2,1)}, bf16[32,4096]{1,0:T(8,128)(2,1)S(1)}, u32[]{:S(2)}, u32[]{:S(2)}) %collective-permute-start.6) | collective-permute-done | bytes 262176 | tf_op jit(solution)/shard_map/ppermute | solution.py:23
  67.6 9.1 %read_out.2 = (bf16[64,4096]{1,0:T(8,128)(2,1)}, f32[16,4096]{1,0:T(8,128)}) custom-call(s32[1]{0:T(128)} %bitcast.refs_0_, f32[128,4096]{1,0:T(8,128)} %get-tuple-element.25.refs_1_, f32[128,4096]{1,0:T(8,128)} %get-tuple-element.26.refs_2_, bf16[128,4096]{1,0:T(8,128)(2,1)} %refs_3_.6, f32[16,4096]{1,0:T(8,128)} %refs_4_.3, f32[1,4096]{1,0:T(1,128)} %bitcast.52, ...), custom_call_target="tpu_custom_call" | custom-call | flops 29360128 | bytes 3145728 | tf_op jit(solution)/shard_map/read_out/pallas_call | solution.py:95
  77.1 1.7 collective-permute-start.15
  78.9 8.3 %read_out.3 = (bf16[64,4096]{1,0:T(8,128)(2,1)}, f32[16,4096]{1,0:T(8,128)}) custom-call(s32[1]{0:T(128)} %bitcast.refs_0_, f32[128,4096]{1,0:T(8,128)} %get-tuple-element.25.refs_1_, f32[128,4096]{1,0:T(8,128)} %get-tuple-element.26.refs_2_, bf16[128,4096]{1,0:T(8,128)(2,1)} %refs_3_.6, f32[16,4096]{1,0:T(8,128)} %refs_4_.3, f32[1,4096]{1,0:T(1,128)} %bitcast.53, ...), custom_call_target="tpu_custom_call" | custom-call | flops 29360128 | bytes 3145728 | tf_op jit(solution)/shard_map/read_out/pallas_call | solution.py:95
  89.2 2.6 collective-permute-done.13.refs_0_.refs_4_
  93.4 2.0 halves.4
  97.7 5.3 %collective-permute-done.21.refs_12_.refs_0_.refs_4_ = bf16[64,4096]{1,0:T(8,128)(2,1)S(1)} collective-permute-done((bf16[64,4096]{1,0:T(8,128)(2,1)}, bf16[64,4096]{1,0:T(8,128)(2,1)S(1)}, u32[]{:S(2)}, u32[]{:S(2)}) %collective-permute-start.21) | collective-permute-done | bytes 524320 | tf_op jit(solution)/shard_map/ppermute | solution.py:23
  103.5 4.4 %collective-permute-done.17.refs_8_.refs_2_ = bf16[64,2048]{1,0:T(8,128)(2,1)S(1)} collective-permute-done((bf16[64,2048]{1,0:T(8,128)(2,1)}, bf16[64,2048]{1,0:T(8,128)(2,1)S(1)}, u32[]{:S(2)}, u32[]{:S(2)}) %collective-permute-start.17) | collective-permute-done | bytes 262176 | tf_op jit(solution)/shard_map/ppermute | solution.py:23
  111.5 10.3 %project.2.refs_12_ = bf16[512,1024]{1,0:T(8,128)(2,1)} custom-call(s32[1]{0:T(128)} %bitcast.refs_0_, bf16[4096,1024]{1,0:T(8,128)(2,1)} %refs_1_.3, bf16[64,4096]{1,0:T(8,128)(2,1)} %get-tuple-element.32.refs_2_, bf16[64,4096]{1,0:T(8,128)(2,1)} %copy-done.70, bf16[64,4096]{1,0:T(8,128)(2,1)} %copy-done.46, bf16[64,4096]{1,0:T(8,128)(2,1)} %copy-done.71, ...), custom_call_target="tpu_custom_call" | custom-call | flops 4294967296 | bytes 13631488 | tf_op jit(solution)/shard_map/project/pallas_call | solution.py:95
  122.3 2.8 cut_columns.4
  125.2 2.2 collective-permute-start.30
  127.9 2.0 halves.5
  131.2 20.5 %collective-permute-done.26.refs_8_ = bf16[64,2048]{1,0:T(8,128)(2,1)S(1)} collective-permute-done((bf16[64,2048]{1,0:T(8,128)(2,1)}, bf16[64,2048]{1,0:T(8,128)(2,1)S(1)}, u32[]{:S(2)}, u32[]{:S(2)}) %collective-permute-start.26) | collective-permute-done | bytes 262176 | tf_op jit(solution)/shard_map/ppermute | solution.py:23
  154.9 10.3 %project.3.refs_3_ = bf16[512,1024]{1,0:T(8,128)(2,1)} custom-call(s32[1]{0:T(128)} %bitcast.refs_0_, bf16[4096,1024]{1,0:T(8,128)(2,1)} %refs_1_.3, bf16[64,4096]{1,0:T(8,128)(2,1)} %get-tuple-element.34.refs_2_, bf16[64,4096]{1,0:T(8,128)(2,1)} %copy-done.69, bf16[64,4096]{1,0:T(8,128)(2,1)} %copy-done.42, ...), custom_call_target="tpu_custom_call" | custom-call | flops 4294967296 | bytes 13631488 | tf_op jit(solution)/shard_map/project/pallas_call | solution.py:95
  167.7 3.4 cut_columns.5
  171.1 1.9 collective-permute-start.31
  174.4 16.8 %reduce-scatter.5.cloned.1.call-done = bf16[128,1024]{1,0:T(8,128)(2,1)} async-done(((bf16[512,1024]{1,0:T(8,128)(2,1)}), bf16[128,1024]{1,0:T(8,128)(2,1)}) %reduce-scatter.5.cloned.1.call-update) | async-done | bytes 262160 | tf_op jit(solution)/shard_map/reduce_scatter | solution.py:754
  194.5 2.5 pick_rows.2
  197.0 2.2 collective-permute-start.32
  199.2 17.2 %collective-permute-done.32.refs_1_.refs_2_ = bf16[192,1024]{1,0:T(8,128)(2,1)S(1)} collective-permute-done((bf16[192,1024]{1,0:T(8,128)(2,1)}, bf16[192,1024]{1,0:T(8,128)(2,1)S(1)}, u32[]{:S(2)}, u32[]{:S(2)}) %collective-permute-start.32) | collective-permute-done | bytes 393248 | tf_op jit(solution)/shard_map/ppermute | solution.py:23
  217.1 2.0 join.4.refs_4_
  220.3 1.5 collective-permute-start.37
  222.5 2.9 collective-permute-start.50
  226.1 2.1 pick_rows.3
  229.2 8.8 %collective-permute-done.35.refs_0_.refs_6_.refs_2_ = bf16[384,1024]{1,0:T(8,128)(2,1)S(1)} collective-permute-done((bf16[384,1024]{1,0:T(8,128)(2,1)}, bf16[384,1024]{1,0:T(8,128)(2,1)S(1)}, u32[]{:S(2)}, u32[]{:S(2)}) %collective-permute-start.35) | collective-permute-done | bytes 786464 | tf_op jit(solution)/shard_map/ppermute | solution.py:23
  239.7 2.3 halves.6
  243.5 4.6 %collective-permute-done.51.refs_1_ = bf16[192,1024]{1,0:T(8,128)(2,1)S(1)} collective-permute-done((bf16[192,1024]{1,0:T(8,128)(2,1)}, bf16[192,1024]{1,0:T(8,128)(2,1)S(1)}, u32[]{:S(2)}, u32[]{:S(2)}) %collective-permute-start.51) | collective-permute-done | bytes 393248 | tf_op jit(solution)/shard_map/ppermute | solution.py:23
  248.8 2.0 join.5.refs_4_
  250.9 1.4 collective-permute-start.53
  252.8 7.6 %collective-permute-done.41.refs_12_ = bf16[192,1024]{1,0:T(8,128)(2,1)S(1)} collective-permute-done((bf16[192,1024]{1,0:T(8,128)(2,1)}, bf16[192,1024]{1,0:T(8,128)(2,1)S(1)}, u32[]{:S(2)}, u32[]{:S(2)}) %collective-permute-start.41) | collective-permute-done | bytes 393248 | tf_op jit(solution)/shard_map/ppermute | solution.py:23
  261.0 2.1 inverse_gains.1.refs_1_
  263.1 12.5 %collective-permute-done.53.refs_0_.refs_6_ = bf16[384,1024]{1,0:T(8,128)(2,1)S(1)} collective-permute-done((bf16[384,1024]{1,0:T(8,128)(2,1)}, bf16[384,1024]{1,0:T(8,128)(2,1)S(1)}, u32[]{:S(2)}, u32[]{:S(2)}) %collective-permute-start.53) | collective-permute-done | bytes 786464 | tf_op jit(solution)/shard_map/ppermute | solution.py:23
  277.0 12.3 %hidden_units.2.refs_2_.refs_9_.refs_1_ = bf16[384,384]{1,0:T(8,128)(2,1)} custom-call(s32[1]{0:T(128)} %bitcast.refs_0_, f32[8,1,1024]{2,1,0:T(1,128)} %inverse_gains.1.refs_1_, bf16[8192,384]{1,0:T(8,128)(2,1)} %bitcast.46, bf16[8192,384]{1,0:T(8,128)(2,1)} %bitcast.48, bf16[384,1024]{1,0:T(8,128)(2,1)} %join.4.refs_4_, bf16[384,1024]{1,0:T(8,128)(2,1)} %copy-done.35, ...), custom_call_target="tpu_custom_call" | custom-call | flops 4831838208 | bytes 18874368 | tf_op jit(solution)/shard_map/hidden_units/pallas_call | solution.py:95
  289.4 2.3 halves.7
  292.8 1.4 collective-permute-start.44
  294.3 8.8 %collective-permute-done.57.refs_10_ = bf16[192,1024]{1,0:T(8,128)(2,1)S(1)} collective-permute-done((bf16[192,1024]{1,0:T(8,128)(2,1)}, bf16[192,1024]{1,0:T(8,128)(2,1)S(1)}, u32[]{:S(2)}, u32[]{:S(2)}) %collective-permute-start.57) | collective-permute-done | bytes 393248 | tf_op jit(solution)/shard_map/ppermute | solution.py:23
  303.1 1.3 collective-permute-done.59.refs_12_
  304.4 5.2 %collective-permute-done.44.refs_11_.refs_3_ = bf16[384,384]{1,0:T(8,128)(2,1)S(1)} collective-permute-done((bf16[384,384]{1,0:T(8,128)(2,1)}, bf16[384,384]{1,0:T(8,128)(2,1)S(1)}, u32[]{:S(2)}, u32[]{:S(2)}) %collective-permute-start.44) | collective-permute-done | bytes 294944 | tf_op jit(solution)/shard_map/ppermute | solution.py:23
  309.7 1.5 collective-permute-start.46
  311.2 6.7 %collective-permute-done.46.refs_13_.refs_5_ = bf16[384,384]{1,0:T(8,128)(2,1)S(1)} collective-permute-done((bf16[384,384]{1,0:T(8,128)(2,1)}, bf16[384,384]{1,0:T(8,128)(2,1)S(1)}, u32[]{:S(2)}, u32[]{:S(2)}) %collective-permute-start.46) | collective-permute-done | bytes 294944 | tf_op jit(solution)/shard_map/ppermute | solution.py:23
  317.9 1.6 collective-permute-start.48
  321.2 12.4 %hidden_units.3.refs_1_.refs_17_ = bf16[384,384]{1,0:T(8,128)(2,1)} custom-call(s32[1]{0:T(128)} %bitcast.refs_0_, f32[8,1,1024]{2,1,0:T(1,128)} %inverse_gains.1.refs_1_, bf16[8192,384]{1,0:T(8,128)(2,1)} %bitcast.47, bf16[8192,384]{1,0:T(8,128)(2,1)} %bitcast.49, bf16[384,1024]{1,0:T(8,128)(2,1)} %join.5.refs_4_, bf16[384,1024]{1,0:T(8,128)(2,1)} %copy-done.36, ...), custom_call_target="tpu_custom_call" | custom-call | flops 4831838208 | bytes 18874368 | tf_op jit(solution)/shard_map/hidden_units/pallas_call | solution.py:95
  333.7 1.5 collective-permute-start.62
  335.7 1.5 collective-permute-start.66
  337.7 6.0 %collective-permute-done.62.refs_3_.refs_19_ = bf16[384,384]{1,0:T(8,128)(2,1)S(1)} collective-permute-done((bf16[384,384]{1,0:T(8,128)(2,1)}, bf16[384,384]{1,0:T(8,128)(2,1)S(1)}, u32[]{:S(2)}, u32[]{:S(2)}) %collective-permute-start.62) | collective-permute-done | bytes 294944 | tf_op jit(solution)/shard_map/ppermute | solution.py:23
  343.8 6.8 %collective-permute-done.64.refs_5_.refs_21_ = bf16[384,384]{1,0:T(8,128)(2,1)S(1)} collective-permute-done((bf16[384,384]{1,0:T(8,128)(2,1)}, bf16[384,384]{1,0:T(8,128)(2,1)S(1)}, u32[]{:S(2)}, u32[]{:S(2)}) %collective-permute-start.64) | collective-permute-done | bytes 294944 | tf_op jit(solution)/shard_map/ppermute | solution.py:23
  353.6 9.4 %down.2.refs_17_ = bf16[576,1024]{1,0:T(8,128)(2,1)} custom-call(s32[1]{0:T(128)} %bitcast.refs_0_, bf16[384,384]{1,0:T(8,128)(2,1)} %hidden_units.3.refs_1_.refs_17_, bf16[384,384]{1,0:T(8,128)(2,1)} %copy-done.22, bf16[384,384]{1,0:T(8,128)(2,1)} %copy-done.19, bf16[384,384]{1,0:T(8,128)(2,1)} %copy-done.23, bf16[384,384]{1,0:T(8,128)(2,1)} %copy-done.20, ...), custom_call_target="tpu_custom_call" | custom-call | flops 3623878656 | bytes 11010048 | tf_op jit(solution)/shard_map/down/pallas_call | solution.py:95
  364.7 2.1 collective-permute-start.69
  369.5 6.7 %down.3.refs_8_ = bf16[192,1024]{1,0:T(8,128)(2,1)} custom-call(s32[1]{0:T(128)} %bitcast.refs_0_, bf16[384,384]{1,0:T(8,128)(2,1)} %hidden_units.2.refs_2_.refs_9_.refs_1_, bf16[384,384]{1,0:T(8,128)(2,1)} %copy-done.14, bf16[384,384]{1,0:T(8,128)(2,1)} %copy-done.12, bf16[384,384]{1,0:T(8,128)(2,1)} %copy-done.16, bf16[384,384]{1,0:T(8,128)(2,1)} %copy-done.13, ...), custom_call_target="tpu_custom_call" | custom-call | flops 1207959552 | bytes 7864320 | tf_op jit(solution)/shard_map/down/pallas_call | solution.py:95
  376.2 4.7 %collective-permute-done.68.refs_9_ = bf16[192,1024]{1,0:T(8,128)(2,1)S(1)} collective-permute-done((bf16[192,1024]{1,0:T(8,128)(2,1)S(1)}, bf16[192,1024]{1,0:T(8,128)(2,1)S(1)}, u32[]{:S(2)}, u32[]{:S(2)}) %collective-permute-start.68) | collective-permute-done | bytes 393248 | tf_op jit(solution)/shard_map/ppermute | solution.py:23
  380.9 12.3 %collective-permute-done.69.refs_10_ = bf16[192,1024]{1,0:T(8,128)(2,1)S(1)} collective-permute-done((bf16[192,1024]{1,0:T(8,128)(2,1)S(1)}, bf16[192,1024]{1,0:T(8,128)(2,1)S(1)}, u32[]{:S(2)}, u32[]{:S(2)}) %collective-permute-start.69) | collective-permute-done | bytes 393248 | tf_op jit(solution)/shard_map/ppermute | solution.py:23
  393.2 8.9 %collective-permute-done.70.refs_11_ = bf16[192,1024]{1,0:T(8,128)(2,1)S(1)} collective-permute-done((bf16[192,1024]{1,0:T(8,128)(2,1)S(1)}, bf16[192,1024]{1,0:T(8,128)(2,1)S(1)}, u32[]{:S(2)}, u32[]{:S(2)}) %collective-permute-start.70) | collective-permute-done | bytes 393248 | tf_op jit(solution)/shard_map/ppermute | solution.py:23
  402.8 3.4 combine.1
  (306 shorter events, 56.4 us)
Async XLA Ops:
  7.2 167.2 %reduce-scatter.3.cloned.1.call-start = ((), (), s32[]{:S(2)}) async-start(), calls=%async_computation.2 | async-start | bytes 1310720 | tf_op jit(solution)/shard_map/reduce_scatter | solution.py:754
  8.1 11.3 %collective-permute-start = (bf16[3,4096]{1,0:T(4,128)(2,1)S(1)}, bf16[3,4096]{1,0:T(4,128)(2,1)S(1)}, u32[]{:S(2)}, u32[]{:S(2)}) collective-permute-start(bf16[3,4096]{1,0:T(4,128)(2,1)S(1)} %slice.40), channel_id=1, source_target_pairs={{0,4},{4,8},{8,12},{12,16},{16,20},{20,24},{24,28},{1,5},{5,9},{9,... | collective-permute-start | bytes 73736 | tf_op jit(solution)/shard_map/ppermute | solution.py:19
  14.2 21.1 %collective-permute-start.1 = (bf16[384,1024]{1,0:T(8,128)(2,1)}, bf16[384,1024]{1,0:T(8,128)(2,1)S(1)}, u32[]{:S(2)}, u32[]{:S(2)}) collective-permute-start(bf16[384,1024]{1,0:T(8,128)(2,1)} %get-tuple-element.28), channel_id=1, source_target_pairs={{0,8},{4,12},{8,0},{12,4},{16,24},{20,28},{24,16},{28,20},{1,9},{5... | collective-permute-start | bytes 2359304 | tf_op jit(solution)/shard_map/ppermute | solution.py:23
  15.9 20.3 %collective-permute-start.2 = (bf16[384,1024]{1,0:T(8,128)(2,1)}, bf16[384,1024]{1,0:T(8,128)(2,1)S(1)}, u32[]{:S(2)}, u32[]{:S(2)}) collective-permute-start(bf16[384,1024]{1,0:T(8,128)(2,1)} %get-tuple-element.29), channel_id=1, source_target_pairs={{0,16},{4,20},{8,24},{12,28},{16,0},{20,4},{24,8},{28,12},{1,17},{... | collective-permute-start | bytes 2359304 | tf_op jit(solution)/shard_map/ppermute | solution.py:23
  17.4 35.1 %collective-permute-start.10 = (bf16[384,1024]{1,0:T(8,128)(2,1)}, bf16[384,1024]{1,0:T(8,128)(2,1)S(1)}, u32[]{:S(2)}, u32[]{:S(2)}) collective-permute-start(bf16[384,1024]{1,0:T(8,128)(2,1)} %get-tuple-element.30), channel_id=1, source_target_pairs={{0,12},{4,8},{8,4},{12,0},{16,28},{20,24},{24,20},{28,16},{1,13},{... | collective-permute-start | bytes 2359304 | tf_op jit(solution)/shard_map/ppermute | solution.py:23
  18.6 46.4 %collective-permute-start.11 = (bf16[384,1024]{1,0:T(8,128)(2,1)}, bf16[384,1024]{1,0:T(8,128)(2,1)S(1)}, u32[]{:S(2)}, u32[]{:S(2)}) collective-permute-start(bf16[384,1024]{1,0:T(8,128)(2,1)} %get-tuple-element.31), channel_id=1, source_target_pairs={{0,20},{4,16},{8,28},{12,24},{16,4},{20,0},{24,12},{28,8},{1,21},{... | collective-permute-start | bytes 2359304 | tf_op jit(solution)/shard_map/ppermute | solution.py:23
  38.8 17.8 %collective-permute-start.4 = (bf16[32,4096]{1,0:T(8,128)(2,1)}, bf16[32,4096]{1,0:T(8,128)(2,1)S(1)}, u32[]{:S(2)}, u32[]{:S(2)}) collective-permute-start(bf16[32,4096]{1,0:T(8,128)(2,1)} %join.3.refs_9_.refs_1_), channel_id=1, source_target_pairs={{0,8},{4,12},{8,0},{12,4},{16,24},{20,28},{24,16},{28,20},{1,9},{5... | collective-permute-start | bytes 786440 | tf_op jit(solution)/shard_map/ppermute | solution.py:23
  39.4 24.9 %collective-permute-start.6 = (bf16[32,4096]{1,0:T(8,128)(2,1)}, bf16[32,4096]{1,0:T(8,128)(2,1)S(1)}, u32[]{:S(2)}, u32[]{:S(2)}) collective-permute-start(bf16[32,4096]{1,0:T(8,128)(2,1)} %join.3.refs_9_.refs_1_), channel_id=1, source_target_pairs={{0,16},{4,20},{8,24},{12,28},{16,0},{20,4},{24,8},{28,12},{1,17},{... | collective-permute-start | bytes 786440 | tf_op jit(solution)/shard_map/ppermute | solution.py:23
  41.0 23.5 %collective-permute-start.8 = (bf16[32,4096]{1,0:T(8,128)(2,1)}, bf16[32,4096]{1,0:T(8,128)(2,1)S(1)}, u32[]{:S(2)}, u32[]{:S(2)}) collective-permute-start(bf16[32,4096]{1,0:T(8,128)(2,1)} %join.3.refs_9_.refs_1_), channel_id=1, source_target_pairs={{0,24},{4,28},{8,16},{12,20},{16,8},{20,12},{24,0},{28,4},{1,25},{... | collective-permute-start | bytes 786440 | tf_op jit(solution)/shard_map/ppermute | solution.py:23
  52.5 12.5 %collective-permute-start.3 = (bf16[32,4096]{1,0:T(8,128)(2,1)}, bf16[32,4096]{1,0:T(8,128)(2,1)S(1)}, u32[]{:S(2)}, u32[]{:S(2)}) collective-permute-start(bf16[32,4096]{1,0:T(8,128)(2,1)} %join.3.refs_9_.refs_1_), channel_id=1, source_target_pairs={{0,4},{4,0},{8,12},{12,8},{16,20},{20,16},{24,28},{28,24},{1,5},{5... | collective-permute-start | bytes 786440 | tf_op jit(solution)/shard_map/ppermute | solution.py:23
  56.6 8.5 %collective-permute-start.5 = (bf16[32,4096]{1,0:T(8,128)(2,1)S(1)}, bf16[32,4096]{1,0:T(8,128)(2,1)S(1)}, u32[]{:S(2)}, u32[]{:S(2)}) collective-permute-start(bf16[32,4096]{1,0:T(8,128)(2,1)S(1)} %collective-permute-done.4.refs_11_.refs_3_), channel_id=1, source_target_pairs={{0,4},{4,0},{8,12},{12,8},{16,20},{20,16},{24,28},{28,24},{1,5},{5... | collective-permute-start | bytes 786440 | tf_op jit(solution)/shard_map/ppermute | solution.py:23
  76.7 15.0 %collective-permute-start.13 = (bf16[64,4096]{1,0:T(8,128)(2,1)}, bf16[64,4096]{1,0:T(8,128)(2,1)S(1)}, u32[]{:S(2)}, u32[]{:S(2)}) collective-permute-start(bf16[64,4096]{1,0:T(8,128)(2,1)} %get-tuple-element.32.refs_2_), channel_id=1, source_target_pairs={{0,8},{4,12},{8,0},{12,4},{16,24},{20,28},{24,16},{28,20},{1,9},{5... | collective-permute-start | bytes 1572872 | tf_op jit(solution)/shard_map/ppermute | solution.py:23
  77.1 14.6 %collective-permute-start.15 = (bf16[64,4096]{1,0:T(8,128)(2,1)}, bf16[64,4096]{1,0:T(8,128)(2,1)S(1)}, u32[]{:S(2)}, u32[]{:S(2)}) collective-permute-start(bf16[64,4096]{1,0:T(8,128)(2,1)} %get-tuple-element.32.refs_2_), channel_id=1, source_target_pairs={{0,16},{4,20},{8,24},{12,28},{16,0},{20,4},{24,8},{28,12},{1,17},{... | collective-permute-start | bytes 1572872 | tf_op jit(solution)/shard_map/ppermute | solution.py:23
  87.2 15.9 %collective-permute-start.21 = (bf16[64,4096]{1,0:T(8,128)(2,1)}, bf16[64,4096]{1,0:T(8,128)(2,1)S(1)}, u32[]{:S(2)}, u32[]{:S(2)}) collective-permute-start(bf16[64,4096]{1,0:T(8,128)(2,1)} %get-tuple-element.34.refs_2_), channel_id=1, source_target_pairs={{0,8},{4,12},{8,0},{12,4},{16,24},{20,28},{24,16},{28,20},{1,9},{5... | collective-permute-start | bytes 1572872 | tf_op jit(solution)/shard_map/ppermute | solution.py:23
  88.2 15.1 %collective-permute-start.22 = (bf16[64,4096]{1,0:T(8,128)(2,1)}, bf16[64,4096]{1,0:T(8,128)(2,1)S(1)}, u32[]{:S(2)}, u32[]{:S(2)}) collective-permute-start(bf16[64,4096]{1,0:T(8,128)(2,1)} %get-tuple-element.34.refs_2_), channel_id=1, source_target_pairs={{0,16},{4,20},{8,24},{12,28},{16,0},{20,4},{24,8},{28,12},{1,17},{... | collective-permute-start | bytes 1572872 | tf_op jit(solution)/shard_map/ppermute | solution.py:23
  89.2 19.3 %collective-permute-start.12 = (bf16[64,4096]{1,0:T(8,128)(2,1)S(1)}, bf16[64,4096]{1,0:T(8,128)(2,1)S(1)}, u32[]{:S(2)}, u32[]{:S(2)}) collective-permute-start(bf16[64,4096]{1,0:T(8,128)(2,1)S(1)} %copy-done.68), channel_id=1, source_target_pairs={{0,4},{4,0},{8,12},{12,8},{16,20},{20,16},{24,28},{28,24},{1,5},{5... | collective-permute-start | bytes 1572872 | tf_op jit(solution)/shard_map/ppermute | solution.py:23
  95.4 12.6 %collective-permute-start.17 = (bf16[64,2048]{1,0:T(8,128)(2,1)}, bf16[64,2048]{1,0:T(8,128)(2,1)S(1)}, u32[]{:S(2)}, u32[]{:S(2)}) collective-permute-start(bf16[64,2048]{1,0:T(8,128)(2,1)} %get-tuple-element.35), channel_id=1, source_target_pairs={{0,16},{4,20},{8,24},{12,28},{16,0},{20,4},{24,8},{28,12},{1,17},{... | collective-permute-start | bytes 786440 | tf_op jit(solution)/shard_map/ppermute | solution.py:23
  96.7 11.3 %collective-permute-start.19 = (bf16[64,2048]{1,0:T(8,128)(2,1)}, bf16[64,2048]{1,0:T(8,128)(2,1)S(1)}, u32[]{:S(2)}, u32[]{:S(2)}) collective-permute-start(bf16[64,2048]{1,0:T(8,128)(2,1)} %get-tuple-element.36), channel_id=1, source_target_pairs={{0,8},{4,12},{8,0},{12,4},{16,24},{20,28},{24,16},{28,20},{1,9},{5... | collective-permute-start | bytes 786440 | tf_op jit(solution)/shard_map/ppermute | solution.py:23
  103.0 6.8 %collective-permute-start.14 = (bf16[64,4096]{1,0:T(8,128)(2,1)}, bf16[64,4096]{1,0:T(8,128)(2,1)S(1)}, u32[]{:S(2)}, u32[]{:S(2)}) collective-permute-start(bf16[64,4096]{1,0:T(8,128)(2,1)} %copy-done.46), channel_id=1, source_target_pairs={{0,4},{4,0},{8,12},{12,8},{16,20},{20,16},{24,28},{28,24},{1,5},{5... | collective-permute-start | bytes 1572872 | tf_op jit(solution)/shard_map/ppermute | solution.py:23
  121.9 69.4 %reduce-scatter.5.cloned.1.call-start = ((), (), s32[]{:S(2)}) async-start(), calls=%async_computation.3 | async-start | bytes 1310720 | tf_op jit(solution)/shard_map/reduce_scatter | solution.py:754
  122.1 8.7 %collective-permute-start.23 = (bf16[64,4096]{1,0:T(8,128)(2,1)S(1)}, bf16[64,4096]{1,0:T(8,128)(2,1)S(1)}, u32[]{:S(2)}, u32[]{:S(2)}) collective-permute-start(bf16[64,4096]{1,0:T(8,128)(2,1)S(1)} %copy-done.41), channel_id=1, source_target_pairs={{0,4},{4,0},{8,12},{12,8},{16,20},{20,16},{24,28},{28,24},{1,5},{5... | collective-permute-start | bytes 1572872 | tf_op jit(solution)/shard_map/ppermute | solution.py:23
  125.2 28.6 %collective-permute-start.30 = (bf16[384,1024]{1,0:T(8,128)(2,1)}, bf16[384,1024]{1,0:T(8,128)(2,1)S(1)}, u32[]{:S(2)}, u32[]{:S(2)}) collective-permute-start(bf16[384,1024]{1,0:T(8,128)(2,1)} %cut_columns.4), channel_id=1, source_target_pairs={{0,24},{4,28},{8,16},{12,20},{16,8},{20,12},{24,0},{28,4},{1,25},{... | collective-permute-start | bytes 2359304 | tf_op jit(solution)/shard_map/ppermute | solution.py:23
  127.3 24.9 %collective-permute-start.24 = (bf16[64,4096]{1,0:T(8,128)(2,1)S(1)}, bf16[64,4096]{1,0:T(8,128)(2,1)}, u32[]{:S(2)}, u32[]{:S(2)}) collective-permute-start(bf16[64,4096]{1,0:T(8,128)(2,1)S(1)} %copy-done.43), channel_id=1, source_target_pairs={{0,4},{4,0},{8,12},{12,8},{16,20},{20,16},{24,28},{28,24},{1,5},{5... | collective-permute-start | bytes 1572872 | tf_op jit(solution)/shard_map/ppermute | solution.py:23
  127.4 24.9 %collective-permute-start.25 = (bf16[64,4096]{1,0:T(8,128)(2,1)S(1)}, bf16[64,4096]{1,0:T(8,128)(2,1)}, u32[]{:S(2)}, u32[]{:S(2)}) collective-permute-start(bf16[64,4096]{1,0:T(8,128)(2,1)S(1)} %copy-done.45), channel_id=1, source_target_pairs={{0,4},{4,0},{8,12},{12,8},{16,20},{20,16},{24,28},{28,24},{1,5},{5... | collective-permute-start | bytes 1572872 | tf_op jit(solution)/shard_map/ppermute | solution.py:23
  129.9 21.8 %collective-permute-start.26 = (bf16[64,2048]{1,0:T(8,128)(2,1)}, bf16[64,2048]{1,0:T(8,128)(2,1)S(1)}, u32[]{:S(2)}, u32[]{:S(2)}) collective-permute-start(bf16[64,2048]{1,0:T(8,128)(2,1)} %get-tuple-element.37), channel_id=1, source_target_pairs={{0,16},{4,20},{8,24},{12,28},{16,0},{20,4},{24,8},{28,12},{1,17},{... | collective-permute-start | bytes 786440 | tf_op jit(solution)/shard_map/ppermute | solution.py:23
  130.9 21.2 %collective-permute-start.28 = (bf16[64,2048]{1,0:T(8,128)(2,1)}, bf16[64,2048]{1,0:T(8,128)(2,1)S(1)}, u32[]{:S(2)}, u32[]{:S(2)}) collective-permute-start(bf16[64,2048]{1,0:T(8,128)(2,1)} %get-tuple-element.38), channel_id=1, source_target_pairs={{0,8},{4,12},{8,0},{12,4},{16,24},{20,28},{24,16},{28,20},{1,9},{5... | collective-permute-start | bytes 786440 | tf_op jit(solution)/shard_map/ppermute | solution.py:23
  171.1 22.5 %collective-permute-start.31 = (bf16[384,1024]{1,0:T(8,128)(2,1)}, bf16[384,1024]{1,0:T(8,128)(2,1)S(1)}, u32[]{:S(2)}, u32[]{:S(2)}) collective-permute-start(bf16[384,1024]{1,0:T(8,128)(2,1)} %get-tuple-element.39), channel_id=1, source_target_pairs={{0,28},{4,24},{8,20},{12,16},{16,12},{20,8},{24,4},{28,0},{1,29},{... | collective-permute-start | bytes 2359304 | tf_op jit(solution)/shard_map/ppermute | solution.py:23
  174.0 25.1 %collective-permute-start.33 = (bf16[384,1024]{1,0:T(8,128)(2,1)}, bf16[384,1024]{1,0:T(8,128)(2,1)S(1)}, u32[]{:S(2)}, u32[]{:S(2)}) collective-permute-start(bf16[384,1024]{1,0:T(8,128)(2,1)} %get-tuple-element.42), channel_id=1, source_target_pairs={{0,4},{4,0},{8,12},{12,8},{16,20},{20,16},{24,28},{28,24},{1,5},{5... | collective-permute-start | bytes 2359304 | tf_op jit(solution)/shard_map/ppermute | solution.py:23
  197.0 19.4 %collective-permute-start.32 = (bf16[192,1024]{1,0:T(8,128)(2,1)}, bf16[192,1024]{1,0:T(8,128)(2,1)S(1)}, u32[]{:S(2)}, u32[]{:S(2)}) collective-permute-start(bf16[192,1024]{1,0:T(8,128)(2,1)} %get-tuple-element.41), channel_id=1, source_target_pairs={{0,2},{1,3},{2,0},{3,1},{4,6},{5,7},{6,4},{7,5},{8,10},{9,11},{10,... | collective-permute-start | bytes 1179656 | tf_op jit(solution)/shard_map/ppermute | solution.py:23
  219.1 18.8 %collective-permute-start.35 = (bf16[384,1024]{1,0:T(8,128)(2,1)}, bf16[384,1024]{1,0:T(8,128)(2,1)S(1)}, u32[]{:S(2)}, u32[]{:S(2)}) collective-permute-start(bf16[384,1024]{1,0:T(8,128)(2,1)} %join.4.refs_4_), channel_id=1, source_target_pairs={{0,8},{4,12},{8,0},{12,4},{16,24},{20,28},{24,16},{28,20},{1,9},{5... | collective-permute-start | bytes 2359304 | tf_op jit(solution)/shard_map/ppermute | solution.py:23
  220.3 18.0 %collective-permute-start.37 = (bf16[384,1024]{1,0:T(8,128)(2,1)}, bf16[384,1024]{1,0:T(8,128)(2,1)S(1)}, u32[]{:S(2)}, u32[]{:S(2)}) collective-permute-start(bf16[384,1024]{1,0:T(8,128)(2,1)} %join.4.refs_4_), channel_id=1, source_target_pairs={{0,16},{4,20},{8,24},{12,28},{16,0},{20,4},{24,8},{28,12},{1,17},{... | collective-permute-start | bytes 2359304 | tf_op jit(solution)/shard_map/ppermute | solution.py:23
  222.3 28.6 %collective-permute-start.34 = (bf16[384,1024]{1,0:T(8,128)(2,1)}, bf16[384,1024]{1,0:T(8,128)(2,1)S(1)}, u32[]{:S(2)}, u32[]{:S(2)}) collective-permute-start(bf16[384,1024]{1,0:T(8,128)(2,1)} %join.4.refs_4_), channel_id=1, source_target_pairs={{0,4},{4,0},{8,12},{12,8},{16,20},{20,16},{24,28},{28,24},{1,5},{5... | collective-permute-start | bytes 2359304 | tf_op jit(solution)/shard_map/ppermute | solution.py:23
  222.5 20.6 %collective-permute-start.50 = (bf16[192,1024]{1,0:T(8,128)(2,1)}, bf16[192,1024]{1,0:T(8,128)(2,1)S(1)}, u32[]{:S(2)}, u32[]{:S(2)}) collective-permute-start(bf16[192,1024]{1,0:T(8,128)(2,1)} %get-tuple-element.45), channel_id=1, source_target_pairs={{0,1},{1,0},{2,3},{3,2},{4,5},{5,4},{6,7},{7,6},{8,9},{9,8},{10,11... | collective-permute-start | bytes 1179656 | tf_op jit(solution)/shard_map/ppermute | solution.py:23
  228.2 19.9 %collective-permute-start.51 = (bf16[192,1024]{1,0:T(8,128)(2,1)}, bf16[192,1024]{1,0:T(8,128)(2,1)S(1)}, u32[]{:S(2)}, u32[]{:S(2)}) collective-permute-start(bf16[192,1024]{1,0:T(8,128)(2,1)} %pick_rows.3), channel_id=1, source_target_pairs={{0,3},{1,2},{2,1},{3,0},{4,7},{5,6},{6,5},{7,4},{8,11},{9,10},{10,... | collective-permute-start | bytes 1179656 | tf_op jit(solution)/shard_map/ppermute | solution.py:23
  242.0 10.2 %collective-permute-start.39 = (bf16[192,1024]{1,0:T(8,128)(2,1)}, bf16[192,1024]{1,0:T(8,128)(2,1)S(1)}, u32[]{:S(2)}, u32[]{:S(2)}) collective-permute-start(bf16[192,1024]{1,0:T(8,128)(2,1)} %get-tuple-element.43), channel_id=1, source_target_pairs={{0,16},{4,20},{8,24},{12,28},{16,0},{20,4},{24,8},{28,12},{1,17},{... | collective-permute-start | bytes 1179656 | tf_op jit(solution)/shard_map/ppermute | solution.py:23
  243.0 17.4 %collective-permute-start.36 = (bf16[384,1024]{1,0:T(8,128)(2,1)}, bf16[384,1024]{1,0:T(8,128)(2,1)S(1)}, u32[]{:S(2)}, u32[]{:S(2)}) collective-permute-start(bf16[384,1024]{1,0:T(8,128)(2,1)} %copy-done.6), channel_id=1, source_target_pairs={{0,4},{4,0},{8,12},{12,8},{16,20},{20,16},{24,28},{28,24},{1,5},{5... | collective-permute-start | bytes 2359304 | tf_op jit(solution)/shard_map/ppermute | solution.py:23
  243.0 17.9 %collective-permute-start.38 = (bf16[384,1024]{1,0:T(8,128)(2,1)}, bf16[384,1024]{1,0:T(8,128)(2,1)S(1)}, u32[]{:S(2)}, u32[]{:S(2)}) collective-permute-start(bf16[384,1024]{1,0:T(8,128)(2,1)} %copy-done.7), channel_id=1, source_target_pairs={{0,4},{4,0},{8,12},{12,8},{16,20},{20,16},{24,28},{28,24},{1,5},{5... | collective-permute-start | bytes 2359304 | tf_op jit(solution)/shard_map/ppermute | solution.py:23
  248.1 12.3 %collective-permute-start.41 = (bf16[192,1024]{1,0:T(8,128)(2,1)}, bf16[192,1024]{1,0:T(8,128)(2,1)S(1)}, u32[]{:S(2)}, u32[]{:S(2)}) collective-permute-start(bf16[192,1024]{1,0:T(8,128)(2,1)} %get-tuple-element.44), channel_id=1, source_target_pairs={{0,8},{4,12},{8,0},{12,4},{16,24},{20,28},{24,16},{28,20},{1,9},{5... | collective-permute-start | bytes 1179656 | tf_op jit(solution)/shard_map/ppermute | solution.py:23
  250.9 24.7 %collective-permute-start.53 = (bf16[384,1024]{1,0:T(8,128)(2,1)}, bf16[384,1024]{1,0:T(8,128)(2,1)S(1)}, u32[]{:S(2)}, u32[]{:S(2)}) collective-permute-start(bf16[384,1024]{1,0:T(8,128)(2,1)} %join.5.refs_4_), channel_id=1, source_target_pairs={{0,8},{4,12},{8,0},{12,4},{16,24},{20,28},{24,16},{28,20},{1,9},{5... | collective-permute-start | bytes 2359304 | tf_op jit(solution)/shard_map/ppermute | solution.py:23
  252.3 23.3 %collective-permute-start.55 = (bf16[384,1024]{1,0:T(8,128)(2,1)}, bf16[384,1024]{1,0:T(8,128)(2,1)S(1)}, u32[]{:S(2)}, u32[]{:S(2)}) collective-permute-start(bf16[384,1024]{1,0:T(8,128)(2,1)} %join.5.refs_4_), channel_id=1, source_target_pairs={{0,16},{4,20},{8,24},{12,28},{16,0},{20,4},{24,8},{28,12},{1,17},{... | collective-permute-start | bytes 2359304 | tf_op jit(solution)/shard_map/ppermute | solution.py:23
  260.4 15.7 %collective-permute-start.40 = (bf16[192,1024]{1,0:T(8,128)(2,1)S(1)}, bf16[192,1024]{1,0:T(8,128)(2,1)S(1)}, u32[]{:S(2)}, u32[]{:S(2)}) collective-permute-start(bf16[192,1024]{1,0:T(8,128)(2,1)S(1)} %collective-permute-done.39.refs_10_), channel_id=1, source_target_pairs={{0,4},{4,0},{8,12},{12,8},{16,20},{20,16},{24,28},{28,24},{1,5},{5... | collective-permute-start | bytes 1179656 | tf_op jit(solution)/shard_map/ppermute | solution.py:23
  260.4 15.7 %collective-permute-start.42 = (bf16[192,1024]{1,0:T(8,128)(2,1)S(1)}, bf16[192,1024]{1,0:T(8,128)(2,1)S(1)}, u32[]{:S(2)}, u32[]{:S(2)}) collective-permute-start(bf16[192,1024]{1,0:T(8,128)(2,1)S(1)} %collective-permute-done.41.refs_12_), channel_id=1, source_target_pairs={{0,4},{4,0},{8,12},{12,8},{16,20},{20,16},{24,28},{28,24},{1,5},{5... | collective-permute-start | bytes 1179656 | tf_op jit(solution)/shard_map/ppermute | solution.py:23
  260.9 31.9 %collective-permute-start.52 = (bf16[384,1024]{1,0:T(8,128)(2,1)}, bf16[384,1024]{1,0:T(8,128)(2,1)S(1)}, u32[]{:S(2)}, u32[]{:S(2)}) collective-permute-start(bf16[384,1024]{1,0:T(8,128)(2,1)} %join.5.refs_4_), channel_id=1, source_target_pairs={{0,4},{4,0},{8,12},{12,8},{16,20},{20,16},{24,28},{28,24},{1,5},{5... | collective-permute-start | bytes 2359304 | tf_op jit(solution)/shard_map/ppermute | solution.py:23
  275.6 42.3 %collective-permute-start.54 = (bf16[384,1024]{1,0:T(8,128)(2,1)S(1)}, bf16[384,1024]{1,0:T(8,128)(2,1)S(1)}, u32[]{:S(2)}, u32[]{:S(2)}) collective-permute-start(bf16[384,1024]{1,0:T(8,128)(2,1)S(1)} %collective-permute-done.53.refs_0_.refs_6_), channel_id=1, source_target_pairs={{0,4},{4,0},{8,12},{12,8},{16,20},{20,16},{24,28},{28,24},{1,5},{5... | collective-permute-start | bytes 2359304 | tf_op jit(solution)/shard_map/ppermute | solution.py:23
  275.6 43.8 %collective-permute-start.56 = (bf16[384,1024]{1,0:T(8,128)(2,1)S(1)}, bf16[384,1024]{1,0:T(8,128)(2,1)S(1)}, u32[]{:S(2)}, u32[]{:S(2)}) collective-permute-start(bf16[384,1024]{1,0:T(8,128)(2,1)S(1)} %collective-permute-done.55.refs_1_.refs_8_), channel_id=1, source_target_pairs={{0,4},{4,0},{8,12},{12,8},{16,20},{20,16},{24,28},{28,24},{1,5},{5... | collective-permute-start | bytes 2359304 | tf_op jit(solution)/shard_map/ppermute | solution.py:23
  291.7 11.4 %collective-permute-start.57 = (bf16[192,1024]{1,0:T(8,128)(2,1)}, bf16[192,1024]{1,0:T(8,128)(2,1)S(1)}, u32[]{:S(2)}, u32[]{:S(2)}) collective-permute-start(bf16[192,1024]{1,0:T(8,128)(2,1)} %get-tuple-element.46), channel_id=1, source_target_pairs={{0,16},{4,20},{8,24},{12,28},{16,0},{20,4},{24,8},{28,12},{1,17},{... | collective-permute-start | bytes 1179656 | tf_op jit(solution)/shard_map/ppermute | solution.py:23
  292.2 12.2 %collective-permute-start.59 = (bf16[192,1024]{1,0:T(8,128)(2,1)}, bf16[192,1024]{1,0:T(8,128)(2,1)S(1)}, u32[]{:S(2)}, u32[]{:S(2)}) collective-permute-start(bf16[192,1024]{1,0:T(8,128)(2,1)} %get-tuple-element.47), channel_id=1, source_target_pairs={{0,8},{4,12},{8,0},{12,4},{16,24},{20,28},{24,16},{28,20},{1,9},{5... | collective-permute-start | bytes 1179656 | tf_op jit(solution)/shard_map/ppermute | solution.py:23
  292.8 16.9 %collective-permute-start.44 = (bf16[384,384]{1,0:T(8,128)(2,1)}, bf16[384,384]{1,0:T(8,128)(2,1)S(1)}, u32[]{:S(2)}, u32[]{:S(2)}) collective-permute-start(bf16[384,384]{1,0:T(8,128)(2,1)} %hidden_units.2.refs_2_.refs_9_.refs_1_), channel_id=1, source_target_pairs={{0,8},{4,12},{8,0},{12,4},{16,24},{20,28},{24,16},{28,20},{1,9},{5... | collective-permute-start | bytes 884744 | tf_op jit(solution)/shard_map/ppermute | solution.py:23
  303.1 16.5 %collective-permute-start.58 = (bf16[192,1024]{1,0:T(8,128)(2,1)S(1)}, bf16[192,1024]{1,0:T(8,128)(2,1)S(1)}, u32[]{:S(2)}, u32[]{:S(2)}) collective-permute-start(bf16[192,1024]{1,0:T(8,128)(2,1)S(1)} %collective-permute-done.57.refs_10_), channel_id=1, source_target_pairs={{0,4},{4,0},{8,12},{12,8},{16,20},{20,16},{24,28},{28,24},{1,5},{5... | collective-permute-start | bytes 1179656 | tf_op jit(solution)/shard_map/ppermute | solution.py:23
  304.4 15.5 %collective-permute-start.60 = (bf16[192,1024]{1,0:T(8,128)(2,1)S(1)}, bf16[192,1024]{1,0:T(8,128)(2,1)S(1)}, u32[]{:S(2)}, u32[]{:S(2)}) collective-permute-start(bf16[192,1024]{1,0:T(8,128)(2,1)S(1)} %collective-permute-done.59.refs_12_), channel_id=1, source_target_pairs={{0,4},{4,0},{8,12},{12,8},{16,20},{20,16},{24,28},{28,24},{1,5},{5... | collective-permute-start | bytes 1179656 | tf_op jit(solution)/shard_map/ppermute | solution.py:23
  309.7 8.2 %collective-permute-start.46 = (bf16[384,384]{1,0:T(8,128)(2,1)}, bf16[384,384]{1,0:T(8,128)(2,1)S(1)}, u32[]{:S(2)}, u32[]{:S(2)}) collective-permute-start(bf16[384,384]{1,0:T(8,128)(2,1)} %hidden_units.2.refs_2_.refs_9_.refs_1_), channel_id=1, source_target_pairs={{0,16},{4,20},{8,24},{12,28},{16,0},{20,4},{24,8},{28,12},{1,17},{... | collective-permute-start | bytes 884744 | tf_op jit(solution)/shard_map/ppermute | solution.py:23
  317.9 17.3 %collective-permute-start.43 = (bf16[384,384]{1,0:T(8,128)(2,1)}, bf16[384,384]{1,0:T(8,128)(2,1)S(1)}, u32[]{:S(2)}, u32[]{:S(2)}) collective-permute-start(bf16[384,384]{1,0:T(8,128)(2,1)} %hidden_units.2.refs_2_.refs_9_.refs_1_), channel_id=1, source_target_pairs={{0,4},{4,0},{8,12},{12,8},{16,20},{20,16},{24,28},{28,24},{1,5},{5... | collective-permute-start | bytes 884744 | tf_op jit(solution)/shard_map/ppermute | solution.py:23
  317.9 17.9 %collective-permute-start.48 = (bf16[384,384]{1,0:T(8,128)(2,1)}, bf16[384,384]{1,0:T(8,128)(2,1)S(1)}, u32[]{:S(2)}, u32[]{:S(2)}) collective-permute-start(bf16[384,384]{1,0:T(8,128)(2,1)} %hidden_units.2.refs_2_.refs_9_.refs_1_), channel_id=1, source_target_pairs={{0,24},{4,28},{8,16},{12,20},{16,8},{20,12},{24,0},{28,4},{1,25},{... | collective-permute-start | bytes 884744 | tf_op jit(solution)/shard_map/ppermute | solution.py:23
  319.4 17.8 %collective-permute-start.45 = (bf16[384,384]{1,0:T(8,128)(2,1)S(1)}, bf16[384,384]{1,0:T(8,128)(2,1)S(1)}, u32[]{:S(2)}, u32[]{:S(2)}) collective-permute-start(bf16[384,384]{1,0:T(8,128)(2,1)S(1)} %collective-permute-done.44.refs_11_.refs_3_), channel_id=1, source_target_pairs={{0,4},{4,0},{8,12},{12,8},{16,20},{20,16},{24,28},{28,24},{1,5},{5... | collective-permute-start | bytes 884744 | tf_op jit(solution)/shard_map/ppermute | solution.py:23
  319.6 17.6 %collective-permute-start.47 = (bf16[384,384]{1,0:T(8,128)(2,1)S(1)}, bf16[384,384]{1,0:T(8,128)(2,1)S(1)}, u32[]{:S(2)}, u32[]{:S(2)}) collective-permute-start(bf16[384,384]{1,0:T(8,128)(2,1)S(1)} %collective-permute-done.46.refs_13_.refs_5_), channel_id=1, source_target_pairs={{0,4},{4,0},{8,12},{12,8},{16,20},{20,16},{24,28},{28,24},{1,5},{5... | collective-permute-start | bytes 884744 | tf_op jit(solution)/shard_map/ppermute | solution.py:23
  333.7 10.1 %collective-permute-start.62 = (bf16[384,384]{1,0:T(8,128)(2,1)}, bf16[384,384]{1,0:T(8,128)(2,1)S(1)}, u32[]{:S(2)}, u32[]{:S(2)}) collective-permute-start(bf16[384,384]{1,0:T(8,128)(2,1)} %hidden_units.3.refs_1_.refs_17_), channel_id=1, source_target_pairs={{0,8},{4,12},{8,0},{12,4},{16,24},{20,28},{24,16},{28,20},{1,9},{5... | collective-permute-start | bytes 884744 | tf_op jit(solution)/shard_map/ppermute | solution.py:23
  335.2 15.4 %collective-permute-start.64 = (bf16[384,384]{1,0:T(8,128)(2,1)}, bf16[384,384]{1,0:T(8,128)(2,1)S(1)}, u32[]{:S(2)}, u32[]{:S(2)}) collective-permute-start(bf16[384,384]{1,0:T(8,128)(2,1)} %hidden_units.3.refs_1_.refs_17_), channel_id=1, source_target_pairs={{0,16},{4,20},{8,24},{12,28},{16,0},{20,4},{24,8},{28,12},{1,17},{... | collective-permute-start | bytes 884744 | tf_op jit(solution)/shard_map/ppermute | solution.py:23
  335.7 14.9 %collective-permute-start.66 = (bf16[384,384]{1,0:T(8,128)(2,1)}, bf16[384,384]{1,0:T(8,128)(2,1)S(1)}, u32[]{:S(2)}, u32[]{:S(2)}) collective-permute-start(bf16[384,384]{1,0:T(8,128)(2,1)} %hidden_units.3.refs_1_.refs_17_), channel_id=1, source_target_pairs={{0,24},{4,28},{8,16},{12,20},{16,8},{20,12},{24,0},{28,4},{1,25},{... | collective-permute-start | bytes 884744 | tf_op jit(solution)/shard_map/ppermute | solution.py:23
  337.2 13.9 %collective-permute-start.49 = (bf16[384,384]{1,0:T(8,128)(2,1)S(1)}, bf16[384,384]{1,0:T(8,128)(2,1)S(1)}, u32[]{:S(2)}, u32[]{:S(2)}) collective-permute-start(bf16[384,384]{1,0:T(8,128)(2,1)S(1)} %collective-permute-done.48.refs_15_.refs_7_), channel_id=1, source_target_pairs={{0,4},{4,0},{8,12},{12,8},{16,20},{20,16},{24,28},{28,24},{1,5},{5... | collective-permute-start | bytes 884744 | tf_op jit(solution)/shard_map/ppermute | solution.py:23
  337.3 13.9 %collective-permute-start.61 = (bf16[384,384]{1,0:T(8,128)(2,1)}, bf16[384,384]{1,0:T(8,128)(2,1)S(1)}, u32[]{:S(2)}, u32[]{:S(2)}) collective-permute-start(bf16[384,384]{1,0:T(8,128)(2,1)} %hidden_units.3.refs_1_.refs_17_), channel_id=1, source_target_pairs={{0,4},{4,0},{8,12},{12,8},{16,20},{20,16},{24,28},{28,24},{1,5},{5... | collective-permute-start | bytes 884744 | tf_op jit(solution)/shard_map/ppermute | solution.py:23
  343.8 7.3 %collective-permute-start.63 = (bf16[384,384]{1,0:T(8,128)(2,1)S(1)}, bf16[384,384]{1,0:T(8,128)(2,1)S(1)}, u32[]{:S(2)}, u32[]{:S(2)}) collective-permute-start(bf16[384,384]{1,0:T(8,128)(2,1)S(1)} %collective-permute-done.62.refs_3_.refs_19_), channel_id=1, source_target_pairs={{0,4},{4,0},{8,12},{12,8},{16,20},{20,16},{24,28},{28,24},{1,5},{5... | collective-permute-start | bytes 884744 | tf_op jit(solution)/shard_map/ppermute | solution.py:23
  364.4 16.6 %collective-permute-start.68 = (bf16[192,1024]{1,0:T(8,128)(2,1)S(1)}, bf16[192,1024]{1,0:T(8,128)(2,1)S(1)}, u32[]{:S(2)}, u32[]{:S(2)}) collective-permute-start(bf16[192,1024]{1,0:T(8,128)(2,1)S(1)} %get-tuple-element.56), channel_id=1, source_target_pairs={{0,1},{1,0},{2,3},{3,2},{4,5},{5,4},{6,7},{7,6},{8,9},{9,8},{10,11... | collective-permute-start | bytes 1179656 | tf_op jit(solution)/shard_map/ppermute | solution.py:23
  364.7 28.4 %collective-permute-start.69 = (bf16[192,1024]{1,0:T(8,128)(2,1)S(1)}, bf16[192,1024]{1,0:T(8,128)(2,1)S(1)}, u32[]{:S(2)}, u32[]{:S(2)}) collective-permute-start(bf16[192,1024]{1,0:T(8,128)(2,1)S(1)} %get-tuple-element.55), channel_id=1, source_target_pairs={{0,2},{1,3},{2,0},{3,1},{4,6},{5,7},{6,4},{7,5},{8,10},{9,11},{10,... | collective-permute-start | bytes 1179656 | tf_op jit(solution)/shard_map/ppermute | solution.py:23
  366.8 35.3 %collective-permute-start.70 = (bf16[192,1024]{1,0:T(8,128)(2,1)S(1)}, bf16[192,1024]{1,0:T(8,128)(2,1)S(1)}, u32[]{:S(2)}, u32[]{:S(2)}) collective-permute-start(bf16[192,1024]{1,0:T(8,128)(2,1)S(1)} %get-tuple-element.54), channel_id=1, source_target_pairs={{0,3},{1,2},{2,1},{3,0},{4,7},{5,6},{6,5},{7,4},{8,11},{9,10},{10,... | collective-permute-start | bytes 1179656 | tf_op jit(solution)/shard_map/ppermute | solution.py:23
  (87 other events, 697.8 us)
Sparse Core Ops, SparseCore 0:
  122.0 25.9 reduce-scatter.2
  165.3 25.9 reduce-scatter.4

commit v3 on v2

--- a/solution.py
+++ b/solution.py
@@ -46,7 +46,7 @@
         [part, part],
         [jax.ShapeDtypeStruct(tuple(shape), first.dtype)] * 2,
         after=after,
-        limit=56,
+        limit=16,
         cost_estimate=cost(0, 6 * first.size),
         name="halves",
     )
@@ -158,7 +158,7 @@
         jax.ShapeDtypeStruct((rows, columns), pieces[0].dtype),
         after=after,
         scratch=[pltpu.SemaphoreType.DMA((len(pieces),))],
-        limit=56,
+        limit=16,
         cost_estimate=cost(0, 4 * rows * columns),
         name="join",
     )
@@ -288,7 +288,7 @@
         [pl.BlockSpec((16, 3 * width), lambda j, me: (1, 0))] * len(ends),
         pl.BlockSpec((len(ends), 1, width), lambda j, me: (0, 0, 0)),
         jax.ShapeDtypeStruct((len(ends), 1, width), jnp.float32),
-        limit=56,
+        limit=16,
         name="inverse_gains",
     )
 
@@ -447,7 +447,7 @@
             pltpu.VMEM((total, depth), jnp.bfloat16),
             pltpu.SemaphoreType.DMA((len(parts),)),
         ],
-        limit=56,
+        limit=40,
         cost_estimate=cost(
             2 * total * depth * columns, 2 * (total * depth + depth * columns + total * columns)
         ),
@@ -513,11 +513,16 @@
         lax.fori_loop(0, out.shape[0] // 64, finish, 0)
 
 
-def hidden_units(me, parts, one_over_gain, gate, up, after=()):
-    slots, depth = parts[0][2].shape
+def hidden_units(me, groups, one_over_gain, gate, up, after=()):
+    depth = groups[0][0][2].shape[1]
     count = lax.axis_size("ctx")
     width = gate.shape[1]
-    layout = [(mask, (which or 0) * slots // 2) for mask, which, _ in parts]
+    layout, parts, slots = [], [], 0
+    for group in groups:
+        rows = group[0][2].shape[0]
+        layout += [(mask, slots + (which or 0) * rows // 2) for mask, which, _ in group]
+        parts += group
+        slots += rows
     block = pl.BlockSpec((2 * depth, width), lambda k, me: ((me[0] // 2) ^ k, 0))
     return launch(
         functools.partial(hidden_kernel, layout),
@@ -538,7 +543,7 @@
             pltpu.VMEM((slots, LANES), jnp.float32),
             pltpu.SemaphoreType.DMA((len(parts),)),
         ],
-        limit=56,
+        limit=40,
         cost_estimate=cost(
             4 * slots * depth * count * width, 2 * count * depth * (slots + 2 * width)
         ),
@@ -599,7 +604,7 @@
             pltpu.VMEM((slots, depth), jnp.bfloat16),
             pltpu.SemaphoreType.DMA((len(units),)),
         ],
-        limit=56,
+        limit=40,
         cost_estimate=cost(
             2 * slots * depth * columns, 2 * (slots * depth + depth * columns + slots * columns)
         ),
@@ -625,7 +630,7 @@
         [whole(shape)] * len(picks),
         [jax.ShapeDtypeStruct(shape, rows.dtype)] * len(picks),
         after=after,
-        limit=56,
+        limit=24,
         cost_estimate=cost(2 * rows.size * shape[0] * len(picks), 4 * rows.size),
         name="pick_rows",
     )
@@ -656,6 +661,7 @@
         cost_estimate=cost(
             2 * mixer_out.size * answers[0].shape[0] * len(answers), 4 * mixer_out.size
         ),
+        limit=24,
         name="combine",
     )
 
@@ -700,10 +706,10 @@
 
     def send_columns(masks, after=()):
         for mask, cut in zip(masks, cut_columns(me, down_rows, width, masks, after)):
-            down_parts[mask] = cut if mask == 0 else swap(cut, "ctx", mask)
+            down_parts[mask] = swap(cut, "ctx", mask)
         return tuple(down_parts[mask] for mask in masks)
 
-    early = send_columns([2, 4, 3, 5])
+    early = send_columns([2, 4])
 
     extra, left = [], norm_gain
     for _ in range(3):
@@ -728,7 +734,7 @@
         b_wide,
     )
     chunks = 2
-    state, ends = prefix_state, gather_parts(join([end], early[:2]))
+    state, ends = prefix_state, gather_parts(join([end], early))
     one_over_gain = inverse_gains(me, ends, width)
     gated = []
     for chunk in range(chunks):
@@ -745,7 +751,6 @@
             c_wide,
             state,
             ends,
-            early[2:],
         )
         ends = []
         gated.append(rows)
@@ -753,13 +758,12 @@
     far = lambda parts: [part for mask, which, part in parts if which is not None][::2]
     scatter = lambda rows: lax.psum_scatter(rows, "exp", scatter_dimension=0, tiled=True)
     front = gather_parts(gated[0], 1, gated[1:])
+    late = send_columns([3, 5, 6, 7, 1] + list(range(8, ctx_count)), near(front))
     back = gather_parts(gated[1], 1, far(front))
-    partial = project(me, front, out_proj, near(back))
+    partial = project(me, front, out_proj, gated[1:])
     projected = [scatter(partial)]
-    (middle,) = send_columns([6], far(front))
-    partial = project(me, back, out_proj, [partial, middle])
+    partial = project(me, back, out_proj, [partial])
     projected.append(scatter(partial))
-    late = send_columns([7, 1] + list(range(8, ctx_count)), [partial])
 
     block_rows = residual.shape[0]
     owners = block_rows // tokens
@@ -784,21 +788,22 @@
     groups = [[0, 2], [1, 3]] if exp_count == 4 else [list(range(exp_count))]
     last = groups[-1][-1] if len(groups) > 1 else None
     masks = [mask for mask in range(exp_count) if mask != last][::-1]
-    rows = dict(zip(masks, pick_rows([picked[mask] for mask in masks], scaled, late[:1])))
+    rows = dict(zip(masks, pick_rows([picked[mask] for mask in masks], scaled)))
     pieces = {mask: swap(rows[mask], "exp", mask) for mask in masks if mask != 0}
     pieces[0] = rows[0]
     if last is not None:
         (sent,) = pick_rows([picked[last]], scaled, (pieces[groups[0][-1]],))
         pieces[last] = swap(sent, "exp", last)
-    segments, after, order = {}, late[1:], ()
-    for group in groups:
-        parts = gather_parts(join([pieces[mask] for mask in group], after), 0, order)
+    arrived, after = [], late
+    for place, group in enumerate(groups):
+        parts = gather_parts(join([pieces[mask] for mask in group], after), 0)
         after = near(parts)
-        hidden = hidden_units(me, parts, one_over_gain, expert_gate[0], expert_up[0])
-        order = [hidden]
-        units = {mask: part for mask, _, part in gather_parts(hidden)}
-        for place, mask in enumerate(group):
-            segments[mask] = ([units[m] for m in range(ctx_count)], place * capacity)
+        arrived.append(parts)
+    hidden = hidden_units(me, arrived, one_over_gain, expert_gate[0], expert_up[0])
+    units = {mask: part for mask, _, part in gather_parts(hidden)}
+    units = [units[mask] for mask in range(ctx_count)]
+    slots_of = [mask for group in groups for mask in group]
+    segments = {mask: (units, place * capacity) for place, mask in enumerate(slots_of)}
     answers = {}
     weights = [None] + [down_parts[mask] for mask in range(1, ctx_count)]
     order = ()

time: 414 us -> 380 us (0.918)
  Pallas kernels: 128 us -> 92.6 us
  local copies, waits for them, and re-layouts: 19.9 us -> 33.3 us
  waiting for transfers between devices: 189 us -> 180 us
  starting transfers between devices: 54.1 us -> 45.8 us
    pallas_call x23 -> x21, Pallas kernels: 128 us -> 92.6 us  [launch(): pl.pallas_call(body, grid_spec=pltpu.PrefetchScalarGridSpec(num_scalar_pr...]
    unnamed x158 -> x154, local copies, waits for them, and re-layouts: 14 us -> 27 us
    ppermute x70 -> x63, starting transfers between devices: 52.1 us -> 44 us  [swap(): lax.ppermute(array, axis, [(i, i ^ mask) for i in range(lax.axis_size(axi...]
    ppermute x70 -> x63, waiting for transfers between devices: 172 us -> 168 us  [swap(): lax.ppermute(array, axis, [(i, i ^ mask) for i in range(lax.axis_size(axi...]
  transfers between devices with their start and end apart: 73 -> 66, of which waited for: 34 -> 34; matrix products, arithmetic and copies ran while one was open for 3% -> 3% of each run, Pallas kernels for 23% -> 13%
where the time goes in v3:
time: 380 us; the launch traced here: 375 us
  waiting for transfers between devices  180 us (47%)
  Pallas kernels  92.6 us (24%)
  starting transfers between devices  45.8 us (12%)
  local copies, waits for them, and re-layouts  33.3 us (9%)
  between operations  15 us (4%)
  other arithmetic  7.85 us (2%)
    ppermute x63, waiting for transfers between devices, swap(): lax.ppermute(array, axis, [(i, i ^ mask) for i in range(lax.axis_size(axi...  168 us
    pallas_call x21, Pallas kernels, launch(): pl.pallas_call(body, grid_spec=pltpu.PrefetchScalarGridSpec(num_scalar_pr...  92.6 us
    ppermute x63, starting transfers between devices, swap(): lax.ppermute(array, axis, [(i, i ^ mask) for i in range(lax.axis_size(axi...  44 us
    unnamed x154, local copies, waits for them, and re-layouts  27 us
    reduce_scatter x2, waiting for transfers between devices, shards(): lax.psum_scatter(rows, 'exp', scatter_dimension=0, tiled=True)  12.8 us
  transfers between devices with their start and end apart: 66, of which 34 were waited for; matrix products, arithmetic and copies ran while one was open for 3% of the time, Pallas kernels for 13%

profile of v3, /device:TPU:8, one launch (start us, length us, event | category | flops | bytes accessed | tf_op | source)
XLA Modules:
  0.0 375.0 jit_solution(14040153657995838534)
XLA Ops:
  8.1 1.7 collective-permute-start
  9.9 3.4 cut_columns.2
  13.3 1.7 collective-permute-start.1
  15.0 1.5 collective-permute-start.2
  18.0 1.3 broadcast_in_dim.20.refs_8_.refs_6_
  19.3 13.9 %local_states.1 = (f32[128,4096]{1,0:T(8,128)}, f32[128,4096]{1,0:T(8,128)}, bf16[32,4096]{1,0:T(8,128)(2,1)}) custom-call(bf16[128,4096]{1,0:T(8,128)(2,1)} %refs_0_.1, f32[8,4096]{1,0:T(8,128)} %pad_convert_fusion.refs_1_, bf16[128,4096]{1,0:T(8,128)(2,1)} %refs_2_.2, f32[4,4096]{1,0:T(4,128)} %refs_3_.4, f32[1,4096]{1,0:T(1,128)} %bitcast.55, ...), custom_call_target="tpu_custom_call" | custom-call | flops 41943040 | bytes 6291456 | tf_op jit(solution)/shard_map/local_states/pallas_call | solution.py:95
  33.3 2.0 collective-permute-done.2.refs_2_.refs_29_.refs_13_
  35.2 1.1 copy-done.60
  36.4 1.6 collective-permute-start.8
  38.2 1.8 collective-permute-start.4
  40.0 6.6 %collective-permute-done.8.refs_15_.refs_7_ = bf16[32,4096]{1,0:T(8,128)(2,1)S(1)} collective-permute-done((bf16[32,4096]{1,0:T(8,128)(2,1)S(1)}, bf16[32,4096]{1,0:T(8,128)(2,1)S(1)}, u32[]{:S(2)}, u32[]{:S(2)}) %collective-permute-start.8) | collective-permute-done | bytes 262176 | tf_op jit(solution)/shard_map/ppermute | solution.py:23
  46.6 4.8 %collective-permute-done.6.refs_13_.refs_5_ = bf16[32,4096]{1,0:T(8,128)(2,1)S(1)} collective-permute-done((bf16[32,4096]{1,0:T(8,128)(2,1)S(1)}, bf16[32,4096]{1,0:T(8,128)(2,1)S(1)}, u32[]{:S(2)}, u32[]{:S(2)}) %collective-permute-start.6) | collective-permute-done | bytes 262176 | tf_op jit(solution)/shard_map/ppermute | solution.py:23
  53.4 1.3 broadcast_in_dim.23.refs_7_
  54.8 9.1 %read_out.2 = (bf16[64,4096]{1,0:T(8,128)(2,1)}, f32[16,4096]{1,0:T(8,128)}) custom-call(s32[1]{0:T(128)} %bitcast.refs_0_, f32[128,4096]{1,0:T(8,128)} %get-tuple-element.26.refs_1_, f32[128,4096]{1,0:T(8,128)} %get-tuple-element.27.refs_2_, bf16[128,4096]{1,0:T(8,128)(2,1)} %refs_3_.6, f32[16,4096]{1,0:T(8,128)} %refs_4_.3, f32[1,4096]{1,0:T(1,128)} %bitcast.48, ...), custom_call_target="tpu_custom_call" | custom-call | flops 29360128 | bytes 3145728 | tf_op jit(solution)/shard_map/read_out/pallas_call | solution.py:95
  64.3 1.7 collective-permute-start.11
  66.1 8.3 %read_out.3 = (bf16[64,4096]{1,0:T(8,128)(2,1)}, f32[16,4096]{1,0:T(8,128)}) custom-call(s32[1]{0:T(128)} %bitcast.refs_0_, f32[128,4096]{1,0:T(8,128)} %get-tuple-element.26.refs_1_, f32[128,4096]{1,0:T(8,128)} %get-tuple-element.27.refs_2_, bf16[128,4096]{1,0:T(8,128)(2,1)} %refs_3_.6, f32[16,4096]{1,0:T(8,128)} %refs_4_.3, f32[1,4096]{1,0:T(1,128)} %bitcast.49, ...), custom_call_target="tpu_custom_call" | custom-call | flops 29360128 | bytes 3145728 | tf_op jit(solution)/shard_map/read_out/pallas_call | solution.py:95
  74.4 3.8 %collective-permute-done.13.refs_1_.refs_6_.refs_7_ = bf16[64,4096]{1,0:T(8,128)(2,1)S(1)} collective-permute-done((bf16[64,4096]{1,0:T(8,128)(2,1)}, bf16[64,4096]{1,0:T(8,128)(2,1)S(1)}, u32[]{:S(2)}, u32[]{:S(2)}) %collective-permute-start.13) | collective-permute-done | bytes 524320 | tf_op jit(solution)/shard_map/ppermute | solution.py:23
  78.3 1.3 copy-done.47
  79.7 1.6 collective-permute-start.15
  82.3 4.9 %collective-permute-done.15.refs_8_.refs_2_ = bf16[64,2048]{1,0:T(8,128)(2,1)S(1)} collective-permute-done((bf16[64,2048]{1,0:T(8,128)(2,1)S(1)}, bf16[64,2048]{1,0:T(8,128)(2,1)S(1)}, u32[]{:S(2)}, u32[]{:S(2)}) %collective-permute-start.15) | collective-permute-done | bytes 262176 | tf_op jit(solution)/shard_map/ppermute | solution.py:23
  90.8 3.4 copy-done.61
  94.2 7.4 %project.2.refs_12_ = bf16[512,1024]{1,0:T(8,128)(2,1)} custom-call(s32[1]{0:T(128)} %bitcast.refs_0_, bf16[4096,1024]{1,0:T(8,128)(2,1)S(1)} %copy-done.61, bf16[64,4096]{1,0:T(8,128)(2,1)S(1)} %copy-done.62, bf16[64,4096]{1,0:T(8,128)(2,1)S(1)} %collective-permute-done.10.refs_3_, bf16[64,4096]{1,0:T(8,128)(2,1)S(1)} %collective-permute-done.11.refs_0_.refs_4_.refs_6_, ...), custom_call_target="tpu_custom_call" | custom-call | flops 4294967296 | bytes 13631488 | tf_op jit(solution)/shard_map/project/pallas_call | solution.py:95
  102.5 1.3 collective-permute-start.20
  103.8 11.9 %collective-permute-done.22.refs_1_.refs_6_ = bf16[64,4096]{1,0:T(8,128)(2,1)S(1)} collective-permute-done((bf16[64,4096]{1,0:T(8,128)(2,1)S(1)}, bf16[64,4096]{1,0:T(8,128)(2,1)S(1)}, u32[]{:S(2)}, u32[]{:S(2)}) %collective-permute-start.22) | collective-permute-done | bytes 524320 | tf_op jit(solution)/shard_map/ppermute | solution.py:23
  116.2 1.3 collective-permute-start.24
  118.4 6.6 %collective-permute-done.24.refs_8_ = bf16[64,2048]{1,0:T(8,128)(2,1)S(1)} collective-permute-done((bf16[64,2048]{1,0:T(8,128)(2,1)S(1)}, bf16[64,2048]{1,0:T(8,128)(2,1)S(1)}, u32[]{:S(2)}, u32[]{:S(2)}) %collective-permute-start.24) | collective-permute-done | bytes 262176 | tf_op jit(solution)/shard_map/ppermute | solution.py:23
  129.5 9.4 %project.3 = bf16[512,1024]{1,0:T(8,128)(2,1)} custom-call(s32[1]{0:T(128)} %bitcast.refs_0_, bf16[4096,1024]{1,0:T(8,128)(2,1)} %refs_1_.3, bf16[64,4096]{1,0:T(8,128)(2,1)S(1)} %copy-done.49, bf16[64,4096]{1,0:T(8,128)(2,1)S(1)} %collective-permute-done.19.refs_3_, bf16[64,4096]{1,0:T(8,128)(2,1)S(1)} %collective-permute-done.20.refs_0_.refs_4_, ...), custom_call_target="tpu_custom_call" | custom-call | flops 4294967296 | bytes 13631488 | tf_op jit(solution)/shard_map/project/pallas_call | solution.py:95
  140.9 4.9 %cut_columns.3 = (bf16[384,1024]{1,0:T(8,128)(2,1)}, bf16[384,1024]{1,0:T(8,128)(2,1)}, bf16[384,1024]{1,0:T(8,128)(2,1)}, bf16[384,1024]{1,0:T(8,128)(2,1)}, bf16[384,1024]{1,0:T(8,128)(2,1)}) custom-call(s32[1]{0:T(128)} %bitcast.refs_0_, bf16[384,8192]{1,0:T(8,128)(2,1)} %bitcast.39, bf16[384,8192]{1,0:T(8,128)(2,1)} %bitcast.40, ...), custom_call_target="tpu_custom_call" | custom-call | bytes 7864320 | tf_op jit(solution)/shard_map/cut_columns/pallas_call | solution.py:95
  148.6 1.4 collective-permute-start.31
  150.0 1.2 collective-permute-start.32
  151.6 12.8 %reduce-scatter.5.cloned.1.call-done = bf16[128,1024]{1,0:T(8,128)(2,1)} async-done(((bf16[512,1024]{1,0:T(8,128)(2,1)}), bf16[128,1024]{1,0:T(8,128)(2,1)}) %reduce-scatter.5.cloned.1.call-update) | async-done | bytes 262160 | tf_op jit(solution)/shard_map/reduce_scatter | solution.py:759
  165.5 2.1 multiply_convert_fusion
  170.3 2.2 collective-permute-start.28
  174.3 26.7 %collective-permute-done.30.refs_3_.refs_30_.refs_14_ = bf16[384,1024]{1,0:T(8,128)(2,1)S(1)} collective-permute-done((bf16[384,1024]{1,0:T(8,128)(2,1)}, bf16[384,1024]{1,0:T(8,128)(2,1)S(1)}, u32[]{:S(2)}, u32[]{:S(2)}) %collective-permute-start.30) | collective-permute-done | bytes 786464 | tf_op jit(solution)/shard_map/ppermute | solution.py:23
  201.1 1.3 copy-done.59
  202.8 1.4 collective-permute-start.37
  206.9 2.8 collective-permute-start.44
  209.7 12.8 %collective-permute-done.37.refs_1_.refs_3_.refs_8_ = bf16[384,1024]{1,0:T(8,128)(2,1)S(1)} collective-permute-done((bf16[384,1024]{1,0:T(8,128)(2,1)S(1)}, bf16[384,1024]{1,0:T(8,128)(2,1)S(1)}, u32[]{:S(2)}, u32[]{:S(2)}) %collective-permute-start.37) | collective-permute-done | bytes 786464 | tf_op jit(solution)/shard_map/ppermute | solution.py:23
  224.3 2.4 collective-permute-done.44.refs_1_
  227.1 1.3 collective-permute-start.48
  229.2 1.2 collective-permute-start.41
  230.4 5.2 %collective-permute-done.39.refs_10_ = bf16[192,1024]{1,0:T(8,128)(2,1)S(1)} collective-permute-done((bf16[192,1024]{1,0:T(8,128)(2,1)S(1)}, bf16[192,1024]{1,0:T(8,128)(2,1)S(1)}, u32[]{:S(2)}, u32[]{:S(2)}) %collective-permute-start.39) | collective-permute-done | bytes 393248 | tf_op jit(solution)/shard_map/ppermute | solution.py:23
  235.6 17.9 %collective-permute-done.41.refs_12_ = bf16[192,1024]{1,0:T(8,128)(2,1)S(1)} collective-permute-done((bf16[192,1024]{1,0:T(8,128)(2,1)S(1)}, bf16[192,1024]{1,0:T(8,128)(2,1)S(1)}, u32[]{:S(2)}, u32[]{:S(2)}) %collective-permute-start.41) | collective-permute-done | bytes 393248 | tf_op jit(solution)/shard_map/ppermute | solution.py:23
  257.8 8.1 %collective-permute-done.50.refs_20_ = bf16[192,1024]{1,0:T(8,128)(2,1)S(1)} collective-permute-done((bf16[192,1024]{1,0:T(8,128)(2,1)S(1)}, bf16[192,1024]{1,0:T(8,128)(2,1)S(1)}, u32[]{:S(2)}, u32[]{:S(2)}) %collective-permute-start.50) | collective-permute-done | bytes 393248 | tf_op jit(solution)/shard_map/ppermute | solution.py:23
  265.8 2.3 collective-permute-done.52.refs_22_
  269.9 18.9 %hidden_units.1.refs_1_.refs_9_.refs_17_ = bf16[768,384]{1,0:T(8,128)(2,1)S(1)} custom-call(s32[1]{0:T(128)} %bitcast.refs_0_, f32[8,1,1024]{2,1,0:T(1,128)S(1)} %inverse_gains.1.refs_1_, bf16[8192,384]{1,0:T(8,128)(2,1)} %bitcast.53, bf16[8192,384]{1,0:T(8,128)(2,1)} %bitcast.54, bf16[384,1024]{1,0:T(8,128)(2,1)S(1)} %join.4.refs_4_, ...), custom_call_target="tpu_custom_call" | custom-call | flops 9663676416 | bytes 25165824 | tf_op jit(solution)/shard_map/hidden_units/pallas_call | solution.py:95
  288.8 1.6 collective-permute-start.59
  291.1 1.2 collective-permute-start.55
  292.3 13.6 %collective-permute-done.59.refs_7_.refs_15_.refs_23_ = bf16[768,384]{1,0:T(8,128)(2,1)S(1)} collective-permute-done((bf16[768,384]{1,0:T(8,128)(2,1)S(1)}, bf16[768,384]{1,0:T(8,128)(2,1)S(1)}, u32[]{:S(2)}, u32[]{:S(2)}) %collective-permute-start.59) | collective-permute-done | bytes 589856 | tf_op jit(solution)/shard_map/ppermute | solution.py:23
  306.0 11.8 %collective-permute-done.57.refs_5_.refs_13_.refs_21_ = bf16[768,384]{1,0:T(8,128)(2,1)S(1)} collective-permute-done((bf16[768,384]{1,0:T(8,128)(2,1)S(1)}, bf16[768,384]{1,0:T(8,128)(2,1)S(1)}, u32[]{:S(2)}, u32[]{:S(2)}) %collective-permute-start.57) | collective-permute-done | bytes 589856 | tf_op jit(solution)/shard_map/ppermute | solution.py:23
  318.3 1.5 collective-permute-done.58.refs_6_.refs_14_.refs_22_
  320.6 7.0 %down.2.refs_17_ = bf16[576,1024]{1,0:T(8,128)(2,1)S(1)} custom-call(s32[1]{0:T(128)} %bitcast.refs_0_, bf16[768,384]{1,0:T(8,128)(2,1)S(1)} %hidden_units.1.refs_1_.refs_9_.refs_17_, bf16[768,384]{1,0:T(8,128)(2,1)S(1)} %collective-permute-done.54.refs_2_.refs_10_.refs_18_, bf16[768,384]{1,0:T(8,128)(2,1)S(1)} %collective-permute-done.55.refs_3_.refs_11_.refs_19_, ...), custom_call_target="tpu_custom_call" | custom-call | flops 3623878656 | bytes 11010048 | tf_op jit(solution)/shard_map/down/pallas_call | solution.py:95
  328.7 2.6 collective-permute-start.63
  331.3 1.1 collective-permute-start.62
  338.7 1.1 copy-done.10
  339.8 1.1 copy-done.13
  340.9 1.1 copy-done.16
  342.1 1.1 copy-done.19
  343.2 1.1 copy-done.22
  344.3 1.1 copy-done.25
  345.5 4.2 %down.3.refs_8_ = bf16[192,1024]{1,0:T(8,128)(2,1)S(1)} custom-call(s32[1]{0:T(128)} %bitcast.refs_0_, bf16[768,384]{1,0:T(8,128)(2,1)S(1)} %hidden_units.1.refs_1_.refs_9_.refs_17_, bf16[768,384]{1,0:T(8,128)(2,1)S(1)} %copy-done.1, bf16[768,384]{1,0:T(8,128)(2,1)S(1)} %collective-permute-done.55.refs_3_.refs_11_.refs_19_, bf16[768,384]{1,0:T(8,128)(2,1)S(1)} %copy-done.7, ...), custom_call_target="tpu_custom_call" | custom-call | flops 1207959552 | bytes 7864320 | tf_op jit(solution)/shard_map/down/pallas_call | solution.py:95
  349.8 8.7 %collective-permute-done.63.refs_11_ = bf16[192,1024]{1,0:T(8,128)(2,1)} collective-permute-done((bf16[192,1024]{1,0:T(8,128)(2,1)}, bf16[192,1024]{1,0:T(8,128)(2,1)}, u32[]{:S(2)}, u32[]{:S(2)}) %collective-permute-start.63) | collective-permute-done | bytes 393248 | tf_op jit(solution)/shard_map/ppermute | solution.py:23
  358.4 6.9 %collective-permute-done.62.refs_10_ = bf16[192,1024]{1,0:T(8,128)(2,1)} collective-permute-done((bf16[192,1024]{1,0:T(8,128)(2,1)}, bf16[192,1024]{1,0:T(8,128)(2,1)}, u32[]{:S(2)}, u32[]{:S(2)}) %collective-permute-start.62) | collective-permute-done | bytes 393248 | tf_op jit(solution)/shard_map/ppermute | solution.py:23
  365.4 2.8 combine.1
  (286 shorter events, 48.9 us)
Async XLA Ops:
  7.2 144.5 %reduce-scatter.3.cloned.1.call-start = ((), (), s32[]{:S(2)}) async-start(), calls=%async_computation.2 | async-start | bytes 1310720 | tf_op jit(solution)/shard_map/reduce_scatter | solution.py:759
  8.1 9.2 %collective-permute-start = (bf16[3,4096]{1,0:T(4,128)(2,1)S(1)}, bf16[3,4096]{1,0:T(4,128)(2,1)S(1)}, u32[]{:S(2)}, u32[]{:S(2)}) collective-permute-start(bf16[3,4096]{1,0:T(4,128)(2,1)S(1)} %slice.40), channel_id=1, source_target_pairs={{0,4},{4,8},{8,12},{12,16},{16,20},{20,24},{24,28},{1,5},{5,9},{9,... | collective-permute-start | bytes 73736 | tf_op jit(solution)/shard_map/ppermute | solution.py:19
  13.3 20.0 %collective-permute-start.1 = (bf16[384,1024]{1,0:T(8,128)(2,1)}, bf16[384,1024]{1,0:T(8,128)(2,1)S(1)}, u32[]{:S(2)}, u32[]{:S(2)}) collective-permute-start(bf16[384,1024]{1,0:T(8,128)(2,1)} %get-tuple-element.29), channel_id=1, source_target_pairs={{0,8},{4,12},{8,0},{12,4},{16,24},{20,28},{24,16},{28,20},{1,9},{5... | collective-permute-start | bytes 2359304 | tf_op jit(solution)/shard_map/ppermute | solution.py:23
  15.0 20.3 %collective-permute-start.2 = (bf16[384,1024]{1,0:T(8,128)(2,1)}, bf16[384,1024]{1,0:T(8,128)(2,1)S(1)}, u32[]{:S(2)}, u32[]{:S(2)}) collective-permute-start(bf16[384,1024]{1,0:T(8,128)(2,1)} %get-tuple-element.30), channel_id=1, source_target_pairs={{0,16},{4,20},{8,24},{12,28},{16,0},{20,4},{24,8},{28,12},{1,17},{... | collective-permute-start | bytes 2359304 | tf_op jit(solution)/shard_map/ppermute | solution.py:23
  36.4 10.2 %collective-permute-start.8 = (bf16[32,4096]{1,0:T(8,128)(2,1)S(1)}, bf16[32,4096]{1,0:T(8,128)(2,1)S(1)}, u32[]{:S(2)}, u32[]{:S(2)}) collective-permute-start(bf16[32,4096]{1,0:T(8,128)(2,1)S(1)} %join.3.refs_9_.refs_1_), channel_id=1, source_target_pairs={{0,24},{4,28},{8,16},{12,20},{16,8},{20,12},{24,0},{28,4},{1,25},{... | collective-permute-start | bytes 786440 | tf_op jit(solution)/shard_map/ppermute | solution.py:23
  38.0 13.4 %collective-permute-start.6 = (bf16[32,4096]{1,0:T(8,128)(2,1)S(1)}, bf16[32,4096]{1,0:T(8,128)(2,1)S(1)}, u32[]{:S(2)}, u32[]{:S(2)}) collective-permute-start(bf16[32,4096]{1,0:T(8,128)(2,1)S(1)} %join.3.refs_9_.refs_1_), channel_id=1, source_target_pairs={{0,16},{4,20},{8,24},{12,28},{16,0},{20,4},{24,8},{28,12},{1,17},{... | collective-permute-start | bytes 786440 | tf_op jit(solution)/shard_map/ppermute | solution.py:23
  38.2 13.2 %collective-permute-start.4 = (bf16[32,4096]{1,0:T(8,128)(2,1)S(1)}, bf16[32,4096]{1,0:T(8,128)(2,1)S(1)}, u32[]{:S(2)}, u32[]{:S(2)}) collective-permute-start(bf16[32,4096]{1,0:T(8,128)(2,1)S(1)} %join.3.refs_9_.refs_1_), channel_id=1, source_target_pairs={{0,8},{4,12},{8,0},{12,4},{16,24},{20,28},{24,16},{28,20},{1,9},{5... | collective-permute-start | bytes 786440 | tf_op jit(solution)/shard_map/ppermute | solution.py:23
  40.0 12.1 %collective-permute-start.3 = (bf16[32,4096]{1,0:T(8,128)(2,1)S(1)}, bf16[32,4096]{1,0:T(8,128)(2,1)S(1)}, u32[]{:S(2)}, u32[]{:S(2)}) collective-permute-start(bf16[32,4096]{1,0:T(8,128)(2,1)S(1)} %join.3.refs_9_.refs_1_), channel_id=1, source_target_pairs={{0,4},{4,0},{8,12},{12,8},{16,20},{20,16},{24,28},{28,24},{1,5},{5... | collective-permute-start | bytes 786440 | tf_op jit(solution)/shard_map/ppermute | solution.py:23
  46.6 5.5 %collective-permute-start.9 = (bf16[32,4096]{1,0:T(8,128)(2,1)S(1)}, bf16[32,4096]{1,0:T(8,128)(2,1)S(1)}, u32[]{:S(2)}, u32[]{:S(2)}) collective-permute-start(bf16[32,4096]{1,0:T(8,128)(2,1)S(1)} %collective-permute-done.8.refs_15_.refs_7_), channel_id=1, source_target_pairs={{0,4},{4,0},{8,12},{12,8},{16,20},{20,16},{24,28},{28,24},{1,5},{5... | collective-permute-start | bytes 786440 | tf_op jit(solution)/shard_map/ppermute | solution.py:23
  51.4 2.0 collective-permute-start.5
  63.9 14.2 %collective-permute-start.13 = (bf16[64,4096]{1,0:T(8,128)(2,1)}, bf16[64,4096]{1,0:T(8,128)(2,1)S(1)}, u32[]{:S(2)}, u32[]{:S(2)}) collective-permute-start(bf16[64,4096]{1,0:T(8,128)(2,1)} %get-tuple-element.31.refs_2_), channel_id=1, source_target_pairs={{0,16},{4,20},{8,24},{12,28},{16,0},{20,4},{24,8},{28,12},{1,17},{... | collective-permute-start | bytes 1572872 | tf_op jit(solution)/shard_map/ppermute | solution.py:23
  64.3 13.9 %collective-permute-start.11 = (bf16[64,4096]{1,0:T(8,128)(2,1)}, bf16[64,4096]{1,0:T(8,128)(2,1)S(1)}, u32[]{:S(2)}, u32[]{:S(2)}) collective-permute-start(bf16[64,4096]{1,0:T(8,128)(2,1)} %get-tuple-element.31.refs_2_), channel_id=1, source_target_pairs={{0,8},{4,12},{8,0},{12,4},{16,24},{20,28},{24,16},{28,20},{1,9},{5... | collective-permute-start | bytes 1572872 | tf_op jit(solution)/shard_map/ppermute | solution.py:23
  66.1 22.1 %collective-permute-start.10 = (bf16[64,4096]{1,0:T(8,128)(2,1)}, bf16[64,4096]{1,0:T(8,128)(2,1)S(1)}, u32[]{:S(2)}, u32[]{:S(2)}) collective-permute-start(bf16[64,4096]{1,0:T(8,128)(2,1)} %get-tuple-element.31.refs_2_), channel_id=1, source_target_pairs={{0,4},{4,0},{8,12},{12,8},{16,20},{20,16},{24,28},{28,24},{1,5},{5... | collective-permute-start | bytes 1572872 | tf_op jit(solution)/shard_map/ppermute | solution.py:23
  79.7 7.6 %collective-permute-start.15 = (bf16[64,2048]{1,0:T(8,128)(2,1)S(1)}, bf16[64,2048]{1,0:T(8,128)(2,1)S(1)}, u32[]{:S(2)}, u32[]{:S(2)}) collective-permute-start(bf16[64,2048]{1,0:T(8,128)(2,1)S(1)} %get-tuple-element.34), channel_id=1, source_target_pairs={{0,16},{4,20},{8,24},{12,28},{16,0},{20,4},{24,8},{28,12},{1,17},{... | collective-permute-start | bytes 786440 | tf_op jit(solution)/shard_map/ppermute | solution.py:23
  81.3 6.9 %collective-permute-start.17 = (bf16[64,2048]{1,0:T(8,128)(2,1)S(1)}, bf16[64,2048]{1,0:T(8,128)(2,1)S(1)}, u32[]{:S(2)}, u32[]{:S(2)}) collective-permute-start(bf16[64,2048]{1,0:T(8,128)(2,1)S(1)} %get-tuple-element.35), channel_id=1, source_target_pairs={{0,8},{4,12},{8,0},{12,4},{16,24},{20,28},{24,16},{28,20},{1,9},{5... | collective-permute-start | bytes 786440 | tf_op jit(solution)/shard_map/ppermute | solution.py:23
  81.8 7.9 %collective-permute-start.14 = (bf16[64,4096]{1,0:T(8,128)(2,1)S(1)}, bf16[64,4096]{1,0:T(8,128)(2,1)S(1)}, u32[]{:S(2)}, u32[]{:S(2)}) collective-permute-start(bf16[64,4096]{1,0:T(8,128)(2,1)S(1)} %collective-permute-done.13.refs_1_.refs_6_.refs_7_), channel_id=1, source_target_pairs={{0,4},{4,0},{8,12},{12,8},{16,20},{20,16},{24,28},{28,24},{1,5},{5... | collective-permute-start | bytes 1572872 | tf_op jit(solution)/shard_map/ppermute | solution.py:23
  81.8 7.9 %collective-permute-start.12 = (bf16[64,4096]{1,0:T(8,128)(2,1)S(1)}, bf16[64,4096]{1,0:T(8,128)(2,1)S(1)}, u32[]{:S(2)}, u32[]{:S(2)}) collective-permute-start(bf16[64,4096]{1,0:T(8,128)(2,1)S(1)} %collective-permute-done.11.refs_0_.refs_4_.refs_6_), channel_id=1, source_target_pairs={{0,4},{4,0},{8,12},{12,8},{16,20},{20,16},{24,28},{28,24},{1,5},{5... | collective-permute-start | bytes 1572872 | tf_op jit(solution)/shard_map/ppermute | solution.py:23
  87.3 1.5 collective-permute-start.16
  101.6 62.8 %reduce-scatter.5.cloned.1.call-start = ((), (), s32[]{:S(2)}) async-start(), calls=%async_computation.3 | async-start | bytes 1310720 | tf_op jit(solution)/shard_map/reduce_scatter | solution.py:759
  101.7 14.0 %collective-permute-start.22 = (bf16[64,4096]{1,0:T(8,128)(2,1)S(1)}, bf16[64,4096]{1,0:T(8,128)(2,1)S(1)}, u32[]{:S(2)}, u32[]{:S(2)}) collective-permute-start(bf16[64,4096]{1,0:T(8,128)(2,1)S(1)} %copy-done.49), channel_id=1, source_target_pairs={{0,16},{4,20},{8,24},{12,28},{16,0},{20,4},{24,8},{28,12},{1,17},{... | collective-permute-start | bytes 1572872 | tf_op jit(solution)/shard_map/ppermute | solution.py:23
  102.5 13.7 %collective-permute-start.20 = (bf16[64,4096]{1,0:T(8,128)(2,1)S(1)}, bf16[64,4096]{1,0:T(8,128)(2,1)S(1)}, u32[]{:S(2)}, u32[]{:S(2)}) collective-permute-start(bf16[64,4096]{1,0:T(8,128)(2,1)S(1)} %copy-done.49), channel_id=1, source_target_pairs={{0,8},{4,12},{8,0},{12,4},{16,24},{20,28},{24,16},{28,20},{1,9},{5... | collective-permute-start | bytes 1572872 | tf_op jit(solution)/shard_map/ppermute | solution.py:23
  103.8 22.9 %collective-permute-start.19 = (bf16[64,4096]{1,0:T(8,128)(2,1)S(1)}, bf16[64,4096]{1,0:T(8,128)(2,1)S(1)}, u32[]{:S(2)}, u32[]{:S(2)}) collective-permute-start(bf16[64,4096]{1,0:T(8,128)(2,1)S(1)} %copy-done.49), channel_id=1, source_target_pairs={{0,4},{4,0},{8,12},{12,8},{16,20},{20,16},{24,28},{28,24},{1,5},{5... | collective-permute-start | bytes 1572872 | tf_op jit(solution)/shard_map/ppermute | solution.py:23
  115.7 11.1 %collective-permute-start.23 = (bf16[64,4096]{1,0:T(8,128)(2,1)S(1)}, bf16[64,4096]{1,0:T(8,128)(2,1)S(1)}, u32[]{:S(2)}, u32[]{:S(2)}) collective-permute-start(bf16[64,4096]{1,0:T(8,128)(2,1)S(1)} %collective-permute-done.22.refs_1_.refs_6_), channel_id=1, source_target_pairs={{0,4},{4,0},{8,12},{12,8},{16,20},{20,16},{24,28},{28,24},{1,5},{5... | collective-permute-start | bytes 1572872 | tf_op jit(solution)/shard_map/ppermute | solution.py:23
  116.2 10.6 %collective-permute-start.21 = (bf16[64,4096]{1,0:T(8,128)(2,1)S(1)}, bf16[64,4096]{1,0:T(8,128)(2,1)}, u32[]{:S(2)}, u32[]{:S(2)}) collective-permute-start(bf16[64,4096]{1,0:T(8,128)(2,1)S(1)} %collective-permute-done.20.refs_0_.refs_4_), channel_id=1, source_target_pairs={{0,4},{4,0},{8,12},{12,8},{16,20},{20,16},{24,28},{28,24},{1,5},{5... | collective-permute-start | bytes 1572872 | tf_op jit(solution)/shard_map/ppermute | solution.py:23
  116.2 8.8 %collective-permute-start.24 = (bf16[64,2048]{1,0:T(8,128)(2,1)S(1)}, bf16[64,2048]{1,0:T(8,128)(2,1)S(1)}, u32[]{:S(2)}, u32[]{:S(2)}) collective-permute-start(bf16[64,2048]{1,0:T(8,128)(2,1)S(1)} %get-tuple-element.36), channel_id=1, source_target_pairs={{0,16},{4,20},{8,24},{12,28},{16,0},{20,4},{24,8},{28,12},{1,17},{... | collective-permute-start | bytes 786440 | tf_op jit(solution)/shard_map/ppermute | solution.py:23
  117.5 8.4 %collective-permute-start.26 = (bf16[64,2048]{1,0:T(8,128)(2,1)S(1)}, bf16[64,2048]{1,0:T(8,128)(2,1)S(1)}, u32[]{:S(2)}, u32[]{:S(2)}) collective-permute-start(bf16[64,2048]{1,0:T(8,128)(2,1)S(1)} %get-tuple-element.37), channel_id=1, source_target_pairs={{0,8},{4,12},{8,0},{12,4},{16,24},{20,28},{24,16},{28,20},{1,9},{5... | collective-permute-start | bytes 786440 | tf_op jit(solution)/shard_map/ppermute | solution.py:23
  125.0 1.7 collective-permute-start.25
  126.0 1.7 collective-permute-start.27
  145.7 24.5 %collective-permute-start.29 = (bf16[384,1024]{1,0:T(8,128)(2,1)}, bf16[384,1024]{1,0:T(8,128)(2,1)S(1)}, u32[]{:S(2)}, u32[]{:S(2)}) collective-permute-start(bf16[384,1024]{1,0:T(8,128)(2,1)} %get-tuple-element.40), channel_id=1, source_target_pairs={{0,12},{4,8},{8,4},{12,0},{16,28},{20,24},{24,20},{28,16},{1,13},{... | collective-permute-start | bytes 2359304 | tf_op jit(solution)/shard_map/ppermute | solution.py:23
  147.5 53.5 %collective-permute-start.30 = (bf16[384,1024]{1,0:T(8,128)(2,1)}, bf16[384,1024]{1,0:T(8,128)(2,1)S(1)}, u32[]{:S(2)}, u32[]{:S(2)}) collective-permute-start(bf16[384,1024]{1,0:T(8,128)(2,1)} %get-tuple-element.41), channel_id=1, source_target_pairs={{0,20},{4,16},{8,28},{12,24},{16,4},{20,0},{24,12},{28,8},{1,21},{... | collective-permute-start | bytes 2359304 | tf_op jit(solution)/shard_map/ppermute | solution.py:23
  148.6 52.4 %collective-permute-start.31 = (bf16[384,1024]{1,0:T(8,128)(2,1)}, bf16[384,1024]{1,0:T(8,128)(2,1)S(1)}, u32[]{:S(2)}, u32[]{:S(2)}) collective-permute-start(bf16[384,1024]{1,0:T(8,128)(2,1)} %get-tuple-element.42), channel_id=1, source_target_pairs={{0,24},{4,28},{8,16},{12,20},{16,8},{20,12},{24,0},{28,4},{1,25},{... | collective-permute-start | bytes 2359304 | tf_op jit(solution)/shard_map/ppermute | solution.py:23
  150.0 51.0 %collective-permute-start.32 = (bf16[384,1024]{1,0:T(8,128)(2,1)}, bf16[384,1024]{1,0:T(8,128)(2,1)S(1)}, u32[]{:S(2)}, u32[]{:S(2)}) collective-permute-start(bf16[384,1024]{1,0:T(8,128)(2,1)} %get-tuple-element.43), channel_id=1, source_target_pairs={{0,28},{4,24},{8,20},{12,16},{16,12},{20,8},{24,4},{28,0},{1,29},{... | collective-permute-start | bytes 2359304 | tf_op jit(solution)/shard_map/ppermute | solution.py:23
  151.2 49.9 %collective-permute-start.33 = (bf16[384,1024]{1,0:T(8,128)(2,1)}, bf16[384,1024]{1,0:T(8,128)(2,1)}, u32[]{:S(2)}, u32[]{:S(2)}) collective-permute-start(bf16[384,1024]{1,0:T(8,128)(2,1)} %get-tuple-element.44), channel_id=1, source_target_pairs={{0,4},{4,0},{8,12},{12,8},{16,20},{20,16},{24,28},{28,24},{1,5},{5... | collective-permute-start | bytes 2359304 | tf_op jit(solution)/shard_map/ppermute | solution.py:23
  170.3 30.7 %collective-permute-start.28 = (bf16[192,1024]{1,0:T(8,128)(2,1)}, bf16[192,1024]{1,0:T(8,128)(2,1)S(1)}, u32[]{:S(2)}, u32[]{:S(2)}) collective-permute-start(bf16[192,1024]{1,0:T(8,128)(2,1)} %get-tuple-element.39), channel_id=1, source_target_pairs={{0,2},{1,3},{2,0},{3,1},{4,6},{5,7},{6,4},{7,5},{8,10},{9,11},{10,... | collective-permute-start | bytes 1179656 | tf_op jit(solution)/shard_map/ppermute | solution.py:23
  202.8 19.7 %collective-permute-start.37 = (bf16[384,1024]{1,0:T(8,128)(2,1)S(1)}, bf16[384,1024]{1,0:T(8,128)(2,1)S(1)}, u32[]{:S(2)}, u32[]{:S(2)}) collective-permute-start(bf16[384,1024]{1,0:T(8,128)(2,1)S(1)} %join.4.refs_4_), channel_id=1, source_target_pairs={{0,16},{4,20},{8,24},{12,28},{16,0},{20,4},{24,8},{28,12},{1,17},{... | collective-permute-start | bytes 2359304 | tf_op jit(solution)/shard_map/ppermute | solution.py:23
  204.2 19.3 %collective-permute-start.35 = (bf16[384,1024]{1,0:T(8,128)(2,1)S(1)}, bf16[384,1024]{1,0:T(8,128)(2,1)S(1)}, u32[]{:S(2)}, u32[]{:S(2)}) collective-permute-start(bf16[384,1024]{1,0:T(8,128)(2,1)S(1)} %join.4.refs_4_), channel_id=1, source_target_pairs={{0,8},{4,12},{8,0},{12,4},{16,24},{20,28},{24,16},{28,20},{1,9},{5... | collective-permute-start | bytes 2359304 | tf_op jit(solution)/shard_map/ppermute | solution.py:23
  205.1 19.3 %collective-permute-start.43 = (bf16[192,1024]{1,0:T(8,128)(2,1)}, bf16[192,1024]{1,0:T(8,128)(2,1)S(1)}, u32[]{:S(2)}, u32[]{:S(2)}) collective-permute-start(bf16[192,1024]{1,0:T(8,128)(2,1)} %copy-done.63), channel_id=1, source_target_pairs={{0,1},{1,0},{2,3},{3,2},{4,5},{5,4},{6,7},{7,6},{8,9},{9,8},{10,11... | collective-permute-start | bytes 1179656 | tf_op jit(solution)/shard_map/ppermute | solution.py:23
  206.9 19.8 %collective-permute-start.44 = (bf16[192,1024]{1,0:T(8,128)(2,1)S(1)}, bf16[192,1024]{1,0:T(8,128)(2,1)S(1)}, u32[]{:S(2)}, u32[]{:S(2)}) collective-permute-start(bf16[192,1024]{1,0:T(8,128)(2,1)S(1)} %pick_rows.3), channel_id=1, source_target_pairs={{0,3},{1,2},{2,1},{3,0},{4,7},{5,6},{6,5},{7,4},{8,11},{9,10},{10,... | collective-permute-start | bytes 1179656 | tf_op jit(solution)/shard_map/ppermute | solution.py:23
  223.5 12.1 %collective-permute-start.39 = (bf16[192,1024]{1,0:T(8,128)(2,1)S(1)}, bf16[192,1024]{1,0:T(8,128)(2,1)S(1)}, u32[]{:S(2)}, u32[]{:S(2)}) collective-permute-start(bf16[192,1024]{1,0:T(8,128)(2,1)S(1)} %get-tuple-element.45), channel_id=1, source_target_pairs={{0,16},{4,20},{8,24},{12,28},{16,0},{20,4},{24,8},{28,12},{1,17},{... | collective-permute-start | bytes 1179656 | tf_op jit(solution)/shard_map/ppermute | solution.py:23
  227.1 26.4 %collective-permute-start.48 = (bf16[384,1024]{1,0:T(8,128)(2,1)S(1)}, bf16[384,1024]{1,0:T(8,128)(2,1)S(1)}, u32[]{:S(2)}, u32[]{:S(2)}) collective-permute-start(bf16[384,1024]{1,0:T(8,128)(2,1)S(1)} %join.5.refs_14_), channel_id=1, source_target_pairs={{0,16},{4,20},{8,24},{12,28},{16,0},{20,4},{24,8},{28,12},{1,17},{... | collective-permute-start | bytes 2359304 | tf_op jit(solution)/shard_map/ppermute | solution.py:23
  228.4 25.6 %collective-permute-start.46 = (bf16[384,1024]{1,0:T(8,128)(2,1)S(1)}, bf16[384,1024]{1,0:T(8,128)(2,1)S(1)}, u32[]{:S(2)}, u32[]{:S(2)}) collective-permute-start(bf16[384,1024]{1,0:T(8,128)(2,1)S(1)} %join.5.refs_14_), channel_id=1, source_target_pairs={{0,8},{4,12},{8,0},{12,4},{16,24},{20,28},{24,16},{28,20},{1,9},{5... | collective-permute-start | bytes 2359304 | tf_op jit(solution)/shard_map/ppermute | solution.py:23
  229.2 24.3 %collective-permute-start.41 = (bf16[192,1024]{1,0:T(8,128)(2,1)S(1)}, bf16[192,1024]{1,0:T(8,128)(2,1)S(1)}, u32[]{:S(2)}, u32[]{:S(2)}) collective-permute-start(bf16[192,1024]{1,0:T(8,128)(2,1)S(1)} %get-tuple-element.46), channel_id=1, source_target_pairs={{0,8},{4,12},{8,0},{12,4},{16,24},{20,28},{24,16},{28,20},{1,9},{5... | collective-permute-start | bytes 1179656 | tf_op jit(solution)/shard_map/ppermute | solution.py:23
  230.4 23.8 %collective-permute-start.34 = (bf16[384,1024]{1,0:T(8,128)(2,1)S(1)}, bf16[384,1024]{1,0:T(8,128)(2,1)S(1)}, u32[]{:S(2)}, u32[]{:S(2)}) collective-permute-start(bf16[384,1024]{1,0:T(8,128)(2,1)S(1)} %join.4.refs_4_), channel_id=1, source_target_pairs={{0,4},{4,0},{8,12},{12,8},{16,20},{20,16},{24,28},{28,24},{1,5},{5... | collective-permute-start | bytes 2359304 | tf_op jit(solution)/shard_map/ppermute | solution.py:23
  235.6 19.1 %collective-permute-start.38 = (bf16[384,1024]{1,0:T(8,128)(2,1)S(1)}, bf16[384,1024]{1,0:T(8,128)(2,1)S(1)}, u32[]{:S(2)}, u32[]{:S(2)}) collective-permute-start(bf16[384,1024]{1,0:T(8,128)(2,1)S(1)} %collective-permute-done.37.refs_1_.refs_3_.refs_8_), channel_id=1, source_target_pairs={{0,4},{4,0},{8,12},{12,8},{16,20},{20,16},{24,28},{28,24},{1,5},{5... | collective-permute-start | bytes 2359304 | tf_op jit(solution)/shard_map/ppermute | solution.py:23
  253.5 4.2 %collective-permute-start.45 = (bf16[384,1024]{1,0:T(8,128)(2,1)S(1)}, bf16[384,1024]{1,0:T(8,128)(2,1)S(1)}, u32[]{:S(2)}, u32[]{:S(2)}) collective-permute-start(bf16[384,1024]{1,0:T(8,128)(2,1)S(1)} %join.5.refs_14_), channel_id=1, source_target_pairs={{0,4},{4,0},{8,12},{12,8},{16,20},{20,16},{24,28},{28,24},{1,5},{5... | collective-permute-start | bytes 2359304 | tf_op jit(solution)/shard_map/ppermute | solution.py:23
  253.5 2.8 collective-permute-start.40
  254.0 2.9 collective-permute-start.42
  254.2 14.9 %collective-permute-start.36 = (bf16[384,1024]{1,0:T(8,128)(2,1)S(1)}, bf16[384,1024]{1,0:T(8,128)(2,1)S(1)}, u32[]{:S(2)}, u32[]{:S(2)}) collective-permute-start(bf16[384,1024]{1,0:T(8,128)(2,1)S(1)} %collective-permute-done.35.refs_0_.refs_2_.refs_6_), channel_id=1, source_target_pairs={{0,4},{4,0},{8,12},{12,8},{16,20},{20,16},{24,28},{28,24},{1,5},{5... | collective-permute-start | bytes 2359304 | tf_op jit(solution)/shard_map/ppermute | solution.py:23
  254.7 11.1 %collective-permute-start.50 = (bf16[192,1024]{1,0:T(8,128)(2,1)S(1)}, bf16[192,1024]{1,0:T(8,128)(2,1)S(1)}, u32[]{:S(2)}, u32[]{:S(2)}) collective-permute-start(bf16[192,1024]{1,0:T(8,128)(2,1)S(1)} %get-tuple-element.48), channel_id=1, source_target_pairs={{0,16},{4,20},{8,24},{12,28},{16,0},{20,4},{24,8},{28,12},{1,17},{... | collective-permute-start | bytes 1179656 | tf_op jit(solution)/shard_map/ppermute | solution.py:23
  256.4 12.8 %collective-permute-start.49 = (bf16[384,1024]{1,0:T(8,128)(2,1)S(1)}, bf16[384,1024]{1,0:T(8,128)(2,1)S(1)}, u32[]{:S(2)}, u32[]{:S(2)}) collective-permute-start(bf16[384,1024]{1,0:T(8,128)(2,1)S(1)} %collective-permute-done.48.refs_1_.refs_18_), channel_id=1, source_target_pairs={{0,4},{4,0},{8,12},{12,8},{16,20},{20,16},{24,28},{28,24},{1,5},{5... | collective-permute-start | bytes 2359304 | tf_op jit(solution)/shard_map/ppermute | solution.py:23
  256.9 11.2 %collective-permute-start.52 = (bf16[192,1024]{1,0:T(8,128)(2,1)S(1)}, bf16[192,1024]{1,0:T(8,128)(2,1)S(1)}, u32[]{:S(2)}, u32[]{:S(2)}) collective-permute-start(bf16[192,1024]{1,0:T(8,128)(2,1)S(1)} %get-tuple-element.49), channel_id=1, source_target_pairs={{0,8},{4,12},{8,0},{12,4},{16,24},{20,28},{24,16},{28,20},{1,9},{5... | collective-permute-start | bytes 1179656 | tf_op jit(solution)/shard_map/ppermute | solution.py:23
  257.8 12.1 %collective-permute-start.47 = (bf16[384,1024]{1,0:T(8,128)(2,1)S(1)}, bf16[384,1024]{1,0:T(8,128)(2,1)S(1)}, u32[]{:S(2)}, u32[]{:S(2)}) collective-permute-start(bf16[384,1024]{1,0:T(8,128)(2,1)S(1)} %collective-permute-done.46.refs_0_.refs_16_), channel_id=1, source_target_pairs={{0,4},{4,0},{8,12},{12,8},{16,20},{20,16},{24,28},{28,24},{1,5},{5... | collective-permute-start | bytes 2359304 | tf_op jit(solution)/shard_map/ppermute | solution.py:23
  265.8 3.3 collective-permute-start.51
  268.1 1.7 collective-permute-start.53
  288.8 17.2 %collective-permute-start.59 = (bf16[768,384]{1,0:T(8,128)(2,1)S(1)}, bf16[768,384]{1,0:T(8,128)(2,1)S(1)}, u32[]{:S(2)}, u32[]{:S(2)}) collective-permute-start(bf16[768,384]{1,0:T(8,128)(2,1)S(1)} %hidden_units.1.refs_1_.refs_9_.refs_17_), channel_id=1, source_target_pairs={{0,24},{4,28},{8,16},{12,20},{16,8},{20,12},{24,0},{28,4},{1,25},{... | collective-permute-start | bytes 1769480 | tf_op jit(solution)/shard_map/ppermute | solution.py:23
  290.4 27.4 %collective-permute-start.57 = (bf16[768,384]{1,0:T(8,128)(2,1)S(1)}, bf16[768,384]{1,0:T(8,128)(2,1)S(1)}, u32[]{:S(2)}, u32[]{:S(2)}) collective-permute-start(bf16[768,384]{1,0:T(8,128)(2,1)S(1)} %hidden_units.1.refs_1_.refs_9_.refs_17_), channel_id=1, source_target_pairs={{0,16},{4,20},{8,24},{12,28},{16,0},{20,4},{24,8},{28,12},{1,17},{... | collective-permute-start | bytes 1769480 | tf_op jit(solution)/shard_map/ppermute | solution.py:23
  291.1 26.6 %collective-permute-start.55 = (bf16[768,384]{1,0:T(8,128)(2,1)S(1)}, bf16[768,384]{1,0:T(8,128)(2,1)S(1)}, u32[]{:S(2)}, u32[]{:S(2)}) collective-permute-start(bf16[768,384]{1,0:T(8,128)(2,1)S(1)} %hidden_units.1.refs_1_.refs_9_.refs_17_), channel_id=1, source_target_pairs={{0,8},{4,12},{8,0},{12,4},{16,24},{20,28},{24,16},{28,20},{1,9},{5... | collective-permute-start | bytes 1769480 | tf_op jit(solution)/shard_map/ppermute | solution.py:23
  292.3 25.9 %collective-permute-start.54 = (bf16[768,384]{1,0:T(8,128)(2,1)S(1)}, bf16[768,384]{1,0:T(8,128)(2,1)S(1)}, u32[]{:S(2)}, u32[]{:S(2)}) collective-permute-start(bf16[768,384]{1,0:T(8,128)(2,1)S(1)} %hidden_units.1.refs_1_.refs_9_.refs_17_), channel_id=1, source_target_pairs={{0,4},{4,0},{8,12},{12,8},{16,20},{20,16},{24,28},{28,24},{1,5},{5... | collective-permute-start | bytes 1769480 | tf_op jit(solution)/shard_map/ppermute | solution.py:23
  306.0 12.3 %collective-permute-start.60 = (bf16[768,384]{1,0:T(8,128)(2,1)S(1)}, bf16[768,384]{1,0:T(8,128)(2,1)S(1)}, u32[]{:S(2)}, u32[]{:S(2)}) collective-permute-start(bf16[768,384]{1,0:T(8,128)(2,1)S(1)} %collective-permute-done.59.refs_7_.refs_15_.refs_23_), channel_id=1, source_target_pairs={{0,4},{4,0},{8,12},{12,8},{16,20},{20,16},{24,28},{28,24},{1,5},{5... | collective-permute-start | bytes 1769480 | tf_op jit(solution)/shard_map/ppermute | solution.py:23
  317.7 2.0 collective-permute-start.58
  317.8 2.8 collective-permute-start.56
  328.7 29.7 %collective-permute-start.63 = (bf16[192,1024]{1,0:T(8,128)(2,1)}, bf16[192,1024]{1,0:T(8,128)(2,1)}, u32[]{:S(2)}, u32[]{:S(2)}) collective-permute-start(bf16[192,1024]{1,0:T(8,128)(2,1)} %get-tuple-element.56), channel_id=1, source_target_pairs={{0,3},{1,2},{2,1},{3,0},{4,7},{5,6},{6,5},{7,4},{8,11},{9,10},{10,... | collective-permute-start | bytes 1179656 | tf_op jit(solution)/shard_map/ppermute | solution.py:23
  331.3 34.0 %collective-permute-start.62 = (bf16[192,1024]{1,0:T(8,128)(2,1)}, bf16[192,1024]{1,0:T(8,128)(2,1)}, u32[]{:S(2)}, u32[]{:S(2)}) collective-permute-start(bf16[192,1024]{1,0:T(8,128)(2,1)} %get-tuple-element.57), channel_id=1, source_target_pairs={{0,2},{1,3},{2,0},{3,1},{4,6},{5,7},{6,4},{7,5},{8,10},{9,11},{10,... | collective-permute-start | bytes 1179656 | tf_op jit(solution)/shard_map/ppermute | solution.py:23
  332.5 32.9 %collective-permute-start.61 = (bf16[192,1024]{1,0:T(8,128)(2,1)}, bf16[192,1024]{1,0:T(8,128)(2,1)}, u32[]{:S(2)}, u32[]{:S(2)}) collective-permute-start(bf16[192,1024]{1,0:T(8,128)(2,1)} %get-tuple-element.58), channel_id=1, source_target_pairs={{0,1},{1,0},{2,3},{3,2},{4,5},{5,4},{6,7},{7,6},{8,9},{9,8},{10,11... | collective-permute-start | bytes 1179656 | tf_op jit(solution)/shard_map/ppermute | solution.py:23
  (78 other events, 1726.8 us)
Sparse Core Ops, SparseCore 0:
  101.7 25.2 reduce-scatter.2
  139.1 25.3 reduce-scatter.4

commit v4 on v3

--- a/solution.py
+++ b/solution.py
@@ -554,17 +554,17 @@
 def down_kernel(layout, me, *refs):
     count = len(layout)
     units, weights, (out, held, sems) = refs[:count], refs[count:-3], refs[-3:]
-    slots, width = held.shape[0], weights[0].shape[0]
-    rows = slots * len(weights) // count
+    width = weights[0].shape[0]
 
     @pl.when(pl.program_id(0) == 0)
     def _():
         copies = []
-        for place, (mask, begin, row) in enumerate(layout):
+        for place, (mask, row) in enumerate(layout):
+            unit = units[place]
             copies.append(
                 pltpu.make_async_copy(
-                    units[place].at[pl.ds(begin, rows), :],
-                    held.at[pl.ds(row, rows), pl.ds(mask * width, width)],
+                    unit,
+                    held.at[pl.ds(row, unit.shape[0]), pl.ds(mask * width, width)],
                     sems.at[place],
                 )
             )
@@ -577,17 +577,14 @@
     out[...] = jnp.dot(held[...], tall, preferred_element_type=jnp.float32).astype(out.dtype)
 
 
-def down(me, segments, rows, weights, own, after=()):
+def down(me, parts, weights, own, after=()):
     columns = weights[-1].shape[1]
     width = own.shape[0]
     depth = width * len(weights)
-    slots = rows * len(segments)
+    slots = parts[0][2].shape[0]
     tile = min(256, columns)
-    layout, units = [], []
-    for place, (parts, begin) in enumerate(segments):
-        for mask, part in enumerate(parts):
-            layout.append((mask, begin, place * rows))
-            units.append(part)
+    layout = [(mask, (which or 0) * slots // 2) for mask, which, _ in parts]
+    units = [part for _, _, part in parts]
     steps = columns // tile
     return launch(
         functools.partial(down_kernel, layout),
@@ -760,7 +757,7 @@
     front = gather_parts(gated[0], 1, gated[1:])
     late = send_columns([3, 5, 6, 7, 1] + list(range(8, ctx_count)), near(front))
     back = gather_parts(gated[1], 1, far(front))
-    partial = project(me, front, out_proj, gated[1:])
+    partial = project(me, front, out_proj, near(back))
     projected = [scatter(partial)]
     partial = project(me, back, out_proj, [partial])
     projected.append(scatter(partial))
@@ -785,32 +782,23 @@
         pick = here[:, None] & (place[:, None] == spots[None, :])
         picked.append(pick.astype(jnp.bfloat16))
 
-    groups = [[0, 2], [1, 3]] if exp_count == 4 else [list(range(exp_count))]
-    last = groups[-1][-1] if len(groups) > 1 else None
-    masks = [mask for mask in range(exp_count) if mask != last][::-1]
-    rows = dict(zip(masks, pick_rows([picked[mask] for mask in masks], scaled)))
-    pieces = {mask: swap(rows[mask], "exp", mask) for mask in masks if mask != 0}
-    pieces[0] = rows[0]
-    if last is not None:
-        (sent,) = pick_rows([picked[last]], scaled, (pieces[groups[0][-1]],))
-        pieces[last] = swap(sent, "exp", last)
-    arrived, after = [], late
-    for place, group in enumerate(groups):
-        parts = gather_parts(join([pieces[mask] for mask in group], after), 0)
+    groups = [[0, 1], [2, 3]] if exp_count == 4 else [list(range(exp_count))]
+    sent = pick_rows(picked, scaled)
+    pieces = [rows if mask == 0 else swap(rows, "exp", mask) for mask, rows in enumerate(sent)]
+    hiddens, after, order = [], late[:3], late[3:]
+    for group in groups:
+        parts = gather_parts(join([pieces[mask] for mask in group], after), 0, order)
         after = near(parts)
-        arrived.append(parts)
-    hidden = hidden_units(me, arrived, one_over_gain, expert_gate[0], expert_up[0])
-    units = {mask: part for mask, _, part in gather_parts(hidden)}
-    units = [units[mask] for mask in range(ctx_count)]
-    slots_of = [mask for group in groups for mask in group]
-    segments = {mask: (units, place * capacity) for place, mask in enumerate(slots_of)}
-    answers = {}
+        hidden = hidden_units(me, [parts], one_over_gain, expert_gate[0], expert_up[0])
+        order = [hidden]
+        hiddens.append(hidden)
+    answers, order = {}, []
     weights = [None] + [down_parts[mask] for mask in range(1, ctx_count)]
-    order = ()
-    for group in [list(range(1, exp_count))[::-1], [0]]:
-        answer = down(
-            me, [segments[mask] for mask in group], capacity, weights, down_rows, order
-        )
+    for group, hidden in zip(groups, hiddens):
+        last = group is groups[-1]
+        units = join([hidden], far(parts)) if not last else hidden
+        units = gather_parts(units, 0, hiddens[-1:] if not last else ())
+        answer = down(me, units, weights, down_rows, order)
         order = [answer]
         for place, mask in enumerate(group):
             piece = lax.slice_in_dim(answer, place * capacity, (place + 1) * capacity, axis=0)

time: 380 us -> 374 us (0.984)
  local copies, waits for them, and re-layouts: 33.3 us -> 23.2 us
  starting transfers between devices: 45.8 us -> 53.8 us
    unnamed x154 -> x96, local copies, waits for them, and re-layouts: 27 us -> 17.6 us
    ppermute x63 -> x74, starting transfers between devices: 44 us -> 51.8 us  [swap(): lax.ppermute(array, axis, [(i, i ^ mask) for i in range(lax.axis_size(axi...]
    reduce_scatter x2, waiting for transfers between devices: 12.8 us -> 16.7 us  [shards(): lax.psum_scatter(rows, 'exp', scatter_dimension=0, tiled=True)]
    ppermute x63 -> x74, waiting for transfers between devices: 168 us -> 164 us  [swap(): lax.ppermute(array, axis, [(i, i ^ mask) for i in range(lax.axis_size(axi...]
    pallas_call x21 -> x24, Pallas kernels: 92.6 us -> 92 us  [launch(): pl.pallas_call(body, grid_spec=pltpu.PrefetchScalarGridSpec(num_scalar_pr...]
  transfers between devices with their start and end apart: 66 -> 77, of which waited for: 34 -> 34; matrix products, arithmetic and copies ran while one was open for 3% -> 3% of each run, Pallas kernels for 13% -> 20%
where the time goes in v4:
time: 374 us; the launch traced here: 372 us
  waiting for transfers between devices  181 us (48%)
  Pallas kernels  92 us (25%)
  starting transfers between devices  53.8 us (14%)
  local copies, waits for them, and re-layouts  23.2 us (6%)
  between operations  14.8 us (4%)
  other arithmetic  7.25 us (2%)
    ppermute x74, waiting for transfers between devices, swap(): lax.ppermute(array, axis, [(i, i ^ mask) for i in range(lax.axis_size(axi...  164 us
    pallas_call x24, Pallas kernels, launch(): pl.pallas_call(body, grid_spec=pltpu.PrefetchScalarGridSpec(num_scalar_pr...  92 us
    ppermute x74, starting transfers between devices, swap(): lax.ppermute(array, axis, [(i, i ^ mask) for i in range(lax.axis_size(axi...  51.8 us
    unnamed x96, local copies, waits for them, and re-layouts  17.6 us
    reduce_scatter x2, waiting for transfers between devices, shards(): lax.psum_scatter(rows, 'exp', scatter_dimension=0, tiled=True)  16.7 us
  transfers between devices with their start and end apart: 77, of which 34 were waited for; matrix products, arithmetic and copies ran while one was open for 3% of the time, Pallas kernels for 20%

profile of v4, /device:TPU:8, one launch (start us, length us, event | category | flops | bytes accessed | tf_op | source)
XLA Modules:
  0.0 372.2 jit_solution(2624523806463594105)
XLA Ops:
  8.1 1.7 collective-permute-start
  9.9 3.4 cut_columns.2
  13.3 1.7 collective-permute-start.1
  14.9 1.5 collective-permute-start.2
  18.0 1.4 broadcast_in_dim.20.refs_8_.refs_6_
  19.4 13.9 %local_states.1 = (f32[128,4096]{1,0:T(8,128)}, f32[128,4096]{1,0:T(8,128)}, bf16[32,4096]{1,0:T(8,128)(2,1)}) custom-call(bf16[128,4096]{1,0:T(8,128)(2,1)} %refs_0_.1, f32[8,4096]{1,0:T(8,128)} %pad_convert_fusion.refs_1_, bf16[128,4096]{1,0:T(8,128)(2,1)} %refs_2_.2, f32[4,4096]{1,0:T(4,128)} %refs_3_.4, f32[1,4096]{1,0:T(1,128)} %bitcast.59, ...), custom_call_target="tpu_custom_call" | custom-call | flops 41943040 | bytes 6291456 | tf_op jit(solution)/shard_map/local_states/pallas_call | solution.py:95
  33.3 1.9 collective-permute-done.2.refs_2_.refs_15_
  36.5 1.8 collective-permute-start.6
  38.3 1.4 collective-permute-start.8
  39.8 5.7 %collective-permute-done.4.refs_11_.refs_3_ = bf16[32,4096]{1,0:T(8,128)(2,1)S(1)} collective-permute-done((bf16[32,4096]{1,0:T(8,128)(2,1)S(1)}, bf16[32,4096]{1,0:T(8,128)(2,1)S(1)}, u32[]{:S(2)}, u32[]{:S(2)}) %collective-permute-start.4) | collective-permute-done | bytes 262176 | tf_op jit(solution)/shard_map/ppermute | solution.py:23
  45.4 4.9 %collective-permute-done.6.refs_13_.refs_5_ = bf16[32,4096]{1,0:T(8,128)(2,1)S(1)} collective-permute-done((bf16[32,4096]{1,0:T(8,128)(2,1)S(1)}, bf16[32,4096]{1,0:T(8,128)(2,1)S(1)}, u32[]{:S(2)}, u32[]{:S(2)}) %collective-permute-start.6) | collective-permute-done | bytes 262176 | tf_op jit(solution)/shard_map/ppermute | solution.py:23
  52.4 1.4 broadcast_in_dim.23.refs_7_
  53.8 9.2 %read_out.2 = (bf16[64,4096]{1,0:T(8,128)(2,1)}, f32[16,4096]{1,0:T(8,128)}) custom-call(s32[1]{0:T(128)} %bitcast.refs_0_, f32[128,4096]{1,0:T(8,128)} %get-tuple-element.31.refs_1_, f32[128,4096]{1,0:T(8,128)} %get-tuple-element.32.refs_2_, bf16[128,4096]{1,0:T(8,128)(2,1)} %refs_3_.6, f32[16,4096]{1,0:T(8,128)} %refs_4_.3, f32[1,4096]{1,0:T(1,128)} %bitcast.54, ...), custom_call_target="tpu_custom_call" | custom-call | flops 29360128 | bytes 3145728 | tf_op jit(solution)/shard_map/read_out/pallas_call | solution.py:95
  63.0 1.7 collective-permute-start.11
  65.1 8.3 %read_out.3 = (bf16[64,4096]{1,0:T(8,128)(2,1)}, f32[16,4096]{1,0:T(8,128)}) custom-call(s32[1]{0:T(128)} %bitcast.refs_0_, f32[128,4096]{1,0:T(8,128)} %get-tuple-element.31.refs_1_, f32[128,4096]{1,0:T(8,128)} %get-tuple-element.32.refs_2_, bf16[128,4096]{1,0:T(8,128)(2,1)} %refs_3_.6, f32[16,4096]{1,0:T(8,128)} %refs_4_.3, f32[1,4096]{1,0:T(1,128)} %bitcast.55, ...), custom_call_target="tpu_custom_call" | custom-call | flops 29360128 | bytes 3145728 | tf_op jit(solution)/shard_map/read_out/pallas_call | solution.py:95
  73.4 1.7 collective-permute-start.19
  75.5 2.6 collective-permute-done.11.refs_0_.refs_4_.refs_6_
  78.0 1.7 collective-permute-done.13.refs_1_.refs_6_.refs_7_
  81.3 1.7 collective-permute-start.17
  82.9 6.3 %collective-permute-done.19.refs_12_.refs_0_.refs_4_ = bf16[64,4096]{1,0:T(8,128)(2,1)S(1)} collective-permute-done((bf16[64,4096]{1,0:T(8,128)(2,1)}, bf16[64,4096]{1,0:T(8,128)(2,1)S(1)}, u32[]{:S(2)}, u32[]{:S(2)}) %collective-permute-start.19) | collective-permute-done | bytes 524320 | tf_op jit(solution)/shard_map/ppermute | solution.py:23
  89.3 1.7 collective-permute-done.20.refs_13_.refs_1_.refs_6_
  91.0 4.5 %collective-permute-done.15.refs_8_.refs_2_ = bf16[64,2048]{1,0:T(8,128)(2,1)S(1)} collective-permute-done((bf16[64,2048]{1,0:T(8,128)(2,1)S(1)}, bf16[64,2048]{1,0:T(8,128)(2,1)S(1)}, u32[]{:S(2)}, u32[]{:S(2)}) %collective-permute-start.15) | collective-permute-done | bytes 262176 | tf_op jit(solution)/shard_map/ppermute | solution.py:23
  97.4 7.6 %project.2.refs_12_ = bf16[512,1024]{1,0:T(8,128)(2,1)S(1)} custom-call(s32[1]{0:T(128)} %bitcast.refs_0_, bf16[4096,1024]{1,0:T(8,128)(2,1)} %refs_1_.3, bf16[64,4096]{1,0:T(8,128)(2,1)S(1)} %copy-done.38, bf16[64,4096]{1,0:T(8,128)(2,1)S(1)} %collective-permute-done.10.refs_3_, bf16[64,4096]{1,0:T(8,128)(2,1)S(1)} %collective-permute-done.11.refs_0_.refs_4_.refs_6_, ...), custom_call_target="tpu_custom_call" | custom-call | flops 4294967296 | bytes 13631488 | tf_op jit(solution)/shard_map/project/pallas_call | solution.py:95
  112.0 1.7 collective-permute-start.26
  114.2 5.7 %collective-permute-done.24.refs_8_ = bf16[64,2048]{1,0:T(8,128)(2,1)S(1)} collective-permute-done((bf16[64,2048]{1,0:T(8,128)(2,1)S(1)}, bf16[64,2048]{1,0:T(8,128)(2,1)S(1)}, u32[]{:S(2)}, u32[]{:S(2)}) %collective-permute-start.24) | collective-permute-done | bytes 262176 | tf_op jit(solution)/shard_map/ppermute | solution.py:23
  121.9 1.2 copy-done.18
  125.2 8.3 %project.3 = bf16[512,1024]{1,0:T(8,128)(2,1)} custom-call(s32[1]{0:T(128)} %bitcast.refs_0_, bf16[4096,1024]{1,0:T(8,128)(2,1)} %refs_1_.3, bf16[64,4096]{1,0:T(8,128)(2,1)S(1)} %copy-done.20, bf16[64,4096]{1,0:T(8,128)(2,1)S(1)} %collective-permute-done.21.refs_3_, bf16[64,4096]{1,0:T(8,128)(2,1)S(1)} %copy-done.23, ...), custom_call_target="tpu_custom_call" | custom-call | flops 4294967296 | bytes 13631488 | tf_op jit(solution)/shard_map/project/pallas_call | solution.py:95
  137.1 4.9 %cut_columns.3 = (bf16[384,1024]{1,0:T(8,128)(2,1)}, bf16[384,1024]{1,0:T(8,128)(2,1)}, bf16[384,1024]{1,0:T(8,128)(2,1)}, bf16[384,1024]{1,0:T(8,128)(2,1)}, bf16[384,1024]{1,0:T(8,128)(2,1)}) custom-call(s32[1]{0:T(128)} %bitcast.refs_0_, bf16[384,8192]{1,0:T(8,128)(2,1)} %bitcast.43, bf16[384,8192]{1,0:T(8,128)(2,1)} %bitcast.44, ...), custom_call_target="tpu_custom_call" | custom-call | bytes 7864320 | tf_op jit(solution)/shard_map/cut_columns/pallas_call | solution.py:95
  142.0 1.2 collective-permute-start.29
  143.8 1.4 collective-permute-start.31
  145.2 16.7 %reduce-scatter.5.cloned.1.call-done = bf16[128,1024]{1,0:T(8,128)(2,1)} async-done(((bf16[512,1024]{1,0:T(8,128)(2,1)}), bf16[128,1024]{1,0:T(8,128)(2,1)}) %reduce-scatter.5.cloned.1.call-update) | async-done | bytes 262160 | tf_op jit(solution)/shard_map/reduce_scatter | solution.py:756
  161.9 1.1 pad_maximum_fusion
  163.0 2.1 multiply_convert_fusion
  166.8 2.7 collective-permute-start.28
  169.5 1.4 collective-permute-start.37
  170.9 1.1 collective-permute-start.38
  172.0 23.3 %collective-permute-done.30.refs_3_.refs_16_ = bf16[384,1024]{1,0:T(8,128)(2,1)S(1)} collective-permute-done((bf16[384,1024]{1,0:T(8,128)(2,1)}, bf16[384,1024]{1,0:T(8,128)(2,1)S(1)}, u32[]{:S(2)}, u32[]{:S(2)}) %collective-permute-start.30) | collective-permute-done | bytes 786464 | tf_op jit(solution)/shard_map/ppermute | solution.py:23
  195.7 1.4 collective-permute-start.33
  197.7 2.0 collective-permute-start.43
  199.8 1.3 collective-permute-start.32
  201.1 14.6 %collective-permute-done.33.refs_0_.refs_6_.refs_2_ = bf16[384,1024]{1,0:T(8,128)(2,1)S(1)} collective-permute-done((bf16[384,1024]{1,0:T(8,128)(2,1)S(1)}, bf16[384,1024]{1,0:T(8,128)(2,1)S(1)}, u32[]{:S(2)}, u32[]{:S(2)}) %collective-permute-start.33) | collective-permute-done | bytes 786464 | tf_op jit(solution)/shard_map/ppermute | solution.py:23
  218.0 7.9 %collective-permute-done.43.refs_0_ = bf16[192,1024]{1,0:T(8,128)(2,1)S(1)} collective-permute-done((bf16[192,1024]{1,0:T(8,128)(2,1)S(1)}, bf16[192,1024]{1,0:T(8,128)(2,1)S(1)}, u32[]{:S(2)}, u32[]{:S(2)}) %collective-permute-start.43) | collective-permute-done | bytes 393248 | tf_op jit(solution)/shard_map/ppermute | solution.py:23
  226.2 8.7 %collective-permute-done.44.refs_1_ = bf16[192,1024]{1,0:T(8,128)(2,1)S(1)} collective-permute-done((bf16[192,1024]{1,0:T(8,128)(2,1)S(1)}, bf16[192,1024]{1,0:T(8,128)(2,1)S(1)}, u32[]{:S(2)}, u32[]{:S(2)}) %collective-permute-start.44) | collective-permute-done | bytes 393248 | tf_op jit(solution)/shard_map/ppermute | solution.py:23
  235.7 10.3 %collective-permute-done.41.refs_12_ = bf16[192,1024]{1,0:T(8,128)(2,1)S(1)} collective-permute-done((bf16[192,1024]{1,0:T(8,128)(2,1)S(1)}, bf16[192,1024]{1,0:T(8,128)(2,1)S(1)}, u32[]{:S(2)}, u32[]{:S(2)}) %collective-permute-start.41) | collective-permute-done | bytes 393248 | tf_op jit(solution)/shard_map/ppermute | solution.py:23
  247.2 1.4 collective-permute-start.46
  249.8 10.2 %hidden_units.2.refs_2_.refs_0_ = bf16[384,384]{1,0:T(8,128)(2,1)S(1)} custom-call(s32[1]{0:T(128)} %bitcast.refs_0_, f32[8,1,1024]{2,1,0:T(1,128)S(1)} %inverse_gains.1.refs_1_, bf16[8192,384]{1,0:T(8,128)(2,1)S(1)} %bitcast.39, bf16[8192,384]{1,0:T(8,128)(2,1)} %bitcast.50, bf16[384,1024]{1,0:T(8,128)(2,1)S(1)} %join.5.refs_4_, ...), custom_call_target="tpu_custom_call" | custom-call | flops 4831838208 | bytes 18874368 | tf_op jit(solution)/shard_map/hidden_units/pallas_call | solution.py:95
  260.0 6.4 %collective-permute-done.45.refs_0_.refs_6_ = bf16[384,1024]{1,0:T(8,128)(2,1)S(1)} collective-permute-done((bf16[384,1024]{1,0:T(8,128)(2,1)S(1)}, bf16[384,1024]{1,0:T(8,128)(2,1)S(1)}, u32[]{:S(2)}, u32[]{:S(2)}) %collective-permute-start.45) | collective-permute-done | bytes 786464 | tf_op jit(solution)/shard_map/ppermute | solution.py:23
  266.9 1.5 collective-permute-start.47
  269.3 8.1 %collective-permute-done.47.refs_1_.refs_10_ = bf16[192,1024]{1,0:T(8,128)(2,1)S(1)} collective-permute-done((bf16[192,1024]{1,0:T(8,128)(2,1)S(1)}, bf16[192,1024]{1,0:T(8,128)(2,1)S(1)}, u32[]{:S(2)}, u32[]{:S(2)}) %collective-permute-start.47) | collective-permute-done | bytes 393248 | tf_op jit(solution)/shard_map/ppermute | solution.py:23
  277.4 2.5 collective-permute-done.48.refs_2_.refs_12_
  280.5 1.5 collective-permute-start.52
  282.0 10.2 %hidden_units.3.refs_2_.refs_1_ = bf16[384,384]{1,0:T(8,128)(2,1)S(1)} custom-call(s32[1]{0:T(128)} %bitcast.refs_0_, f32[8,1,1024]{2,1,0:T(1,128)S(1)} %inverse_gains.1.refs_1_, bf16[8192,384]{1,0:T(8,128)(2,1)S(1)} %bitcast.40, bf16[8192,384]{1,0:T(8,128)(2,1)} %bitcast.51, bf16[384,1024]{1,0:T(8,128)(2,1)S(1)} %join.6.refs_4_, ...), custom_call_target="tpu_custom_call" | custom-call | flops 4831838208 | bytes 18874368 | tf_op jit(solution)/shard_map/hidden_units/pallas_call | solution.py:95
  292.9 1.7 collective-permute-start.61
  294.9 1.5 collective-permute-start.67
  296.4 2.7 collective-permute-done.59.refs_7_
  299.6 5.0 %collective-permute-done.65.refs_0_.refs_3_ = bf16[384,384]{1,0:T(8,128)(2,1)S(1)} collective-permute-done((bf16[384,384]{1,0:T(8,128)(2,1)S(1)}, bf16[384,384]{1,0:T(8,128)(2,1)S(1)}, u32[]{:S(2)}, u32[]{:S(2)}) %collective-permute-start.65) | collective-permute-done | bytes 294944 | tf_op jit(solution)/shard_map/ppermute | solution.py:23
  305.2 1.6 collective-permute-start.69
  308.1 5.4 %down.2.refs_19_ = bf16[384,1024]{1,0:T(8,128)(2,1)S(1)} custom-call(s32[1]{0:T(128)} %bitcast.refs_0_, bf16[384,384]{1,0:T(8,128)(2,1)S(1)} %join.7.refs_1_, bf16[384,384]{1,0:T(8,128)(2,1)S(1)} %collective-permute-done.49.refs_2_, bf16[384,384]{1,0:T(8,128)(2,1)S(1)} %collective-permute-done.50.refs_0_.refs_3_, ...), custom_call_target="tpu_custom_call" | custom-call | flops 2415919104 | bytes 9437184 | tf_op jit(solution)/shard_map/down/pallas_call | solution.py:95
  315.2 5.4 %down.3 = bf16[384,1024]{1,0:T(8,128)(2,1)S(1)} custom-call(s32[1]{0:T(128)} %bitcast.refs_0_, bf16[384,384]{1,0:T(8,128)(2,1)S(1)} %hidden_units.3.refs_2_.refs_1_, bf16[384,384]{1,0:T(8,128)(2,1)S(1)} %collective-permute-done.64.refs_2_, bf16[384,384]{1,0:T(8,128)(2,1)S(1)} %collective-permute-done.65.refs_0_.refs_3_, ...), custom_call_target="tpu_custom_call" | custom-call | flops 2415919104 | bytes 9437184 | tf_op jit(solution)/shard_map/down/pallas_call | solution.py:95
  320.6 3.8 %collective-permute-start.73 = (bf16[192,1024]{1,0:T(8,128)(2,1)S(1)}, bf16[192,1024]{1,0:T(8,128)(2,1)S(1)}, u32[]{:S(2)}, u32[]{:S(2)}) collective-permute-start(bf16[192,1024]{1,0:T(8,128)(2,1)S(1)} %get-tuple-element.67), channel_id=1, source_target_pairs={{0,2},{1,3},{2,0},{3,1},{4,6},{5,7},{6,4},{7,5},{8,10},{9,11},{10,... | collective-permute-start | bytes 1179656 | tf_op jit(solution)/shard_map/ppermute | solution.py:23
  324.6 3.2 collective-permute-done.63.refs_9_
  327.9 22.5 %collective-permute-done.73.refs_10_ = bf16[192,1024]{1,0:T(8,128)(2,1)S(1)} collective-permute-done((bf16[192,1024]{1,0:T(8,128)(2,1)S(1)}, bf16[192,1024]{1,0:T(8,128)(2,1)S(1)}, u32[]{:S(2)}, u32[]{:S(2)}) %collective-permute-start.73) | collective-permute-done | bytes 393248 | tf_op jit(solution)/shard_map/ppermute | solution.py:23
  350.3 7.9 %collective-permute-done.74.refs_11_ = bf16[192,1024]{1,0:T(8,128)(2,1)S(1)} collective-permute-done((bf16[192,1024]{1,0:T(8,128)(2,1)S(1)}, bf16[192,1024]{1,0:T(8,128)(2,1)S(1)}, u32[]{:S(2)}, u32[]{:S(2)}) %collective-permute-start.74) | collective-permute-done | bytes 393248 | tf_op jit(solution)/shard_map/ppermute | solution.py:23
  362.8 2.6 combine.1
  (255 shorter events, 45.9 us)
Async XLA Ops:
  7.2 138.1 %reduce-scatter.3.cloned.1.call-start = ((), (), s32[]{:S(2)}) async-start(), calls=%async_computation.2 | async-start | bytes 1310720 | tf_op jit(solution)/shard_map/reduce_scatter | solution.py:756
  8.1 9.2 %collective-permute-start = (bf16[3,4096]{1,0:T(4,128)(2,1)S(1)}, bf16[3,4096]{1,0:T(4,128)(2,1)S(1)}, u32[]{:S(2)}, u32[]{:S(2)}) collective-permute-start(bf16[3,4096]{1,0:T(4,128)(2,1)S(1)} %slice.43), channel_id=1, source_target_pairs={{0,4},{4,8},{8,12},{12,16},{16,20},{20,24},{24,28},{1,5},{5,9},{9,... | collective-permute-start | bytes 73736 | tf_op jit(solution)/shard_map/ppermute | solution.py:19
  13.3 20.0 %collective-permute-start.1 = (bf16[384,1024]{1,0:T(8,128)(2,1)}, bf16[384,1024]{1,0:T(8,128)(2,1)S(1)}, u32[]{:S(2)}, u32[]{:S(2)}) collective-permute-start(bf16[384,1024]{1,0:T(8,128)(2,1)} %get-tuple-element.34), channel_id=1, source_target_pairs={{0,8},{4,12},{8,0},{12,4},{16,24},{20,28},{24,16},{28,20},{1,9},{5... | collective-permute-start | bytes 2359304 | tf_op jit(solution)/shard_map/ppermute | solution.py:23
  14.9 20.3 %collective-permute-start.2 = (bf16[384,1024]{1,0:T(8,128)(2,1)}, bf16[384,1024]{1,0:T(8,128)(2,1)S(1)}, u32[]{:S(2)}, u32[]{:S(2)}) collective-permute-start(bf16[384,1024]{1,0:T(8,128)(2,1)} %get-tuple-element.35), channel_id=1, source_target_pairs={{0,16},{4,20},{8,24},{12,28},{16,0},{20,4},{24,8},{28,12},{1,17},{... | collective-permute-start | bytes 2359304 | tf_op jit(solution)/shard_map/ppermute | solution.py:23
  36.2 9.2 %collective-permute-start.4 = (bf16[32,4096]{1,0:T(8,128)(2,1)S(1)}, bf16[32,4096]{1,0:T(8,128)(2,1)S(1)}, u32[]{:S(2)}, u32[]{:S(2)}) collective-permute-start(bf16[32,4096]{1,0:T(8,128)(2,1)S(1)} %join.4.refs_9_.refs_1_), channel_id=1, source_target_pairs={{0,8},{4,12},{8,0},{12,4},{16,24},{20,28},{24,16},{28,20},{1,9},{5... | collective-permute-start | bytes 786440 | tf_op jit(solution)/shard_map/ppermute | solution.py:23
  36.5 13.8 %collective-permute-start.6 = (bf16[32,4096]{1,0:T(8,128)(2,1)S(1)}, bf16[32,4096]{1,0:T(8,128)(2,1)S(1)}, u32[]{:S(2)}, u32[]{:S(2)}) collective-permute-start(bf16[32,4096]{1,0:T(8,128)(2,1)S(1)} %join.4.refs_9_.refs_1_), channel_id=1, source_target_pairs={{0,16},{4,20},{8,24},{12,28},{16,0},{20,4},{24,8},{28,12},{1,17},{... | collective-permute-start | bytes 786440 | tf_op jit(solution)/shard_map/ppermute | solution.py:23
  38.3 12.0 %collective-permute-start.8 = (bf16[32,4096]{1,0:T(8,128)(2,1)S(1)}, bf16[32,4096]{1,0:T(8,128)(2,1)S(1)}, u32[]{:S(2)}, u32[]{:S(2)}) collective-permute-start(bf16[32,4096]{1,0:T(8,128)(2,1)S(1)} %join.4.refs_9_.refs_1_), channel_id=1, source_target_pairs={{0,24},{4,28},{8,16},{12,20},{16,8},{20,12},{24,0},{28,4},{1,25},{... | collective-permute-start | bytes 786440 | tf_op jit(solution)/shard_map/ppermute | solution.py:23
  39.8 11.3 %collective-permute-start.3 = (bf16[32,4096]{1,0:T(8,128)(2,1)S(1)}, bf16[32,4096]{1,0:T(8,128)(2,1)S(1)}, u32[]{:S(2)}, u32[]{:S(2)}) collective-permute-start(bf16[32,4096]{1,0:T(8,128)(2,1)S(1)} %join.4.refs_9_.refs_1_), channel_id=1, source_target_pairs={{0,4},{4,0},{8,12},{12,8},{16,20},{20,16},{24,28},{28,24},{1,5},{5... | collective-permute-start | bytes 786440 | tf_op jit(solution)/shard_map/ppermute | solution.py:23
  45.4 5.6 %collective-permute-start.5 = (bf16[32,4096]{1,0:T(8,128)(2,1)S(1)}, bf16[32,4096]{1,0:T(8,128)(2,1)S(1)}, u32[]{:S(2)}, u32[]{:S(2)}) collective-permute-start(bf16[32,4096]{1,0:T(8,128)(2,1)S(1)} %collective-permute-done.4.refs_11_.refs_3_), channel_id=1, source_target_pairs={{0,4},{4,0},{8,12},{12,8},{16,20},{20,16},{24,28},{28,24},{1,5},{5... | collective-permute-start | bytes 786440 | tf_op jit(solution)/shard_map/ppermute | solution.py:23
  63.0 15.0 %collective-permute-start.11 = (bf16[64,4096]{1,0:T(8,128)(2,1)}, bf16[64,4096]{1,0:T(8,128)(2,1)S(1)}, u32[]{:S(2)}, u32[]{:S(2)}) collective-permute-start(bf16[64,4096]{1,0:T(8,128)(2,1)} %get-tuple-element.36.refs_2_), channel_id=1, source_target_pairs={{0,8},{4,12},{8,0},{12,4},{16,24},{20,28},{24,16},{28,20},{1,9},{5... | collective-permute-start | bytes 1572872 | tf_op jit(solution)/shard_map/ppermute | solution.py:23
  64.7 15.0 %collective-permute-start.13 = (bf16[64,4096]{1,0:T(8,128)(2,1)}, bf16[64,4096]{1,0:T(8,128)(2,1)S(1)}, u32[]{:S(2)}, u32[]{:S(2)}) collective-permute-start(bf16[64,4096]{1,0:T(8,128)(2,1)} %get-tuple-element.36.refs_2_), channel_id=1, source_target_pairs={{0,16},{4,20},{8,24},{12,28},{16,0},{20,4},{24,8},{28,12},{1,17},{... | collective-permute-start | bytes 1572872 | tf_op jit(solution)/shard_map/ppermute | solution.py:23
  73.4 15.8 %collective-permute-start.19 = (bf16[64,4096]{1,0:T(8,128)(2,1)}, bf16[64,4096]{1,0:T(8,128)(2,1)S(1)}, u32[]{:S(2)}, u32[]{:S(2)}) collective-permute-start(bf16[64,4096]{1,0:T(8,128)(2,1)} %get-tuple-element.38.refs_2_), channel_id=1, source_target_pairs={{0,8},{4,12},{8,0},{12,4},{16,24},{20,28},{24,16},{28,20},{1,9},{5... | collective-permute-start | bytes 1572872 | tf_op jit(solution)/shard_map/ppermute | solution.py:23
  75.1 15.8 %collective-permute-start.20 = (bf16[64,4096]{1,0:T(8,128)(2,1)}, bf16[64,4096]{1,0:T(8,128)(2,1)S(1)}, u32[]{:S(2)}, u32[]{:S(2)}) collective-permute-start(bf16[64,4096]{1,0:T(8,128)(2,1)} %get-tuple-element.38.refs_2_), channel_id=1, source_target_pairs={{0,16},{4,20},{8,24},{12,28},{16,0},{20,4},{24,8},{28,12},{1,17},{... | collective-permute-start | bytes 1572872 | tf_op jit(solution)/shard_map/ppermute | solution.py:23
  75.5 20.5 %collective-permute-start.10 = (bf16[64,4096]{1,0:T(8,128)(2,1)S(1)}, bf16[64,4096]{1,0:T(8,128)(2,1)S(1)}, u32[]{:S(2)}, u32[]{:S(2)}) collective-permute-start(bf16[64,4096]{1,0:T(8,128)(2,1)S(1)} %copy-done.38), channel_id=1, source_target_pairs={{0,4},{4,0},{8,12},{12,8},{16,20},{20,16},{24,28},{28,24},{1,5},{5... | collective-permute-start | bytes 1572872 | tf_op jit(solution)/shard_map/ppermute | solution.py:23
  80.8 14.7 %collective-permute-start.15 = (bf16[64,2048]{1,0:T(8,128)(2,1)S(1)}, bf16[64,2048]{1,0:T(8,128)(2,1)S(1)}, u32[]{:S(2)}, u32[]{:S(2)}) collective-permute-start(bf16[64,2048]{1,0:T(8,128)(2,1)S(1)} %get-tuple-element.39), channel_id=1, source_target_pairs={{0,16},{4,20},{8,24},{12,28},{16,0},{20,4},{24,8},{28,12},{1,17},{... | collective-permute-start | bytes 786440 | tf_op jit(solution)/shard_map/ppermute | solution.py:23
  81.3 14.2 %collective-permute-start.17 = (bf16[64,2048]{1,0:T(8,128)(2,1)S(1)}, bf16[64,2048]{1,0:T(8,128)(2,1)S(1)}, u32[]{:S(2)}, u32[]{:S(2)}) collective-permute-start(bf16[64,2048]{1,0:T(8,128)(2,1)S(1)} %get-tuple-element.40), channel_id=1, source_target_pairs={{0,8},{4,12},{8,0},{12,4},{16,24},{20,28},{24,16},{28,20},{1,9},{5... | collective-permute-start | bytes 786440 | tf_op jit(solution)/shard_map/ppermute | solution.py:23
  89.3 8.1 %collective-permute-start.12 = (bf16[64,4096]{1,0:T(8,128)(2,1)S(1)}, bf16[64,4096]{1,0:T(8,128)(2,1)S(1)}, u32[]{:S(2)}, u32[]{:S(2)}) collective-permute-start(bf16[64,4096]{1,0:T(8,128)(2,1)S(1)} %collective-permute-done.11.refs_0_.refs_4_.refs_6_), channel_id=1, source_target_pairs={{0,4},{4,0},{8,12},{12,8},{16,20},{20,16},{24,28},{28,24},{1,5},{5... | collective-permute-start | bytes 1572872 | tf_op jit(solution)/shard_map/ppermute | solution.py:23
  91.0 6.4 %collective-permute-start.14 = (bf16[64,4096]{1,0:T(8,128)(2,1)S(1)}, bf16[64,4096]{1,0:T(8,128)(2,1)S(1)}, u32[]{:S(2)}, u32[]{:S(2)}) collective-permute-start(bf16[64,4096]{1,0:T(8,128)(2,1)S(1)} %collective-permute-done.13.refs_1_.refs_6_.refs_7_), channel_id=1, source_target_pairs={{0,4},{4,0},{8,12},{12,8},{16,20},{20,16},{24,28},{28,24},{1,5},{5... | collective-permute-start | bytes 1572872 | tf_op jit(solution)/shard_map/ppermute | solution.py:23
  108.3 53.7 %reduce-scatter.5.cloned.1.call-start = ((), (), s32[]{:S(2)}) async-start(), calls=%async_computation.3 | async-start | bytes 1310720 | tf_op jit(solution)/shard_map/reduce_scatter | solution.py:756
  111.6 8.4 %collective-permute-start.24 = (bf16[64,2048]{1,0:T(8,128)(2,1)S(1)}, bf16[64,2048]{1,0:T(8,128)(2,1)S(1)}, u32[]{:S(2)}, u32[]{:S(2)}) collective-permute-start(bf16[64,2048]{1,0:T(8,128)(2,1)S(1)} %get-tuple-element.41), channel_id=1, source_target_pairs={{0,16},{4,20},{8,24},{12,28},{16,0},{20,4},{24,8},{28,12},{1,17},{... | collective-permute-start | bytes 786440 | tf_op jit(solution)/shard_map/ppermute | solution.py:23
  112.0 8.1 %collective-permute-start.26 = (bf16[64,2048]{1,0:T(8,128)(2,1)S(1)}, bf16[64,2048]{1,0:T(8,128)(2,1)S(1)}, u32[]{:S(2)}, u32[]{:S(2)}) collective-permute-start(bf16[64,2048]{1,0:T(8,128)(2,1)S(1)} %get-tuple-element.42), channel_id=1, source_target_pairs={{0,8},{4,12},{8,0},{12,4},{16,24},{20,28},{24,16},{28,20},{1,9},{5... | collective-permute-start | bytes 786440 | tf_op jit(solution)/shard_map/ppermute | solution.py:23
  113.7 6.8 %collective-permute-start.21 = (bf16[64,4096]{1,0:T(8,128)(2,1)S(1)}, bf16[64,4096]{1,0:T(8,128)(2,1)S(1)}, u32[]{:S(2)}, u32[]{:S(2)}) collective-permute-start(bf16[64,4096]{1,0:T(8,128)(2,1)S(1)} %copy-done.20), channel_id=1, source_target_pairs={{0,4},{4,0},{8,12},{12,8},{16,20},{20,16},{24,28},{28,24},{1,5},{5... | collective-permute-start | bytes 1572872 | tf_op jit(solution)/shard_map/ppermute | solution.py:23
  113.7 6.8 %collective-permute-start.22 = (bf16[64,4096]{1,0:T(8,128)(2,1)}, bf16[64,4096]{1,0:T(8,128)(2,1)S(1)}, u32[]{:S(2)}, u32[]{:S(2)}) collective-permute-start(bf16[64,4096]{1,0:T(8,128)(2,1)} %copy-done.21), channel_id=1, source_target_pairs={{0,4},{4,0},{8,12},{12,8},{16,20},{20,16},{24,28},{28,24},{1,5},{5... | collective-permute-start | bytes 1572872 | tf_op jit(solution)/shard_map/ppermute | solution.py:23
  114.2 6.3 %collective-permute-start.23 = (bf16[64,4096]{1,0:T(8,128)(2,1)}, bf16[64,4096]{1,0:T(8,128)(2,1)S(1)}, u32[]{:S(2)}, u32[]{:S(2)}) collective-permute-start(bf16[64,4096]{1,0:T(8,128)(2,1)} %copy-done.24), channel_id=1, source_target_pairs={{0,4},{4,0},{8,12},{12,8},{16,20},{20,16},{24,28},{28,24},{1,5},{5... | collective-permute-start | bytes 1572872 | tf_op jit(solution)/shard_map/ppermute | solution.py:23
  142.0 28.9 %collective-permute-start.29 = (bf16[384,1024]{1,0:T(8,128)(2,1)}, bf16[384,1024]{1,0:T(8,128)(2,1)S(1)}, u32[]{:S(2)}, u32[]{:S(2)}) collective-permute-start(bf16[384,1024]{1,0:T(8,128)(2,1)} %get-tuple-element.45), channel_id=1, source_target_pairs={{0,12},{4,8},{8,4},{12,0},{16,28},{20,24},{24,20},{28,16},{1,13},{... | collective-permute-start | bytes 2359304 | tf_op jit(solution)/shard_map/ppermute | solution.py:23
  143.2 52.1 %collective-permute-start.30 = (bf16[384,1024]{1,0:T(8,128)(2,1)}, bf16[384,1024]{1,0:T(8,128)(2,1)S(1)}, u32[]{:S(2)}, u32[]{:S(2)}) collective-permute-start(bf16[384,1024]{1,0:T(8,128)(2,1)} %get-tuple-element.46), channel_id=1, source_target_pairs={{0,20},{4,16},{8,28},{12,24},{16,4},{20,0},{24,12},{28,8},{1,21},{... | collective-permute-start | bytes 2359304 | tf_op jit(solution)/shard_map/ppermute | solution.py:23
  143.8 51.5 %collective-permute-start.31 = (bf16[384,1024]{1,0:T(8,128)(2,1)}, bf16[384,1024]{1,0:T(8,128)(2,1)}, u32[]{:S(2)}, u32[]{:S(2)}) collective-permute-start(bf16[384,1024]{1,0:T(8,128)(2,1)} %get-tuple-element.47), channel_id=1, source_target_pairs={{0,24},{4,28},{8,16},{12,20},{16,8},{20,12},{24,0},{28,4},{1,25},{... | collective-permute-start | bytes 2359304 | tf_op jit(solution)/shard_map/ppermute | solution.py:23
  166.8 28.4 %collective-permute-start.28 = (bf16[192,1024]{1,0:T(8,128)(2,1)S(1)}, bf16[192,1024]{1,0:T(8,128)(2,1)S(1)}, u32[]{:S(2)}, u32[]{:S(2)}) collective-permute-start(bf16[192,1024]{1,0:T(8,128)(2,1)S(1)} %get-tuple-element.44), channel_id=1, source_target_pairs={{0,1},{1,0},{2,3},{3,2},{4,5},{5,4},{6,7},{7,6},{8,9},{9,8},{10,11... | collective-permute-start | bytes 1179656 | tf_op jit(solution)/shard_map/ppermute | solution.py:23
  169.5 30.3 %collective-permute-start.37 = (bf16[384,1024]{1,0:T(8,128)(2,1)}, bf16[384,1024]{1,0:T(8,128)(2,1)S(1)}, u32[]{:S(2)}, u32[]{:S(2)}) collective-permute-start(bf16[384,1024]{1,0:T(8,128)(2,1)} %get-tuple-element.48), channel_id=1, source_target_pairs={{0,28},{4,24},{8,20},{12,16},{16,12},{20,8},{24,4},{28,0},{1,29},{... | collective-permute-start | bytes 2359304 | tf_op jit(solution)/shard_map/ppermute | solution.py:23
  170.9 28.9 %collective-permute-start.38 = (bf16[384,1024]{1,0:T(8,128)(2,1)}, bf16[384,1024]{1,0:T(8,128)(2,1)S(1)}, u32[]{:S(2)}, u32[]{:S(2)}) collective-permute-start(bf16[384,1024]{1,0:T(8,128)(2,1)} %get-tuple-element.49), channel_id=1, source_target_pairs={{0,4},{4,0},{8,12},{12,8},{16,20},{20,16},{24,28},{28,24},{1,5},{5... | collective-permute-start | bytes 2359304 | tf_op jit(solution)/shard_map/ppermute | solution.py:23
  195.7 20.0 %collective-permute-start.33 = (bf16[384,1024]{1,0:T(8,128)(2,1)S(1)}, bf16[384,1024]{1,0:T(8,128)(2,1)S(1)}, u32[]{:S(2)}, u32[]{:S(2)}) collective-permute-start(bf16[384,1024]{1,0:T(8,128)(2,1)S(1)} %join.5.refs_4_), channel_id=1, source_target_pairs={{0,8},{4,12},{8,0},{12,4},{16,24},{20,28},{24,16},{28,20},{1,9},{5... | collective-permute-start | bytes 2359304 | tf_op jit(solution)/shard_map/ppermute | solution.py:23
  197.1 20.0 %collective-permute-start.35 = (bf16[384,1024]{1,0:T(8,128)(2,1)S(1)}, bf16[384,1024]{1,0:T(8,128)(2,1)S(1)}, u32[]{:S(2)}, u32[]{:S(2)}) collective-permute-start(bf16[384,1024]{1,0:T(8,128)(2,1)S(1)} %join.5.refs_4_), channel_id=1, source_target_pairs={{0,16},{4,20},{8,24},{12,28},{16,0},{20,4},{24,8},{28,12},{1,17},{... | collective-permute-start | bytes 2359304 | tf_op jit(solution)/shard_map/ppermute | solution.py:23
  197.7 28.2 %collective-permute-start.43 = (bf16[192,1024]{1,0:T(8,128)(2,1)S(1)}, bf16[192,1024]{1,0:T(8,128)(2,1)S(1)}, u32[]{:S(2)}, u32[]{:S(2)}) collective-permute-start(bf16[192,1024]{1,0:T(8,128)(2,1)S(1)} %get-tuple-element.52), channel_id=1, source_target_pairs={{0,2},{1,3},{2,0},{3,1},{4,6},{5,7},{6,4},{7,5},{8,10},{9,11},{10,... | collective-permute-start | bytes 1179656 | tf_op jit(solution)/shard_map/ppermute | solution.py:23
  199.8 35.1 %collective-permute-start.44 = (bf16[192,1024]{1,0:T(8,128)(2,1)S(1)}, bf16[192,1024]{1,0:T(8,128)(2,1)S(1)}, u32[]{:S(2)}, u32[]{:S(2)}) collective-permute-start(bf16[192,1024]{1,0:T(8,128)(2,1)S(1)} %get-tuple-element.53), channel_id=1, source_target_pairs={{0,3},{1,2},{2,1},{3,0},{4,7},{5,6},{6,5},{7,4},{8,11},{9,10},{10,... | collective-permute-start | bytes 1179656 | tf_op jit(solution)/shard_map/ppermute | solution.py:23
  199.8 46.6 %collective-permute-start.32 = (bf16[384,1024]{1,0:T(8,128)(2,1)S(1)}, bf16[384,1024]{1,0:T(8,128)(2,1)S(1)}, u32[]{:S(2)}, u32[]{:S(2)}) collective-permute-start(bf16[384,1024]{1,0:T(8,128)(2,1)S(1)} %join.5.refs_4_), channel_id=1, source_target_pairs={{0,4},{4,0},{8,12},{12,8},{16,20},{20,16},{24,28},{28,24},{1,5},{5... | collective-permute-start | bytes 2359304 | tf_op jit(solution)/shard_map/ppermute | solution.py:23
  215.7 31.5 %collective-permute-start.34 = (bf16[384,1024]{1,0:T(8,128)(2,1)S(1)}, bf16[384,1024]{1,0:T(8,128)(2,1)S(1)}, u32[]{:S(2)}, u32[]{:S(2)}) collective-permute-start(bf16[384,1024]{1,0:T(8,128)(2,1)S(1)} %collective-permute-done.33.refs_0_.refs_6_.refs_2_), channel_id=1, source_target_pairs={{0,4},{4,0},{8,12},{12,8},{16,20},{20,16},{24,28},{28,24},{1,5},{5... | collective-permute-start | bytes 2359304 | tf_op jit(solution)/shard_map/ppermute | solution.py:23
  217.1 18.6 %collective-permute-start.39 = (bf16[192,1024]{1,0:T(8,128)(2,1)S(1)}, bf16[192,1024]{1,0:T(8,128)(2,1)S(1)}, u32[]{:S(2)}, u32[]{:S(2)}) collective-permute-start(bf16[192,1024]{1,0:T(8,128)(2,1)S(1)} %get-tuple-element.50), channel_id=1, source_target_pairs={{0,16},{4,20},{8,24},{12,28},{16,0},{20,4},{24,8},{28,12},{1,17},{... | collective-permute-start | bytes 1179656 | tf_op jit(solution)/shard_map/ppermute | solution.py:23
  226.0 23.7 %collective-permute-start.36 = (bf16[384,1024]{1,0:T(8,128)(2,1)S(1)}, bf16[384,1024]{1,0:T(8,128)(2,1)S(1)}, u32[]{:S(2)}, u32[]{:S(2)}) collective-permute-start(bf16[384,1024]{1,0:T(8,128)(2,1)S(1)} %collective-permute-done.35.refs_1_.refs_8_.refs_3_), channel_id=1, source_target_pairs={{0,4},{4,0},{8,12},{12,8},{16,20},{20,16},{24,28},{28,24},{1,5},{5... | collective-permute-start | bytes 2359304 | tf_op jit(solution)/shard_map/ppermute | solution.py:23
  234.9 11.1 %collective-permute-start.41 = (bf16[192,1024]{1,0:T(8,128)(2,1)S(1)}, bf16[192,1024]{1,0:T(8,128)(2,1)S(1)}, u32[]{:S(2)}, u32[]{:S(2)}) collective-permute-start(bf16[192,1024]{1,0:T(8,128)(2,1)S(1)} %get-tuple-element.51), channel_id=1, source_target_pairs={{0,8},{4,12},{8,0},{12,4},{16,24},{20,28},{24,16},{28,20},{1,9},{5... | collective-permute-start | bytes 1179656 | tf_op jit(solution)/shard_map/ppermute | solution.py:23
  235.7 14.1 %collective-permute-start.40 = (bf16[192,1024]{1,0:T(8,128)(2,1)S(1)}, bf16[192,1024]{1,0:T(8,128)(2,1)S(1)}, u32[]{:S(2)}, u32[]{:S(2)}) collective-permute-start(bf16[192,1024]{1,0:T(8,128)(2,1)S(1)} %collective-permute-done.39.refs_10_), channel_id=1, source_target_pairs={{0,4},{4,0},{8,12},{12,8},{16,20},{20,16},{24,28},{28,24},{1,5},{5... | collective-permute-start | bytes 1179656 | tf_op jit(solution)/shard_map/ppermute | solution.py:23
  246.4 20.0 %collective-permute-start.45 = (bf16[384,1024]{1,0:T(8,128)(2,1)S(1)}, bf16[384,1024]{1,0:T(8,128)(2,1)S(1)}, u32[]{:S(2)}, u32[]{:S(2)}) collective-permute-start(bf16[384,1024]{1,0:T(8,128)(2,1)S(1)} %join.6.refs_4_), channel_id=1, source_target_pairs={{0,8},{4,12},{8,0},{12,4},{16,24},{20,28},{24,16},{28,20},{1,9},{5... | collective-permute-start | bytes 2359304 | tf_op jit(solution)/shard_map/ppermute | solution.py:23
  247.2 19.7 %collective-permute-start.46 = (bf16[384,1024]{1,0:T(8,128)(2,1)S(1)}, bf16[384,1024]{1,0:T(8,128)(2,1)S(1)}, u32[]{:S(2)}, u32[]{:S(2)}) collective-permute-start(bf16[384,1024]{1,0:T(8,128)(2,1)S(1)} %join.6.refs_4_), channel_id=1, source_target_pairs={{0,16},{4,20},{8,24},{12,28},{16,0},{20,4},{24,8},{28,12},{1,17},{... | collective-permute-start | bytes 2359304 | tf_op jit(solution)/shard_map/ppermute | solution.py:23
  249.7 30.4 %collective-permute-start.54 = (bf16[384,1024]{1,0:T(8,128)(2,1)S(1)}, bf16[384,1024]{1,0:T(8,128)(2,1)S(1)}, u32[]{:S(2)}, u32[]{:S(2)}) collective-permute-start(bf16[384,1024]{1,0:T(8,128)(2,1)S(1)} %join.6.refs_4_), channel_id=1, source_target_pairs={{0,4},{4,0},{8,12},{12,8},{16,20},{20,16},{24,28},{28,24},{1,5},{5... | collective-permute-start | bytes 2359304 | tf_op jit(solution)/shard_map/ppermute | solution.py:23
  266.9 10.5 %collective-permute-start.47 = (bf16[192,1024]{1,0:T(8,128)(2,1)S(1)}, bf16[192,1024]{1,0:T(8,128)(2,1)S(1)}, u32[]{:S(2)}, u32[]{:S(2)}) collective-permute-start(bf16[192,1024]{1,0:T(8,128)(2,1)S(1)} %get-tuple-element.54), channel_id=1, source_target_pairs={{0,16},{4,20},{8,24},{12,28},{16,0},{20,4},{24,8},{28,12},{1,17},{... | collective-permute-start | bytes 1179656 | tf_op jit(solution)/shard_map/ppermute | solution.py:23
  268.4 12.1 %collective-permute-start.55 = (bf16[384,1024]{1,0:T(8,128)(2,1)S(1)}, bf16[384,1024]{1,0:T(8,128)(2,1)S(1)}, u32[]{:S(2)}, u32[]{:S(2)}) collective-permute-start(bf16[384,1024]{1,0:T(8,128)(2,1)S(1)} %collective-permute-done.45.refs_0_.refs_6_), channel_id=1, source_target_pairs={{0,4},{4,0},{8,12},{12,8},{16,20},{20,16},{24,28},{28,24},{1,5},{5... | collective-permute-start | bytes 2359304 | tf_op jit(solution)/shard_map/ppermute | solution.py:23
  268.4 13.6 %collective-permute-start.56 = (bf16[384,1024]{1,0:T(8,128)(2,1)S(1)}, bf16[384,1024]{1,0:T(8,128)(2,1)S(1)}, u32[]{:S(2)}, u32[]{:S(2)}) collective-permute-start(bf16[384,1024]{1,0:T(8,128)(2,1)S(1)} %collective-permute-done.46.refs_1_.refs_8_), channel_id=1, source_target_pairs={{0,4},{4,0},{8,12},{12,8},{16,20},{20,16},{24,28},{28,24},{1,5},{5... | collective-permute-start | bytes 2359304 | tf_op jit(solution)/shard_map/ppermute | solution.py:23
  268.9 11.0 %collective-permute-start.48 = (bf16[192,1024]{1,0:T(8,128)(2,1)S(1)}, bf16[192,1024]{1,0:T(8,128)(2,1)S(1)}, u32[]{:S(2)}, u32[]{:S(2)}) collective-permute-start(bf16[192,1024]{1,0:T(8,128)(2,1)S(1)} %get-tuple-element.55), channel_id=1, source_target_pairs={{0,8},{4,12},{8,0},{12,4},{16,24},{20,28},{24,16},{28,20},{1,9},{5... | collective-permute-start | bytes 1179656 | tf_op jit(solution)/shard_map/ppermute | solution.py:23
  280.1 12.2 %collective-permute-start.50 = (bf16[384,384]{1,0:T(8,128)(2,1)S(1)}, bf16[384,384]{1,0:T(8,128)(2,1)S(1)}, u32[]{:S(2)}, u32[]{:S(2)}) collective-permute-start(bf16[384,384]{1,0:T(8,128)(2,1)S(1)} %join.7.refs_1_), channel_id=1, source_target_pairs={{0,8},{4,12},{8,0},{12,4},{16,24},{20,28},{24,16},{28,20},{1,9},{5... | collective-permute-start | bytes 884744 | tf_op jit(solution)/shard_map/ppermute | solution.py:23
  280.5 11.7 %collective-permute-start.52 = (bf16[384,384]{1,0:T(8,128)(2,1)S(1)}, bf16[384,384]{1,0:T(8,128)(2,1)S(1)}, u32[]{:S(2)}, u32[]{:S(2)}) collective-permute-start(bf16[384,384]{1,0:T(8,128)(2,1)S(1)} %join.7.refs_1_), channel_id=1, source_target_pairs={{0,16},{4,20},{8,24},{12,28},{16,0},{20,4},{24,8},{28,12},{1,17},{... | collective-permute-start | bytes 884744 | tf_op jit(solution)/shard_map/ppermute | solution.py:23
  292.3 6.8 %collective-permute-start.59 = (bf16[192,384]{1,0:T(8,128)(2,1)S(1)}, bf16[192,384]{1,0:T(8,128)(2,1)S(1)}, u32[]{:S(2)}, u32[]{:S(2)}) collective-permute-start(bf16[192,384]{1,0:T(8,128)(2,1)S(1)} %get-tuple-element.56), channel_id=1, source_target_pairs={{0,16},{4,20},{8,24},{12,28},{16,0},{20,4},{24,8},{28,12},{1,17},{... | collective-permute-start | bytes 442376 | tf_op jit(solution)/shard_map/ppermute | solution.py:23
  292.9 6.8 %collective-permute-start.61 = (bf16[192,384]{1,0:T(8,128)(2,1)S(1)}, bf16[192,384]{1,0:T(8,128)(2,1)S(1)}, u32[]{:S(2)}, u32[]{:S(2)}) collective-permute-start(bf16[192,384]{1,0:T(8,128)(2,1)S(1)} %get-tuple-element.57), channel_id=1, source_target_pairs={{0,8},{4,12},{8,0},{12,4},{16,24},{20,28},{24,16},{28,20},{1,9},{5... | collective-permute-start | bytes 442376 | tf_op jit(solution)/shard_map/ppermute | solution.py:23
  294.5 10.1 %collective-permute-start.65 = (bf16[384,384]{1,0:T(8,128)(2,1)S(1)}, bf16[384,384]{1,0:T(8,128)(2,1)S(1)}, u32[]{:S(2)}, u32[]{:S(2)}) collective-permute-start(bf16[384,384]{1,0:T(8,128)(2,1)S(1)} %hidden_units.3.refs_2_.refs_1_), channel_id=1, source_target_pairs={{0,8},{4,12},{8,0},{12,4},{16,24},{20,28},{24,16},{28,20},{1,9},{5... | collective-permute-start | bytes 884744 | tf_op jit(solution)/shard_map/ppermute | solution.py:23
  294.9 9.7 %collective-permute-start.67 = (bf16[384,384]{1,0:T(8,128)(2,1)S(1)}, bf16[384,384]{1,0:T(8,128)(2,1)S(1)}, u32[]{:S(2)}, u32[]{:S(2)}) collective-permute-start(bf16[384,384]{1,0:T(8,128)(2,1)S(1)} %hidden_units.3.refs_2_.refs_1_), channel_id=1, source_target_pairs={{0,16},{4,20},{8,24},{12,28},{16,0},{20,4},{24,8},{28,12},{1,17},{... | collective-permute-start | bytes 884744 | tf_op jit(solution)/shard_map/ppermute | solution.py:23
  296.4 8.8 %collective-permute-start.49 = (bf16[384,384]{1,0:T(8,128)(2,1)S(1)}, bf16[384,384]{1,0:T(8,128)(2,1)S(1)}, u32[]{:S(2)}, u32[]{:S(2)}) collective-permute-start(bf16[384,384]{1,0:T(8,128)(2,1)S(1)} %join.7.refs_1_), channel_id=1, source_target_pairs={{0,4},{4,0},{8,12},{12,8},{16,20},{20,16},{24,28},{28,24},{1,5},{5... | collective-permute-start | bytes 884744 | tf_op jit(solution)/shard_map/ppermute | solution.py:23
  299.1 6.2 %collective-permute-start.51 = (bf16[384,384]{1,0:T(8,128)(2,1)S(1)}, bf16[384,384]{1,0:T(8,128)(2,1)S(1)}, u32[]{:S(2)}, u32[]{:S(2)}) collective-permute-start(bf16[384,384]{1,0:T(8,128)(2,1)S(1)} %collective-permute-done.50.refs_0_.refs_3_), channel_id=1, source_target_pairs={{0,4},{4,0},{8,12},{12,8},{16,20},{20,16},{24,28},{28,24},{1,5},{5... | collective-permute-start | bytes 884744 | tf_op jit(solution)/shard_map/ppermute | solution.py:23
  299.6 7.2 %collective-permute-start.53 = (bf16[384,384]{1,0:T(8,128)(2,1)S(1)}, bf16[384,384]{1,0:T(8,128)(2,1)S(1)}, u32[]{:S(2)}, u32[]{:S(2)}) collective-permute-start(bf16[384,384]{1,0:T(8,128)(2,1)S(1)} %collective-permute-done.52.refs_1_.refs_5_), channel_id=1, source_target_pairs={{0,4},{4,0},{8,12},{12,8},{16,20},{20,16},{24,28},{28,24},{1,5},{5... | collective-permute-start | bytes 884744 | tf_op jit(solution)/shard_map/ppermute | solution.py:23
  305.2 9.7 %collective-permute-start.64 = (bf16[384,384]{1,0:T(8,128)(2,1)S(1)}, bf16[384,384]{1,0:T(8,128)(2,1)S(1)}, u32[]{:S(2)}, u32[]{:S(2)}) collective-permute-start(bf16[384,384]{1,0:T(8,128)(2,1)S(1)} %hidden_units.3.refs_2_.refs_1_), channel_id=1, source_target_pairs={{0,4},{4,0},{8,12},{12,8},{16,20},{20,16},{24,28},{28,24},{1,5},{5... | collective-permute-start | bytes 884744 | tf_op jit(solution)/shard_map/ppermute | solution.py:23
  305.2 8.2 %collective-permute-start.69 = (bf16[192,384]{1,0:T(8,128)(2,1)S(1)}, bf16[192,384]{1,0:T(8,128)(2,1)S(1)}, u32[]{:S(2)}, u32[]{:S(2)}) collective-permute-start(bf16[192,384]{1,0:T(8,128)(2,1)S(1)} %get-tuple-element.58), channel_id=1, source_target_pairs={{0,16},{4,20},{8,24},{12,28},{16,0},{20,4},{24,8},{28,12},{1,17},{... | collective-permute-start | bytes 442376 | tf_op jit(solution)/shard_map/ppermute | solution.py:23
  306.8 7.0 %collective-permute-start.71 = (bf16[192,384]{1,0:T(8,128)(2,1)S(1)}, bf16[192,384]{1,0:T(8,128)(2,1)S(1)}, u32[]{:S(2)}, u32[]{:S(2)}) collective-permute-start(bf16[192,384]{1,0:T(8,128)(2,1)S(1)} %get-tuple-element.59), channel_id=1, source_target_pairs={{0,8},{4,12},{8,0},{12,4},{16,24},{20,28},{24,16},{28,20},{1,9},{5... | collective-permute-start | bytes 442376 | tf_op jit(solution)/shard_map/ppermute | solution.py:23
  307.6 7.3 %collective-permute-start.66 = (bf16[384,384]{1,0:T(8,128)(2,1)S(1)}, bf16[384,384]{1,0:T(8,128)(2,1)S(1)}, u32[]{:S(2)}, u32[]{:S(2)}) collective-permute-start(bf16[384,384]{1,0:T(8,128)(2,1)S(1)} %collective-permute-done.65.refs_0_.refs_3_), channel_id=1, source_target_pairs={{0,4},{4,0},{8,12},{12,8},{16,20},{20,16},{24,28},{28,24},{1,5},{5... | collective-permute-start | bytes 884744 | tf_op jit(solution)/shard_map/ppermute | solution.py:23
  307.6 7.3 %collective-permute-start.68 = (bf16[384,384]{1,0:T(8,128)(2,1)S(1)}, bf16[384,384]{1,0:T(8,128)(2,1)S(1)}, u32[]{:S(2)}, u32[]{:S(2)}) collective-permute-start(bf16[384,384]{1,0:T(8,128)(2,1)S(1)} %collective-permute-done.67.refs_1_.refs_5_), channel_id=1, source_target_pairs={{0,4},{4,0},{8,12},{12,8},{16,20},{20,16},{24,28},{28,24},{1,5},{5... | collective-permute-start | bytes 884744 | tf_op jit(solution)/shard_map/ppermute | solution.py:23
  314.9 13.0 %collective-permute-start.63 = (bf16[192,1024]{1,0:T(8,128)(2,1)}, bf16[192,1024]{1,0:T(8,128)(2,1)}, u32[]{:S(2)}, u32[]{:S(2)}) collective-permute-start(bf16[192,1024]{1,0:T(8,128)(2,1)} %get-tuple-element.68), channel_id=1, source_target_pairs={{0,1},{1,0},{2,3},{3,2},{4,5},{5,4},{6,7},{7,6},{8,9},{9,8},{10,11... | collective-permute-start | bytes 1179656 | tf_op jit(solution)/shard_map/ppermute | solution.py:23
  320.6 29.7 %collective-permute-start.73 = (bf16[192,1024]{1,0:T(8,128)(2,1)S(1)}, bf16[192,1024]{1,0:T(8,128)(2,1)S(1)}, u32[]{:S(2)}, u32[]{:S(2)}) collective-permute-start(bf16[192,1024]{1,0:T(8,128)(2,1)S(1)} %get-tuple-element.67), channel_id=1, source_target_pairs={{0,2},{1,3},{2,0},{3,1},{4,6},{5,7},{6,4},{7,5},{8,10},{9,11},{10,... | collective-permute-start | bytes 1179656 | tf_op jit(solution)/shard_map/ppermute | solution.py:23
  324.4 33.8 %collective-permute-start.74 = (bf16[192,1024]{1,0:T(8,128)(2,1)S(1)}, bf16[192,1024]{1,0:T(8,128)(2,1)S(1)}, u32[]{:S(2)}, u32[]{:S(2)}) collective-permute-start(bf16[192,1024]{1,0:T(8,128)(2,1)S(1)} %get-tuple-element.66), channel_id=1, source_target_pairs={{0,3},{1,2},{2,1},{3,0},{4,7},{5,6},{6,5},{7,4},{8,11},{9,10},{10,... | collective-permute-start | bytes 1179656 | tf_op jit(solution)/shard_map/ppermute | solution.py:23
  (60 other events, 1081.8 us)
Sparse Core Ops, SparseCore 0:
  108.4 25.2 reduce-scatter.2
  136.1 25.7 reduce-scatter.4

commit v5 on v4

--- a/solution.py
+++ b/solution.py
@@ -107,27 +107,34 @@
     )(*scalars, *operands, *after)
 
 
-def cut_kernel(count, *refs):
-    for source, out in zip(refs[-2 * count : -count], refs[-count:]):
-        out[...] = source[...]
-
-
-def cut_columns(me, rows, width, masks, after=()):
+def cut_kernel(layout, me, *refs):
+    count = sum(len(pieces) for pieces in layout)
+    sources, outs = iter(refs[:count]), refs[count:]
+    for pieces, out in zip(layout, outs):
+        width = out.shape[1] // len(pieces)
+        for place in range(len(pieces)):
+            out[:, place * width : (place + 1) * width] = next(sources)[...]
+
+
+def cut_columns(me, rows, width, layout, after=()):
     step = rows.shape[0] // 3
-
-    def block(mask):
-        return pl.BlockSpec((step, width), lambda i, me: (i, me[0] ^ mask))
-
-    return launch(
-        functools.partial(cut_kernel, len(masks)),
+    parts = rows.shape[1] // lax.axis_size("ctx") // width
+
+    def block(mask, part):
+        return pl.BlockSpec((step, width), lambda i, me: (i, (me[0] ^ mask) * parts + part))
+
+    flat = [piece for pieces in layout for piece in pieces]
+    widths = [width * len(pieces) for pieces in layout]
+    return launch(
+        functools.partial(cut_kernel, layout),
         [me],
-        [rows] * len(masks),
-        [block(mask) for mask in masks],
-        [pl.BlockSpec((step, width), lambda i, me: (i, 0))] * len(masks),
-        [jax.ShapeDtypeStruct((rows.shape[0], width), rows.dtype)] * len(masks),
+        [rows] * len(flat),
+        [block(*piece) for piece in flat],
+        [pl.BlockSpec((step, wide), lambda i, me: (i, 0)) for wide in widths],
+        [jax.ShapeDtypeStruct((rows.shape[0], wide), rows.dtype) for wide in widths],
         after=after,
         grid=(3,),
-        cost_estimate=cost(0, 4 * rows.shape[0] * width * len(masks)),
+        cost_estimate=cost(0, 4 * rows.shape[0] * width * len(flat)),
         name="cut_columns",
     )
 
@@ -606,6 +613,112 @@
             2 * slots * depth * columns, 2 * (slots * depth + depth * columns + slots * columns)
         ),
         name="down",
+    )
+
+
+def cross_kernel(me, *refs):
+    units, (own, *sent), refs = refs[:6], refs[6:12], refs[12:]
+    keep, give_a, give_b, held, sems = refs
+    width = own.shape[0]
+    turn = pl.program_id(0)
+
+    @pl.when(turn == 0)
+    def _():
+        copies = []
+        for mask, unit in enumerate(units):
+            column = (2, 3, 0, 1, 4, 5)[mask] * width
+            copies.append(
+                pltpu.make_async_copy(unit, held.at[:, pl.ds(column, width)], sems.at[mask])
+            )
+        for copy in copies:
+            copy.start()
+        for copy in copies:
+            copy.wait()
+
+    def summed(first, weights):
+        tall = jnp.concatenate([weight[...] for weight in weights], axis=0)
+        rows = held[:, first * width : (first + 4) * width]
+        return jnp.dot(rows, tall, preferred_element_type=jnp.float32).astype(keep.dtype)
+
+    for step, out in enumerate((keep, give_a, keep, give_b)):
+
+        @pl.when(turn == step)
+        def _():
+            if step < 2:
+                out[...] = summed(0, [sent[1], sent[2], own, sent[0]])
+            else:
+                out[...] = summed(2, [own, sent[0], sent[3], sent[4]])
+
+
+def cross_down(me, units, weights, own, after=()):
+    width = own.shape[0]
+    half = weights[2].shape[1] // 2
+    slots = units[0].shape[0]
+
+    def mine(j, me):
+        return (0, (me[0] ^ (jnp.where(j == 1, 4, 0) + jnp.where(j == 3, 2, 0))) * 2 + j // 2)
+
+    front = pl.BlockSpec((width, half), lambda j, me: (0, jnp.minimum(j, 1)))
+    back = pl.BlockSpec((width, half), lambda j, me: (0, jnp.maximum(j - 2, 0)))
+    given = pl.BlockSpec((slots, half), lambda j, me: (0, 0))
+    return launch(
+        cross_kernel,
+        [me],
+        [units[mask] for mask in range(6)] + [own] + [weights[mask] for mask in range(1, 6)],
+        [ANY] * 6
+        + [
+            pl.BlockSpec((width, half), mine),
+            pl.BlockSpec((width, half), lambda j, me: (0, j)),
+            front,
+            front,
+            back,
+            back,
+        ],
+        [pl.BlockSpec((slots, half), lambda j, me: (0, j // 2)), given, given],
+        [
+            jax.ShapeDtypeStruct((slots, 2 * half), jnp.bfloat16),
+            jax.ShapeDtypeStruct((slots, half), jnp.bfloat16),
+            jax.ShapeDtypeStruct((slots, half), jnp.bfloat16),
+        ],
+        after=after,
+        grid=(4,),
+        scratch=[
+            pltpu.VMEM((slots, 6 * width), jnp.bfloat16),
+            pltpu.SemaphoreType.DMA((6,)),
+        ],
+        limit=40,
+        cost_estimate=cost(16 * slots * 4 * width * half, 24 * width * half * 2),
+        name="cross_down",
+    )
+
+
+def settle_kernel(keep, first, second, *outs):
+    half = first.shape[1]
+    rows = outs[0].shape[0]
+    for place, out in enumerate(outs):
+        spot = slice(place * rows, (place + 1) * rows)
+        for column, other in ((0, first), (half, second)):
+            total = keep[spot, column : column + half].astype(jnp.float32)
+            out[:, column : column + half] = (
+                total + other[spot, :].astype(jnp.float32)
+            ).astype(out.dtype)
+
+
+def settle(keep, first, second, count, after=()):
+    slots, columns = keep.shape
+    whole = lambda array: pl.BlockSpec(array.shape, lambda j: (0, 0))
+    shape = (slots // count, columns)
+    return launch(
+        settle_kernel,
+        [],
+        [keep, first, second],
+        [whole(keep), whole(first), whole(second)],
+        [pl.BlockSpec(shape, lambda j: (0, 0))] * count,
+        [jax.ShapeDtypeStruct(shape, keep.dtype)] * count,
+        after=after,
+        limit=24,
+        cost_estimate=cost(2 * keep.size, 6 * keep.size),
+        name="settle",
     )
 
 
@@ -700,9 +813,17 @@
     width = out_proj.shape[1]
     down_rows = expert_down[0]
     down_parts = {}
+    crossing = ctx_count == 8
 
     def send_columns(masks, after=()):
-        for mask, cut in zip(masks, cut_columns(me, down_rows, width, masks, after)):
+        if crossing:
+            layouts = {1: [(1, 0), (5, 0), (1, 1), (3, 1)]}
+            layouts.update({mask: [(mask, 0), (mask ^ 4, 0)] for mask in (2, 3)})
+            layouts.update({mask: [(mask, 1), (mask ^ 2, 1)] for mask in (4, 5)})
+            cuts = cut_columns(me, down_rows, width // 2, [layouts[m] for m in masks], after)
+        else:
+            cuts = cut_columns(me, down_rows, width, [[(m, 0)] for m in masks], after)
+        for mask, cut in zip(masks, cuts):
             down_parts[mask] = swap(cut, "ctx", mask)
         return tuple(down_parts[mask] for mask in masks)
 
@@ -755,7 +876,8 @@
     far = lambda parts: [part for mask, which, part in parts if which is not None][::2]
     scatter = lambda rows: lax.psum_scatter(rows, "exp", scatter_dimension=0, tiled=True)
     front = gather_parts(gated[0], 1, gated[1:])
-    late = send_columns([3, 5, 6, 7, 1] + list(range(8, ctx_count)), near(front))
+    late_masks = [3, 5, 1] if crossing else [1, 3] + list(range(5, ctx_count))
+    late = send_columns(late_masks, near(front))
     back = gather_parts(gated[1], 1, far(front))
     partial = project(me, front, out_proj, near(back))
     projected = [scatter(partial)]
@@ -783,9 +905,9 @@
         picked.append(pick.astype(jnp.bfloat16))
 
     groups = [[0, 1], [2, 3]] if exp_count == 4 else [list(range(exp_count))]
-    sent = pick_rows(picked, scaled)
+    sent = pick_rows(picked, scaled, late)
     pieces = [rows if mask == 0 else swap(rows, "exp", mask) for mask, rows in enumerate(sent)]
-    hiddens, after, order = [], late[:3], late[3:]
+    hiddens, after, order = [], (), ()
     for group in groups:
         parts = gather_parts(join([pieces[mask] for mask in group], after), 0, order)
         after = near(parts)
@@ -793,15 +915,26 @@
         order = [hidden]
         hiddens.append(hidden)
     answers, order = {}, []
-    weights = [None] + [down_parts[mask] for mask in range(1, ctx_count)]
+    weights = [None] + [down_parts[mask] for mask in sorted(down_parts)]
+    settled = []
     for group, hidden in zip(groups, hiddens):
-        last = group is groups[-1]
-        units = join([hidden], far(parts)) if not last else hidden
-        units = gather_parts(units, 0, hiddens[-1:] if not last else ())
-        answer = down(me, units, weights, down_rows, order)
-        order = [answer]
-        for place, mask in enumerate(group):
-            piece = lax.slice_in_dim(answer, place * capacity, (place + 1) * capacity, axis=0)
+        rows = hidden if group is groups[-1] else join([hidden], far(parts))
+        if crossing:
+            units = {0: rows, 2: swap(rows, "ctx", 2), 4: swap(rows, "ctx", 4)}
+            units.update({mask + 1: swap(units[mask], "ctx", 1) for mask in (0, 2, 4)})
+            keep, first, second = cross_down(me, units, weights, down_rows, order)
+            order = [keep]
+            settled.append((keep, swap(first, "ctx", 4), swap(second, "ctx", 2)))
+        else:
+            answer = down(me, gather_parts(rows), weights, down_rows, order)
+            order = [answer]
+            settled.append([answer])
+    for group, sums in zip(groups, settled):
+        if crossing:
+            pieces = settle(*sums, len(group), order)
+        else:
+            pieces = jnp.split(sums[0], len(group))
+        for mask, piece in zip(group, pieces):
             answers[mask] = piece if mask == 0 else swap(piece, "exp", mask)
     block_out = combine(
         exp_me.astype(jnp.int32).reshape(1),

time: 374 us -> 376 us (level)
  waiting for transfers between devices: 181 us -> 200 us
  starting transfers between devices: 53.8 us -> 45.5 us
  local copies, waits for them, and re-layouts: 23.2 us -> 16.7 us
    ppermute x74 -> x68, waiting for transfers between devices: 164 us -> 175 us  [swap(): lax.ppermute(array, axis, [(i, i ^ mask) for i in range(lax.axis_size(axi...]
    reduce_scatter x2, waiting for transfers between devices: 16.7 us -> 25.3 us  [shards(): lax.psum_scatter(rows, 'exp', scatter_dimension=0, tiled=True)]
    ppermute x74 -> x68, starting transfers between devices: 51.8 us -> 43.5 us  [swap(): lax.ppermute(array, axis, [(i, i ^ mask) for i in range(lax.axis_size(axi...]
    unnamed x96 -> x98, local copies, waits for them, and re-layouts: 17.6 us -> 12.1 us
  transfers between devices with their start and end apart: 77 -> 71, of which waited for: 34 -> 33; matrix products, arithmetic and copies ran while one was open for 3% -> 2% of each run, Pallas kernels for 20% -> 19%
where the time goes in v5:
time: 376 us; the launch traced here: 374 us
  waiting for transfers between devices  200 us (53%)
  Pallas kernels  92.5 us (25%)
  starting transfers between devices  45.5 us (12%)
  local copies, waits for them, and re-layouts  16.7 us (4%)
  between operations  14.8 us (4%)
  other arithmetic  4.76 us (1%)
    ppermute x68, waiting for transfers between devices, swap(): lax.ppermute(array, axis, [(i, i ^ mask) for i in range(lax.axis_size(axi...  175 us
    pallas_call x24, Pallas kernels, launch(): pl.pallas_call(body, grid_spec=pltpu.PrefetchScalarGridSpec(num_scalar_pr...  92.5 us
    ppermute x68, starting transfers between devices, swap(): lax.ppermute(array, axis, [(i, i ^ mask) for i in range(lax.axis_size(axi...  43.5 us
    reduce_scatter x2, waiting for transfers between devices, shards(): lax.psum_scatter(rows, 'exp', scatter_dimension=0, tiled=True)  25.3 us
    unnamed x98, local copies, waits for them, and re-layouts  12.1 us
  transfers between devices with their start and end apart: 71, of which 33 were waited for; matrix products, arithmetic and copies ran while one was open for 2% of the time, Pallas kernels for 19%

profile of v5, /device:TPU:8, one launch (start us, length us, event | category | flops | bytes accessed | tf_op | source)
XLA Modules:
  0.0 374.2 jit_solution(7837035098308285099)
XLA Ops:
  8.1 1.7 collective-permute-start
  9.9 3.5 cut_columns.2
  13.3 1.7 collective-permute-start.1
  15.0 1.5 collective-permute-start.2
  18.0 1.3 broadcast_in_dim.20.refs_8_.refs_6_
  19.3 13.9 %local_states.1 = (f32[128,4096]{1,0:T(8,128)}, f32[128,4096]{1,0:T(8,128)}, bf16[32,4096]{1,0:T(8,128)(2,1)}) custom-call(bf16[128,4096]{1,0:T(8,128)(2,1)} %refs_0_.1, f32[8,4096]{1,0:T(8,128)} %pad_convert_fusion.refs_1_, bf16[128,4096]{1,0:T(8,128)(2,1)} %refs_2_.2, f32[4,4096]{1,0:T(4,128)} %refs_3_.4, f32[1,4096]{1,0:T(1,128)} %bitcast.66, ...), custom_call_target="tpu_custom_call" | custom-call | flops 41943040 | bytes 6291456 | tf_op jit(solution)/shard_map/local_states/pallas_call | solution.py:95
  33.2 2.0 collective-permute-done.2.refs_2_.refs_11_
  35.3 1.1 copy-done.31
  36.7 1.8 collective-permute-start.6
  38.6 1.4 collective-permute-start.8
  40.0 5.7 %collective-permute-done.4.refs_11_.refs_3_ = bf16[32,4096]{1,0:T(8,128)(2,1)S(1)} collective-permute-done((bf16[32,4096]{1,0:T(8,128)(2,1)S(1)}, bf16[32,4096]{1,0:T(8,128)(2,1)S(1)}, u32[]{:S(2)}, u32[]{:S(2)}) %collective-permute-start.4) | collective-permute-done | bytes 262176 | tf_op jit(solution)/shard_map/ppermute | solution.py:23
  45.7 4.9 %collective-permute-done.6.refs_13_.refs_5_ = bf16[32,4096]{1,0:T(8,128)(2,1)S(1)} collective-permute-done((bf16[32,4096]{1,0:T(8,128)(2,1)S(1)}, bf16[32,4096]{1,0:T(8,128)(2,1)S(1)}, u32[]{:S(2)}, u32[]{:S(2)}) %collective-permute-start.6) | collective-permute-done | bytes 262176 | tf_op jit(solution)/shard_map/ppermute | solution.py:23
  52.5 1.3 broadcast_in_dim.23.refs_7_
  53.9 9.1 %read_out.2 = (bf16[64,4096]{1,0:T(8,128)(2,1)}, f32[16,4096]{1,0:T(8,128)}) custom-call(s32[1]{0:T(128)} %bitcast.refs_0_, f32[128,4096]{1,0:T(8,128)} %get-tuple-element.35.refs_1_, f32[128,4096]{1,0:T(8,128)} %get-tuple-element.36.refs_2_, bf16[128,4096]{1,0:T(8,128)(2,1)} %refs_3_.6, f32[16,4096]{1,0:T(8,128)} %refs_4_.3, f32[1,4096]{1,0:T(1,128)} %bitcast.61, ...), custom_call_target="tpu_custom_call" | custom-call | flops 29360128 | bytes 3145728 | tf_op jit(solution)/shard_map/read_out/pallas_call | solution.py:95
  63.0 1.7 collective-permute-start.11
  65.1 8.3 %read_out.3 = (bf16[64,4096]{1,0:T(8,128)(2,1)}, f32[16,4096]{1,0:T(8,128)}) custom-call(s32[1]{0:T(128)} %bitcast.refs_0_, f32[128,4096]{1,0:T(8,128)} %get-tuple-element.35.refs_1_, f32[128,4096]{1,0:T(8,128)} %get-tuple-element.36.refs_2_, bf16[128,4096]{1,0:T(8,128)(2,1)} %refs_3_.6, f32[16,4096]{1,0:T(8,128)} %refs_4_.3, f32[1,4096]{1,0:T(1,128)} %bitcast.62, ...), custom_call_target="tpu_custom_call" | custom-call | flops 29360128 | bytes 3145728 | tf_op jit(solution)/shard_map/read_out/pallas_call | solution.py:95
  73.4 1.7 collective-permute-start.19
  75.5 2.6 collective-permute-done.11.refs_0_.refs_4_.refs_9_
  78.1 1.7 collective-permute-done.13.refs_1_.refs_6_.refs_10_
  81.3 1.7 collective-permute-start.17
  83.0 6.4 %collective-permute-done.19.refs_12_.refs_0_.refs_4_ = bf16[64,4096]{1,0:T(8,128)(2,1)S(1)} collective-permute-done((bf16[64,4096]{1,0:T(8,128)(2,1)}, bf16[64,4096]{1,0:T(8,128)(2,1)S(1)}, u32[]{:S(2)}, u32[]{:S(2)}) %collective-permute-start.19) | collective-permute-done | bytes 524320 | tf_op jit(solution)/shard_map/ppermute | solution.py:23
  89.3 1.7 collective-permute-done.20.refs_13_.refs_1_.refs_6_
  91.0 4.6 %collective-permute-done.15.refs_8_.refs_2_ = bf16[64,2048]{1,0:T(8,128)(2,1)S(1)} collective-permute-done((bf16[64,2048]{1,0:T(8,128)(2,1)S(1)}, bf16[64,2048]{1,0:T(8,128)(2,1)S(1)}, u32[]{:S(2)}, u32[]{:S(2)}) %collective-permute-start.15) | collective-permute-done | bytes 262176 | tf_op jit(solution)/shard_map/ppermute | solution.py:23
  97.5 8.3 %project.2.refs_12_ = bf16[512,1024]{1,0:T(8,128)(2,1)} custom-call(s32[1]{0:T(128)} %bitcast.refs_0_, bf16[4096,1024]{1,0:T(8,128)(2,1)} %refs_1_.3, bf16[64,4096]{1,0:T(8,128)(2,1)S(1)} %copy-done.32, bf16[64,4096]{1,0:T(8,128)(2,1)S(1)} %collective-permute-done.10.refs_3_, bf16[64,4096]{1,0:T(8,128)(2,1)S(1)} %collective-permute-done.11.refs_0_.refs_4_.refs_9_, ...), custom_call_target="tpu_custom_call" | custom-call | flops 4294967296 | bytes 13631488 | tf_op jit(solution)/shard_map/project/pallas_call | solution.py:95
  106.6 1.7 collective-permute-start.26
  108.8 5.7 %collective-permute-done.24.refs_8_ = bf16[64,2048]{1,0:T(8,128)(2,1)S(1)} collective-permute-done((bf16[64,2048]{1,0:T(8,128)(2,1)S(1)}, bf16[64,2048]{1,0:T(8,128)(2,1)S(1)}, u32[]{:S(2)}, u32[]{:S(2)}) %collective-permute-start.24) | collective-permute-done | bytes 262176 | tf_op jit(solution)/shard_map/ppermute | solution.py:23
  116.4 8.4 %project.3 = bf16[512,1024]{1,0:T(8,128)(2,1)} custom-call(s32[1]{0:T(128)} %bitcast.refs_0_, bf16[4096,1024]{1,0:T(8,128)(2,1)} %refs_1_.3, bf16[64,4096]{1,0:T(8,128)(2,1)S(1)} %copy-done.30, bf16[64,4096]{1,0:T(8,128)(2,1)S(1)} %collective-permute-done.21.refs_3_, bf16[64,4096]{1,0:T(8,128)(2,1)S(1)} %collective-permute-done.19.refs_12_.refs_0_.refs_4_, ...), custom_call_target="tpu_custom_call" | custom-call | flops 4294967296 | bytes 13631488 | tf_op jit(solution)/shard_map/project/pallas_call | solution.py:95
  127.0 4.5 %cut_columns.3 = (bf16[384,1024]{1,0:T(8,128)(2,1)}, bf16[384,1024]{1,0:T(8,128)(2,1)}, bf16[384,2048]{1,0:T(8,128)(2,1)}) custom-call(s32[1]{0:T(128)} %bitcast.refs_0_, bf16[384,8192]{1,0:T(8,128)(2,1)} %bitcast.41, bf16[384,8192]{1,0:T(8,128)(2,1)} %bitcast.42, bf16[384,8192]{1,0:T(8,128)(2,1)} %bitcast.43, bf16[384,8192]{1,0:T(8,128)(2,1)} %bitcast.44, ...), custom_call_target="tpu_custom_call" | custom-call | bytes 6291456 | tf_op jit(solution)/shard_map/cut_columns/pallas_call | solution.py:95
  132.1 1.4 collective-permute-start.28
  134.3 25.3 %reduce-scatter.5.cloned.1.call-done = bf16[128,1024]{1,0:T(8,128)(2,1)} async-done(((bf16[512,1024]{1,0:T(8,128)(2,1)}), bf16[128,1024]{1,0:T(8,128)(2,1)}) %reduce-scatter.5.cloned.1.call-update) | async-done | bytes 262160 | tf_op jit(solution)/shard_map/reduce_scatter | solution.py:877
  159.5 1.1 pad_maximum_fusion
  161.6 2.7 collective-permute-start.31
  164.3 8.9 %collective-permute-done.31.refs_1_ = bf16[192,1024]{1,0:T(8,128)(2,1)S(1)} collective-permute-done((bf16[192,1024]{1,0:T(8,128)(2,1)S(1)}, bf16[192,1024]{1,0:T(8,128)(2,1)S(1)}, u32[]{:S(2)}, u32[]{:S(2)}) %collective-permute-start.31) | collective-permute-done | bytes 393248 | tf_op jit(solution)/shard_map/ppermute | solution.py:23
  173.7 1.5 collective-permute-start.33
  175.2 1.5 collective-permute-start.35
  176.7 1.2 collective-permute-start.41
  177.9 2.0 collective-permute-start.42
  179.9 12.4 %collective-permute-done.33.refs_0_.refs_6_.refs_2_ = bf16[384,1024]{1,0:T(8,128)(2,1)S(1)} collective-permute-done((bf16[384,1024]{1,0:T(8,128)(2,1)S(1)}, bf16[384,1024]{1,0:T(8,128)(2,1)S(1)}, u32[]{:S(2)}, u32[]{:S(2)}) %collective-permute-start.33) | collective-permute-done | bytes 786464 | tf_op jit(solution)/shard_map/ppermute | solution.py:23
  192.3 1.2 collective-permute-done.35.refs_1_.refs_8_.refs_3_
  193.5 1.5 collective-permute-start.37
  195.1 9.1 %collective-permute-done.41.refs_0_ = bf16[192,1024]{1,0:T(8,128)(2,1)S(1)} collective-permute-done((bf16[192,1024]{1,0:T(8,128)(2,1)S(1)}, bf16[192,1024]{1,0:T(8,128)(2,1)S(1)}, u32[]{:S(2)}, u32[]{:S(2)}) %collective-permute-start.41) | collective-permute-done | bytes 393248 | tf_op jit(solution)/shard_map/ppermute | solution.py:23
  204.2 10.2 %collective-permute-done.42.refs_1_ = bf16[192,1024]{1,0:T(8,128)(2,1)S(1)} collective-permute-done((bf16[192,1024]{1,0:T(8,128)(2,1)S(1)}, bf16[192,1024]{1,0:T(8,128)(2,1)S(1)}, u32[]{:S(2)}, u32[]{:S(2)}) %collective-permute-start.42) | collective-permute-done | bytes 393248 | tf_op jit(solution)/shard_map/ppermute | solution.py:23
  215.4 1.5 collective-permute-start.39
  216.9 25.9 %collective-permute-done.39.refs_12_ = bf16[192,1024]{1,0:T(8,128)(2,1)S(1)} collective-permute-done((bf16[192,1024]{1,0:T(8,128)(2,1)S(1)}, bf16[192,1024]{1,0:T(8,128)(2,1)S(1)}, u32[]{:S(2)}, u32[]{:S(2)}) %collective-permute-start.39) | collective-permute-done | bytes 393248 | tf_op jit(solution)/shard_map/ppermute | solution.py:23
  244.5 10.2 %hidden_units.2.refs_2_.refs_0_ = bf16[384,384]{1,0:T(8,128)(2,1)S(1)} custom-call(s32[1]{0:T(128)} %bitcast.refs_0_, f32[8,1,1024]{2,1,0:T(1,128)S(1)} %inverse_gains.1.refs_1_, bf16[8192,384]{1,0:T(8,128)(2,1)S(1)} %bitcast.55, bf16[8192,384]{1,0:T(8,128)(2,1)} %bitcast.57, bf16[384,1024]{1,0:T(8,128)(2,1)S(1)} %join.5.refs_4_, ...), custom_call_target="tpu_custom_call" | custom-call | flops 4831838208 | bytes 18874368 | tf_op jit(solution)/shard_map/hidden_units/pallas_call | solution.py:95
  254.7 8.0 %collective-permute-done.44.refs_1_.refs_8_ = bf16[384,1024]{1,0:T(8,128)(2,1)S(1)} collective-permute-done((bf16[384,1024]{1,0:T(8,128)(2,1)S(1)}, bf16[384,1024]{1,0:T(8,128)(2,1)S(1)}, u32[]{:S(2)}, u32[]{:S(2)}) %collective-permute-start.44) | collective-permute-done | bytes 786464 | tf_op jit(solution)/shard_map/ppermute | solution.py:23
  264.0 9.6 %collective-permute-done.45.refs_1_.refs_10_ = bf16[192,1024]{1,0:T(8,128)(2,1)S(1)} collective-permute-done((bf16[192,1024]{1,0:T(8,128)(2,1)S(1)}, bf16[192,1024]{1,0:T(8,128)(2,1)S(1)}, u32[]{:S(2)}, u32[]{:S(2)}) %collective-permute-start.45) | collective-permute-done | bytes 393248 | tf_op jit(solution)/shard_map/ppermute | solution.py:23
  273.6 1.3 collective-permute-done.46.refs_2_.refs_12_
  276.2 1.5 collective-permute-start.50
  277.7 2.8 copy-done
  280.4 11.0 %hidden_units.3.refs_1_ = bf16[384,384]{1,0:T(8,128)(2,1)} custom-call(s32[1]{0:T(128)} %bitcast.refs_0_, f32[8,1,1024]{2,1,0:T(1,128)S(1)} %inverse_gains.1.refs_1_, bf16[8192,384]{1,0:T(8,128)(2,1)S(1)} %bitcast.56, bf16[8192,384]{1,0:T(8,128)(2,1)} %bitcast.58, bf16[384,1024]{1,0:T(8,128)(2,1)S(1)} %join.6.refs_4_, ...), custom_call_target="tpu_custom_call" | custom-call | flops 4831838208 | bytes 18874368 | tf_op jit(solution)/shard_map/hidden_units/pallas_call | solution.py:95
  291.5 1.6 collective-permute-start.60
  295.6 4.7 %collective-permute-done.60.refs_3_ = bf16[384,384]{1,0:T(8,128)(2,1)S(1)} collective-permute-done((bf16[384,384]{1,0:T(8,128)(2,1)}, bf16[384,384]{1,0:T(8,128)(2,1)S(1)}, u32[]{:S(2)}, u32[]{:S(2)}) %collective-permute-start.60) | collective-permute-done | bytes 294944 | tf_op jit(solution)/shard_map/ppermute | solution.py:23
  301.5 1.1 copy-done.24
  304.5 4.9 %cross_down.2 = (bf16[384,1024]{1,0:T(8,128)(2,1)S(1)}, bf16[384,512]{1,0:T(8,128)(2,1)S(1)}, bf16[384,512]{1,0:T(8,128)(2,1)S(1)}) custom-call(s32[1]{0:T(128)} %bitcast.refs_0_, bf16[384,384]{1,0:T(8,128)(2,1)S(1)} %join.7.refs_1_, bf16[384,384]{1,0:T(8,128)(2,1)S(1)} %copy-done.34, bf16[384,384]{1,0:T(8,128)(2,1)S(1)} %collective-permute-done.48.refs_3_, ...), custom_call_target="tpu_custom_call" | custom-call | flops 4831838208 | bytes 9437184 | tf_op jit(solution)/shard_map/cross_down/pallas_call | solution.py:95
  310.4 1.2 collective-permute-start.53
  311.7 1.1 copy-done.25
  312.8 1.1 copy-done.28
  314.0 6.0 %cross_down.3 = (bf16[384,1024]{1,0:T(8,128)(2,1)S(1)}, bf16[384,512]{1,0:T(8,128)(2,1)S(1)}, bf16[384,512]{1,0:T(8,128)(2,1)S(1)}) custom-call(s32[1]{0:T(128)} %bitcast.refs_0_, bf16[384,384]{1,0:T(8,128)(2,1)} %hidden_units.3.refs_1_, bf16[384,384]{1,0:T(8,128)(2,1)S(1)} %collective-permute-done.59.refs_2_, ...), custom_call_target="tpu_custom_call" | custom-call | flops 4831838208 | bytes 9437184 | tf_op jit(solution)/shard_map/cross_down/pallas_call | solution.py:95
  320.7 1.2 collective-permute-start.66
  322.2 8.8 %collective-permute-done.65.refs_1_ = bf16[384,512]{1,0:T(8,128)(2,1)S(1)} collective-permute-done((bf16[384,512]{1,0:T(8,128)(2,1)S(1)}, bf16[384,512]{1,0:T(8,128)(2,1)S(1)}, u32[]{:S(2)}, u32[]{:S(2)}) %collective-permute-start.65) | collective-permute-done | bytes 393248 | tf_op jit(solution)/shard_map/ppermute | solution.py:23
  332.6 25.2 %collective-permute-done.67.refs_10_ = bf16[192,1024]{1,0:T(8,128)(2,1)S(1)} collective-permute-done((bf16[192,1024]{1,0:T(8,128)(2,1)}, bf16[192,1024]{1,0:T(8,128)(2,1)S(1)}, u32[]{:S(2)}, u32[]{:S(2)}) %collective-permute-start.67) | collective-permute-done | bytes 393248 | tf_op jit(solution)/shard_map/ppermute | solution.py:23
  357.8 8.0 %collective-permute-done.68.refs_11_ = bf16[192,1024]{1,0:T(8,128)(2,1)S(1)} collective-permute-done((bf16[192,1024]{1,0:T(8,128)(2,1)}, bf16[192,1024]{1,0:T(8,128)(2,1)S(1)}, u32[]{:S(2)}, u32[]{:S(2)}) %collective-permute-start.68) | collective-permute-done | bytes 393248 | tf_op jit(solution)/shard_map/ppermute | solution.py:23
  365.8 1.6 combine.1
  (244 shorter events, 31.1 us)
Async XLA Ops:
  7.2 127.1 %reduce-scatter.3.cloned.1.call-start = ((), (), s32[]{:S(2)}) async-start(), calls=%async_computation.2 | async-start | bytes 1310720 | tf_op jit(solution)/shard_map/reduce_scatter | solution.py:877
  8.1 9.2 %collective-permute-start = (bf16[3,4096]{1,0:T(4,128)(2,1)S(1)}, bf16[3,4096]{1,0:T(4,128)(2,1)S(1)}, u32[]{:S(2)}, u32[]{:S(2)}) collective-permute-start(bf16[3,4096]{1,0:T(4,128)(2,1)S(1)} %slice.31), channel_id=1, source_target_pairs={{0,4},{4,8},{8,12},{12,16},{16,20},{20,24},{24,28},{1,5},{5,9},{9,... | collective-permute-start | bytes 73736 | tf_op jit(solution)/shard_map/ppermute | solution.py:19
  13.3 19.9 %collective-permute-start.1 = (bf16[384,1024]{1,0:T(8,128)(2,1)}, bf16[384,1024]{1,0:T(8,128)(2,1)S(1)}, u32[]{:S(2)}, u32[]{:S(2)}) collective-permute-start(bf16[384,1024]{1,0:T(8,128)(2,1)} %get-tuple-element.38), channel_id=1, source_target_pairs={{0,8},{4,12},{8,0},{12,4},{16,24},{20,28},{24,16},{28,20},{1,9},{5... | collective-permute-start | bytes 2359304 | tf_op jit(solution)/shard_map/ppermute | solution.py:23
  15.0 20.3 %collective-permute-start.2 = (bf16[384,1024]{1,0:T(8,128)(2,1)}, bf16[384,1024]{1,0:T(8,128)(2,1)S(1)}, u32[]{:S(2)}, u32[]{:S(2)}) collective-permute-start(bf16[384,1024]{1,0:T(8,128)(2,1)} %get-tuple-element.39), channel_id=1, source_target_pairs={{0,16},{4,20},{8,24},{12,28},{16,0},{20,4},{24,8},{28,12},{1,17},{... | collective-permute-start | bytes 2359304 | tf_op jit(solution)/shard_map/ppermute | solution.py:23
  36.4 9.2 %collective-permute-start.4 = (bf16[32,4096]{1,0:T(8,128)(2,1)S(1)}, bf16[32,4096]{1,0:T(8,128)(2,1)S(1)}, u32[]{:S(2)}, u32[]{:S(2)}) collective-permute-start(bf16[32,4096]{1,0:T(8,128)(2,1)S(1)} %join.4.refs_9_.refs_1_), channel_id=1, source_target_pairs={{0,8},{4,12},{8,0},{12,4},{16,24},{20,28},{24,16},{28,20},{1,9},{5... | collective-permute-start | bytes 786440 | tf_op jit(solution)/shard_map/ppermute | solution.py:23
  36.7 13.9 %collective-permute-start.6 = (bf16[32,4096]{1,0:T(8,128)(2,1)S(1)}, bf16[32,4096]{1,0:T(8,128)(2,1)S(1)}, u32[]{:S(2)}, u32[]{:S(2)}) collective-permute-start(bf16[32,4096]{1,0:T(8,128)(2,1)S(1)} %join.4.refs_9_.refs_1_), channel_id=1, source_target_pairs={{0,16},{4,20},{8,24},{12,28},{16,0},{20,4},{24,8},{28,12},{1,17},{... | collective-permute-start | bytes 786440 | tf_op jit(solution)/shard_map/ppermute | solution.py:23
  38.6 12.1 %collective-permute-start.8 = (bf16[32,4096]{1,0:T(8,128)(2,1)S(1)}, bf16[32,4096]{1,0:T(8,128)(2,1)S(1)}, u32[]{:S(2)}, u32[]{:S(2)}) collective-permute-start(bf16[32,4096]{1,0:T(8,128)(2,1)S(1)} %join.4.refs_9_.refs_1_), channel_id=1, source_target_pairs={{0,24},{4,28},{8,16},{12,20},{16,8},{20,12},{24,0},{28,4},{1,25},{... | collective-permute-start | bytes 786440 | tf_op jit(solution)/shard_map/ppermute | solution.py:23
  40.0 11.4 %collective-permute-start.3 = (bf16[32,4096]{1,0:T(8,128)(2,1)S(1)}, bf16[32,4096]{1,0:T(8,128)(2,1)S(1)}, u32[]{:S(2)}, u32[]{:S(2)}) collective-permute-start(bf16[32,4096]{1,0:T(8,128)(2,1)S(1)} %join.4.refs_9_.refs_1_), channel_id=1, source_target_pairs={{0,4},{4,0},{8,12},{12,8},{16,20},{20,16},{24,28},{28,24},{1,5},{5... | collective-permute-start | bytes 786440 | tf_op jit(solution)/shard_map/ppermute | solution.py:23
  45.7 5.7 %collective-permute-start.5 = (bf16[32,4096]{1,0:T(8,128)(2,1)S(1)}, bf16[32,4096]{1,0:T(8,128)(2,1)S(1)}, u32[]{:S(2)}, u32[]{:S(2)}) collective-permute-start(bf16[32,4096]{1,0:T(8,128)(2,1)S(1)} %collective-permute-done.4.refs_11_.refs_3_), channel_id=1, source_target_pairs={{0,4},{4,0},{8,12},{12,8},{16,20},{20,16},{24,28},{28,24},{1,5},{5... | collective-permute-start | bytes 786440 | tf_op jit(solution)/shard_map/ppermute | solution.py:23
  63.0 15.0 %collective-permute-start.11 = (bf16[64,4096]{1,0:T(8,128)(2,1)}, bf16[64,4096]{1,0:T(8,128)(2,1)S(1)}, u32[]{:S(2)}, u32[]{:S(2)}) collective-permute-start(bf16[64,4096]{1,0:T(8,128)(2,1)} %get-tuple-element.40.refs_2_), channel_id=1, source_target_pairs={{0,8},{4,12},{8,0},{12,4},{16,24},{20,28},{24,16},{28,20},{1,9},{5... | collective-permute-start | bytes 1572872 | tf_op jit(solution)/shard_map/ppermute | solution.py:23
  64.7 15.0 %collective-permute-start.13 = (bf16[64,4096]{1,0:T(8,128)(2,1)}, bf16[64,4096]{1,0:T(8,128)(2,1)S(1)}, u32[]{:S(2)}, u32[]{:S(2)}) collective-permute-start(bf16[64,4096]{1,0:T(8,128)(2,1)} %get-tuple-element.40.refs_2_), channel_id=1, source_target_pairs={{0,16},{4,20},{8,24},{12,28},{16,0},{20,4},{24,8},{28,12},{1,17},{... | collective-permute-start | bytes 1572872 | tf_op jit(solution)/shard_map/ppermute | solution.py:23
  73.4 15.9 %collective-permute-start.19 = (bf16[64,4096]{1,0:T(8,128)(2,1)}, bf16[64,4096]{1,0:T(8,128)(2,1)S(1)}, u32[]{:S(2)}, u32[]{:S(2)}) collective-permute-start(bf16[64,4096]{1,0:T(8,128)(2,1)} %get-tuple-element.42.refs_2_), channel_id=1, source_target_pairs={{0,8},{4,12},{8,0},{12,4},{16,24},{20,28},{24,16},{28,20},{1,9},{5... | collective-permute-start | bytes 1572872 | tf_op jit(solution)/shard_map/ppermute | solution.py:23
  75.1 15.8 %collective-permute-start.20 = (bf16[64,4096]{1,0:T(8,128)(2,1)}, bf16[64,4096]{1,0:T(8,128)(2,1)S(1)}, u32[]{:S(2)}, u32[]{:S(2)}) collective-permute-start(bf16[64,4096]{1,0:T(8,128)(2,1)} %get-tuple-element.42.refs_2_), channel_id=1, source_target_pairs={{0,16},{4,20},{8,24},{12,28},{16,0},{20,4},{24,8},{28,12},{1,17},{... | collective-permute-start | bytes 1572872 | tf_op jit(solution)/shard_map/ppermute | solution.py:23
  75.5 20.6 %collective-permute-start.10 = (bf16[64,4096]{1,0:T(8,128)(2,1)S(1)}, bf16[64,4096]{1,0:T(8,128)(2,1)S(1)}, u32[]{:S(2)}, u32[]{:S(2)}) collective-permute-start(bf16[64,4096]{1,0:T(8,128)(2,1)S(1)} %copy-done.32), channel_id=1, source_target_pairs={{0,4},{4,0},{8,12},{12,8},{16,20},{20,16},{24,28},{28,24},{1,5},{5... | collective-permute-start | bytes 1572872 | tf_op jit(solution)/shard_map/ppermute | solution.py:23
  80.8 14.7 %collective-permute-start.15 = (bf16[64,2048]{1,0:T(8,128)(2,1)S(1)}, bf16[64,2048]{1,0:T(8,128)(2,1)S(1)}, u32[]{:S(2)}, u32[]{:S(2)}) collective-permute-start(bf16[64,2048]{1,0:T(8,128)(2,1)S(1)} %get-tuple-element.43), channel_id=1, source_target_pairs={{0,16},{4,20},{8,24},{12,28},{16,0},{20,4},{24,8},{28,12},{1,17},{... | collective-permute-start | bytes 786440 | tf_op jit(solution)/shard_map/ppermute | solution.py:23
  81.3 14.3 %collective-permute-start.17 = (bf16[64,2048]{1,0:T(8,128)(2,1)S(1)}, bf16[64,2048]{1,0:T(8,128)(2,1)S(1)}, u32[]{:S(2)}, u32[]{:S(2)}) collective-permute-start(bf16[64,2048]{1,0:T(8,128)(2,1)S(1)} %get-tuple-element.44), channel_id=1, source_target_pairs={{0,8},{4,12},{8,0},{12,4},{16,24},{20,28},{24,16},{28,20},{1,9},{5... | collective-permute-start | bytes 786440 | tf_op jit(solution)/shard_map/ppermute | solution.py:23
  89.3 8.2 %collective-permute-start.12 = (bf16[64,4096]{1,0:T(8,128)(2,1)S(1)}, bf16[64,4096]{1,0:T(8,128)(2,1)S(1)}, u32[]{:S(2)}, u32[]{:S(2)}) collective-permute-start(bf16[64,4096]{1,0:T(8,128)(2,1)S(1)} %collective-permute-done.11.refs_0_.refs_4_.refs_9_), channel_id=1, source_target_pairs={{0,4},{4,0},{8,12},{12,8},{16,20},{20,16},{24,28},{28,24},{1,5},{5... | collective-permute-start | bytes 1572872 | tf_op jit(solution)/shard_map/ppermute | solution.py:23
  91.0 6.5 %collective-permute-start.14 = (bf16[64,4096]{1,0:T(8,128)(2,1)S(1)}, bf16[64,4096]{1,0:T(8,128)(2,1)S(1)}, u32[]{:S(2)}, u32[]{:S(2)}) collective-permute-start(bf16[64,4096]{1,0:T(8,128)(2,1)S(1)} %collective-permute-done.13.refs_1_.refs_6_.refs_10_), channel_id=1, source_target_pairs={{0,4},{4,0},{8,12},{12,8},{16,20},{20,16},{24,28},{28,24},{1,5},{5... | collective-permute-start | bytes 1572872 | tf_op jit(solution)/shard_map/ppermute | solution.py:23
  105.8 53.7 %reduce-scatter.5.cloned.1.call-start = ((), (), s32[]{:S(2)}) async-start(), calls=%async_computation.3 | async-start | bytes 1310720 | tf_op jit(solution)/shard_map/reduce_scatter | solution.py:877
  106.1 8.4 %collective-permute-start.24 = (bf16[64,2048]{1,0:T(8,128)(2,1)S(1)}, bf16[64,2048]{1,0:T(8,128)(2,1)S(1)}, u32[]{:S(2)}, u32[]{:S(2)}) collective-permute-start(bf16[64,2048]{1,0:T(8,128)(2,1)S(1)} %get-tuple-element.45), channel_id=1, source_target_pairs={{0,16},{4,20},{8,24},{12,28},{16,0},{20,4},{24,8},{28,12},{1,17},{... | collective-permute-start | bytes 786440 | tf_op jit(solution)/shard_map/ppermute | solution.py:23
  106.6 8.1 %collective-permute-start.26 = (bf16[64,2048]{1,0:T(8,128)(2,1)S(1)}, bf16[64,2048]{1,0:T(8,128)(2,1)S(1)}, u32[]{:S(2)}, u32[]{:S(2)}) collective-permute-start(bf16[64,2048]{1,0:T(8,128)(2,1)S(1)} %get-tuple-element.46), channel_id=1, source_target_pairs={{0,8},{4,12},{8,0},{12,4},{16,24},{20,28},{24,16},{28,20},{1,9},{5... | collective-permute-start | bytes 786440 | tf_op jit(solution)/shard_map/ppermute | solution.py:23
  108.2 6.8 %collective-permute-start.21 = (bf16[64,4096]{1,0:T(8,128)(2,1)S(1)}, bf16[64,4096]{1,0:T(8,128)(2,1)S(1)}, u32[]{:S(2)}, u32[]{:S(2)}) collective-permute-start(bf16[64,4096]{1,0:T(8,128)(2,1)S(1)} %copy-done.30), channel_id=1, source_target_pairs={{0,4},{4,0},{8,12},{12,8},{16,20},{20,16},{24,28},{28,24},{1,5},{5... | collective-permute-start | bytes 1572872 | tf_op jit(solution)/shard_map/ppermute | solution.py:23
  108.3 6.8 %collective-permute-start.22 = (bf16[64,4096]{1,0:T(8,128)(2,1)S(1)}, bf16[64,4096]{1,0:T(8,128)(2,1)S(1)}, u32[]{:S(2)}, u32[]{:S(2)}) collective-permute-start(bf16[64,4096]{1,0:T(8,128)(2,1)S(1)} %collective-permute-done.19.refs_12_.refs_0_.refs_4_), channel_id=1, source_target_pairs={{0,4},{4,0},{8,12},{12,8},{16,20},{20,16},{24,28},{28,24},{1,5},{5... | collective-permute-start | bytes 1572872 | tf_op jit(solution)/shard_map/ppermute | solution.py:23
  108.8 6.3 %collective-permute-start.23 = (bf16[64,4096]{1,0:T(8,128)(2,1)S(1)}, bf16[64,4096]{1,0:T(8,128)(2,1)S(1)}, u32[]{:S(2)}, u32[]{:S(2)}) collective-permute-start(bf16[64,4096]{1,0:T(8,128)(2,1)S(1)} %collective-permute-done.20.refs_13_.refs_1_.refs_6_), channel_id=1, source_target_pairs={{0,4},{4,0},{8,12},{12,8},{16,20},{20,16},{24,28},{28,24},{1,5},{5... | collective-permute-start | bytes 1572872 | tf_op jit(solution)/shard_map/ppermute | solution.py:23
  131.5 29.5 %collective-permute-start.30 = (bf16[384,2048]{1,0:T(8,128)(2,1)}, bf16[384,2048]{1,0:T(8,128)(2,1)}, u32[]{:S(2)}, u32[]{:S(2)}) collective-permute-start(bf16[384,2048]{1,0:T(8,128)(2,1)} %get-tuple-element.49), channel_id=1, source_target_pairs={{0,4},{4,0},{8,12},{12,8},{16,20},{20,16},{24,28},{28,24},{1,5},{5... | collective-permute-start | bytes 4718600 | tf_op jit(solution)/shard_map/ppermute | solution.py:23
  132.1 28.9 %collective-permute-start.28 = (bf16[384,1024]{1,0:T(8,128)(2,1)}, bf16[384,1024]{1,0:T(8,128)(2,1)S(1)}, u32[]{:S(2)}, u32[]{:S(2)}) collective-permute-start(bf16[384,1024]{1,0:T(8,128)(2,1)} %get-tuple-element.47), channel_id=1, source_target_pairs={{0,12},{4,8},{8,4},{12,0},{16,28},{20,24},{24,20},{28,16},{1,13},{... | collective-permute-start | bytes 2359304 | tf_op jit(solution)/shard_map/ppermute | solution.py:23
  133.5 27.5 %collective-permute-start.29 = (bf16[384,1024]{1,0:T(8,128)(2,1)}, bf16[384,1024]{1,0:T(8,128)(2,1)S(1)}, u32[]{:S(2)}, u32[]{:S(2)}) collective-permute-start(bf16[384,1024]{1,0:T(8,128)(2,1)} %get-tuple-element.48), channel_id=1, source_target_pairs={{0,20},{4,16},{8,28},{12,24},{16,4},{20,0},{24,12},{28,8},{1,21},{... | collective-permute-start | bytes 2359304 | tf_op jit(solution)/shard_map/ppermute | solution.py:23
  161.6 11.6 %collective-permute-start.31 = (bf16[192,1024]{1,0:T(8,128)(2,1)S(1)}, bf16[192,1024]{1,0:T(8,128)(2,1)S(1)}, u32[]{:S(2)}, u32[]{:S(2)}) collective-permute-start(bf16[192,1024]{1,0:T(8,128)(2,1)S(1)} %get-tuple-element.51), channel_id=1, source_target_pairs={{0,1},{1,0},{2,3},{3,2},{4,5},{5,4},{6,7},{7,6},{8,9},{9,8},{10,11... | collective-permute-start | bytes 1179656 | tf_op jit(solution)/shard_map/ppermute | solution.py:23
  173.7 18.6 %collective-permute-start.33 = (bf16[384,1024]{1,0:T(8,128)(2,1)S(1)}, bf16[384,1024]{1,0:T(8,128)(2,1)S(1)}, u32[]{:S(2)}, u32[]{:S(2)}) collective-permute-start(bf16[384,1024]{1,0:T(8,128)(2,1)S(1)} %join.5.refs_4_), channel_id=1, source_target_pairs={{0,8},{4,12},{8,0},{12,4},{16,24},{20,28},{24,16},{28,20},{1,9},{5... | collective-permute-start | bytes 2359304 | tf_op jit(solution)/shard_map/ppermute | solution.py:23
  175.2 18.3 %collective-permute-start.35 = (bf16[384,1024]{1,0:T(8,128)(2,1)S(1)}, bf16[384,1024]{1,0:T(8,128)(2,1)S(1)}, u32[]{:S(2)}, u32[]{:S(2)}) collective-permute-start(bf16[384,1024]{1,0:T(8,128)(2,1)S(1)} %join.5.refs_4_), channel_id=1, source_target_pairs={{0,16},{4,20},{8,24},{12,28},{16,0},{20,4},{24,8},{28,12},{1,17},{... | collective-permute-start | bytes 2359304 | tf_op jit(solution)/shard_map/ppermute | solution.py:23
  176.7 38.7 %collective-permute-start.32 = (bf16[384,1024]{1,0:T(8,128)(2,1)S(1)}, bf16[384,1024]{1,0:T(8,128)(2,1)S(1)}, u32[]{:S(2)}, u32[]{:S(2)}) collective-permute-start(bf16[384,1024]{1,0:T(8,128)(2,1)S(1)} %join.5.refs_4_), channel_id=1, source_target_pairs={{0,4},{4,0},{8,12},{12,8},{16,20},{20,16},{24,28},{28,24},{1,5},{5... | collective-permute-start | bytes 2359304 | tf_op jit(solution)/shard_map/ppermute | solution.py:23
  176.7 27.5 %collective-permute-start.41 = (bf16[192,1024]{1,0:T(8,128)(2,1)S(1)}, bf16[192,1024]{1,0:T(8,128)(2,1)S(1)}, u32[]{:S(2)}, u32[]{:S(2)}) collective-permute-start(bf16[192,1024]{1,0:T(8,128)(2,1)S(1)} %get-tuple-element.54), channel_id=1, source_target_pairs={{0,2},{1,3},{2,0},{3,1},{4,6},{5,7},{6,4},{7,5},{8,10},{9,11},{10,... | collective-permute-start | bytes 1179656 | tf_op jit(solution)/shard_map/ppermute | solution.py:23
  177.9 36.5 %collective-permute-start.42 = (bf16[192,1024]{1,0:T(8,128)(2,1)S(1)}, bf16[192,1024]{1,0:T(8,128)(2,1)S(1)}, u32[]{:S(2)}, u32[]{:S(2)}) collective-permute-start(bf16[192,1024]{1,0:T(8,128)(2,1)S(1)} %get-tuple-element.55), channel_id=1, source_target_pairs={{0,3},{1,2},{2,1},{3,0},{4,7},{5,6},{6,5},{7,4},{8,11},{9,10},{10,... | collective-permute-start | bytes 1179656 | tf_op jit(solution)/shard_map/ppermute | solution.py:23
  192.3 50.5 %collective-permute-start.34 = (bf16[384,1024]{1,0:T(8,128)(2,1)S(1)}, bf16[384,1024]{1,0:T(8,128)(2,1)S(1)}, u32[]{:S(2)}, u32[]{:S(2)}) collective-permute-start(bf16[384,1024]{1,0:T(8,128)(2,1)S(1)} %collective-permute-done.33.refs_0_.refs_6_.refs_2_), channel_id=1, source_target_pairs={{0,4},{4,0},{8,12},{12,8},{16,20},{20,16},{24,28},{28,24},{1,5},{5... | collective-permute-start | bytes 2359304 | tf_op jit(solution)/shard_map/ppermute | solution.py:23
  193.5 23.3 %collective-permute-start.37 = (bf16[192,1024]{1,0:T(8,128)(2,1)S(1)}, bf16[192,1024]{1,0:T(8,128)(2,1)S(1)}, u32[]{:S(2)}, u32[]{:S(2)}) collective-permute-start(bf16[192,1024]{1,0:T(8,128)(2,1)S(1)} %get-tuple-element.52), channel_id=1, source_target_pairs={{0,16},{4,20},{8,24},{12,28},{16,0},{20,4},{24,8},{28,12},{1,17},{... | collective-permute-start | bytes 1179656 | tf_op jit(solution)/shard_map/ppermute | solution.py:23
  204.2 39.3 %collective-permute-start.36 = (bf16[384,1024]{1,0:T(8,128)(2,1)S(1)}, bf16[384,1024]{1,0:T(8,128)(2,1)S(1)}, u32[]{:S(2)}, u32[]{:S(2)}) collective-permute-start(bf16[384,1024]{1,0:T(8,128)(2,1)S(1)} %collective-permute-done.35.refs_1_.refs_8_.refs_3_), channel_id=1, source_target_pairs={{0,4},{4,0},{8,12},{12,8},{16,20},{20,16},{24,28},{28,24},{1,5},{5... | collective-permute-start | bytes 2359304 | tf_op jit(solution)/shard_map/ppermute | solution.py:23
  214.8 29.0 %collective-permute-start.43 = (bf16[384,1024]{1,0:T(8,128)(2,1)S(1)}, bf16[384,1024]{1,0:T(8,128)(2,1)S(1)}, u32[]{:S(2)}, u32[]{:S(2)}) collective-permute-start(bf16[384,1024]{1,0:T(8,128)(2,1)S(1)} %join.6.refs_4_), channel_id=1, source_target_pairs={{0,8},{4,12},{8,0},{12,4},{16,24},{20,28},{24,16},{28,20},{1,9},{5... | collective-permute-start | bytes 2359304 | tf_op jit(solution)/shard_map/ppermute | solution.py:23
  215.4 27.4 %collective-permute-start.39 = (bf16[192,1024]{1,0:T(8,128)(2,1)S(1)}, bf16[192,1024]{1,0:T(8,128)(2,1)S(1)}, u32[]{:S(2)}, u32[]{:S(2)}) collective-permute-start(bf16[192,1024]{1,0:T(8,128)(2,1)S(1)} %get-tuple-element.53), channel_id=1, source_target_pairs={{0,8},{4,12},{8,0},{12,4},{16,24},{20,28},{24,16},{28,20},{1,9},{5... | collective-permute-start | bytes 1179656 | tf_op jit(solution)/shard_map/ppermute | solution.py:23
  216.9 27.2 %collective-permute-start.38 = (bf16[192,1024]{1,0:T(8,128)(2,1)S(1)}, bf16[192,1024]{1,0:T(8,128)(2,1)S(1)}, u32[]{:S(2)}, u32[]{:S(2)}) collective-permute-start(bf16[192,1024]{1,0:T(8,128)(2,1)S(1)} %collective-permute-done.37.refs_10_), channel_id=1, source_target_pairs={{0,4},{4,0},{8,12},{12,8},{16,20},{20,16},{24,28},{28,24},{1,5},{5... | collective-permute-start | bytes 1179656 | tf_op jit(solution)/shard_map/ppermute | solution.py:23
  242.8 20.0 %collective-permute-start.44 = (bf16[384,1024]{1,0:T(8,128)(2,1)S(1)}, bf16[384,1024]{1,0:T(8,128)(2,1)S(1)}, u32[]{:S(2)}, u32[]{:S(2)}) collective-permute-start(bf16[384,1024]{1,0:T(8,128)(2,1)S(1)} %join.6.refs_4_), channel_id=1, source_target_pairs={{0,16},{4,20},{8,24},{12,28},{16,0},{20,4},{24,8},{28,12},{1,17},{... | collective-permute-start | bytes 2359304 | tf_op jit(solution)/shard_map/ppermute | solution.py:23
  243.5 31.6 %collective-permute-start.54 = (bf16[384,1024]{1,0:T(8,128)(2,1)S(1)}, bf16[384,1024]{1,0:T(8,128)(2,1)S(1)}, u32[]{:S(2)}, u32[]{:S(2)}) collective-permute-start(bf16[384,1024]{1,0:T(8,128)(2,1)S(1)} %join.6.refs_4_), channel_id=1, source_target_pairs={{0,4},{4,0},{8,12},{12,8},{16,20},{20,16},{24,28},{28,24},{1,5},{5... | collective-permute-start | bytes 2359304 | tf_op jit(solution)/shard_map/ppermute | solution.py:23
  243.8 31.8 %collective-permute-start.55 = (bf16[384,1024]{1,0:T(8,128)(2,1)S(1)}, bf16[384,1024]{1,0:T(8,128)(2,1)S(1)}, u32[]{:S(2)}, u32[]{:S(2)}) collective-permute-start(bf16[384,1024]{1,0:T(8,128)(2,1)S(1)} %collective-permute-done.43.refs_0_.refs_6_), channel_id=1, source_target_pairs={{0,4},{4,0},{8,12},{12,8},{16,20},{20,16},{24,28},{28,24},{1,5},{5... | collective-permute-start | bytes 2359304 | tf_op jit(solution)/shard_map/ppermute | solution.py:23
  262.8 10.8 %collective-permute-start.45 = (bf16[192,1024]{1,0:T(8,128)(2,1)S(1)}, bf16[192,1024]{1,0:T(8,128)(2,1)S(1)}, u32[]{:S(2)}, u32[]{:S(2)}) collective-permute-start(bf16[192,1024]{1,0:T(8,128)(2,1)S(1)} %get-tuple-element.56), channel_id=1, source_target_pairs={{0,16},{4,20},{8,24},{12,28},{16,0},{20,4},{24,8},{28,12},{1,17},{... | collective-permute-start | bytes 1179656 | tf_op jit(solution)/shard_map/ppermute | solution.py:23
  263.4 12.8 %collective-permute-start.56 = (bf16[384,1024]{1,0:T(8,128)(2,1)S(1)}, bf16[384,1024]{1,0:T(8,128)(2,1)S(1)}, u32[]{:S(2)}, u32[]{:S(2)}) collective-permute-start(bf16[384,1024]{1,0:T(8,128)(2,1)S(1)} %collective-permute-done.44.refs_1_.refs_8_), channel_id=1, source_target_pairs={{0,4},{4,0},{8,12},{12,8},{16,20},{20,16},{24,28},{28,24},{1,5},{5... | collective-permute-start | bytes 2359304 | tf_op jit(solution)/shard_map/ppermute | solution.py:23
  263.4 11.5 %collective-permute-start.46 = (bf16[192,1024]{1,0:T(8,128)(2,1)S(1)}, bf16[192,1024]{1,0:T(8,128)(2,1)S(1)}, u32[]{:S(2)}, u32[]{:S(2)}) collective-permute-start(bf16[192,1024]{1,0:T(8,128)(2,1)S(1)} %get-tuple-element.57), channel_id=1, source_target_pairs={{0,8},{4,12},{8,0},{12,4},{16,24},{20,28},{24,16},{28,20},{1,9},{5... | collective-permute-start | bytes 1179656 | tf_op jit(solution)/shard_map/ppermute | solution.py:23
  273.6 4.0 %collective-permute-start.57 = (bf16[192,1024]{1,0:T(8,128)(2,1)S(1)}, bf16[192,1024]{1,0:T(8,128)(2,1)S(1)}, u32[]{:S(2)}, u32[]{:S(2)}) collective-permute-start(bf16[192,1024]{1,0:T(8,128)(2,1)S(1)} %collective-permute-done.45.refs_1_.refs_10_), channel_id=1, source_target_pairs={{0,4},{4,0},{8,12},{12,8},{16,20},{20,16},{24,28},{28,24},{1,5},{5... | collective-permute-start | bytes 1179656 | tf_op jit(solution)/shard_map/ppermute | solution.py:23
  275.0 2.7 collective-permute-start.58
  275.1 19.8 %collective-permute-start.47 = (bf16[384,384]{1,0:T(8,128)(2,1)S(1)}, bf16[384,384]{1,0:T(8,128)(2,1)S(1)}, u32[]{:S(2)}, u32[]{:S(2)}) collective-permute-start(bf16[384,384]{1,0:T(8,128)(2,1)S(1)} %join.7.refs_1_), channel_id=1, source_target_pairs={{0,4},{4,0},{8,12},{12,8},{16,20},{20,16},{24,28},{28,24},{1,5},{5... | collective-permute-start | bytes 884744 | tf_op jit(solution)/shard_map/ppermute | solution.py:23
  275.6 18.0 %collective-permute-start.48 = (bf16[384,384]{1,0:T(8,128)(2,1)S(1)}, bf16[384,384]{1,0:T(8,128)(2,1)S(1)}, u32[]{:S(2)}, u32[]{:S(2)}) collective-permute-start(bf16[384,384]{1,0:T(8,128)(2,1)S(1)} %join.7.refs_1_), channel_id=1, source_target_pairs={{0,8},{4,12},{8,0},{12,4},{16,24},{20,28},{24,16},{28,20},{1,9},{5... | collective-permute-start | bytes 884744 | tf_op jit(solution)/shard_map/ppermute | solution.py:23
  276.2 17.4 %collective-permute-start.50 = (bf16[384,384]{1,0:T(8,128)(2,1)S(1)}, bf16[384,384]{1,0:T(8,128)(2,1)S(1)}, u32[]{:S(2)}, u32[]{:S(2)}) collective-permute-start(bf16[384,384]{1,0:T(8,128)(2,1)S(1)} %join.7.refs_1_), channel_id=1, source_target_pairs={{0,16},{4,20},{8,24},{12,28},{16,0},{20,4},{24,8},{28,12},{1,17},{... | collective-permute-start | bytes 884744 | tf_op jit(solution)/shard_map/ppermute | solution.py:23
  291.5 8.9 %collective-permute-start.60 = (bf16[384,384]{1,0:T(8,128)(2,1)}, bf16[384,384]{1,0:T(8,128)(2,1)S(1)}, u32[]{:S(2)}, u32[]{:S(2)}) collective-permute-start(bf16[384,384]{1,0:T(8,128)(2,1)} %hidden_units.3.refs_1_), channel_id=1, source_target_pairs={{0,8},{4,12},{8,0},{12,4},{16,24},{20,28},{24,16},{28,20},{1,9},{5... | collective-permute-start | bytes 884744 | tf_op jit(solution)/shard_map/ppermute | solution.py:23
  293.0 8.4 %collective-permute-start.62 = (bf16[384,384]{1,0:T(8,128)(2,1)}, bf16[384,384]{1,0:T(8,128)(2,1)S(1)}, u32[]{:S(2)}, u32[]{:S(2)}) collective-permute-start(bf16[384,384]{1,0:T(8,128)(2,1)} %hidden_units.3.refs_1_), channel_id=1, source_target_pairs={{0,16},{4,20},{8,24},{12,28},{16,0},{20,4},{24,8},{28,12},{1,17},{... | collective-permute-start | bytes 884744 | tf_op jit(solution)/shard_map/ppermute | solution.py:23
  293.6 7.8 %collective-permute-start.49 = (bf16[384,384]{1,0:T(8,128)(2,1)S(1)}, bf16[384,384]{1,0:T(8,128)(2,1)S(1)}, u32[]{:S(2)}, u32[]{:S(2)}) collective-permute-start(bf16[384,384]{1,0:T(8,128)(2,1)S(1)} %collective-permute-done.48.refs_3_), channel_id=1, source_target_pairs={{0,4},{4,0},{8,12},{12,8},{16,20},{20,16},{24,28},{28,24},{1,5},{5... | collective-permute-start | bytes 884744 | tf_op jit(solution)/shard_map/ppermute | solution.py:23
  293.6 7.8 %collective-permute-start.51 = (bf16[384,384]{1,0:T(8,128)(2,1)S(1)}, bf16[384,384]{1,0:T(8,128)(2,1)S(1)}, u32[]{:S(2)}, u32[]{:S(2)}) collective-permute-start(bf16[384,384]{1,0:T(8,128)(2,1)S(1)} %collective-permute-done.50.refs_5_), channel_id=1, source_target_pairs={{0,4},{4,0},{8,12},{12,8},{16,20},{20,16},{24,28},{28,24},{1,5},{5... | collective-permute-start | bytes 884744 | tf_op jit(solution)/shard_map/ppermute | solution.py:23
  295.5 16.1 %collective-permute-start.59 = (bf16[384,384]{1,0:T(8,128)(2,1)}, bf16[384,384]{1,0:T(8,128)(2,1)S(1)}, u32[]{:S(2)}, u32[]{:S(2)}) collective-permute-start(bf16[384,384]{1,0:T(8,128)(2,1)} %hidden_units.3.refs_1_), channel_id=1, source_target_pairs={{0,4},{4,0},{8,12},{12,8},{16,20},{20,16},{24,28},{28,24},{1,5},{5... | collective-permute-start | bytes 884744 | tf_op jit(solution)/shard_map/ppermute | solution.py:23
  300.4 11.3 %collective-permute-start.61 = (bf16[384,384]{1,0:T(8,128)(2,1)S(1)}, bf16[384,384]{1,0:T(8,128)(2,1)S(1)}, u32[]{:S(2)}, u32[]{:S(2)}) collective-permute-start(bf16[384,384]{1,0:T(8,128)(2,1)S(1)} %collective-permute-done.60.refs_3_), channel_id=1, source_target_pairs={{0,4},{4,0},{8,12},{12,8},{16,20},{20,16},{24,28},{28,24},{1,5},{5... | collective-permute-start | bytes 884744 | tf_op jit(solution)/shard_map/ppermute | solution.py:23
  301.4 10.3 %collective-permute-start.63 = (bf16[384,384]{1,0:T(8,128)(2,1)S(1)}, bf16[384,384]{1,0:T(8,128)(2,1)S(1)}, u32[]{:S(2)}, u32[]{:S(2)}) collective-permute-start(bf16[384,384]{1,0:T(8,128)(2,1)S(1)} %collective-permute-done.62.refs_5_), channel_id=1, source_target_pairs={{0,4},{4,0},{8,12},{12,8},{16,20},{20,16},{24,28},{28,24},{1,5},{5... | collective-permute-start | bytes 884744 | tf_op jit(solution)/shard_map/ppermute | solution.py:23
  309.4 12.5 %collective-permute-start.52 = (bf16[384,512]{1,0:T(8,128)(2,1)S(1)}, bf16[384,512]{1,0:T(8,128)(2,1)S(1)}, u32[]{:S(2)}, u32[]{:S(2)}) collective-permute-start(bf16[384,512]{1,0:T(8,128)(2,1)S(1)} %get-tuple-element.59), channel_id=1, source_target_pairs={{0,16},{4,20},{8,24},{12,28},{16,0},{20,4},{24,8},{28,12},{1,17},{... | collective-permute-start | bytes 1179656 | tf_op jit(solution)/shard_map/ppermute | solution.py:23
  310.4 11.5 %collective-permute-start.53 = (bf16[384,512]{1,0:T(8,128)(2,1)S(1)}, bf16[384,512]{1,0:T(8,128)(2,1)S(1)}, u32[]{:S(2)}, u32[]{:S(2)}) collective-permute-start(bf16[384,512]{1,0:T(8,128)(2,1)S(1)} %get-tuple-element.60), channel_id=1, source_target_pairs={{0,8},{4,12},{8,0},{12,4},{16,24},{20,28},{24,16},{28,20},{1,9},{5... | collective-permute-start | bytes 1179656 | tf_op jit(solution)/shard_map/ppermute | solution.py:23
  320.0 11.0 %collective-permute-start.65 = (bf16[384,512]{1,0:T(8,128)(2,1)S(1)}, bf16[384,512]{1,0:T(8,128)(2,1)S(1)}, u32[]{:S(2)}, u32[]{:S(2)}) collective-permute-start(bf16[384,512]{1,0:T(8,128)(2,1)S(1)} %get-tuple-element.64), channel_id=1, source_target_pairs={{0,16},{4,20},{8,24},{12,28},{16,0},{20,4},{24,8},{28,12},{1,17},{... | collective-permute-start | bytes 1179656 | tf_op jit(solution)/shard_map/ppermute | solution.py:23
  320.7 10.6 %collective-permute-start.66 = (bf16[384,512]{1,0:T(8,128)(2,1)S(1)}, bf16[384,512]{1,0:T(8,128)(2,1)S(1)}, u32[]{:S(2)}, u32[]{:S(2)}) collective-permute-start(bf16[384,512]{1,0:T(8,128)(2,1)S(1)} %get-tuple-element.65), channel_id=1, source_target_pairs={{0,8},{4,12},{8,0},{12,4},{16,24},{20,28},{24,16},{28,20},{1,9},{5... | collective-permute-start | bytes 1179656 | tf_op jit(solution)/shard_map/ppermute | solution.py:23
  322.1 10.5 %collective-permute-start.64 = (bf16[192,1024]{1,0:T(8,128)(2,1)S(1)}, bf16[192,1024]{1,0:T(8,128)(2,1)S(1)}, u32[]{:S(2)}, u32[]{:S(2)}) collective-permute-start(bf16[192,1024]{1,0:T(8,128)(2,1)S(1)} %get-tuple-element.63), channel_id=1, source_target_pairs={{0,1},{1,0},{2,3},{3,2},{4,5},{5,4},{6,7},{7,6},{8,9},{9,8},{10,11... | collective-permute-start | bytes 1179656 | tf_op jit(solution)/shard_map/ppermute | solution.py:23
  332.3 25.6 %collective-permute-start.67 = (bf16[192,1024]{1,0:T(8,128)(2,1)}, bf16[192,1024]{1,0:T(8,128)(2,1)S(1)}, u32[]{:S(2)}, u32[]{:S(2)}) collective-permute-start(bf16[192,1024]{1,0:T(8,128)(2,1)} %get-tuple-element.66), channel_id=1, source_target_pairs={{0,2},{1,3},{2,0},{3,1},{4,6},{5,7},{6,4},{7,5},{8,10},{9,11},{10,... | collective-permute-start | bytes 1179656 | tf_op jit(solution)/shard_map/ppermute | solution.py:23
  332.3 33.6 %collective-permute-start.68 = (bf16[192,1024]{1,0:T(8,128)(2,1)}, bf16[192,1024]{1,0:T(8,128)(2,1)S(1)}, u32[]{:S(2)}, u32[]{:S(2)}) collective-permute-start(bf16[192,1024]{1,0:T(8,128)(2,1)} %get-tuple-element.67), channel_id=1, source_target_pairs={{0,3},{1,2},{2,1},{3,0},{4,7},{5,6},{6,5},{7,4},{8,11},{9,10},{10,... | collective-permute-start | bytes 1179656 | tf_op jit(solution)/shard_map/ppermute | solution.py:23
  (55 other events, 1489.3 us)
Sparse Core Ops, SparseCore 0:
  106.0 25.2 reduce-scatter.2
  133.7 25.7 reduce-scatter.4

commit v6 on v5

--- a/solution.py
+++ b/solution.py
@@ -904,31 +904,28 @@
         pick = here[:, None] & (place[:, None] == spots[None, :])
         picked.append(pick.astype(jnp.bfloat16))
 
-    groups = [[0, 1], [2, 3]] if exp_count == 4 else [list(range(exp_count))]
+    groups = [[0], list(range(1, exp_count))]
     sent = pick_rows(picked, scaled, late)
     pieces = [rows if mask == 0 else swap(rows, "exp", mask) for mask, rows in enumerate(sent)]
-    hiddens, after, order = [], (), ()
+    weights = [None] + [down_parts[mask] for mask in sorted(down_parts)]
+    settled, arrived, order = [], (), ()
     for group in groups:
-        parts = gather_parts(join([pieces[mask] for mask in group], after), 0, order)
-        after = near(parts)
+        rows = [pieces[mask] for mask in group]
+        rows = join(rows, arrived) if len(group) > 1 else rows[0]
+        parts = gather_parts(rows, 0, order)
+        arrived = far(parts)
         hidden = hidden_units(me, [parts], one_over_gain, expert_gate[0], expert_up[0])
-        order = [hidden]
-        hiddens.append(hidden)
-    answers, order = {}, []
-    weights = [None] + [down_parts[mask] for mask in sorted(down_parts)]
-    settled = []
-    for group, hidden in zip(groups, hiddens):
-        rows = hidden if group is groups[-1] else join([hidden], far(parts))
         if crossing:
-            units = {0: rows, 2: swap(rows, "ctx", 2), 4: swap(rows, "ctx", 4)}
+            units = {0: hidden, 2: swap(hidden, "ctx", 2), 4: swap(hidden, "ctx", 4)}
             units.update({mask + 1: swap(units[mask], "ctx", 1) for mask in (0, 2, 4)})
-            keep, first, second = cross_down(me, units, weights, down_rows, order)
+            keep, first, second = cross_down(me, units, weights, down_rows)
             order = [keep]
             settled.append((keep, swap(first, "ctx", 4), swap(second, "ctx", 2)))
         else:
-            answer = down(me, gather_parts(rows), weights, down_rows, order)
+            answer = down(me, gather_parts(hidden), weights, down_rows)
             order = [answer]
             settled.append([answer])
+    answers = {}
     for group, sums in zip(groups, settled):
         if crossing:
             pieces = settle(*sums, len(group), order)

time: 376 us -> 374 us (level)
  waiting for transfers between devices: 200 us -> 183 us
  starting transfers between devices: 45.5 us -> 59.8 us
  local copies, waits for them, and re-layouts: 16.7 us -> 9.56 us
  Pallas kernels: 92.5 us -> 98 us
    ppermute x68, waiting for transfers between devices: 175 us -> 158 us  [swap(): lax.ppermute(array, axis, [(i, i ^ mask) for i in range(lax.axis_size(axi...]
    ppermute x68, starting transfers between devices: 43.5 us -> 58.4 us  [swap(): lax.ppermute(array, axis, [(i, i ^ mask) for i in range(lax.axis_size(axi...]
    unnamed x98 -> x100, local copies, waits for them, and re-layouts: 12.1 us -> 4.97 us
    pallas_call x24 -> x22, Pallas kernels: 92.5 us -> 98 us  [launch(): pl.pallas_call(body, grid_spec=pltpu.PrefetchScalarGridSpec(num_scalar_pr...]
  transfers between devices with their start and end apart: 71 -> 71, of which waited for: 33 -> 42; matrix products, arithmetic and copies ran while one was open for 2% -> 3% of each run, Pallas kernels for 19% -> 14%
where the time goes in v6:
time: 374 us; the launch traced here: 373 us
  waiting for transfers between devices  183 us (49%)
  Pallas kernels  98 us (26%)
  starting transfers between devices  59.8 us (16%)
  between operations  14.8 us (4%)
  local copies, waits for them, and re-layouts  9.56 us (3%)
  other arithmetic  7.44 us (2%)
    ppermute x68, waiting for transfers between devices, swap(): lax.ppermute(array, axis, [(i, i ^ mask) for i in range(lax.axis_size(axi...  158 us
    pallas_call x22, Pallas kernels, launch(): pl.pallas_call(body, grid_spec=pltpu.PrefetchScalarGridSpec(num_scalar_pr...  98 us
    ppermute x68, starting transfers between devices, swap(): lax.ppermute(array, axis, [(i, i ^ mask) for i in range(lax.axis_size(axi...  58.4 us
    reduce_scatter x2, waiting for transfers between devices, shards(): lax.psum_scatter(rows, 'exp', scatter_dimension=0, tiled=True)  24.9 us
  transfers between devices with their start and end apart: 71, of which 42 were waited for; matrix products, arithmetic and copies ran while one was open for 3% of the time, Pallas kernels for 14%

profile of v6, /device:TPU:8, one launch (start us, length us, event | category | flops | bytes accessed | tf_op | source)
XLA Modules:
  0.0 372.9 jit_solution(3408428431181554657)
XLA Ops:
  7.2 3.5 cut_columns.2
  10.7 1.5 collective-permute-start.1
  12.2 1.5 collective-permute-start.2
  14.6 1.3 collective-permute-start
  17.4 1.3 broadcast_in_dim.20.refs_8_.refs_6_
  18.7 13.9 %local_states.1 = (f32[128,4096]{1,0:T(8,128)}, f32[128,4096]{1,0:T(8,128)}, bf16[32,4096]{1,0:T(8,128)(2,1)}) custom-call(bf16[128,4096]{1,0:T(8,128)(2,1)} %refs_0_.1, f32[8,4096]{1,0:T(8,128)} %pad_convert_fusion.refs_1_, bf16[128,4096]{1,0:T(8,128)(2,1)} %refs_2_.2, f32[4,4096]{1,0:T(4,128)} %refs_3_.4, f32[1,4096]{1,0:T(1,128)} %bitcast.66, ...), custom_call_target="tpu_custom_call" | custom-call | flops 41943040 | bytes 6291456 | tf_op jit(solution)/shard_map/local_states/pallas_call | solution.py:95
  33.8 14.6 %collective-permute-start.4 = (bf16[32,4096]{1,0:T(8,128)(2,1)S(1)}, bf16[32,4096]{1,0:T(8,128)(2,1)S(1)}, u32[]{:S(2)}, u32[]{:S(2)}) collective-permute-start(bf16[32,4096]{1,0:T(8,128)(2,1)S(1)} %join.2.refs_9_.refs_1_), channel_id=1, source_target_pairs={{0,8},{4,12},{8,0},{12,4},{16,24},{20,28},{24,16},{28,20},{1,9},{5... | collective-permute-start | bytes 786440 | tf_op jit(solution)/shard_map/ppermute | solution.py:23
  48.4 1.5 collective-permute-start.6
  50.0 5.7 %collective-permute-done.4.refs_11_.refs_3_ = bf16[32,4096]{1,0:T(8,128)(2,1)S(1)} collective-permute-done((bf16[32,4096]{1,0:T(8,128)(2,1)S(1)}, bf16[32,4096]{1,0:T(8,128)(2,1)S(1)}, u32[]{:S(2)}, u32[]{:S(2)}) %collective-permute-start.4) | collective-permute-done | bytes 262176 | tf_op jit(solution)/shard_map/ppermute | solution.py:23
  55.6 3.9 %collective-permute-done.6.refs_13_.refs_5_ = bf16[32,4096]{1,0:T(8,128)(2,1)S(1)} collective-permute-done((bf16[32,4096]{1,0:T(8,128)(2,1)S(1)}, bf16[32,4096]{1,0:T(8,128)(2,1)S(1)}, u32[]{:S(2)}, u32[]{:S(2)}) %collective-permute-start.6) | collective-permute-done | bytes 262176 | tf_op jit(solution)/shard_map/ppermute | solution.py:23
  59.5 1.4 collective-permute-done.8.refs_15_.refs_7_
  61.1 1.4 collective-permute-done.9.refs_16_.refs_8_
  62.5 1.3 broadcast_in_dim.23.refs_7_
  63.9 9.1 %read_out.2 = (bf16[64,4096]{1,0:T(8,128)(2,1)}, f32[16,4096]{1,0:T(8,128)}) custom-call(s32[1]{0:T(128)} %bitcast.refs_0_, f32[128,4096]{1,0:T(8,128)} %get-tuple-element.34.refs_1_, f32[128,4096]{1,0:T(8,128)} %get-tuple-element.35.refs_2_, bf16[128,4096]{1,0:T(8,128)(2,1)} %refs_3_.6, f32[16,4096]{1,0:T(8,128)} %refs_4_.3, f32[1,4096]{1,0:T(1,128)} %bitcast.61, ...), custom_call_target="tpu_custom_call" | custom-call | flops 29360128 | bytes 3145728 | tf_op jit(solution)/shard_map/read_out/pallas_call | solution.py:95
  73.0 1.2 collective-permute-start.11
  74.3 1.5 collective-permute-start.13
  75.8 8.3 %read_out.3 = (bf16[64,4096]{1,0:T(8,128)(2,1)}, f32[16,4096]{1,0:T(8,128)}) custom-call(s32[1]{0:T(128)} %bitcast.refs_0_, f32[128,4096]{1,0:T(8,128)} %get-tuple-element.34.refs_1_, f32[128,4096]{1,0:T(8,128)} %get-tuple-element.35.refs_2_, bf16[128,4096]{1,0:T(8,128)(2,1)} %refs_3_.6, f32[16,4096]{1,0:T(8,128)} %refs_4_.3, f32[1,4096]{1,0:T(1,128)} %bitcast.62, ...), custom_call_target="tpu_custom_call" | custom-call | flops 29360128 | bytes 3145728 | tf_op jit(solution)/shard_map/read_out/pallas_call | solution.py:95
  85.6 2.3 collective-permute-done.11.refs_0_.refs_4_.refs_9_
  87.9 1.3 collective-permute-done.13.refs_1_.refs_6_.refs_10_
  90.2 1.7 collective-permute-start.15
  92.7 6.5 %collective-permute-done.19.refs_12_.refs_0_.refs_4_ = bf16[64,4096]{1,0:T(8,128)(2,1)S(1)} collective-permute-done((bf16[64,4096]{1,0:T(8,128)(2,1)}, bf16[64,4096]{1,0:T(8,128)(2,1)S(1)}, u32[]{:S(2)}, u32[]{:S(2)}) %collective-permute-start.19) | collective-permute-done | bytes 524320 | tf_op jit(solution)/shard_map/ppermute | solution.py:23
  100.4 4.6 %collective-permute-done.15.refs_8_.refs_2_ = bf16[64,2048]{1,0:T(8,128)(2,1)S(1)} collective-permute-done((bf16[64,2048]{1,0:T(8,128)(2,1)S(1)}, bf16[64,2048]{1,0:T(8,128)(2,1)S(1)}, u32[]{:S(2)}, u32[]{:S(2)}) %collective-permute-start.15) | collective-permute-done | bytes 262176 | tf_op jit(solution)/shard_map/ppermute | solution.py:23
  106.9 8.3 %project.2.refs_12_ = bf16[512,1024]{1,0:T(8,128)(2,1)} custom-call(s32[1]{0:T(128)} %bitcast.refs_0_, bf16[4096,1024]{1,0:T(8,128)(2,1)} %refs_1_.3, bf16[64,4096]{1,0:T(8,128)(2,1)S(1)} %copy-done.38, bf16[64,4096]{1,0:T(8,128)(2,1)S(1)} %collective-permute-done.10.refs_3_, bf16[64,4096]{1,0:T(8,128)(2,1)S(1)} %collective-permute-done.11.refs_0_.refs_4_.refs_9_, ...), custom_call_target="tpu_custom_call" | custom-call | flops 4294967296 | bytes 13631488 | tf_op jit(solution)/shard_map/project/pallas_call | solution.py:95
  115.4 1.6 collective-permute-start.24
  118.4 5.5 %collective-permute-done.24.refs_8_ = bf16[64,2048]{1,0:T(8,128)(2,1)S(1)} collective-permute-done((bf16[64,2048]{1,0:T(8,128)(2,1)S(1)}, bf16[64,2048]{1,0:T(8,128)(2,1)S(1)}, u32[]{:S(2)}, u32[]{:S(2)}) %collective-permute-start.24) | collective-permute-done | bytes 262176 | tf_op jit(solution)/shard_map/ppermute | solution.py:23
  123.8 1.3 collective-permute-done.26.refs_10_
  125.4 1.3 collective-permute-done.27.refs_11_
  126.6 8.4 %project.3 = bf16[512,1024]{1,0:T(8,128)(2,1)} custom-call(s32[1]{0:T(128)} %bitcast.refs_0_, bf16[4096,1024]{1,0:T(8,128)(2,1)} %refs_1_.3, bf16[64,4096]{1,0:T(8,128)(2,1)S(1)} %copy-done.34, bf16[64,4096]{1,0:T(8,128)(2,1)S(1)} %collective-permute-done.21.refs_3_, bf16[64,4096]{1,0:T(8,128)(2,1)S(1)} %collective-permute-done.19.refs_12_.refs_0_.refs_4_, ...), custom_call_target="tpu_custom_call" | custom-call | flops 4294967296 | bytes 13631488 | tf_op jit(solution)/shard_map/project/pallas_call | solution.py:95
  137.1 4.5 %cut_columns.3 = (bf16[384,1024]{1,0:T(8,128)(2,1)}, bf16[384,1024]{1,0:T(8,128)(2,1)}, bf16[384,2048]{1,0:T(8,128)(2,1)}) custom-call(s32[1]{0:T(128)} %bitcast.refs_0_, bf16[384,8192]{1,0:T(8,128)(2,1)} %bitcast.41, bf16[384,8192]{1,0:T(8,128)(2,1)} %bitcast.42, bf16[384,8192]{1,0:T(8,128)(2,1)} %bitcast.43, bf16[384,8192]{1,0:T(8,128)(2,1)} %bitcast.44, ...), custom_call_target="tpu_custom_call" | custom-call | bytes 6291456 | tf_op jit(solution)/shard_map/cut_columns/pallas_call | solution.py:95
  144.4 24.9 %reduce-scatter.5.cloned.1.call-done = bf16[128,1024]{1,0:T(8,128)(2,1)} async-done(((bf16[512,1024]{1,0:T(8,128)(2,1)}), bf16[128,1024]{1,0:T(8,128)(2,1)}) %reduce-scatter.5.cloned.1.call-update) | async-done | bytes 262160 | tf_op jit(solution)/shard_map/reduce_scatter | solution.py:877
  170.4 2.3 multiply_convert_fusion
  173.4 1.5 collective-permute-start.32
  174.9 1.5 collective-permute-start.34
  176.3 2.6 collective-permute-start.47
  180.4 3.9 %collective-permute-done.32.refs_0_.refs_6_ = bf16[192,1024]{1,0:T(8,128)(2,1)S(1)} collective-permute-done((bf16[192,1024]{1,0:T(8,128)(2,1)S(1)}, bf16[192,1024]{1,0:T(8,128)(2,1)S(1)}, u32[]{:S(2)}, u32[]{:S(2)}) %collective-permute-start.32) | collective-permute-done | bytes 393248 | tf_op jit(solution)/shard_map/ppermute | solution.py:23
  185.6 1.5 collective-permute-start.36
  187.1 6.9 %collective-permute-done.47.refs_0_ = bf16[192,1024]{1,0:T(8,128)(2,1)S(1)} collective-permute-done((bf16[192,1024]{1,0:T(8,128)(2,1)S(1)}, bf16[192,1024]{1,0:T(8,128)(2,1)S(1)}, u32[]{:S(2)}, u32[]{:S(2)}) %collective-permute-start.47) | collective-permute-done | bytes 393248 | tf_op jit(solution)/shard_map/ppermute | solution.py:23
  194.6 11.8 %collective-permute-done.48.refs_1_ = bf16[192,1024]{1,0:T(8,128)(2,1)S(1)} collective-permute-done((bf16[192,1024]{1,0:T(8,128)(2,1)S(1)}, bf16[192,1024]{1,0:T(8,128)(2,1)S(1)}, u32[]{:S(2)}, u32[]{:S(2)}) %collective-permute-start.48) | collective-permute-done | bytes 393248 | tf_op jit(solution)/shard_map/ppermute | solution.py:23
  206.4 7.4 %collective-permute-done.49.refs_2_ = bf16[192,1024]{1,0:T(8,128)(2,1)S(1)} collective-permute-done((bf16[192,1024]{1,0:T(8,128)(2,1)S(1)}, bf16[192,1024]{1,0:T(8,128)(2,1)S(1)}, u32[]{:S(2)}, u32[]{:S(2)}) %collective-permute-start.49) | collective-permute-done | bytes 393248 | tf_op jit(solution)/shard_map/ppermute | solution.py:23
  213.9 1.6 join.3.refs_4_
  219.6 7.1 %hidden_units.2.refs_1_ = bf16[192,384]{1,0:T(8,128)(2,1)S(1)} custom-call(s32[1]{0:T(128)} %bitcast.refs_0_, f32[8,1,1024]{2,1,0:T(1,128)S(1)} %inverse_gains.1.refs_1_, bf16[8192,384]{1,0:T(8,128)(2,1)S(1)} %bitcast.56, bf16[8192,384]{1,0:T(8,128)(2,1)} %bitcast.57, bf16[192,1024]{1,0:T(8,128)(2,1)S(1)} %get-tuple-element.49.refs_4_, ...), custom_call_target="tpu_custom_call" | custom-call | flops 2415919104 | bytes 15728640 | tf_op jit(solution)/shard_map/hidden_units/pallas_call | solution.py:95
  226.7 1.5 collective-permute-start.41
  228.2 1.5 collective-permute-start.43
  229.7 15.3 %collective-permute-done.41.refs_3_ = bf16[192,384]{1,0:T(8,128)(2,1)S(1)} collective-permute-done((bf16[192,384]{1,0:T(8,128)(2,1)S(1)}, bf16[192,384]{1,0:T(8,128)(2,1)S(1)}, u32[]{:S(2)}, u32[]{:S(2)}) %collective-permute-start.41) | collective-permute-done | bytes 147488 | tf_op jit(solution)/shard_map/ppermute | solution.py:23
  246.7 3.7 cross_down.2
  250.4 1.8 halves.7
  253.4 1.6 collective-permute-start.57
  255.0 12.8 %collective-permute-done.55.refs_10_ = bf16[288,1024]{1,0:T(8,128)(2,1)S(1)} collective-permute-done((bf16[288,1024]{1,0:T(8,128)(2,1)S(1)}, bf16[288,1024]{1,0:T(8,128)(2,1)S(1)}, u32[]{:S(2)}, u32[]{:S(2)}) %collective-permute-start.55) | collective-permute-done | bytes 589856 | tf_op jit(solution)/shard_map/ppermute | solution.py:23
  270.6 1.3 copy-done.37
  271.9 15.1 %hidden_units.3.refs_1_ = bf16[576,384]{1,0:T(8,128)(2,1)S(1)} custom-call(s32[1]{0:T(128)} %bitcast.refs_0_, f32[8,1,1024]{2,1,0:T(1,128)S(1)} %inverse_gains.1.refs_1_, bf16[8192,384]{1,0:T(8,128)(2,1)} %bitcast.53, bf16[8192,384]{1,0:T(8,128)(2,1)} %bitcast.58, bf16[576,1024]{1,0:T(8,128)(2,1)} %join.3.refs_4_, bf16[576,1024]{1,0:T(8,128)(2,1)S(1)} %copy-done.37, ...), custom_call_target="tpu_custom_call" | custom-call | flops 7247757312 | bytes 22020096 | tf_op jit(solution)/shard_map/hidden_units/pallas_call | solution.py:95
  287.1 1.6 collective-permute-start.60
  288.7 1.5 collective-permute-start.62
  290.2 9.1 %collective-permute-done.60.refs_3_ = bf16[576,384]{1,0:T(8,128)(2,1)S(1)} collective-permute-done((bf16[576,384]{1,0:T(8,128)(2,1)S(1)}, bf16[576,384]{1,0:T(8,128)(2,1)S(1)}, u32[]{:S(2)}, u32[]{:S(2)}) %collective-permute-start.60) | collective-permute-done | bytes 442400 | tf_op jit(solution)/shard_map/ppermute | solution.py:23
  299.3 1.3 collective-permute-done.62.refs_5_
  301.1 1.3 collective-permute-done.63.refs_6_
  302.4 6.2 %cross_down.3 = (bf16[576,1024]{1,0:T(8,128)(2,1)S(1)}, bf16[576,512]{1,0:T(8,128)(2,1)S(1)}, bf16[576,512]{1,0:T(8,128)(2,1)S(1)}) custom-call(s32[1]{0:T(128)} %bitcast.refs_0_, bf16[576,384]{1,0:T(8,128)(2,1)S(1)} %hidden_units.3.refs_1_, bf16[576,384]{1,0:T(8,128)(2,1)S(1)} %collective-permute-done.59.refs_2_, ...), custom_call_target="tpu_custom_call" | custom-call | flops 7247757312 | bytes 9437184 | tf_op jit(solution)/shard_map/cross_down/pallas_call | solution.py:95
  308.6 1.5 collective-permute-start.64
  311.1 13.0 %collective-permute-done.64.refs_1_ = bf16[576,512]{1,0:T(8,128)(2,1)S(1)} collective-permute-done((bf16[576,512]{1,0:T(8,128)(2,1)S(1)}, bf16[576,512]{1,0:T(8,128)(2,1)S(1)}, u32[]{:S(2)}, u32[]{:S(2)}) %collective-permute-start.64) | collective-permute-done | bytes 589856 | tf_op jit(solution)/shard_map/ppermute | solution.py:23
  326.5 2.9 collective-permute-start.67
  331.7 4.1 %collective-permute-done.45.refs_1_ = bf16[192,512]{1,0:T(8,128)(2,1)S(1)} collective-permute-done((bf16[192,512]{1,0:T(8,128)(2,1)}, bf16[192,512]{1,0:T(8,128)(2,1)S(1)}, u32[]{:S(2)}, u32[]{:S(2)}) %collective-permute-start.45) | collective-permute-done | bytes 196640 | tf_op jit(solution)/shard_map/ppermute | solution.py:23
  337.5 4.2 %collective-permute-done.66.refs_9_ = bf16[192,1024]{1,0:T(8,128)(2,1)S(1)} collective-permute-done((bf16[192,1024]{1,0:T(8,128)(2,1)}, bf16[192,1024]{1,0:T(8,128)(2,1)S(1)}, u32[]{:S(2)}, u32[]{:S(2)}) %collective-permute-start.66) | collective-permute-done | bytes 393248 | tf_op jit(solution)/shard_map/ppermute | solution.py:23
  341.8 14.4 %collective-permute-done.67.refs_10_ = bf16[192,1024]{1,0:T(8,128)(2,1)} collective-permute-done((bf16[192,1024]{1,0:T(8,128)(2,1)}, bf16[192,1024]{1,0:T(8,128)(2,1)}, u32[]{:S(2)}, u32[]{:S(2)}) %collective-permute-start.67) | collective-permute-done | bytes 393248 | tf_op jit(solution)/shard_map/ppermute | solution.py:23
  356.1 7.2 %collective-permute-done.68.refs_11_ = bf16[192,1024]{1,0:T(8,128)(2,1)} collective-permute-done((bf16[192,1024]{1,0:T(8,128)(2,1)}, bf16[192,1024]{1,0:T(8,128)(2,1)}, u32[]{:S(2)}, u32[]{:S(2)}) %collective-permute-start.68) | collective-permute-done | bytes 393248 | tf_op jit(solution)/shard_map/ppermute | solution.py:23
  363.4 2.7 combine.1
  (244 shorter events, 39.3 us)
Async XLA Ops:
  7.2 137.2 %reduce-scatter.3.cloned.1.call-start = ((), (), s32[]{:S(2)}) async-start(), calls=%async_computation.2 | async-start | bytes 1310720 | tf_op jit(solution)/shard_map/reduce_scatter | solution.py:877
  10.7 21.9 %collective-permute-start.1 = (bf16[384,1024]{1,0:T(8,128)(2,1)}, bf16[384,1024]{1,0:T(8,128)(2,1)S(1)}, u32[]{:S(2)}, u32[]{:S(2)}) collective-permute-start(bf16[384,1024]{1,0:T(8,128)(2,1)} %get-tuple-element.37), channel_id=1, source_target_pairs={{0,8},{4,12},{8,0},{12,4},{16,24},{20,28},{24,16},{28,20},{1,9},{5... | collective-permute-start | bytes 2359304 | tf_op jit(solution)/shard_map/ppermute | solution.py:23
  12.2 20.4 %collective-permute-start.2 = (bf16[384,1024]{1,0:T(8,128)(2,1)}, bf16[384,1024]{1,0:T(8,128)(2,1)S(1)}, u32[]{:S(2)}, u32[]{:S(2)}) collective-permute-start(bf16[384,1024]{1,0:T(8,128)(2,1)} %get-tuple-element.38), channel_id=1, source_target_pairs={{0,16},{4,20},{8,24},{12,28},{16,0},{20,4},{24,8},{28,12},{1,17},{... | collective-permute-start | bytes 2359304 | tf_op jit(solution)/shard_map/ppermute | solution.py:23
  14.6 2.1 collective-permute-start
  33.8 21.8 %collective-permute-start.4 = (bf16[32,4096]{1,0:T(8,128)(2,1)S(1)}, bf16[32,4096]{1,0:T(8,128)(2,1)S(1)}, u32[]{:S(2)}, u32[]{:S(2)}) collective-permute-start(bf16[32,4096]{1,0:T(8,128)(2,1)S(1)} %join.2.refs_9_.refs_1_), channel_id=1, source_target_pairs={{0,8},{4,12},{8,0},{12,4},{16,24},{20,28},{24,16},{28,20},{1,9},{5... | collective-permute-start | bytes 786440 | tf_op jit(solution)/shard_map/ppermute | solution.py:23
  48.4 11.1 %collective-permute-start.6 = (bf16[32,4096]{1,0:T(8,128)(2,1)S(1)}, bf16[32,4096]{1,0:T(8,128)(2,1)S(1)}, u32[]{:S(2)}, u32[]{:S(2)}) collective-permute-start(bf16[32,4096]{1,0:T(8,128)(2,1)S(1)} %join.2.refs_9_.refs_1_), channel_id=1, source_target_pairs={{0,16},{4,20},{8,24},{12,28},{16,0},{20,4},{24,8},{28,12},{1,17},{... | collective-permute-start | bytes 786440 | tf_op jit(solution)/shard_map/ppermute | solution.py:23
  50.0 10.9 %collective-permute-start.8 = (bf16[32,4096]{1,0:T(8,128)(2,1)S(1)}, bf16[32,4096]{1,0:T(8,128)(2,1)S(1)}, u32[]{:S(2)}, u32[]{:S(2)}) collective-permute-start(bf16[32,4096]{1,0:T(8,128)(2,1)S(1)} %join.2.refs_9_.refs_1_), channel_id=1, source_target_pairs={{0,24},{4,28},{8,16},{12,20},{16,8},{20,12},{24,0},{28,4},{1,25},{... | collective-permute-start | bytes 786440 | tf_op jit(solution)/shard_map/ppermute | solution.py:23
  50.0 11.1 %collective-permute-start.3 = (bf16[32,4096]{1,0:T(8,128)(2,1)S(1)}, bf16[32,4096]{1,0:T(8,128)(2,1)S(1)}, u32[]{:S(2)}, u32[]{:S(2)}) collective-permute-start(bf16[32,4096]{1,0:T(8,128)(2,1)S(1)} %join.2.refs_9_.refs_1_), channel_id=1, source_target_pairs={{0,4},{4,0},{8,12},{12,8},{16,20},{20,16},{24,28},{28,24},{1,5},{5... | collective-permute-start | bytes 786440 | tf_op jit(solution)/shard_map/ppermute | solution.py:23
  55.6 5.4 %collective-permute-start.5 = (bf16[32,4096]{1,0:T(8,128)(2,1)S(1)}, bf16[32,4096]{1,0:T(8,128)(2,1)S(1)}, u32[]{:S(2)}, u32[]{:S(2)}) collective-permute-start(bf16[32,4096]{1,0:T(8,128)(2,1)S(1)} %collective-permute-done.4.refs_11_.refs_3_), channel_id=1, source_target_pairs={{0,4},{4,0},{8,12},{12,8},{16,20},{20,16},{24,28},{28,24},{1,5},{5... | collective-permute-start | bytes 786440 | tf_op jit(solution)/shard_map/ppermute | solution.py:23
  59.5 1.6 collective-permute-start.7
  60.9 1.7 collective-permute-start.9
  73.0 14.9 %collective-permute-start.11 = (bf16[64,4096]{1,0:T(8,128)(2,1)}, bf16[64,4096]{1,0:T(8,128)(2,1)S(1)}, u32[]{:S(2)}, u32[]{:S(2)}) collective-permute-start(bf16[64,4096]{1,0:T(8,128)(2,1)} %get-tuple-element.39.refs_2_), channel_id=1, source_target_pairs={{0,8},{4,12},{8,0},{12,4},{16,24},{20,28},{24,16},{28,20},{1,9},{5... | collective-permute-start | bytes 1572872 | tf_op jit(solution)/shard_map/ppermute | solution.py:23
  74.3 14.9 %collective-permute-start.13 = (bf16[64,4096]{1,0:T(8,128)(2,1)}, bf16[64,4096]{1,0:T(8,128)(2,1)S(1)}, u32[]{:S(2)}, u32[]{:S(2)}) collective-permute-start(bf16[64,4096]{1,0:T(8,128)(2,1)} %get-tuple-element.39.refs_2_), channel_id=1, source_target_pairs={{0,16},{4,20},{8,24},{12,28},{16,0},{20,4},{24,8},{28,12},{1,17},{... | collective-permute-start | bytes 1572872 | tf_op jit(solution)/shard_map/ppermute | solution.py:23
  84.1 15.1 %collective-permute-start.19 = (bf16[64,4096]{1,0:T(8,128)(2,1)}, bf16[64,4096]{1,0:T(8,128)(2,1)S(1)}, u32[]{:S(2)}, u32[]{:S(2)}) collective-permute-start(bf16[64,4096]{1,0:T(8,128)(2,1)} %get-tuple-element.41.refs_2_), channel_id=1, source_target_pairs={{0,8},{4,12},{8,0},{12,4},{16,24},{20,28},{24,16},{28,20},{1,9},{5... | collective-permute-start | bytes 1572872 | tf_op jit(solution)/shard_map/ppermute | solution.py:23
  85.0 15.4 %collective-permute-start.20 = (bf16[64,4096]{1,0:T(8,128)(2,1)}, bf16[64,4096]{1,0:T(8,128)(2,1)S(1)}, u32[]{:S(2)}, u32[]{:S(2)}) collective-permute-start(bf16[64,4096]{1,0:T(8,128)(2,1)} %get-tuple-element.41.refs_2_), channel_id=1, source_target_pairs={{0,16},{4,20},{8,24},{12,28},{16,0},{20,4},{24,8},{28,12},{1,17},{... | collective-permute-start | bytes 1572872 | tf_op jit(solution)/shard_map/ppermute | solution.py:23
  85.5 20.0 %collective-permute-start.10 = (bf16[64,4096]{1,0:T(8,128)(2,1)S(1)}, bf16[64,4096]{1,0:T(8,128)(2,1)S(1)}, u32[]{:S(2)}, u32[]{:S(2)}) collective-permute-start(bf16[64,4096]{1,0:T(8,128)(2,1)S(1)} %copy-done.38), channel_id=1, source_target_pairs={{0,4},{4,0},{8,12},{12,8},{16,20},{20,16},{24,28},{28,24},{1,5},{5... | collective-permute-start | bytes 1572872 | tf_op jit(solution)/shard_map/ppermute | solution.py:23
  90.2 14.8 %collective-permute-start.15 = (bf16[64,2048]{1,0:T(8,128)(2,1)S(1)}, bf16[64,2048]{1,0:T(8,128)(2,1)S(1)}, u32[]{:S(2)}, u32[]{:S(2)}) collective-permute-start(bf16[64,2048]{1,0:T(8,128)(2,1)S(1)} %get-tuple-element.42), channel_id=1, source_target_pairs={{0,16},{4,20},{8,24},{12,28},{16,0},{20,4},{24,8},{28,12},{1,17},{... | collective-permute-start | bytes 786440 | tf_op jit(solution)/shard_map/ppermute | solution.py:23
  92.0 13.1 %collective-permute-start.17 = (bf16[64,2048]{1,0:T(8,128)(2,1)S(1)}, bf16[64,2048]{1,0:T(8,128)(2,1)S(1)}, u32[]{:S(2)}, u32[]{:S(2)}) collective-permute-start(bf16[64,2048]{1,0:T(8,128)(2,1)S(1)} %get-tuple-element.43), channel_id=1, source_target_pairs={{0,8},{4,12},{8,0},{12,4},{16,24},{20,28},{24,16},{28,20},{1,9},{5... | collective-permute-start | bytes 786440 | tf_op jit(solution)/shard_map/ppermute | solution.py:23
  99.2 7.7 %collective-permute-start.12 = (bf16[64,4096]{1,0:T(8,128)(2,1)S(1)}, bf16[64,4096]{1,0:T(8,128)(2,1)S(1)}, u32[]{:S(2)}, u32[]{:S(2)}) collective-permute-start(bf16[64,4096]{1,0:T(8,128)(2,1)S(1)} %collective-permute-done.11.refs_0_.refs_4_.refs_9_), channel_id=1, source_target_pairs={{0,4},{4,0},{8,12},{12,8},{16,20},{20,16},{24,28},{28,24},{1,5},{5... | collective-permute-start | bytes 1572872 | tf_op jit(solution)/shard_map/ppermute | solution.py:23
  100.4 6.5 %collective-permute-start.14 = (bf16[64,4096]{1,0:T(8,128)(2,1)S(1)}, bf16[64,4096]{1,0:T(8,128)(2,1)S(1)}, u32[]{:S(2)}, u32[]{:S(2)}) collective-permute-start(bf16[64,4096]{1,0:T(8,128)(2,1)S(1)} %collective-permute-done.13.refs_1_.refs_6_.refs_10_), channel_id=1, source_target_pairs={{0,4},{4,0},{8,12},{12,8},{16,20},{20,16},{24,28},{28,24},{1,5},{5... | collective-permute-start | bytes 1572872 | tf_op jit(solution)/shard_map/ppermute | solution.py:23
  105.0 1.9 collective-permute-start.18
  115.3 54.0 %reduce-scatter.5.cloned.1.call-start = ((), (), s32[]{:S(2)}) async-start(), calls=%async_computation.3 | async-start | bytes 1310720 | tf_op jit(solution)/shard_map/reduce_scatter | solution.py:877
  115.4 8.4 %collective-permute-start.24 = (bf16[64,2048]{1,0:T(8,128)(2,1)S(1)}, bf16[64,2048]{1,0:T(8,128)(2,1)S(1)}, u32[]{:S(2)}, u32[]{:S(2)}) collective-permute-start(bf16[64,2048]{1,0:T(8,128)(2,1)S(1)} %get-tuple-element.44), channel_id=1, source_target_pairs={{0,16},{4,20},{8,24},{12,28},{16,0},{20,4},{24,8},{28,12},{1,17},{... | collective-permute-start | bytes 786440 | tf_op jit(solution)/shard_map/ppermute | solution.py:23
  117.0 8.1 %collective-permute-start.26 = (bf16[64,2048]{1,0:T(8,128)(2,1)S(1)}, bf16[64,2048]{1,0:T(8,128)(2,1)S(1)}, u32[]{:S(2)}, u32[]{:S(2)}) collective-permute-start(bf16[64,2048]{1,0:T(8,128)(2,1)S(1)} %get-tuple-element.45), channel_id=1, source_target_pairs={{0,8},{4,12},{8,0},{12,4},{16,24},{20,28},{24,16},{28,20},{1,9},{5... | collective-permute-start | bytes 786440 | tf_op jit(solution)/shard_map/ppermute | solution.py:23
  117.8 7.3 %collective-permute-start.21 = (bf16[64,4096]{1,0:T(8,128)(2,1)S(1)}, bf16[64,4096]{1,0:T(8,128)(2,1)S(1)}, u32[]{:S(2)}, u32[]{:S(2)}) collective-permute-start(bf16[64,4096]{1,0:T(8,128)(2,1)S(1)} %copy-done.34), channel_id=1, source_target_pairs={{0,4},{4,0},{8,12},{12,8},{16,20},{20,16},{24,28},{28,24},{1,5},{5... | collective-permute-start | bytes 1572872 | tf_op jit(solution)/shard_map/ppermute | solution.py:23
  117.8 7.3 %collective-permute-start.22 = (bf16[64,4096]{1,0:T(8,128)(2,1)S(1)}, bf16[64,4096]{1,0:T(8,128)(2,1)S(1)}, u32[]{:S(2)}, u32[]{:S(2)}) collective-permute-start(bf16[64,4096]{1,0:T(8,128)(2,1)S(1)} %collective-permute-done.19.refs_12_.refs_0_.refs_4_), channel_id=1, source_target_pairs={{0,4},{4,0},{8,12},{12,8},{16,20},{20,16},{24,28},{28,24},{1,5},{5... | collective-permute-start | bytes 1572872 | tf_op jit(solution)/shard_map/ppermute | solution.py:23
  118.3 6.8 %collective-permute-start.23 = (bf16[64,4096]{1,0:T(8,128)(2,1)S(1)}, bf16[64,4096]{1,0:T(8,128)(2,1)S(1)}, u32[]{:S(2)}, u32[]{:S(2)}) collective-permute-start(bf16[64,4096]{1,0:T(8,128)(2,1)S(1)} %collective-permute-done.20.refs_13_.refs_1_.refs_6_), channel_id=1, source_target_pairs={{0,4},{4,0},{8,12},{12,8},{16,20},{20,16},{24,28},{28,24},{1,5},{5... | collective-permute-start | bytes 1572872 | tf_op jit(solution)/shard_map/ppermute | solution.py:23
  141.6 31.0 %collective-permute-start.30 = (bf16[384,2048]{1,0:T(8,128)(2,1)}, bf16[384,2048]{1,0:T(8,128)(2,1)S(1)}, u32[]{:S(2)}, u32[]{:S(2)}) collective-permute-start(bf16[384,2048]{1,0:T(8,128)(2,1)} %get-tuple-element.48), channel_id=1, source_target_pairs={{0,4},{4,0},{8,12},{12,8},{16,20},{20,16},{24,28},{28,24},{1,5},{5... | collective-permute-start | bytes 4718600 | tf_op jit(solution)/shard_map/ppermute | solution.py:23
  142.3 30.4 %collective-permute-start.28 = (bf16[384,1024]{1,0:T(8,128)(2,1)}, bf16[384,1024]{1,0:T(8,128)(2,1)S(1)}, u32[]{:S(2)}, u32[]{:S(2)}) collective-permute-start(bf16[384,1024]{1,0:T(8,128)(2,1)} %get-tuple-element.46), channel_id=1, source_target_pairs={{0,12},{4,8},{8,4},{12,0},{16,28},{20,24},{24,20},{28,16},{1,13},{... | collective-permute-start | bytes 2359304 | tf_op jit(solution)/shard_map/ppermute | solution.py:23
  143.1 29.6 %collective-permute-start.29 = (bf16[384,1024]{1,0:T(8,128)(2,1)}, bf16[384,1024]{1,0:T(8,128)(2,1)S(1)}, u32[]{:S(2)}, u32[]{:S(2)}) collective-permute-start(bf16[384,1024]{1,0:T(8,128)(2,1)} %get-tuple-element.47), channel_id=1, source_target_pairs={{0,20},{4,16},{8,28},{12,24},{16,4},{20,0},{24,12},{28,8},{1,21},{... | collective-permute-start | bytes 2359304 | tf_op jit(solution)/shard_map/ppermute | solution.py:23
  173.4 11.0 %collective-permute-start.32 = (bf16[192,1024]{1,0:T(8,128)(2,1)S(1)}, bf16[192,1024]{1,0:T(8,128)(2,1)S(1)}, u32[]{:S(2)}, u32[]{:S(2)}) collective-permute-start(bf16[192,1024]{1,0:T(8,128)(2,1)S(1)} %get-tuple-element.49.refs_4_), channel_id=1, source_target_pairs={{0,8},{4,12},{8,0},{12,4},{16,24},{20,28},{24,16},{28,20},{1,9},{5... | collective-permute-start | bytes 1179656 | tf_op jit(solution)/shard_map/ppermute | solution.py:23
  174.9 10.7 %collective-permute-start.34 = (bf16[192,1024]{1,0:T(8,128)(2,1)S(1)}, bf16[192,1024]{1,0:T(8,128)(2,1)S(1)}, u32[]{:S(2)}, u32[]{:S(2)}) collective-permute-start(bf16[192,1024]{1,0:T(8,128)(2,1)S(1)} %get-tuple-element.49.refs_4_), channel_id=1, source_target_pairs={{0,16},{4,20},{8,24},{12,28},{16,0},{20,4},{24,8},{28,12},{1,17},{... | collective-permute-start | bytes 1179656 | tf_op jit(solution)/shard_map/ppermute | solution.py:23
  176.3 17.7 %collective-permute-start.47 = (bf16[192,1024]{1,0:T(8,128)(2,1)S(1)}, bf16[192,1024]{1,0:T(8,128)(2,1)S(1)}, u32[]{:S(2)}, u32[]{:S(2)}) collective-permute-start(bf16[192,1024]{1,0:T(8,128)(2,1)S(1)} %get-tuple-element.55), channel_id=1, source_target_pairs={{0,1},{1,0},{2,3},{3,2},{4,5},{5,4},{6,7},{7,6},{8,9},{9,8},{10,11... | collective-permute-start | bytes 1179656 | tf_op jit(solution)/shard_map/ppermute | solution.py:23
  179.0 27.5 %collective-permute-start.48 = (bf16[192,1024]{1,0:T(8,128)(2,1)S(1)}, bf16[192,1024]{1,0:T(8,128)(2,1)S(1)}, u32[]{:S(2)}, u32[]{:S(2)}) collective-permute-start(bf16[192,1024]{1,0:T(8,128)(2,1)S(1)} %get-tuple-element.56), channel_id=1, source_target_pairs={{0,2},{1,3},{2,0},{3,1},{4,6},{5,7},{6,4},{7,5},{8,10},{9,11},{10,... | collective-permute-start | bytes 1179656 | tf_op jit(solution)/shard_map/ppermute | solution.py:23
  180.0 33.9 %collective-permute-start.49 = (bf16[192,1024]{1,0:T(8,128)(2,1)S(1)}, bf16[192,1024]{1,0:T(8,128)(2,1)S(1)}, u32[]{:S(2)}, u32[]{:S(2)}) collective-permute-start(bf16[192,1024]{1,0:T(8,128)(2,1)S(1)} %get-tuple-element.57), channel_id=1, source_target_pairs={{0,3},{1,2},{2,1},{3,0},{4,7},{5,6},{6,5},{7,4},{8,11},{9,10},{10,... | collective-permute-start | bytes 1179656 | tf_op jit(solution)/shard_map/ppermute | solution.py:23
  184.3 32.8 %collective-permute-start.31 = (bf16[192,1024]{1,0:T(8,128)(2,1)S(1)}, bf16[192,1024]{1,0:T(8,128)(2,1)S(1)}, u32[]{:S(2)}, u32[]{:S(2)}) collective-permute-start(bf16[192,1024]{1,0:T(8,128)(2,1)S(1)} %get-tuple-element.49.refs_4_), channel_id=1, source_target_pairs={{0,4},{4,0},{8,12},{12,8},{16,20},{20,16},{24,28},{28,24},{1,5},{5... | collective-permute-start | bytes 1179656 | tf_op jit(solution)/shard_map/ppermute | solution.py:23
  185.6 28.2 %collective-permute-start.36 = (bf16[96,1024]{1,0:T(8,128)(2,1)S(1)}, bf16[96,1024]{1,0:T(8,128)(2,1)S(1)}, u32[]{:S(2)}, u32[]{:S(2)}) collective-permute-start(bf16[96,1024]{1,0:T(8,128)(2,1)S(1)} %get-tuple-element.50), channel_id=1, source_target_pairs={{0,16},{4,20},{8,24},{12,28},{16,0},{20,4},{24,8},{28,12},{1,17},{... | collective-permute-start | bytes 589832 | tf_op jit(solution)/shard_map/ppermute | solution.py:23
  194.0 19.8 %collective-permute-start.38 = (bf16[96,1024]{1,0:T(8,128)(2,1)S(1)}, bf16[96,1024]{1,0:T(8,128)(2,1)S(1)}, u32[]{:S(2)}, u32[]{:S(2)}) collective-permute-start(bf16[96,1024]{1,0:T(8,128)(2,1)S(1)} %get-tuple-element.51), channel_id=1, source_target_pairs={{0,8},{4,12},{8,0},{12,4},{16,24},{20,28},{24,16},{28,20},{1,9},{5... | collective-permute-start | bytes 589832 | tf_op jit(solution)/shard_map/ppermute | solution.py:23
  215.5 35.0 %collective-permute-start.51 = (bf16[576,1024]{1,0:T(8,128)(2,1)}, bf16[576,1024]{1,0:T(8,128)(2,1)}, u32[]{:S(2)}, u32[]{:S(2)}) collective-permute-start(bf16[576,1024]{1,0:T(8,128)(2,1)} %join.3.refs_4_), channel_id=1, source_target_pairs={{0,8},{4,12},{8,0},{12,4},{16,24},{20,28},{24,16},{28,20},{1,9},{5... | collective-permute-start | bytes 3538952 | tf_op jit(solution)/shard_map/ppermute | solution.py:23
  216.1 34.3 %collective-permute-start.53 = (bf16[576,1024]{1,0:T(8,128)(2,1)}, bf16[576,1024]{1,0:T(8,128)(2,1)}, u32[]{:S(2)}, u32[]{:S(2)}) collective-permute-start(bf16[576,1024]{1,0:T(8,128)(2,1)} %join.3.refs_4_), channel_id=1, source_target_pairs={{0,16},{4,20},{8,24},{12,28},{16,0},{20,4},{24,8},{28,12},{1,17},{... | collective-permute-start | bytes 3538952 | tf_op jit(solution)/shard_map/ppermute | solution.py:23
  216.6 2.9 collective-permute-start.33
  217.1 2.4 collective-permute-start.35
  226.7 18.4 %collective-permute-start.41 = (bf16[192,384]{1,0:T(8,128)(2,1)S(1)}, bf16[192,384]{1,0:T(8,128)(2,1)S(1)}, u32[]{:S(2)}, u32[]{:S(2)}) collective-permute-start(bf16[192,384]{1,0:T(8,128)(2,1)S(1)} %hidden_units.2.refs_1_), channel_id=1, source_target_pairs={{0,8},{4,12},{8,0},{12,4},{16,24},{20,28},{24,16},{28,20},{1,9},{5... | collective-permute-start | bytes 442376 | tf_op jit(solution)/shard_map/ppermute | solution.py:23
  228.2 17.1 %collective-permute-start.43 = (bf16[192,384]{1,0:T(8,128)(2,1)S(1)}, bf16[192,384]{1,0:T(8,128)(2,1)S(1)}, u32[]{:S(2)}, u32[]{:S(2)}) collective-permute-start(bf16[192,384]{1,0:T(8,128)(2,1)S(1)} %hidden_units.2.refs_1_), channel_id=1, source_target_pairs={{0,16},{4,20},{8,24},{12,28},{16,0},{20,4},{24,8},{28,12},{1,17},{... | collective-permute-start | bytes 442376 | tf_op jit(solution)/shard_map/ppermute | solution.py:23
  229.7 15.9 %collective-permute-start.40 = (bf16[192,384]{1,0:T(8,128)(2,1)S(1)}, bf16[192,384]{1,0:T(8,128)(2,1)S(1)}, u32[]{:S(2)}, u32[]{:S(2)}) collective-permute-start(bf16[192,384]{1,0:T(8,128)(2,1)S(1)} %hidden_units.2.refs_1_), channel_id=1, source_target_pairs={{0,4},{4,0},{8,12},{12,8},{16,20},{20,16},{24,28},{28,24},{1,5},{5... | collective-permute-start | bytes 442376 | tf_op jit(solution)/shard_map/ppermute | solution.py:23
  245.5 23.1 %collective-permute-start.50 = (bf16[576,1024]{1,0:T(8,128)(2,1)}, bf16[576,1024]{1,0:T(8,128)(2,1)S(1)}, u32[]{:S(2)}, u32[]{:S(2)}) collective-permute-start(bf16[576,1024]{1,0:T(8,128)(2,1)} %join.3.refs_4_), channel_id=1, source_target_pairs={{0,4},{4,0},{8,12},{12,8},{16,20},{20,16},{24,28},{28,24},{1,5},{5... | collective-permute-start | bytes 3538952 | tf_op jit(solution)/shard_map/ppermute | solution.py:23
  252.3 15.5 %collective-permute-start.55 = (bf16[288,1024]{1,0:T(8,128)(2,1)S(1)}, bf16[288,1024]{1,0:T(8,128)(2,1)S(1)}, u32[]{:S(2)}, u32[]{:S(2)}) collective-permute-start(bf16[288,1024]{1,0:T(8,128)(2,1)S(1)} %get-tuple-element.58), channel_id=1, source_target_pairs={{0,16},{4,20},{8,24},{12,28},{16,0},{20,4},{24,8},{28,12},{1,17},{... | collective-permute-start | bytes 1769480 | tf_op jit(solution)/shard_map/ppermute | solution.py:23
  252.9 16.8 %collective-permute-start.52 = (bf16[576,1024]{1,0:T(8,128)(2,1)}, bf16[576,1024]{1,0:T(8,128)(2,1)S(1)}, u32[]{:S(2)}, u32[]{:S(2)}) collective-permute-start(bf16[576,1024]{1,0:T(8,128)(2,1)} %collective-permute-done.51.refs_0_.refs_6_), channel_id=1, source_target_pairs={{0,4},{4,0},{8,12},{12,8},{16,20},{20,16},{24,28},{28,24},{1,5},{5... | collective-permute-start | bytes 3538952 | tf_op jit(solution)/shard_map/ppermute | solution.py:23
  252.9 16.8 %collective-permute-start.54 = (bf16[576,1024]{1,0:T(8,128)(2,1)}, bf16[576,1024]{1,0:T(8,128)(2,1)S(1)}, u32[]{:S(2)}, u32[]{:S(2)}) collective-permute-start(bf16[576,1024]{1,0:T(8,128)(2,1)} %collective-permute-done.53.refs_1_.refs_8_), channel_id=1, source_target_pairs={{0,4},{4,0},{8,12},{12,8},{16,20},{20,16},{24,28},{28,24},{1,5},{5... | collective-permute-start | bytes 3538952 | tf_op jit(solution)/shard_map/ppermute | solution.py:23
  253.4 15.2 %collective-permute-start.57 = (bf16[288,1024]{1,0:T(8,128)(2,1)S(1)}, bf16[288,1024]{1,0:T(8,128)(2,1)S(1)}, u32[]{:S(2)}, u32[]{:S(2)}) collective-permute-start(bf16[288,1024]{1,0:T(8,128)(2,1)S(1)} %get-tuple-element.59), channel_id=1, source_target_pairs={{0,8},{4,12},{8,0},{12,4},{16,24},{20,28},{24,16},{28,20},{1,9},{5... | collective-permute-start | bytes 1769480 | tf_op jit(solution)/shard_map/ppermute | solution.py:23
  267.8 2.0 collective-permute-start.56
  268.6 2.0 collective-permute-start.58
  287.1 12.3 %collective-permute-start.60 = (bf16[576,384]{1,0:T(8,128)(2,1)S(1)}, bf16[576,384]{1,0:T(8,128)(2,1)S(1)}, u32[]{:S(2)}, u32[]{:S(2)}) collective-permute-start(bf16[576,384]{1,0:T(8,128)(2,1)S(1)} %hidden_units.3.refs_1_), channel_id=1, source_target_pairs={{0,8},{4,12},{8,0},{12,4},{16,24},{20,28},{24,16},{28,20},{1,9},{5... | collective-permute-start | bytes 1327112 | tf_op jit(solution)/shard_map/ppermute | solution.py:23
  288.7 11.9 %collective-permute-start.62 = (bf16[576,384]{1,0:T(8,128)(2,1)S(1)}, bf16[576,384]{1,0:T(8,128)(2,1)S(1)}, u32[]{:S(2)}, u32[]{:S(2)}) collective-permute-start(bf16[576,384]{1,0:T(8,128)(2,1)S(1)} %hidden_units.3.refs_1_), channel_id=1, source_target_pairs={{0,16},{4,20},{8,24},{12,28},{16,0},{20,4},{24,8},{28,12},{1,17},{... | collective-permute-start | bytes 1327112 | tf_op jit(solution)/shard_map/ppermute | solution.py:23
  290.2 10.5 %collective-permute-start.59 = (bf16[576,384]{1,0:T(8,128)(2,1)S(1)}, bf16[576,384]{1,0:T(8,128)(2,1)S(1)}, u32[]{:S(2)}, u32[]{:S(2)}) collective-permute-start(bf16[576,384]{1,0:T(8,128)(2,1)S(1)} %hidden_units.3.refs_1_), channel_id=1, source_target_pairs={{0,4},{4,0},{8,12},{12,8},{16,20},{20,16},{24,28},{28,24},{1,5},{5... | collective-permute-start | bytes 1327112 | tf_op jit(solution)/shard_map/ppermute | solution.py:23
  299.3 1.8 collective-permute-start.61
  300.6 1.8 collective-permute-start.63
  308.6 15.4 %collective-permute-start.64 = (bf16[576,512]{1,0:T(8,128)(2,1)S(1)}, bf16[576,512]{1,0:T(8,128)(2,1)S(1)}, u32[]{:S(2)}, u32[]{:S(2)}) collective-permute-start(bf16[576,512]{1,0:T(8,128)(2,1)S(1)} %get-tuple-element.61), channel_id=1, source_target_pairs={{0,16},{4,20},{8,24},{12,28},{16,0},{20,4},{24,8},{28,12},{1,17},{... | collective-permute-start | bytes 1769480 | tf_op jit(solution)/shard_map/ppermute | solution.py:23
  310.2 15.1 %collective-permute-start.65 = (bf16[576,512]{1,0:T(8,128)(2,1)S(1)}, bf16[576,512]{1,0:T(8,128)(2,1)S(1)}, u32[]{:S(2)}, u32[]{:S(2)}) collective-permute-start(bf16[576,512]{1,0:T(8,128)(2,1)S(1)} %get-tuple-element.62), channel_id=1, source_target_pairs={{0,8},{4,12},{8,0},{12,4},{16,24},{20,28},{24,16},{28,20},{1,9},{5... | collective-permute-start | bytes 1769480 | tf_op jit(solution)/shard_map/ppermute | solution.py:23
  326.4 15.3 %collective-permute-start.66 = (bf16[192,1024]{1,0:T(8,128)(2,1)}, bf16[192,1024]{1,0:T(8,128)(2,1)S(1)}, u32[]{:S(2)}, u32[]{:S(2)}) collective-permute-start(bf16[192,1024]{1,0:T(8,128)(2,1)} %get-tuple-element.63), channel_id=1, source_target_pairs={{0,1},{1,0},{2,3},{3,2},{4,5},{5,4},{6,7},{7,6},{8,9},{9,8},{10,11... | collective-permute-start | bytes 1179656 | tf_op jit(solution)/shard_map/ppermute | solution.py:23
  326.5 29.6 %collective-permute-start.67 = (bf16[192,1024]{1,0:T(8,128)(2,1)}, bf16[192,1024]{1,0:T(8,128)(2,1)}, u32[]{:S(2)}, u32[]{:S(2)}) collective-permute-start(bf16[192,1024]{1,0:T(8,128)(2,1)} %get-tuple-element.64), channel_id=1, source_target_pairs={{0,2},{1,3},{2,0},{3,1},{4,6},{5,7},{6,4},{7,5},{8,10},{9,11},{10,... | collective-permute-start | bytes 1179656 | tf_op jit(solution)/shard_map/ppermute | solution.py:23
  329.4 33.9 %collective-permute-start.68 = (bf16[192,1024]{1,0:T(8,128)(2,1)}, bf16[192,1024]{1,0:T(8,128)(2,1)}, u32[]{:S(2)}, u32[]{:S(2)}) collective-permute-start(bf16[192,1024]{1,0:T(8,128)(2,1)} %get-tuple-element.65), channel_id=1, source_target_pairs={{0,3},{1,2},{2,1},{3,0},{4,7},{5,6},{6,5},{7,4},{8,11},{9,10},{10,... | collective-permute-start | bytes 1179656 | tf_op jit(solution)/shard_map/ppermute | solution.py:23
  330.0 5.9 %collective-permute-start.45 = (bf16[192,512]{1,0:T(8,128)(2,1)}, bf16[192,512]{1,0:T(8,128)(2,1)S(1)}, u32[]{:S(2)}, u32[]{:S(2)}) collective-permute-start(bf16[192,512]{1,0:T(8,128)(2,1)} %get-tuple-element.53), channel_id=1, source_target_pairs={{0,16},{4,20},{8,24},{12,28},{16,0},{20,4},{24,8},{28,12},{1,17},{... | collective-permute-start | bytes 589832 | tf_op jit(solution)/shard_map/ppermute | solution.py:23
  330.5 6.0 %collective-permute-start.46 = (bf16[192,512]{1,0:T(8,128)(2,1)}, bf16[192,512]{1,0:T(8,128)(2,1)}, u32[]{:S(2)}, u32[]{:S(2)}) collective-permute-start(bf16[192,512]{1,0:T(8,128)(2,1)} %get-tuple-element.54), channel_id=1, source_target_pairs={{0,8},{4,12},{8,0},{12,4},{16,24},{20,28},{24,16},{28,20},{1,9},{5... | collective-permute-start | bytes 589832 | tf_op jit(solution)/shard_map/ppermute | solution.py:23
  (56 other events, 1155.9 us)
Sparse Core Ops, SparseCore 0:
  115.4 25.5 reduce-scatter.2
  143.4 25.8 reduce-scatter.4

commit v7 on v6

--- a/solution.py
+++ b/solution.py
@@ -827,7 +827,7 @@
             down_parts[mask] = swap(cut, "ctx", mask)
         return tuple(down_parts[mask] for mask in masks)
 
-    early = send_columns([2, 4])
+    early = send_columns([2, 4], [rim_rows])
 
     extra, left = [], norm_gain
     for _ in range(3):
@@ -908,27 +908,29 @@
     sent = pick_rows(picked, scaled, late)
     pieces = [rows if mask == 0 else swap(rows, "exp", mask) for mask, rows in enumerate(sent)]
     weights = [None] + [down_parts[mask] for mask in sorted(down_parts)]
-    settled, arrived, order = [], (), ()
+    settled, arrived, order, first_units, keeps = [], (), (), (), ()
     for group in groups:
         rows = [pieces[mask] for mask in group]
         rows = join(rows, arrived) if len(group) > 1 else rows[0]
         parts = gather_parts(rows, 0, order)
         arrived = far(parts)
-        hidden = hidden_units(me, [parts], one_over_gain, expert_gate[0], expert_up[0])
+        hidden = hidden_units(me, [parts], one_over_gain, expert_gate[0], expert_up[0], first_units)
+        order = [hidden]
         if crossing:
             units = {0: hidden, 2: swap(hidden, "ctx", 2), 4: swap(hidden, "ctx", 4)}
             units.update({mask + 1: swap(units[mask], "ctx", 1) for mask in (0, 2, 4)})
-            keep, first, second = cross_down(me, units, weights, down_rows)
-            order = [keep]
+            first_units = [units[2], units[4]]
+            keep, first, second = cross_down(me, units, weights, down_rows, keeps)
+            keeps = [keep]
             settled.append((keep, swap(first, "ctx", 4), swap(second, "ctx", 2)))
         else:
-            answer = down(me, gather_parts(hidden), weights, down_rows)
-            order = [answer]
+            answer = down(me, gather_parts(hidden), weights, down_rows, keeps)
+            keeps = [answer]
             settled.append([answer])
     answers = {}
     for group, sums in zip(groups, settled):
         if crossing:
-            pieces = settle(*sums, len(group), order)
+            pieces = settle(*sums, len(group), keeps)
         else:
             pieces = jnp.split(sums[0], len(group))
         for mask, piece in zip(group, pieces):

time: 374 us -> 361 us (0.965)
  starting transfers between devices: 59.8 us -> 50.8 us
    ppermute x68, starting transfers between devices: 58.4 us -> 49 us  [swap(): lax.ppermute(array, axis, [(i, i ^ mask) for i in range(lax.axis_size(axi...]
  transfers between devices with their start and end apart: 71 -> 71, of which waited for: 42 -> 43; matrix products, arithmetic and copies ran while one was open for 3% -> 3% of each run, Pallas kernels for 14% -> 13%
where the time goes in v7:
time: 361 us
  waiting for transfers between devices  182 us (50%)
  Pallas kernels  96.1 us (27%)
  starting transfers between devices  50.8 us (14%)
  between operations  14.8 us (4%)
  local copies, waits for them, and re-layouts  9.12 us (3%)
  other arithmetic  8.15 us (2%)
    ppermute x68, waiting for transfers between devices, swap(): lax.ppermute(array, axis, [(i, i ^ mask) for i in range(lax.axis_size(axi...  156 us
    pallas_call x22, Pallas kernels, launch(): pl.pallas_call(body, grid_spec=pltpu.PrefetchScalarGridSpec(num_scalar_pr...  96.1 us
    ppermute x68, starting transfers between devices, swap(): lax.ppermute(array, axis, [(i, i ^ mask) for i in range(lax.axis_size(axi...  49 us
    reduce_scatter x2, waiting for transfers between devices, shards(): lax.psum_scatter(rows, 'exp', scatter_dimension=0, tiled=True)  24.4 us
  transfers between devices with their start and end apart: 71, of which 43 were waited for; matrix products, arithmetic and copies ran while one was open for 3% of the time, Pallas kernels for 13%

profile of v7, /device:TPU:8, one launch (start us, length us, event | category | flops | bytes accessed | tf_op | source)
XLA Modules:
  0.0 360.6 jit_solution(5338560175761629811)
XLA Ops:
  8.1 1.7 collective-permute-start
  10.7 1.4 select_convert_fusion.refs_5_
  12.1 3.5 cut_columns.2
  15.6 3.4 collective-permute-start.1
  19.0 1.5 collective-permute-start.2
  22.0 1.3 broadcast_in_dim.20.refs_8_.refs_6_
  23.3 13.9 %local_states.1 = (f32[128,4096]{1,0:T(8,128)}, f32[128,4096]{1,0:T(8,128)}, bf16[32,4096]{1,0:T(8,128)(2,1)}) custom-call(bf16[128,4096]{1,0:T(8,128)(2,1)} %refs_0_.1, f32[8,4096]{1,0:T(8,128)} %pad.8.refs_1_, bf16[128,4096]{1,0:T(8,128)(2,1)} %refs_2_.2, f32[4,4096]{1,0:T(4,128)} %refs_3_.4, f32[1,4096]{1,0:T(1,128)} %bitcast.66, f32[1,4096]{1,0:T(1,128)} %bitcast.67, ...), custom_call_target="tpu_custom_call" | custom-call | flops 41943040 | bytes 6291456 | tf_op jit(solution)/shard_map/local_states/pallas_call | solution.py:95
  40.9 1.4 collective-permute-start.8
  42.3 5.6 %collective-permute-done.4.refs_11_.refs_3_ = bf16[32,4096]{1,0:T(8,128)(2,1)S(1)} collective-permute-done((bf16[32,4096]{1,0:T(8,128)(2,1)S(1)}, bf16[32,4096]{1,0:T(8,128)(2,1)S(1)}, u32[]{:S(2)}, u32[]{:S(2)}) %collective-permute-start.4) | collective-permute-done | bytes 262176 | tf_op jit(solution)/shard_map/ppermute | solution.py:23
  48.0 3.6 collective-permute-done.6.refs_13_.refs_5_
  53.6 1.3 broadcast_in_dim.23.refs_7_
  55.0 9.2 %read_out.2 = (bf16[64,4096]{1,0:T(8,128)(2,1)}, f32[16,4096]{1,0:T(8,128)}) custom-call(s32[1]{0:T(128)} %bitcast.refs_0_, f32[128,4096]{1,0:T(8,128)} %get-tuple-element.34.refs_1_, f32[128,4096]{1,0:T(8,128)} %get-tuple-element.35.refs_2_, bf16[128,4096]{1,0:T(8,128)(2,1)} %refs_3_.6, f32[16,4096]{1,0:T(8,128)} %refs_4_.3, f32[1,4096]{1,0:T(1,128)} %bitcast.61, ...), custom_call_target="tpu_custom_call" | custom-call | flops 29360128 | bytes 3145728 | tf_op jit(solution)/shard_map/read_out/pallas_call | solution.py:95
  65.9 8.3 %read_out.3 = (bf16[64,4096]{1,0:T(8,128)(2,1)}, f32[16,4096]{1,0:T(8,128)}) custom-call(s32[1]{0:T(128)} %bitcast.refs_0_, f32[128,4096]{1,0:T(8,128)} %get-tuple-element.34.refs_1_, f32[128,4096]{1,0:T(8,128)} %get-tuple-element.35.refs_2_, bf16[128,4096]{1,0:T(8,128)(2,1)} %refs_3_.6, f32[16,4096]{1,0:T(8,128)} %refs_4_.3, f32[1,4096]{1,0:T(1,128)} %bitcast.62, ...), custom_call_target="tpu_custom_call" | custom-call | flops 29360128 | bytes 3145728 | tf_op jit(solution)/shard_map/read_out/pallas_call | solution.py:95
  74.3 1.3 collective-permute-start.19
  76.6 2.5 collective-permute-done.11.refs_0_.refs_4_.refs_9_
  82.0 1.3 collective-permute-start.17
  83.3 7.1 %collective-permute-done.19.refs_12_.refs_0_.refs_4_ = bf16[64,4096]{1,0:T(8,128)(2,1)S(1)} collective-permute-done((bf16[64,4096]{1,0:T(8,128)(2,1)}, bf16[64,4096]{1,0:T(8,128)(2,1)S(1)}, u32[]{:S(2)}, u32[]{:S(2)}) %collective-permute-start.19) | collective-permute-done | bytes 524320 | tf_op jit(solution)/shard_map/ppermute | solution.py:23
  91.4 4.5 %collective-permute-done.15.refs_8_.refs_2_ = bf16[64,2048]{1,0:T(8,128)(2,1)S(1)} collective-permute-done((bf16[64,2048]{1,0:T(8,128)(2,1)S(1)}, bf16[64,2048]{1,0:T(8,128)(2,1)S(1)}, u32[]{:S(2)}, u32[]{:S(2)}) %collective-permute-start.15) | collective-permute-done | bytes 262176 | tf_op jit(solution)/shard_map/ppermute | solution.py:23
  97.8 8.3 %project.2.refs_12_ = bf16[512,1024]{1,0:T(8,128)(2,1)} custom-call(s32[1]{0:T(128)} %bitcast.refs_0_, bf16[4096,1024]{1,0:T(8,128)(2,1)} %refs_1_.3, bf16[64,4096]{1,0:T(8,128)(2,1)S(1)} %copy-done.36, bf16[64,4096]{1,0:T(8,128)(2,1)S(1)} %collective-permute-done.10.refs_3_, bf16[64,4096]{1,0:T(8,128)(2,1)S(1)} %collective-permute-done.11.refs_0_.refs_4_.refs_9_, ...), custom_call_target="tpu_custom_call" | custom-call | flops 4294967296 | bytes 13631488 | tf_op jit(solution)/shard_map/project/pallas_call | solution.py:95
  107.2 1.2 collective-permute-start.26
  108.9 5.8 %collective-permute-done.24.refs_8_ = bf16[64,2048]{1,0:T(8,128)(2,1)S(1)} collective-permute-done((bf16[64,2048]{1,0:T(8,128)(2,1)S(1)}, bf16[64,2048]{1,0:T(8,128)(2,1)S(1)}, u32[]{:S(2)}, u32[]{:S(2)}) %collective-permute-start.24) | collective-permute-done | bytes 262176 | tf_op jit(solution)/shard_map/ppermute | solution.py:23
  116.8 8.4 %project.3 = bf16[512,1024]{1,0:T(8,128)(2,1)} custom-call(s32[1]{0:T(128)} %bitcast.refs_0_, bf16[4096,1024]{1,0:T(8,128)(2,1)} %refs_1_.3, bf16[64,4096]{1,0:T(8,128)(2,1)S(1)} %copy-done.32, bf16[64,4096]{1,0:T(8,128)(2,1)S(1)} %collective-permute-done.21.refs_3_, bf16[64,4096]{1,0:T(8,128)(2,1)S(1)} %collective-permute-done.19.refs_12_.refs_0_.refs_4_, ...), custom_call_target="tpu_custom_call" | custom-call | flops 4294967296 | bytes 13631488 | tf_op jit(solution)/shard_map/project/pallas_call | solution.py:95
  127.3 4.5 %cut_columns.3 = (bf16[384,1024]{1,0:T(8,128)(2,1)}, bf16[384,1024]{1,0:T(8,128)(2,1)}, bf16[384,2048]{1,0:T(8,128)(2,1)}) custom-call(s32[1]{0:T(128)} %bitcast.refs_0_, bf16[384,8192]{1,0:T(8,128)(2,1)} %bitcast.41, bf16[384,8192]{1,0:T(8,128)(2,1)} %bitcast.42, bf16[384,8192]{1,0:T(8,128)(2,1)} %bitcast.43, bf16[384,8192]{1,0:T(8,128)(2,1)} %bitcast.44, ...), custom_call_target="tpu_custom_call" | custom-call | bytes 6291456 | tf_op jit(solution)/shard_map/cut_columns/pallas_call | solution.py:95
  132.4 1.3 collective-permute-start.28
  135.4 24.4 %reduce-scatter.5.cloned.1.call-done = bf16[128,1024]{1,0:T(8,128)(2,1)} async-done(((bf16[512,1024]{1,0:T(8,128)(2,1)}), bf16[128,1024]{1,0:T(8,128)(2,1)}) %reduce-scatter.5.cloned.1.call-update) | async-done | bytes 262160 | tf_op jit(solution)/shard_map/reduce_scatter | solution.py:877
  160.9 2.3 multiply_convert_fusion
  163.9 1.5 collective-permute-start.32
  165.4 1.5 collective-permute-start.34
  166.9 2.6 collective-permute-start.47
  171.0 3.9 %collective-permute-done.32.refs_0_.refs_6_ = bf16[192,1024]{1,0:T(8,128)(2,1)S(1)} collective-permute-done((bf16[192,1024]{1,0:T(8,128)(2,1)S(1)}, bf16[192,1024]{1,0:T(8,128)(2,1)S(1)}, u32[]{:S(2)}, u32[]{:S(2)}) %collective-permute-start.32) | collective-permute-done | bytes 393248 | tf_op jit(solution)/shard_map/ppermute | solution.py:23
  176.2 1.6 collective-permute-start.36
  178.3 6.3 %collective-permute-done.47.refs_0_ = bf16[192,1024]{1,0:T(8,128)(2,1)S(1)} collective-permute-done((bf16[192,1024]{1,0:T(8,128)(2,1)S(1)}, bf16[192,1024]{1,0:T(8,128)(2,1)S(1)}, u32[]{:S(2)}, u32[]{:S(2)}) %collective-permute-start.47) | collective-permute-done | bytes 393248 | tf_op jit(solution)/shard_map/ppermute | solution.py:23
  184.6 12.4 %collective-permute-done.48.refs_1_ = bf16[192,1024]{1,0:T(8,128)(2,1)S(1)} collective-permute-done((bf16[192,1024]{1,0:T(8,128)(2,1)S(1)}, bf16[192,1024]{1,0:T(8,128)(2,1)S(1)}, u32[]{:S(2)}, u32[]{:S(2)}) %collective-permute-start.48) | collective-permute-done | bytes 393248 | tf_op jit(solution)/shard_map/ppermute | solution.py:23
  197.0 7.4 %collective-permute-done.49.refs_2_ = bf16[192,1024]{1,0:T(8,128)(2,1)S(1)} collective-permute-done((bf16[192,1024]{1,0:T(8,128)(2,1)S(1)}, bf16[192,1024]{1,0:T(8,128)(2,1)S(1)}, u32[]{:S(2)}, u32[]{:S(2)}) %collective-permute-start.49) | collective-permute-done | bytes 393248 | tf_op jit(solution)/shard_map/ppermute | solution.py:23
  204.4 1.6 join.3.refs_4_
  207.7 1.2 collective-permute-done.31.refs_5_
  211.0 6.8 %hidden_units.2.refs_1_.refs_2_ = bf16[192,384]{1,0:T(8,128)(2,1)S(1)} custom-call(s32[1]{0:T(128)} %bitcast.refs_0_, f32[8,1,1024]{2,1,0:T(1,128)S(1)} %inverse_gains.1.refs_1_, bf16[8192,384]{1,0:T(8,128)(2,1)S(1)} %bitcast.56, bf16[8192,384]{1,0:T(8,128)(2,1)} %bitcast.57, bf16[192,1024]{1,0:T(8,128)(2,1)S(1)} %get-tuple-element.49.refs_4_, ...), custom_call_target="tpu_custom_call" | custom-call | flops 2415919104 | bytes 15728640 | tf_op jit(solution)/shard_map/hidden_units/pallas_call | solution.py:95
  217.8 1.5 collective-permute-start.41
  219.3 1.5 collective-permute-start.43
  220.8 13.2 %collective-permute-done.51.refs_0_.refs_6_ = bf16[576,1024]{1,0:T(8,128)(2,1)S(1)} collective-permute-done((bf16[576,1024]{1,0:T(8,128)(2,1)}, bf16[576,1024]{1,0:T(8,128)(2,1)S(1)}, u32[]{:S(2)}, u32[]{:S(2)}) %collective-permute-start.51) | collective-permute-done | bytes 1179680 | tf_op jit(solution)/shard_map/ppermute | solution.py:23
  234.0 1.7 collective-permute-done.53.refs_1_.refs_8_
  237.0 2.0 collective-permute-done.43.refs_5_.refs_15_
  238.9 1.6 collective-permute-start.57
  240.5 8.0 %collective-permute-done.55.refs_10_ = bf16[288,1024]{1,0:T(8,128)(2,1)S(1)} collective-permute-done((bf16[288,1024]{1,0:T(8,128)(2,1)S(1)}, bf16[288,1024]{1,0:T(8,128)(2,1)S(1)}, u32[]{:S(2)}, u32[]{:S(2)}) %collective-permute-start.55) | collective-permute-done | bytes 589856 | tf_op jit(solution)/shard_map/ppermute | solution.py:23
  248.5 3.8 %collective-permute-done.57.refs_12_ = bf16[288,1024]{1,0:T(8,128)(2,1)S(1)} collective-permute-done((bf16[288,1024]{1,0:T(8,128)(2,1)S(1)}, bf16[288,1024]{1,0:T(8,128)(2,1)S(1)}, u32[]{:S(2)}, u32[]{:S(2)}) %collective-permute-start.57) | collective-permute-done | bytes 589856 | tf_op jit(solution)/shard_map/ppermute | solution.py:23
  252.4 2.0 collective-permute-done.58.refs_13_
  254.3 15.1 %hidden_units.3.refs_1_ = bf16[576,384]{1,0:T(8,128)(2,1)S(1)} custom-call(s32[1]{0:T(128)} %bitcast.refs_0_, f32[8,1,1024]{2,1,0:T(1,128)S(1)} %inverse_gains.1.refs_1_, bf16[8192,384]{1,0:T(8,128)(2,1)} %bitcast.53, bf16[8192,384]{1,0:T(8,128)(2,1)} %bitcast.58, bf16[576,1024]{1,0:T(8,128)(2,1)} %join.3.refs_4_, ...), custom_call_target="tpu_custom_call" | custom-call | flops 7247757312 | bytes 22020096 | tf_op jit(solution)/shard_map/hidden_units/pallas_call | solution.py:95
  269.4 1.5 collective-permute-start.60
  271.0 1.5 collective-permute-start.62
  273.0 8.7 %collective-permute-done.60.refs_3_ = bf16[576,384]{1,0:T(8,128)(2,1)S(1)} collective-permute-done((bf16[576,384]{1,0:T(8,128)(2,1)S(1)}, bf16[576,384]{1,0:T(8,128)(2,1)S(1)}, u32[]{:S(2)}, u32[]{:S(2)}) %collective-permute-start.60) | collective-permute-done | bytes 442400 | tf_op jit(solution)/shard_map/ppermute | solution.py:23
  281.7 1.2 collective-permute-done.62.refs_5_
  283.4 1.5 collective-permute-done.42.refs_4_
  285.2 3.7 %cross_down.2 = (bf16[192,1024]{1,0:T(8,128)(2,1)S(1)}, bf16[192,512]{1,0:T(8,128)(2,1)}, bf16[192,512]{1,0:T(8,128)(2,1)}) custom-call(s32[1]{0:T(128)} %bitcast.refs_0_, bf16[192,384]{1,0:T(8,128)(2,1)S(1)} %hidden_units.2.refs_1_.refs_2_, bf16[192,384]{1,0:T(8,128)(2,1)S(1)} %collective-permute-done.40.refs_2_, ...), custom_call_target="tpu_custom_call" | custom-call | flops 2415919104 | bytes 9437184 | tf_op jit(solution)/shard_map/cross_down/pallas_call | solution.py:95
  288.9 1.2 copy-done.1
  290.1 6.2 %cross_down.3 = (bf16[576,1024]{1,0:T(8,128)(2,1)S(1)}, bf16[576,512]{1,0:T(8,128)(2,1)S(1)}, bf16[576,512]{1,0:T(8,128)(2,1)S(1)}) custom-call(s32[1]{0:T(128)} %bitcast.refs_0_, bf16[576,384]{1,0:T(8,128)(2,1)S(1)} %hidden_units.3.refs_1_, bf16[576,384]{1,0:T(8,128)(2,1)S(1)} %collective-permute-done.59.refs_2_, ...), custom_call_target="tpu_custom_call" | custom-call | flops 7247757312 | bytes 9437184 | tf_op jit(solution)/shard_map/cross_down/pallas_call | solution.py:95
  296.4 1.6 collective-permute-start.64
  298.9 12.9 %collective-permute-done.64.refs_1_ = bf16[576,512]{1,0:T(8,128)(2,1)S(1)} collective-permute-done((bf16[576,512]{1,0:T(8,128)(2,1)S(1)}, bf16[576,512]{1,0:T(8,128)(2,1)S(1)}, u32[]{:S(2)}, u32[]{:S(2)}) %collective-permute-start.64) | collective-permute-done | bytes 589856 | tf_op jit(solution)/shard_map/ppermute | solution.py:23
  311.8 1.2 collective-permute-done.65.refs_2_
  314.3 3.0 collective-permute-start.67
  319.5 4.1 %collective-permute-done.45.refs_1_ = bf16[192,512]{1,0:T(8,128)(2,1)S(1)} collective-permute-done((bf16[192,512]{1,0:T(8,128)(2,1)}, bf16[192,512]{1,0:T(8,128)(2,1)S(1)}, u32[]{:S(2)}, u32[]{:S(2)}) %collective-permute-start.45) | collective-permute-done | bytes 196640 | tf_op jit(solution)/shard_map/ppermute | solution.py:23
  325.3 4.3 %collective-permute-done.66.refs_9_ = bf16[192,1024]{1,0:T(8,128)(2,1)S(1)} collective-permute-done((bf16[192,1024]{1,0:T(8,128)(2,1)}, bf16[192,1024]{1,0:T(8,128)(2,1)S(1)}, u32[]{:S(2)}, u32[]{:S(2)}) %collective-permute-start.66) | collective-permute-done | bytes 393248 | tf_op jit(solution)/shard_map/ppermute | solution.py:23
  329.5 14.4 %collective-permute-done.67.refs_10_ = bf16[192,1024]{1,0:T(8,128)(2,1)} collective-permute-done((bf16[192,1024]{1,0:T(8,128)(2,1)}, bf16[192,1024]{1,0:T(8,128)(2,1)}, u32[]{:S(2)}, u32[]{:S(2)}) %collective-permute-start.67) | collective-permute-done | bytes 393248 | tf_op jit(solution)/shard_map/ppermute | solution.py:23
  344.0 7.1 %collective-permute-done.68.refs_11_ = bf16[192,1024]{1,0:T(8,128)(2,1)} collective-permute-done((bf16[192,1024]{1,0:T(8,128)(2,1)}, bf16[192,1024]{1,0:T(8,128)(2,1)}, u32[]{:S(2)}, u32[]{:S(2)}) %collective-permute-start.68) | collective-permute-done | bytes 393248 | tf_op jit(solution)/shard_map/ppermute | solution.py:23
  351.1 2.7 combine.1
  (240 shorter events, 42.8 us)
Async XLA Ops:
  7.2 128.3 %reduce-scatter.3.cloned.1.call-start = ((), (), s32[]{:S(2)}) async-start(), calls=%async_computation.2 | async-start | bytes 1310720 | tf_op jit(solution)/shard_map/reduce_scatter | solution.py:877
  8.1 2.6 collective-permute-start
  15.6 21.6 %collective-permute-start.1 = (bf16[384,1024]{1,0:T(8,128)(2,1)}, bf16[384,1024]{1,0:T(8,128)(2,1)S(1)}, u32[]{:S(2)}, u32[]{:S(2)}) collective-permute-start(bf16[384,1024]{1,0:T(8,128)(2,1)} %get-tuple-element.37), channel_id=1, source_target_pairs={{0,8},{4,12},{8,0},{12,4},{16,24},{20,28},{24,16},{28,20},{1,9},{5... | collective-permute-start | bytes 2359304 | tf_op jit(solution)/shard_map/ppermute | solution.py:23
  19.0 18.7 %collective-permute-start.2 = (bf16[384,1024]{1,0:T(8,128)(2,1)}, bf16[384,1024]{1,0:T(8,128)(2,1)S(1)}, u32[]{:S(2)}, u32[]{:S(2)}) collective-permute-start(bf16[384,1024]{1,0:T(8,128)(2,1)} %get-tuple-element.38), channel_id=1, source_target_pairs={{0,16},{4,20},{8,24},{12,28},{16,0},{20,4},{24,8},{28,12},{1,17},{... | collective-permute-start | bytes 2359304 | tf_op jit(solution)/shard_map/ppermute | solution.py:23
  38.8 9.2 %collective-permute-start.4 = (bf16[32,4096]{1,0:T(8,128)(2,1)S(1)}, bf16[32,4096]{1,0:T(8,128)(2,1)S(1)}, u32[]{:S(2)}, u32[]{:S(2)}) collective-permute-start(bf16[32,4096]{1,0:T(8,128)(2,1)S(1)} %join.2.refs_9_.refs_1_), channel_id=1, source_target_pairs={{0,8},{4,12},{8,0},{12,4},{16,24},{20,28},{24,16},{28,20},{1,9},{5... | collective-permute-start | bytes 786440 | tf_op jit(solution)/shard_map/ppermute | solution.py:23
  39.9 11.6 %collective-permute-start.6 = (bf16[32,4096]{1,0:T(8,128)(2,1)S(1)}, bf16[32,4096]{1,0:T(8,128)(2,1)S(1)}, u32[]{:S(2)}, u32[]{:S(2)}) collective-permute-start(bf16[32,4096]{1,0:T(8,128)(2,1)S(1)} %join.2.refs_9_.refs_1_), channel_id=1, source_target_pairs={{0,16},{4,20},{8,24},{12,28},{16,0},{20,4},{24,8},{28,12},{1,17},{... | collective-permute-start | bytes 786440 | tf_op jit(solution)/shard_map/ppermute | solution.py:23
  40.9 10.7 %collective-permute-start.8 = (bf16[32,4096]{1,0:T(8,128)(2,1)S(1)}, bf16[32,4096]{1,0:T(8,128)(2,1)S(1)}, u32[]{:S(2)}, u32[]{:S(2)}) collective-permute-start(bf16[32,4096]{1,0:T(8,128)(2,1)S(1)} %join.2.refs_9_.refs_1_), channel_id=1, source_target_pairs={{0,24},{4,28},{8,16},{12,20},{16,8},{20,12},{24,0},{28,4},{1,25},{... | collective-permute-start | bytes 786440 | tf_op jit(solution)/shard_map/ppermute | solution.py:23
  42.3 9.9 %collective-permute-start.3 = (bf16[32,4096]{1,0:T(8,128)(2,1)S(1)}, bf16[32,4096]{1,0:T(8,128)(2,1)S(1)}, u32[]{:S(2)}, u32[]{:S(2)}) collective-permute-start(bf16[32,4096]{1,0:T(8,128)(2,1)S(1)} %join.2.refs_9_.refs_1_), channel_id=1, source_target_pairs={{0,4},{4,0},{8,12},{12,8},{16,20},{20,16},{24,28},{28,24},{1,5},{5... | collective-permute-start | bytes 786440 | tf_op jit(solution)/shard_map/ppermute | solution.py:23
  48.0 4.3 %collective-permute-start.5 = (bf16[32,4096]{1,0:T(8,128)(2,1)S(1)}, bf16[32,4096]{1,0:T(8,128)(2,1)S(1)}, u32[]{:S(2)}, u32[]{:S(2)}) collective-permute-start(bf16[32,4096]{1,0:T(8,128)(2,1)S(1)} %collective-permute-done.4.refs_11_.refs_3_), channel_id=1, source_target_pairs={{0,4},{4,0},{8,12},{12,8},{16,20},{20,16},{24,28},{28,24},{1,5},{5... | collective-permute-start | bytes 786440 | tf_op jit(solution)/shard_map/ppermute | solution.py:23
  51.6 2.0 collective-permute-start.9
  64.1 15.0 %collective-permute-start.11 = (bf16[64,4096]{1,0:T(8,128)(2,1)}, bf16[64,4096]{1,0:T(8,128)(2,1)S(1)}, u32[]{:S(2)}, u32[]{:S(2)}) collective-permute-start(bf16[64,4096]{1,0:T(8,128)(2,1)} %get-tuple-element.39.refs_2_), channel_id=1, source_target_pairs={{0,8},{4,12},{8,0},{12,4},{16,24},{20,28},{24,16},{28,20},{1,9},{5... | collective-permute-start | bytes 1572872 | tf_op jit(solution)/shard_map/ppermute | solution.py:23
  65.1 15.0 %collective-permute-start.13 = (bf16[64,4096]{1,0:T(8,128)(2,1)}, bf16[64,4096]{1,0:T(8,128)(2,1)S(1)}, u32[]{:S(2)}, u32[]{:S(2)}) collective-permute-start(bf16[64,4096]{1,0:T(8,128)(2,1)} %get-tuple-element.39.refs_2_), channel_id=1, source_target_pairs={{0,16},{4,20},{8,24},{12,28},{16,0},{20,4},{24,8},{28,12},{1,17},{... | collective-permute-start | bytes 1572872 | tf_op jit(solution)/shard_map/ppermute | solution.py:23
  74.3 16.1 %collective-permute-start.19 = (bf16[64,4096]{1,0:T(8,128)(2,1)}, bf16[64,4096]{1,0:T(8,128)(2,1)S(1)}, u32[]{:S(2)}, u32[]{:S(2)}) collective-permute-start(bf16[64,4096]{1,0:T(8,128)(2,1)} %get-tuple-element.41.refs_2_), channel_id=1, source_target_pairs={{0,8},{4,12},{8,0},{12,4},{16,24},{20,28},{24,16},{28,20},{1,9},{5... | collective-permute-start | bytes 1572872 | tf_op jit(solution)/shard_map/ppermute | solution.py:23
  75.5 15.8 %collective-permute-start.20 = (bf16[64,4096]{1,0:T(8,128)(2,1)}, bf16[64,4096]{1,0:T(8,128)(2,1)S(1)}, u32[]{:S(2)}, u32[]{:S(2)}) collective-permute-start(bf16[64,4096]{1,0:T(8,128)(2,1)} %get-tuple-element.41.refs_2_), channel_id=1, source_target_pairs={{0,16},{4,20},{8,24},{12,28},{16,0},{20,4},{24,8},{28,12},{1,17},{... | collective-permute-start | bytes 1572872 | tf_op jit(solution)/shard_map/ppermute | solution.py:23
  76.6 19.8 %collective-permute-start.10 = (bf16[64,4096]{1,0:T(8,128)(2,1)S(1)}, bf16[64,4096]{1,0:T(8,128)(2,1)S(1)}, u32[]{:S(2)}, u32[]{:S(2)}) collective-permute-start(bf16[64,4096]{1,0:T(8,128)(2,1)S(1)} %copy-done.36), channel_id=1, source_target_pairs={{0,4},{4,0},{8,12},{12,8},{16,20},{20,16},{24,28},{28,24},{1,5},{5... | collective-permute-start | bytes 1572872 | tf_op jit(solution)/shard_map/ppermute | solution.py:23
  81.2 14.7 %collective-permute-start.15 = (bf16[64,2048]{1,0:T(8,128)(2,1)S(1)}, bf16[64,2048]{1,0:T(8,128)(2,1)S(1)}, u32[]{:S(2)}, u32[]{:S(2)}) collective-permute-start(bf16[64,2048]{1,0:T(8,128)(2,1)S(1)} %get-tuple-element.42), channel_id=1, source_target_pairs={{0,16},{4,20},{8,24},{12,28},{16,0},{20,4},{24,8},{28,12},{1,17},{... | collective-permute-start | bytes 786440 | tf_op jit(solution)/shard_map/ppermute | solution.py:23
  82.0 13.9 %collective-permute-start.17 = (bf16[64,2048]{1,0:T(8,128)(2,1)S(1)}, bf16[64,2048]{1,0:T(8,128)(2,1)S(1)}, u32[]{:S(2)}, u32[]{:S(2)}) collective-permute-start(bf16[64,2048]{1,0:T(8,128)(2,1)S(1)} %get-tuple-element.43), channel_id=1, source_target_pairs={{0,8},{4,12},{8,0},{12,4},{16,24},{20,28},{24,16},{28,20},{1,9},{5... | collective-permute-start | bytes 786440 | tf_op jit(solution)/shard_map/ppermute | solution.py:23
  90.4 7.4 %collective-permute-start.12 = (bf16[64,4096]{1,0:T(8,128)(2,1)S(1)}, bf16[64,4096]{1,0:T(8,128)(2,1)S(1)}, u32[]{:S(2)}, u32[]{:S(2)}) collective-permute-start(bf16[64,4096]{1,0:T(8,128)(2,1)S(1)} %collective-permute-done.11.refs_0_.refs_4_.refs_9_), channel_id=1, source_target_pairs={{0,4},{4,0},{8,12},{12,8},{16,20},{20,16},{24,28},{28,24},{1,5},{5... | collective-permute-start | bytes 1572872 | tf_op jit(solution)/shard_map/ppermute | solution.py:23
  91.4 6.4 %collective-permute-start.14 = (bf16[64,4096]{1,0:T(8,128)(2,1)S(1)}, bf16[64,4096]{1,0:T(8,128)(2,1)S(1)}, u32[]{:S(2)}, u32[]{:S(2)}) collective-permute-start(bf16[64,4096]{1,0:T(8,128)(2,1)S(1)} %collective-permute-done.13.refs_1_.refs_6_.refs_10_), channel_id=1, source_target_pairs={{0,4},{4,0},{8,12},{12,8},{16,20},{20,16},{24,28},{28,24},{1,5},{5... | collective-permute-start | bytes 1572872 | tf_op jit(solution)/shard_map/ppermute | solution.py:23
  95.9 1.9 collective-permute-start.18
  106.2 53.6 %reduce-scatter.5.cloned.1.call-start = ((), (), s32[]{:S(2)}) async-start(), calls=%async_computation.3 | async-start | bytes 1310720 | tf_op jit(solution)/shard_map/reduce_scatter | solution.py:877
  106.3 8.4 %collective-permute-start.24 = (bf16[64,2048]{1,0:T(8,128)(2,1)S(1)}, bf16[64,2048]{1,0:T(8,128)(2,1)S(1)}, u32[]{:S(2)}, u32[]{:S(2)}) collective-permute-start(bf16[64,2048]{1,0:T(8,128)(2,1)S(1)} %get-tuple-element.44), channel_id=1, source_target_pairs={{0,16},{4,20},{8,24},{12,28},{16,0},{20,4},{24,8},{28,12},{1,17},{... | collective-permute-start | bytes 786440 | tf_op jit(solution)/shard_map/ppermute | solution.py:23
  107.2 8.1 %collective-permute-start.26 = (bf16[64,2048]{1,0:T(8,128)(2,1)S(1)}, bf16[64,2048]{1,0:T(8,128)(2,1)S(1)}, u32[]{:S(2)}, u32[]{:S(2)}) collective-permute-start(bf16[64,2048]{1,0:T(8,128)(2,1)S(1)} %get-tuple-element.45), channel_id=1, source_target_pairs={{0,8},{4,12},{8,0},{12,4},{16,24},{20,28},{24,16},{28,20},{1,9},{5... | collective-permute-start | bytes 786440 | tf_op jit(solution)/shard_map/ppermute | solution.py:23
  108.4 6.9 %collective-permute-start.21 = (bf16[64,4096]{1,0:T(8,128)(2,1)S(1)}, bf16[64,4096]{1,0:T(8,128)(2,1)S(1)}, u32[]{:S(2)}, u32[]{:S(2)}) collective-permute-start(bf16[64,4096]{1,0:T(8,128)(2,1)S(1)} %copy-done.32), channel_id=1, source_target_pairs={{0,4},{4,0},{8,12},{12,8},{16,20},{20,16},{24,28},{28,24},{1,5},{5... | collective-permute-start | bytes 1572872 | tf_op jit(solution)/shard_map/ppermute | solution.py:23
  108.4 6.9 %collective-permute-start.22 = (bf16[64,4096]{1,0:T(8,128)(2,1)S(1)}, bf16[64,4096]{1,0:T(8,128)(2,1)S(1)}, u32[]{:S(2)}, u32[]{:S(2)}) collective-permute-start(bf16[64,4096]{1,0:T(8,128)(2,1)S(1)} %collective-permute-done.19.refs_12_.refs_0_.refs_4_), channel_id=1, source_target_pairs={{0,4},{4,0},{8,12},{12,8},{16,20},{20,16},{24,28},{28,24},{1,5},{5... | collective-permute-start | bytes 1572872 | tf_op jit(solution)/shard_map/ppermute | solution.py:23
  108.9 6.4 %collective-permute-start.23 = (bf16[64,4096]{1,0:T(8,128)(2,1)S(1)}, bf16[64,4096]{1,0:T(8,128)(2,1)S(1)}, u32[]{:S(2)}, u32[]{:S(2)}) collective-permute-start(bf16[64,4096]{1,0:T(8,128)(2,1)S(1)} %collective-permute-done.20.refs_13_.refs_1_.refs_6_), channel_id=1, source_target_pairs={{0,4},{4,0},{8,12},{12,8},{16,20},{20,16},{24,28},{28,24},{1,5},{5... | collective-permute-start | bytes 1572872 | tf_op jit(solution)/shard_map/ppermute | solution.py:23
  131.8 31.4 %collective-permute-start.30 = (bf16[384,2048]{1,0:T(8,128)(2,1)}, bf16[384,2048]{1,0:T(8,128)(2,1)S(1)}, u32[]{:S(2)}, u32[]{:S(2)}) collective-permute-start(bf16[384,2048]{1,0:T(8,128)(2,1)} %get-tuple-element.48), channel_id=1, source_target_pairs={{0,4},{4,0},{8,12},{12,8},{16,20},{20,16},{24,28},{28,24},{1,5},{5... | collective-permute-start | bytes 4718600 | tf_op jit(solution)/shard_map/ppermute | solution.py:23
  132.4 30.8 %collective-permute-start.28 = (bf16[384,1024]{1,0:T(8,128)(2,1)}, bf16[384,1024]{1,0:T(8,128)(2,1)S(1)}, u32[]{:S(2)}, u32[]{:S(2)}) collective-permute-start(bf16[384,1024]{1,0:T(8,128)(2,1)} %get-tuple-element.46), channel_id=1, source_target_pairs={{0,12},{4,8},{8,4},{12,0},{16,28},{20,24},{24,20},{28,16},{1,13},{... | collective-permute-start | bytes 2359304 | tf_op jit(solution)/shard_map/ppermute | solution.py:23
  133.6 29.6 %collective-permute-start.29 = (bf16[384,1024]{1,0:T(8,128)(2,1)}, bf16[384,1024]{1,0:T(8,128)(2,1)S(1)}, u32[]{:S(2)}, u32[]{:S(2)}) collective-permute-start(bf16[384,1024]{1,0:T(8,128)(2,1)} %get-tuple-element.47), channel_id=1, source_target_pairs={{0,20},{4,16},{8,28},{12,24},{16,4},{20,0},{24,12},{28,8},{1,21},{... | collective-permute-start | bytes 2359304 | tf_op jit(solution)/shard_map/ppermute | solution.py:23
  163.9 11.0 %collective-permute-start.32 = (bf16[192,1024]{1,0:T(8,128)(2,1)S(1)}, bf16[192,1024]{1,0:T(8,128)(2,1)S(1)}, u32[]{:S(2)}, u32[]{:S(2)}) collective-permute-start(bf16[192,1024]{1,0:T(8,128)(2,1)S(1)} %get-tuple-element.49.refs_4_), channel_id=1, source_target_pairs={{0,8},{4,12},{8,0},{12,4},{16,24},{20,28},{24,16},{28,20},{1,9},{5... | collective-permute-start | bytes 1179656 | tf_op jit(solution)/shard_map/ppermute | solution.py:23
  165.4 10.6 %collective-permute-start.34 = (bf16[192,1024]{1,0:T(8,128)(2,1)S(1)}, bf16[192,1024]{1,0:T(8,128)(2,1)S(1)}, u32[]{:S(2)}, u32[]{:S(2)}) collective-permute-start(bf16[192,1024]{1,0:T(8,128)(2,1)S(1)} %get-tuple-element.49.refs_4_), channel_id=1, source_target_pairs={{0,16},{4,20},{8,24},{12,28},{16,0},{20,4},{24,8},{28,12},{1,17},{... | collective-permute-start | bytes 1179656 | tf_op jit(solution)/shard_map/ppermute | solution.py:23
  166.9 17.7 %collective-permute-start.47 = (bf16[192,1024]{1,0:T(8,128)(2,1)S(1)}, bf16[192,1024]{1,0:T(8,128)(2,1)S(1)}, u32[]{:S(2)}, u32[]{:S(2)}) collective-permute-start(bf16[192,1024]{1,0:T(8,128)(2,1)S(1)} %get-tuple-element.55), channel_id=1, source_target_pairs={{0,1},{1,0},{2,3},{3,2},{4,5},{5,4},{6,7},{7,6},{8,9},{9,8},{10,11... | collective-permute-start | bytes 1179656 | tf_op jit(solution)/shard_map/ppermute | solution.py:23
  169.5 27.5 %collective-permute-start.48 = (bf16[192,1024]{1,0:T(8,128)(2,1)S(1)}, bf16[192,1024]{1,0:T(8,128)(2,1)S(1)}, u32[]{:S(2)}, u32[]{:S(2)}) collective-permute-start(bf16[192,1024]{1,0:T(8,128)(2,1)S(1)} %get-tuple-element.56), channel_id=1, source_target_pairs={{0,2},{1,3},{2,0},{3,1},{4,6},{5,7},{6,4},{7,5},{8,10},{9,11},{10,... | collective-permute-start | bytes 1179656 | tf_op jit(solution)/shard_map/ppermute | solution.py:23
  170.6 33.9 %collective-permute-start.49 = (bf16[192,1024]{1,0:T(8,128)(2,1)S(1)}, bf16[192,1024]{1,0:T(8,128)(2,1)S(1)}, u32[]{:S(2)}, u32[]{:S(2)}) collective-permute-start(bf16[192,1024]{1,0:T(8,128)(2,1)S(1)} %get-tuple-element.57), channel_id=1, source_target_pairs={{0,3},{1,2},{2,1},{3,0},{4,7},{5,6},{6,5},{7,4},{8,11},{9,10},{10,... | collective-permute-start | bytes 1179656 | tf_op jit(solution)/shard_map/ppermute | solution.py:23
  176.2 28.3 %collective-permute-start.36 = (bf16[96,1024]{1,0:T(8,128)(2,1)S(1)}, bf16[96,1024]{1,0:T(8,128)(2,1)S(1)}, u32[]{:S(2)}, u32[]{:S(2)}) collective-permute-start(bf16[96,1024]{1,0:T(8,128)(2,1)S(1)} %get-tuple-element.50), channel_id=1, source_target_pairs={{0,16},{4,20},{8,24},{12,28},{16,0},{20,4},{24,8},{28,12},{1,17},{... | collective-permute-start | bytes 589832 | tf_op jit(solution)/shard_map/ppermute | solution.py:23
  177.7 26.7 %collective-permute-start.38 = (bf16[96,1024]{1,0:T(8,128)(2,1)S(1)}, bf16[96,1024]{1,0:T(8,128)(2,1)S(1)}, u32[]{:S(2)}, u32[]{:S(2)}) collective-permute-start(bf16[96,1024]{1,0:T(8,128)(2,1)S(1)} %get-tuple-element.51), channel_id=1, source_target_pairs={{0,8},{4,12},{8,0},{12,4},{16,24},{20,28},{24,16},{28,20},{1,9},{5... | collective-permute-start | bytes 589832 | tf_op jit(solution)/shard_map/ppermute | solution.py:23
  206.0 28.0 %collective-permute-start.51 = (bf16[576,1024]{1,0:T(8,128)(2,1)}, bf16[576,1024]{1,0:T(8,128)(2,1)S(1)}, u32[]{:S(2)}, u32[]{:S(2)}) collective-permute-start(bf16[576,1024]{1,0:T(8,128)(2,1)} %join.3.refs_4_), channel_id=1, source_target_pairs={{0,8},{4,12},{8,0},{12,4},{16,24},{20,28},{24,16},{28,20},{1,9},{5... | collective-permute-start | bytes 3538952 | tf_op jit(solution)/shard_map/ppermute | solution.py:23
  206.7 29.1 %collective-permute-start.53 = (bf16[576,1024]{1,0:T(8,128)(2,1)}, bf16[576,1024]{1,0:T(8,128)(2,1)S(1)}, u32[]{:S(2)}, u32[]{:S(2)}) collective-permute-start(bf16[576,1024]{1,0:T(8,128)(2,1)} %join.3.refs_4_), channel_id=1, source_target_pairs={{0,16},{4,20},{8,24},{12,28},{16,0},{20,4},{24,8},{28,12},{1,17},{... | collective-permute-start | bytes 3538952 | tf_op jit(solution)/shard_map/ppermute | solution.py:23
  207.2 2.0 collective-permute-start.37
  207.7 3.2 collective-permute-start.33
  208.9 2.0 collective-permute-start.35
  217.8 18.7 %collective-permute-start.41 = (bf16[192,384]{1,0:T(8,128)(2,1)S(1)}, bf16[192,384]{1,0:T(8,128)(2,1)S(1)}, u32[]{:S(2)}, u32[]{:S(2)}) collective-permute-start(bf16[192,384]{1,0:T(8,128)(2,1)S(1)} %hidden_units.2.refs_1_.refs_2_), channel_id=1, source_target_pairs={{0,8},{4,12},{8,0},{12,4},{16,24},{20,28},{24,16},{28,20},{1,9},{5... | collective-permute-start | bytes 442376 | tf_op jit(solution)/shard_map/ppermute | solution.py:23
  219.3 19.6 %collective-permute-start.43 = (bf16[192,384]{1,0:T(8,128)(2,1)S(1)}, bf16[192,384]{1,0:T(8,128)(2,1)S(1)}, u32[]{:S(2)}, u32[]{:S(2)}) collective-permute-start(bf16[192,384]{1,0:T(8,128)(2,1)S(1)} %hidden_units.2.refs_1_.refs_2_), channel_id=1, source_target_pairs={{0,16},{4,20},{8,24},{12,28},{16,0},{20,4},{24,8},{28,12},{1,17},{... | collective-permute-start | bytes 442376 | tf_op jit(solution)/shard_map/ppermute | solution.py:23
  220.8 31.5 %collective-permute-start.50 = (bf16[576,1024]{1,0:T(8,128)(2,1)}, bf16[576,1024]{1,0:T(8,128)(2,1)S(1)}, u32[]{:S(2)}, u32[]{:S(2)}) collective-permute-start(bf16[576,1024]{1,0:T(8,128)(2,1)} %join.3.refs_4_), channel_id=1, source_target_pairs={{0,4},{4,0},{8,12},{12,8},{16,20},{20,16},{24,28},{28,24},{1,5},{5... | collective-permute-start | bytes 3538952 | tf_op jit(solution)/shard_map/ppermute | solution.py:23
  235.8 12.6 %collective-permute-start.55 = (bf16[288,1024]{1,0:T(8,128)(2,1)S(1)}, bf16[288,1024]{1,0:T(8,128)(2,1)S(1)}, u32[]{:S(2)}, u32[]{:S(2)}) collective-permute-start(bf16[288,1024]{1,0:T(8,128)(2,1)S(1)} %get-tuple-element.58), channel_id=1, source_target_pairs={{0,16},{4,20},{8,24},{12,28},{16,0},{20,4},{24,8},{28,12},{1,17},{... | collective-permute-start | bytes 1769480 | tf_op jit(solution)/shard_map/ppermute | solution.py:23
  236.5 15.9 %collective-permute-start.52 = (bf16[576,1024]{1,0:T(8,128)(2,1)S(1)}, bf16[576,1024]{1,0:T(8,128)(2,1)S(1)}, u32[]{:S(2)}, u32[]{:S(2)}) collective-permute-start(bf16[576,1024]{1,0:T(8,128)(2,1)S(1)} %collective-permute-done.51.refs_0_.refs_6_), channel_id=1, source_target_pairs={{0,4},{4,0},{8,12},{12,8},{16,20},{20,16},{24,28},{28,24},{1,5},{5... | collective-permute-start | bytes 3538952 | tf_op jit(solution)/shard_map/ppermute | solution.py:23
  236.5 15.9 %collective-permute-start.54 = (bf16[576,1024]{1,0:T(8,128)(2,1)S(1)}, bf16[576,1024]{1,0:T(8,128)(2,1)S(1)}, u32[]{:S(2)}, u32[]{:S(2)}) collective-permute-start(bf16[576,1024]{1,0:T(8,128)(2,1)S(1)} %collective-permute-done.53.refs_1_.refs_8_), channel_id=1, source_target_pairs={{0,4},{4,0},{8,12},{12,8},{16,20},{20,16},{24,28},{28,24},{1,5},{5... | collective-permute-start | bytes 3538952 | tf_op jit(solution)/shard_map/ppermute | solution.py:23
  238.9 13.4 %collective-permute-start.57 = (bf16[288,1024]{1,0:T(8,128)(2,1)S(1)}, bf16[288,1024]{1,0:T(8,128)(2,1)S(1)}, u32[]{:S(2)}, u32[]{:S(2)}) collective-permute-start(bf16[288,1024]{1,0:T(8,128)(2,1)S(1)} %get-tuple-element.59), channel_id=1, source_target_pairs={{0,8},{4,12},{8,0},{12,4},{16,24},{20,28},{24,16},{28,20},{1,9},{5... | collective-permute-start | bytes 1769480 | tf_op jit(solution)/shard_map/ppermute | solution.py:23
  248.5 3.9 %collective-permute-start.56 = (bf16[288,1024]{1,0:T(8,128)(2,1)S(1)}, bf16[288,1024]{1,0:T(8,128)(2,1)S(1)}, u32[]{:S(2)}, u32[]{:S(2)}) collective-permute-start(bf16[288,1024]{1,0:T(8,128)(2,1)S(1)} %collective-permute-done.55.refs_10_), channel_id=1, source_target_pairs={{0,4},{4,0},{8,12},{12,8},{16,20},{20,16},{24,28},{28,24},{1,5},{5... | collective-permute-start | bytes 1769480 | tf_op jit(solution)/shard_map/ppermute | solution.py:23
  252.3 2.0 collective-permute-start.58
  269.4 12.3 %collective-permute-start.60 = (bf16[576,384]{1,0:T(8,128)(2,1)S(1)}, bf16[576,384]{1,0:T(8,128)(2,1)S(1)}, u32[]{:S(2)}, u32[]{:S(2)}) collective-permute-start(bf16[576,384]{1,0:T(8,128)(2,1)S(1)} %hidden_units.3.refs_1_), channel_id=1, source_target_pairs={{0,8},{4,12},{8,0},{12,4},{16,24},{20,28},{24,16},{28,20},{1,9},{5... | collective-permute-start | bytes 1327112 | tf_op jit(solution)/shard_map/ppermute | solution.py:23
  271.0 11.9 %collective-permute-start.62 = (bf16[576,384]{1,0:T(8,128)(2,1)S(1)}, bf16[576,384]{1,0:T(8,128)(2,1)S(1)}, u32[]{:S(2)}, u32[]{:S(2)}) collective-permute-start(bf16[576,384]{1,0:T(8,128)(2,1)S(1)} %hidden_units.3.refs_1_), channel_id=1, source_target_pairs={{0,16},{4,20},{8,24},{12,28},{16,0},{20,4},{24,8},{28,12},{1,17},{... | collective-permute-start | bytes 1327112 | tf_op jit(solution)/shard_map/ppermute | solution.py:23
  272.5 11.0 %collective-permute-start.40 = (bf16[192,384]{1,0:T(8,128)(2,1)S(1)}, bf16[192,384]{1,0:T(8,128)(2,1)S(1)}, u32[]{:S(2)}, u32[]{:S(2)}) collective-permute-start(bf16[192,384]{1,0:T(8,128)(2,1)S(1)} %hidden_units.2.refs_1_.refs_2_), channel_id=1, source_target_pairs={{0,4},{4,0},{8,12},{12,8},{16,20},{20,16},{24,28},{28,24},{1,5},{5... | collective-permute-start | bytes 442376 | tf_op jit(solution)/shard_map/ppermute | solution.py:23
  272.5 16.4 %collective-permute-start.59 = (bf16[576,384]{1,0:T(8,128)(2,1)S(1)}, bf16[576,384]{1,0:T(8,128)(2,1)S(1)}, u32[]{:S(2)}, u32[]{:S(2)}) collective-permute-start(bf16[576,384]{1,0:T(8,128)(2,1)S(1)} %hidden_units.3.refs_1_), channel_id=1, source_target_pairs={{0,4},{4,0},{8,12},{12,8},{16,20},{20,16},{24,28},{28,24},{1,5},{5... | collective-permute-start | bytes 1327112 | tf_op jit(solution)/shard_map/ppermute | solution.py:23
  281.7 7.2 %collective-permute-start.61 = (bf16[576,384]{1,0:T(8,128)(2,1)S(1)}, bf16[576,384]{1,0:T(8,128)(2,1)S(1)}, u32[]{:S(2)}, u32[]{:S(2)}) collective-permute-start(bf16[576,384]{1,0:T(8,128)(2,1)S(1)} %collective-permute-done.60.refs_3_), channel_id=1, source_target_pairs={{0,4},{4,0},{8,12},{12,8},{16,20},{20,16},{24,28},{28,24},{1,5},{5... | collective-permute-start | bytes 1327112 | tf_op jit(solution)/shard_map/ppermute | solution.py:23
  282.9 6.0 %collective-permute-start.63 = (bf16[576,384]{1,0:T(8,128)(2,1)S(1)}, bf16[576,384]{1,0:T(8,128)(2,1)S(1)}, u32[]{:S(2)}, u32[]{:S(2)}) collective-permute-start(bf16[576,384]{1,0:T(8,128)(2,1)S(1)} %collective-permute-done.62.refs_5_), channel_id=1, source_target_pairs={{0,4},{4,0},{8,12},{12,8},{16,20},{20,16},{24,28},{28,24},{1,5},{5... | collective-permute-start | bytes 1327112 | tf_op jit(solution)/shard_map/ppermute | solution.py:23
  282.9 2.0 collective-permute-start.42
  296.4 15.4 %collective-permute-start.64 = (bf16[576,512]{1,0:T(8,128)(2,1)S(1)}, bf16[576,512]{1,0:T(8,128)(2,1)S(1)}, u32[]{:S(2)}, u32[]{:S(2)}) collective-permute-start(bf16[576,512]{1,0:T(8,128)(2,1)S(1)} %get-tuple-element.61), channel_id=1, source_target_pairs={{0,16},{4,20},{8,24},{12,28},{16,0},{20,4},{24,8},{28,12},{1,17},{... | collective-permute-start | bytes 1769480 | tf_op jit(solution)/shard_map/ppermute | solution.py:23
  297.9 15.1 %collective-permute-start.65 = (bf16[576,512]{1,0:T(8,128)(2,1)S(1)}, bf16[576,512]{1,0:T(8,128)(2,1)S(1)}, u32[]{:S(2)}, u32[]{:S(2)}) collective-permute-start(bf16[576,512]{1,0:T(8,128)(2,1)S(1)} %get-tuple-element.62), channel_id=1, source_target_pairs={{0,8},{4,12},{8,0},{12,4},{16,24},{20,28},{24,16},{28,20},{1,9},{5... | collective-permute-start | bytes 1769480 | tf_op jit(solution)/shard_map/ppermute | solution.py:23
  314.2 15.4 %collective-permute-start.66 = (bf16[192,1024]{1,0:T(8,128)(2,1)}, bf16[192,1024]{1,0:T(8,128)(2,1)S(1)}, u32[]{:S(2)}, u32[]{:S(2)}) collective-permute-start(bf16[192,1024]{1,0:T(8,128)(2,1)} %get-tuple-element.63), channel_id=1, source_target_pairs={{0,1},{1,0},{2,3},{3,2},{4,5},{5,4},{6,7},{7,6},{8,9},{9,8},{10,11... | collective-permute-start | bytes 1179656 | tf_op jit(solution)/shard_map/ppermute | solution.py:23
  314.3 29.7 %collective-permute-start.67 = (bf16[192,1024]{1,0:T(8,128)(2,1)}, bf16[192,1024]{1,0:T(8,128)(2,1)}, u32[]{:S(2)}, u32[]{:S(2)}) collective-permute-start(bf16[192,1024]{1,0:T(8,128)(2,1)} %get-tuple-element.64), channel_id=1, source_target_pairs={{0,2},{1,3},{2,0},{3,1},{4,6},{5,7},{6,4},{7,5},{8,10},{9,11},{10,... | collective-permute-start | bytes 1179656 | tf_op jit(solution)/shard_map/ppermute | solution.py:23
  317.2 33.8 %collective-permute-start.68 = (bf16[192,1024]{1,0:T(8,128)(2,1)}, bf16[192,1024]{1,0:T(8,128)(2,1)}, u32[]{:S(2)}, u32[]{:S(2)}) collective-permute-start(bf16[192,1024]{1,0:T(8,128)(2,1)} %get-tuple-element.65), channel_id=1, source_target_pairs={{0,3},{1,2},{2,1},{3,0},{4,7},{5,6},{6,5},{7,4},{8,11},{9,10},{10,... | collective-permute-start | bytes 1179656 | tf_op jit(solution)/shard_map/ppermute | solution.py:23
  317.7 5.9 %collective-permute-start.45 = (bf16[192,512]{1,0:T(8,128)(2,1)}, bf16[192,512]{1,0:T(8,128)(2,1)S(1)}, u32[]{:S(2)}, u32[]{:S(2)}) collective-permute-start(bf16[192,512]{1,0:T(8,128)(2,1)} %get-tuple-element.53), channel_id=1, source_target_pairs={{0,16},{4,20},{8,24},{12,28},{16,0},{20,4},{24,8},{28,12},{1,17},{... | collective-permute-start | bytes 589832 | tf_op jit(solution)/shard_map/ppermute | solution.py:23
  318.3 6.0 %collective-permute-start.46 = (bf16[192,512]{1,0:T(8,128)(2,1)}, bf16[192,512]{1,0:T(8,128)(2,1)}, u32[]{:S(2)}, u32[]{:S(2)}) collective-permute-start(bf16[192,512]{1,0:T(8,128)(2,1)} %get-tuple-element.54), channel_id=1, source_target_pairs={{0,8},{4,12},{8,0},{12,4},{16,24},{20,28},{24,16},{28,20},{1,9},{5... | collective-permute-start | bytes 589832 | tf_op jit(solution)/shard_map/ppermute | solution.py:23
  (54 other events, 1149.6 us)
Sparse Core Ops, SparseCore 0:
  106.3 25.2 reduce-scatter.2
  134.0 25.7 reduce-scatter.4

commit v8 on v7

--- a/solution.py
+++ b/solution.py
@@ -827,7 +827,6 @@
             down_parts[mask] = swap(cut, "ctx", mask)
         return tuple(down_parts[mask] for mask in masks)
 
-    early = send_columns([2, 4], [rim_rows])
 
     extra, left = [], norm_gain
     for _ in range(3):
@@ -852,7 +851,7 @@
         b_wide,
     )
     chunks = 2
-    state, ends = prefix_state, gather_parts(join([end], early))
+    state, ends = prefix_state, gather_parts(end)
     one_over_gain = inverse_gains(me, ends, width)
     gated = []
     for chunk in range(chunks):
@@ -876,8 +875,7 @@
     far = lambda parts: [part for mask, which, part in parts if which is not None][::2]
     scatter = lambda rows: lax.psum_scatter(rows, "exp", scatter_dimension=0, tiled=True)
     front = gather_parts(gated[0], 1, gated[1:])
-    late_masks = [3, 5, 1] if crossing else [1, 3] + list(range(5, ctx_count))
-    late = send_columns(late_masks, near(front))
+    late = send_columns([3, 5, 1, 2, 4] if crossing else list(range(1, ctx_count)), near(front))
     back = gather_parts(gated[1], 1, far(front))
     partial = project(me, front, out_proj, near(back))
     projected = [scatter(partial)]
@@ -908,32 +906,32 @@
     sent = pick_rows(picked, scaled, late)
     pieces = [rows if mask == 0 else swap(rows, "exp", mask) for mask, rows in enumerate(sent)]
     weights = [None] + [down_parts[mask] for mask in sorted(down_parts)]
-    settled, arrived, order, first_units, keeps = [], (), (), (), ()
+    gathered_units, arrived, order, ready = [], (), (), ()
     for group in groups:
         rows = [pieces[mask] for mask in group]
         rows = join(rows, arrived) if len(group) > 1 else rows[0]
         parts = gather_parts(rows, 0, order)
         arrived = far(parts)
-        hidden = hidden_units(me, [parts], one_over_gain, expert_gate[0], expert_up[0], first_units)
+        hidden = hidden_units(me, [parts], one_over_gain, expert_gate[0], expert_up[0], ready)
         order = [hidden]
         if crossing:
             units = {0: hidden, 2: swap(hidden, "ctx", 2), 4: swap(hidden, "ctx", 4)}
             units.update({mask + 1: swap(units[mask], "ctx", 1) for mask in (0, 2, 4)})
-            first_units = [units[2], units[4]]
-            keep, first, second = cross_down(me, units, weights, down_rows, keeps)
-            keeps = [keep]
-            settled.append((keep, swap(first, "ctx", 4), swap(second, "ctx", 2)))
+            ready = [units[2], units[4]]
         else:
-            answer = down(me, gather_parts(hidden), weights, down_rows, keeps)
-            keeps = [answer]
-            settled.append([answer])
-    answers = {}
-    for group, sums in zip(groups, settled):
+            units = gather_parts(hidden)
+        gathered_units.append(units)
+    answers, order, before = {}, (), ()
+    for group, units in list(zip(groups, gathered_units))[::-1]:
         if crossing:
-            pieces = settle(*sums, len(group), keeps)
+            keep, first, second = cross_down(me, units, weights, down_rows, order)
+            first, second = swap(first, "ctx", 4), swap(second, "ctx", 2)
+            before = settle(keep, first, second, len(group), before)
         else:
-            pieces = jnp.split(sums[0], len(group))
-        for mask, piece in zip(group, pieces):
+            keep = down(me, units, weights, down_rows, order)
+            before = jnp.split(keep, len(group))
+        order = [keep]
+        for mask, piece in zip(group, before):
             answers[mask] = piece if mask == 0 else swap(piece, "exp", mask)
     block_out = combine(
         exp_me.astype(jnp.int32).reshape(1),

time: 361 us -> 352 us (0.975)
  starting transfers between devices: 50.8 us -> 46.9 us
    ppermute x68, starting transfers between devices: 49 us -> 44.9 us  [swap(): lax.ppermute(array, axis, [(i, i ^ mask) for i in range(lax.axis_size(axi...]
    pallas_call x22 -> x20, Pallas kernels: 96.1 us -> 92.5 us  [launch(): pl.pallas_call(body, grid_spec=pltpu.PrefetchScalarGridSpec(num_scalar_pr...]
  transfers between devices with their start and end apart: 71 -> 71, of which waited for: 43 -> 42; matrix products, arithmetic and copies ran while one was open for 3% -> 3% of each run, Pallas kernels for 13% -> 10%
where the time goes in v8:
time: 352 us; the launch traced here: 351 us
  waiting for transfers between devices  179 us (51%)
  Pallas kernels  92.5 us (26%)
  starting transfers between devices  46.9 us (13%)
  between operations  14.6 us (4%)
  other arithmetic  8.89 us (3%)
  local copies, waits for them, and re-layouts  8.51 us (2%)
    ppermute x68, waiting for transfers between devices, swap(): lax.ppermute(array, axis, [(i, i ^ mask) for i in range(lax.axis_size(axi...  159 us
    pallas_call x20, Pallas kernels, launch(): pl.pallas_call(body, grid_spec=pltpu.PrefetchScalarGridSpec(num_scalar_pr...  92.5 us
    ppermute x68, starting transfers between devices, swap(): lax.ppermute(array, axis, [(i, i ^ mask) for i in range(lax.axis_size(axi...  44.9 us
    reduce_scatter x2, waiting for transfers between devices, shards(): lax.psum_scatter(rows, 'exp', scatter_dimension=0, tiled=True)  20.9 us
  transfers between devices with their start and end apart: 71, of which 42 were waited for; matrix products, arithmetic and copies ran while one was open for 3% of the time, Pallas kernels for 10%

profile of v8, /device:TPU:8, one launch (start us, length us, event | category | flops | bytes accessed | tf_op | source)
XLA Modules:
  0.0 350.9 jit_solution(12903129424491077533)
XLA Ops:
  8.1 1.7 collective-permute-start
  13.5 1.3 broadcast_in_dim.20.refs_8_.refs_6_
  14.8 13.9 %local_states.1 = (f32[128,4096]{1,0:T(8,128)}, f32[128,4096]{1,0:T(8,128)}, bf16[32,4096]{1,0:T(8,128)(2,1)}) custom-call(bf16[128,4096]{1,0:T(8,128)(2,1)} %refs_0_.1, f32[8,4096]{1,0:T(8,128)} %pad_convert_fusion.refs_1_, bf16[128,4096]{1,0:T(8,128)(2,1)} %refs_2_.2, f32[4,4096]{1,0:T(4,128)} %refs_3_.4, f32[1,4096]{1,0:T(1,128)} %bitcast.66, ...), custom_call_target="tpu_custom_call" | custom-call | flops 41943040 | bytes 6291456 | tf_op jit(solution)/shard_map/local_states/pallas_call | solution.py:95
  28.7 2.1 collective-permute-start.2
  30.8 1.5 collective-permute-start.4
  33.1 4.9 %collective-permute-done.2.refs_11_.refs_3_ = bf16[32,4096]{1,0:T(8,128)(2,1)S(1)} collective-permute-done((bf16[32,4096]{1,0:T(8,128)(2,1)}, bf16[32,4096]{1,0:T(8,128)(2,1)S(1)}, u32[]{:S(2)}, u32[]{:S(2)}) %collective-permute-start.2) | collective-permute-done | bytes 262176 | tf_op jit(solution)/shard_map/ppermute | solution.py:23
  38.3 6.7 %collective-permute-done.4.refs_13_.refs_5_ = bf16[32,4096]{1,0:T(8,128)(2,1)S(1)} collective-permute-done((bf16[32,4096]{1,0:T(8,128)(2,1)}, bf16[32,4096]{1,0:T(8,128)(2,1)S(1)}, u32[]{:S(2)}, u32[]{:S(2)}) %collective-permute-start.4) | collective-permute-done | bytes 262176 | tf_op jit(solution)/shard_map/ppermute | solution.py:23
  46.9 1.3 broadcast_in_dim.23.refs_7_
  48.3 9.1 %read_out.2 = (bf16[64,4096]{1,0:T(8,128)(2,1)}, f32[16,4096]{1,0:T(8,128)}) custom-call(s32[1]{0:T(128)} %bitcast.refs_0_, f32[128,4096]{1,0:T(8,128)} %get-tuple-element.34.refs_1_, f32[128,4096]{1,0:T(8,128)} %get-tuple-element.35.refs_2_, bf16[128,4096]{1,0:T(8,128)(2,1)} %refs_3_.6, f32[16,4096]{1,0:T(8,128)} %refs_4_.3, f32[1,4096]{1,0:T(1,128)} %bitcast.61, ...), custom_call_target="tpu_custom_call" | custom-call | flops 29360128 | bytes 3145728 | tf_op jit(solution)/shard_map/read_out/pallas_call | solution.py:95
  57.9 1.7 collective-permute-start.9
  59.6 8.3 %read_out.3 = (bf16[64,4096]{1,0:T(8,128)(2,1)}, f32[16,4096]{1,0:T(8,128)}) custom-call(s32[1]{0:T(128)} %bitcast.refs_0_, f32[128,4096]{1,0:T(8,128)} %get-tuple-element.34.refs_1_, f32[128,4096]{1,0:T(8,128)} %get-tuple-element.35.refs_2_, bf16[128,4096]{1,0:T(8,128)(2,1)} %refs_3_.6, f32[16,4096]{1,0:T(8,128)} %refs_4_.3, f32[1,4096]{1,0:T(1,128)} %bitcast.62, ...), custom_call_target="tpu_custom_call" | custom-call | flops 29360128 | bytes 3145728 | tf_op jit(solution)/shard_map/read_out/pallas_call | solution.py:95
  68.3 1.6 collective-permute-start.18
  69.9 2.5 collective-permute-done.11.refs_1_.refs_6_.refs_14_
  72.9 1.0 copy-done.20
  74.0 1.7 collective-permute-start.13
  76.2 7.9 %collective-permute-done.17.refs_12_.refs_0_.refs_4_ = bf16[64,4096]{1,0:T(8,128)(2,1)S(1)} collective-permute-done((bf16[64,4096]{1,0:T(8,128)(2,1)}, bf16[64,4096]{1,0:T(8,128)(2,1)S(1)}, u32[]{:S(2)}, u32[]{:S(2)}) %collective-permute-start.17) | collective-permute-done | bytes 524320 | tf_op jit(solution)/shard_map/ppermute | solution.py:23
  84.6 3.9 %collective-permute-done.13.refs_8_.refs_2_ = bf16[64,2048]{1,0:T(8,128)(2,1)S(1)} collective-permute-done((bf16[64,2048]{1,0:T(8,128)(2,1)S(1)}, bf16[64,2048]{1,0:T(8,128)(2,1)S(1)}, u32[]{:S(2)}, u32[]{:S(2)}) %collective-permute-start.13) | collective-permute-done | bytes 262176 | tf_op jit(solution)/shard_map/ppermute | solution.py:23
  89.0 1.0 collective-permute-done.14.refs_9_
  90.4 8.3 %project.2.refs_12_ = bf16[512,1024]{1,0:T(8,128)(2,1)} custom-call(s32[1]{0:T(128)} %bitcast.refs_0_, bf16[4096,1024]{1,0:T(8,128)(2,1)} %refs_1_.3, bf16[64,4096]{1,0:T(8,128)(2,1)S(1)} %copy-done.24, bf16[64,4096]{1,0:T(8,128)(2,1)S(1)} %collective-permute-done.8.refs_3_, bf16[64,4096]{1,0:T(8,128)(2,1)S(1)} %collective-permute-done.9.refs_0_.refs_4_.refs_13_, ...), custom_call_target="tpu_custom_call" | custom-call | flops 4294967296 | bytes 13631488 | tf_op jit(solution)/shard_map/project/pallas_call | solution.py:95
  99.1 1.4 collective-permute-start.22
  101.8 5.7 %collective-permute-done.22.refs_8_ = bf16[64,2048]{1,0:T(8,128)(2,1)S(1)} collective-permute-done((bf16[64,2048]{1,0:T(8,128)(2,1)S(1)}, bf16[64,2048]{1,0:T(8,128)(2,1)S(1)}, u32[]{:S(2)}, u32[]{:S(2)}) %collective-permute-start.22) | collective-permute-done | bytes 262176 | tf_op jit(solution)/shard_map/ppermute | solution.py:23
  107.5 1.1 collective-permute-done.24.refs_10_
  109.1 1.1 collective-permute-done.25.refs_11_
  110.1 8.4 %project.3 = bf16[512,1024]{1,0:T(8,128)(2,1)} custom-call(s32[1]{0:T(128)} %bitcast.refs_0_, bf16[4096,1024]{1,0:T(8,128)(2,1)} %refs_1_.3, bf16[64,4096]{1,0:T(8,128)(2,1)S(1)} %copy-done.21, bf16[64,4096]{1,0:T(8,128)(2,1)S(1)} %collective-permute-done.19.refs_3_, bf16[64,4096]{1,0:T(8,128)(2,1)S(1)} %collective-permute-done.17.refs_12_.refs_0_.refs_4_, ...), custom_call_target="tpu_custom_call" | custom-call | flops 4294967296 | bytes 13631488 | tf_op jit(solution)/shard_map/project/pallas_call | solution.py:95
  120.6 5.5 %cut_columns.1 = (bf16[384,1024]{1,0:T(8,128)(2,1)}, bf16[384,1024]{1,0:T(8,128)(2,1)}, bf16[384,2048]{1,0:T(8,128)(2,1)}, bf16[384,1024]{1,0:T(8,128)(2,1)}, bf16[384,1024]{1,0:T(8,128)(2,1)}) custom-call(s32[1]{0:T(128)} %bitcast.refs_0_, bf16[384,8192]{1,0:T(8,128)(2,1)} %bitcast.37, bf16[384,8192]{1,0:T(8,128)(2,1)} %bitcast.38, ...), custom_call_target="tpu_custom_call" | custom-call | bytes 9437184 | tf_op jit(solution)/shard_map/cut_columns/pallas_call | solution.py:95
  127.6 1.1 collective-permute-start.27
  129.3 1.4 collective-permute-start.30
  131.6 20.9 %reduce-scatter.5.cloned.1.call-done = bf16[128,1024]{1,0:T(8,128)(2,1)} async-done(((bf16[512,1024]{1,0:T(8,128)(2,1)}), bf16[128,1024]{1,0:T(8,128)(2,1)}) %reduce-scatter.5.cloned.1.call-update) | async-done | bytes 262160 | tf_op jit(solution)/shard_map/reduce_scatter | solution.py:876
  152.5 1.1 pad_maximum_fusion
  153.6 2.3 multiply_convert_fusion
  155.9 8.0 %collective-permute-done.29.refs_8_.refs_9_ = bf16[384,1024]{1,0:T(8,128)(2,1)} collective-permute-done((bf16[384,1024]{1,0:T(8,128)(2,1)}, bf16[384,1024]{1,0:T(8,128)(2,1)}, u32[]{:S(2)}, u32[]{:S(2)}) %collective-permute-start.29) | collective-permute-done | bytes 786464 | tf_op jit(solution)/shard_map/ppermute | solution.py:23
  165.2 1.4 collective-permute-start.32
  167.7 2.6 collective-permute-start.46
  170.8 5.3 %collective-permute-done.32.refs_0_.refs_6_ = bf16[192,1024]{1,0:T(8,128)(2,1)S(1)} collective-permute-done((bf16[192,1024]{1,0:T(8,128)(2,1)S(1)}, bf16[192,1024]{1,0:T(8,128)(2,1)S(1)}, u32[]{:S(2)}, u32[]{:S(2)}) %collective-permute-start.32) | collective-permute-done | bytes 393248 | tf_op jit(solution)/shard_map/ppermute | solution.py:23
  176.1 1.0 collective-permute-done.34.refs_1_.refs_8_
  178.0 1.4 collective-permute-start.38
  179.4 3.4 collective-permute-done.45.refs_0_
  182.8 14.0 %collective-permute-done.46.refs_1_ = bf16[192,1024]{1,0:T(8,128)(2,1)S(1)} collective-permute-done((bf16[192,1024]{1,0:T(8,128)(2,1)S(1)}, bf16[192,1024]{1,0:T(8,128)(2,1)S(1)}, u32[]{:S(2)}, u32[]{:S(2)}) %collective-permute-start.46) | collective-permute-done | bytes 393248 | tf_op jit(solution)/shard_map/ppermute | solution.py:23
  196.7 7.3 %collective-permute-done.47.refs_2_ = bf16[192,1024]{1,0:T(8,128)(2,1)S(1)} collective-permute-done((bf16[192,1024]{1,0:T(8,128)(2,1)S(1)}, bf16[192,1024]{1,0:T(8,128)(2,1)S(1)}, u32[]{:S(2)}, u32[]{:S(2)}) %collective-permute-start.47) | collective-permute-done | bytes 393248 | tf_op jit(solution)/shard_map/ppermute | solution.py:23
  204.6 1.5 collective-permute-start.49
  207.3 1.2 collective-permute-done.31.refs_5_
  209.1 1.4 collective-permute-done.39.refs_13_
  210.5 6.8 %hidden_units.2.refs_2_.refs_1_ = bf16[192,384]{1,0:T(8,128)(2,1)S(1)} custom-call(s32[1]{0:T(128)} %bitcast.refs_0_, f32[8,1,1024]{2,1,0:T(1,128)S(1)} %inverse_gains.1.refs_1_, bf16[8192,384]{1,0:T(8,128)(2,1)S(1)} %bitcast.56, bf16[8192,384]{1,0:T(8,128)(2,1)} %bitcast.57, bf16[192,1024]{1,0:T(8,128)(2,1)S(1)} %get-tuple-element.49.refs_4_, ...), custom_call_target="tpu_custom_call" | custom-call | flops 2415919104 | bytes 15728640 | tf_op jit(solution)/shard_map/hidden_units/pallas_call | solution.py:95
  217.3 1.4 collective-permute-start.41
  219.4 13.2 %collective-permute-done.49.refs_0_.refs_6_ = bf16[576,1024]{1,0:T(8,128)(2,1)S(1)} collective-permute-done((bf16[576,1024]{1,0:T(8,128)(2,1)S(1)}, bf16[576,1024]{1,0:T(8,128)(2,1)S(1)}, u32[]{:S(2)}, u32[]{:S(2)}) %collective-permute-start.49) | collective-permute-done | bytes 1179680 | tf_op jit(solution)/shard_map/ppermute | solution.py:23
  232.6 2.4 collective-permute-done.51.refs_1_.refs_8_
  235.8 1.3 collective-permute-start.55
  238.2 9.4 %collective-permute-done.53.refs_10_ = bf16[288,1024]{1,0:T(8,128)(2,1)S(1)} collective-permute-done((bf16[288,1024]{1,0:T(8,128)(2,1)S(1)}, bf16[288,1024]{1,0:T(8,128)(2,1)S(1)}, u32[]{:S(2)}, u32[]{:S(2)}) %collective-permute-start.53) | collective-permute-done | bytes 589856 | tf_op jit(solution)/shard_map/ppermute | solution.py:23
  248.1 1.5 collective-permute-done.54.refs_11_
  250.4 15.4 %hidden_units.3.refs_1_ = bf16[576,384]{1,0:T(8,128)(2,1)S(1)} custom-call(s32[1]{0:T(128)} %bitcast.refs_0_, f32[8,1,1024]{2,1,0:T(1,128)S(1)} %inverse_gains.1.refs_1_, bf16[8192,384]{1,0:T(8,128)(2,1)} %bitcast.53, bf16[8192,384]{1,0:T(8,128)(2,1)} %bitcast.58, bf16[576,1024]{1,0:T(8,128)(2,1)S(1)} %join.1.refs_4_, ...), custom_call_target="tpu_custom_call" | custom-call | flops 7247757312 | bytes 22020096 | tf_op jit(solution)/shard_map/hidden_units/pallas_call | solution.py:95
  266.6 1.4 collective-permute-start.60
  267.9 10.2 %collective-permute-done.58.refs_3_ = bf16[576,384]{1,0:T(8,128)(2,1)S(1)} collective-permute-done((bf16[576,384]{1,0:T(8,128)(2,1)S(1)}, bf16[576,384]{1,0:T(8,128)(2,1)S(1)}, u32[]{:S(2)}, u32[]{:S(2)}) %collective-permute-start.58) | collective-permute-done | bytes 442400 | tf_op jit(solution)/shard_map/ppermute | solution.py:23
  278.7 1.3 collective-permute-done.59.refs_4_
  280.6 6.5 %cross_down.2 = (bf16[576,1024]{1,0:T(8,128)(2,1)S(1)}, bf16[576,512]{1,0:T(8,128)(2,1)S(1)}, bf16[576,512]{1,0:T(8,128)(2,1)S(1)}) custom-call(s32[1]{0:T(128)} %bitcast.refs_0_, bf16[576,384]{1,0:T(8,128)(2,1)S(1)} %hidden_units.3.refs_1_, bf16[576,384]{1,0:T(8,128)(2,1)S(1)} %collective-permute-done.57.refs_2_, ...), custom_call_target="tpu_custom_call" | custom-call | flops 7247757312 | bytes 9437184 | tf_op jit(solution)/shard_map/cross_down/pallas_call | solution.py:95
  287.0 1.2 collective-permute-start.64
  289.6 12.8 %collective-permute-done.64.refs_1_ = bf16[576,512]{1,0:T(8,128)(2,1)S(1)} collective-permute-done((bf16[576,512]{1,0:T(8,128)(2,1)S(1)}, bf16[576,512]{1,0:T(8,128)(2,1)S(1)}, u32[]{:S(2)}, u32[]{:S(2)}) %collective-permute-start.64) | collective-permute-done | bytes 589856 | tf_op jit(solution)/shard_map/ppermute | solution.py:23
  303.3 1.1 settle.2
  304.4 3.0 collective-permute-start.67
  307.9 4.9 %cross_down.3 = (bf16[192,1024]{1,0:T(8,128)(2,1)S(1)}, bf16[192,512]{1,0:T(8,128)(2,1)}, bf16[192,512]{1,0:T(8,128)(2,1)}) custom-call(s32[1]{0:T(128)} %bitcast.refs_0_, bf16[192,384]{1,0:T(8,128)(2,1)S(1)} %hidden_units.2.refs_2_.refs_1_, bf16[192,384]{1,0:T(8,128)(2,1)S(1)} %collective-permute-done.40.refs_2_, ...), custom_call_target="tpu_custom_call" | custom-call | flops 2415919104 | bytes 9437184 | tf_op jit(solution)/shard_map/cross_down/pallas_call | solution.py:95
  314.5 1.1 collective-permute-start.63
  315.9 3.6 %collective-permute-done.62.refs_1_ = bf16[192,512]{1,0:T(8,128)(2,1)S(1)} collective-permute-done((bf16[192,512]{1,0:T(8,128)(2,1)}, bf16[192,512]{1,0:T(8,128)(2,1)S(1)}, u32[]{:S(2)}, u32[]{:S(2)}) %collective-permute-start.62) | collective-permute-done | bytes 196640 | tf_op jit(solution)/shard_map/ppermute | solution.py:23
  321.5 12.6 %collective-permute-done.67.refs_10_ = bf16[192,1024]{1,0:T(8,128)(2,1)} collective-permute-done((bf16[192,1024]{1,0:T(8,128)(2,1)}, bf16[192,1024]{1,0:T(8,128)(2,1)}, u32[]{:S(2)}, u32[]{:S(2)}) %collective-permute-start.67) | collective-permute-done | bytes 393248 | tf_op jit(solution)/shard_map/ppermute | solution.py:23
  334.1 7.1 %collective-permute-done.68.refs_11_ = bf16[192,1024]{1,0:T(8,128)(2,1)} collective-permute-done((bf16[192,1024]{1,0:T(8,128)(2,1)}, bf16[192,1024]{1,0:T(8,128)(2,1)}, u32[]{:S(2)}, u32[]{:S(2)}) %collective-permute-start.68) | collective-permute-done | bytes 393248 | tf_op jit(solution)/shard_map/ppermute | solution.py:23
  341.2 2.8 combine.1
  (210 shorter events, 36.2 us)
Async XLA Ops:
  7.2 124.5 %reduce-scatter.3.cloned.1.call-start = ((), (), s32[]{:S(2)}) async-start(), calls=%async_computation.2 | async-start | bytes 1310720 | tf_op jit(solution)/shard_map/reduce_scatter | solution.py:876
  8.1 3.9 %collective-permute-start = (bf16[3,4096]{1,0:T(4,128)(2,1)S(1)}, bf16[3,4096]{1,0:T(4,128)(2,1)S(1)}, u32[]{:S(2)}, u32[]{:S(2)}) collective-permute-start(bf16[3,4096]{1,0:T(4,128)(2,1)S(1)} %slice.31), channel_id=1, source_target_pairs={{0,4},{4,8},{8,12},{12,16},{16,20},{20,24},{24,28},{1,5},{5,9},{9,... | collective-permute-start | bytes 73736 | tf_op jit(solution)/shard_map/ppermute | solution.py:19
  28.7 9.4 %collective-permute-start.2 = (bf16[32,4096]{1,0:T(8,128)(2,1)}, bf16[32,4096]{1,0:T(8,128)(2,1)S(1)}, u32[]{:S(2)}, u32[]{:S(2)}) collective-permute-start(bf16[32,4096]{1,0:T(8,128)(2,1)} %get-tuple-element.36.refs_9_.refs_1_), channel_id=1, source_target_pairs={{0,8},{4,12},{8,0},{12,4},{16,24},{20,28},{24,16},{28,20},{1,9},{5... | collective-permute-start | bytes 786440 | tf_op jit(solution)/shard_map/ppermute | solution.py:23
  30.8 14.2 %collective-permute-start.4 = (bf16[32,4096]{1,0:T(8,128)(2,1)}, bf16[32,4096]{1,0:T(8,128)(2,1)S(1)}, u32[]{:S(2)}, u32[]{:S(2)}) collective-permute-start(bf16[32,4096]{1,0:T(8,128)(2,1)} %get-tuple-element.36.refs_9_.refs_1_), channel_id=1, source_target_pairs={{0,16},{4,20},{8,24},{12,28},{16,0},{20,4},{24,8},{28,12},{1,17},{... | collective-permute-start | bytes 786440 | tf_op jit(solution)/shard_map/ppermute | solution.py:23
  32.3 12.7 %collective-permute-start.6 = (bf16[32,4096]{1,0:T(8,128)(2,1)}, bf16[32,4096]{1,0:T(8,128)(2,1)S(1)}, u32[]{:S(2)}, u32[]{:S(2)}) collective-permute-start(bf16[32,4096]{1,0:T(8,128)(2,1)} %get-tuple-element.36.refs_9_.refs_1_), channel_id=1, source_target_pairs={{0,24},{4,28},{8,16},{12,20},{16,8},{20,12},{24,0},{28,4},{1,25},{... | collective-permute-start | bytes 786440 | tf_op jit(solution)/shard_map/ppermute | solution.py:23
  33.1 12.6 %collective-permute-start.1 = (bf16[32,4096]{1,0:T(8,128)(2,1)}, bf16[32,4096]{1,0:T(8,128)(2,1)S(1)}, u32[]{:S(2)}, u32[]{:S(2)}) collective-permute-start(bf16[32,4096]{1,0:T(8,128)(2,1)} %get-tuple-element.36.refs_9_.refs_1_), channel_id=1, source_target_pairs={{0,4},{4,0},{8,12},{12,8},{16,20},{20,16},{24,28},{28,24},{1,5},{5... | collective-permute-start | bytes 786440 | tf_op jit(solution)/shard_map/ppermute | solution.py:23
  38.1 7.6 %collective-permute-start.3 = (bf16[32,4096]{1,0:T(8,128)(2,1)S(1)}, bf16[32,4096]{1,0:T(8,128)(2,1)S(1)}, u32[]{:S(2)}, u32[]{:S(2)}) collective-permute-start(bf16[32,4096]{1,0:T(8,128)(2,1)S(1)} %collective-permute-done.2.refs_11_.refs_3_), channel_id=1, source_target_pairs={{0,4},{4,0},{8,12},{12,8},{16,20},{20,16},{24,28},{28,24},{1,5},{5... | collective-permute-start | bytes 786440 | tf_op jit(solution)/shard_map/ppermute | solution.py:23
  45.0 1.9 collective-permute-start.7
  57.4 15.0 %collective-permute-start.11 = (bf16[64,4096]{1,0:T(8,128)(2,1)}, bf16[64,4096]{1,0:T(8,128)(2,1)S(1)}, u32[]{:S(2)}, u32[]{:S(2)}) collective-permute-start(bf16[64,4096]{1,0:T(8,128)(2,1)} %get-tuple-element.37.refs_2_), channel_id=1, source_target_pairs={{0,16},{4,20},{8,24},{12,28},{16,0},{20,4},{24,8},{28,12},{1,17},{... | collective-permute-start | bytes 1572872 | tf_op jit(solution)/shard_map/ppermute | solution.py:23
  57.9 15.0 %collective-permute-start.9 = (bf16[64,4096]{1,0:T(8,128)(2,1)}, bf16[64,4096]{1,0:T(8,128)(2,1)S(1)}, u32[]{:S(2)}, u32[]{:S(2)}) collective-permute-start(bf16[64,4096]{1,0:T(8,128)(2,1)} %get-tuple-element.37.refs_2_), channel_id=1, source_target_pairs={{0,8},{4,12},{8,0},{12,4},{16,24},{20,28},{24,16},{28,20},{1,9},{5... | collective-permute-start | bytes 1572872 | tf_op jit(solution)/shard_map/ppermute | solution.py:23
  67.9 16.2 %collective-permute-start.17 = (bf16[64,4096]{1,0:T(8,128)(2,1)}, bf16[64,4096]{1,0:T(8,128)(2,1)S(1)}, u32[]{:S(2)}, u32[]{:S(2)}) collective-permute-start(bf16[64,4096]{1,0:T(8,128)(2,1)} %get-tuple-element.39.refs_2_), channel_id=1, source_target_pairs={{0,8},{4,12},{8,0},{12,4},{16,24},{20,28},{24,16},{28,20},{1,9},{5... | collective-permute-start | bytes 1572872 | tf_op jit(solution)/shard_map/ppermute | solution.py:23
  68.3 15.8 %collective-permute-start.18 = (bf16[64,4096]{1,0:T(8,128)(2,1)}, bf16[64,4096]{1,0:T(8,128)(2,1)S(1)}, u32[]{:S(2)}, u32[]{:S(2)}) collective-permute-start(bf16[64,4096]{1,0:T(8,128)(2,1)} %get-tuple-element.39.refs_2_), channel_id=1, source_target_pairs={{0,16},{4,20},{8,24},{12,28},{16,0},{20,4},{24,8},{28,12},{1,17},{... | collective-permute-start | bytes 1572872 | tf_op jit(solution)/shard_map/ppermute | solution.py:23
  69.9 19.1 %collective-permute-start.8 = (bf16[64,4096]{1,0:T(8,128)(2,1)S(1)}, bf16[64,4096]{1,0:T(8,128)(2,1)S(1)}, u32[]{:S(2)}, u32[]{:S(2)}) collective-permute-start(bf16[64,4096]{1,0:T(8,128)(2,1)S(1)} %copy-done.24), channel_id=1, source_target_pairs={{0,4},{4,0},{8,12},{12,8},{16,20},{20,16},{24,28},{28,24},{1,5},{5... | collective-permute-start | bytes 1572872 | tf_op jit(solution)/shard_map/ppermute | solution.py:23
  74.0 14.5 %collective-permute-start.13 = (bf16[64,2048]{1,0:T(8,128)(2,1)S(1)}, bf16[64,2048]{1,0:T(8,128)(2,1)S(1)}, u32[]{:S(2)}, u32[]{:S(2)}) collective-permute-start(bf16[64,2048]{1,0:T(8,128)(2,1)S(1)} %get-tuple-element.40), channel_id=1, source_target_pairs={{0,16},{4,20},{8,24},{12,28},{16,0},{20,4},{24,8},{28,12},{1,17},{... | collective-permute-start | bytes 786440 | tf_op jit(solution)/shard_map/ppermute | solution.py:23
  75.7 13.0 %collective-permute-start.15 = (bf16[64,2048]{1,0:T(8,128)(2,1)S(1)}, bf16[64,2048]{1,0:T(8,128)(2,1)S(1)}, u32[]{:S(2)}, u32[]{:S(2)}) collective-permute-start(bf16[64,2048]{1,0:T(8,128)(2,1)S(1)} %get-tuple-element.41), channel_id=1, source_target_pairs={{0,8},{4,12},{8,0},{12,4},{16,24},{20,28},{24,16},{28,20},{1,9},{5... | collective-permute-start | bytes 786440 | tf_op jit(solution)/shard_map/ppermute | solution.py:23
  84.1 6.3 %collective-permute-start.10 = (bf16[64,4096]{1,0:T(8,128)(2,1)S(1)}, bf16[64,4096]{1,0:T(8,128)(2,1)S(1)}, u32[]{:S(2)}, u32[]{:S(2)}) collective-permute-start(bf16[64,4096]{1,0:T(8,128)(2,1)S(1)} %collective-permute-done.9.refs_0_.refs_4_.refs_13_), channel_id=1, source_target_pairs={{0,4},{4,0},{8,12},{12,8},{16,20},{20,16},{24,28},{28,24},{1,5},{5... | collective-permute-start | bytes 1572872 | tf_op jit(solution)/shard_map/ppermute | solution.py:23
  84.1 6.3 %collective-permute-start.12 = (bf16[64,4096]{1,0:T(8,128)(2,1)S(1)}, bf16[64,4096]{1,0:T(8,128)(2,1)S(1)}, u32[]{:S(2)}, u32[]{:S(2)}) collective-permute-start(bf16[64,4096]{1,0:T(8,128)(2,1)S(1)} %collective-permute-done.11.refs_1_.refs_6_.refs_14_), channel_id=1, source_target_pairs={{0,4},{4,0},{8,12},{12,8},{16,20},{20,16},{24,28},{28,24},{1,5},{5... | collective-permute-start | bytes 1572872 | tf_op jit(solution)/shard_map/ppermute | solution.py:23
  98.8 53.7 %reduce-scatter.5.cloned.1.call-start = ((), (), s32[]{:S(2)}) async-start(), calls=%async_computation.3 | async-start | bytes 1310720 | tf_op jit(solution)/shard_map/reduce_scatter | solution.py:876
  99.1 8.4 %collective-permute-start.22 = (bf16[64,2048]{1,0:T(8,128)(2,1)S(1)}, bf16[64,2048]{1,0:T(8,128)(2,1)S(1)}, u32[]{:S(2)}, u32[]{:S(2)}) collective-permute-start(bf16[64,2048]{1,0:T(8,128)(2,1)S(1)} %get-tuple-element.42), channel_id=1, source_target_pairs={{0,16},{4,20},{8,24},{12,28},{16,0},{20,4},{24,8},{28,12},{1,17},{... | collective-permute-start | bytes 786440 | tf_op jit(solution)/shard_map/ppermute | solution.py:23
  100.5 8.1 %collective-permute-start.24 = (bf16[64,2048]{1,0:T(8,128)(2,1)S(1)}, bf16[64,2048]{1,0:T(8,128)(2,1)S(1)}, u32[]{:S(2)}, u32[]{:S(2)}) collective-permute-start(bf16[64,2048]{1,0:T(8,128)(2,1)S(1)} %get-tuple-element.43), channel_id=1, source_target_pairs={{0,8},{4,12},{8,0},{12,4},{16,24},{20,28},{24,16},{28,20},{1,9},{5... | collective-permute-start | bytes 786440 | tf_op jit(solution)/shard_map/ppermute | solution.py:23
  101.2 7.4 %collective-permute-start.19 = (bf16[64,4096]{1,0:T(8,128)(2,1)S(1)}, bf16[64,4096]{1,0:T(8,128)(2,1)S(1)}, u32[]{:S(2)}, u32[]{:S(2)}) collective-permute-start(bf16[64,4096]{1,0:T(8,128)(2,1)S(1)} %copy-done.21), channel_id=1, source_target_pairs={{0,4},{4,0},{8,12},{12,8},{16,20},{20,16},{24,28},{28,24},{1,5},{5... | collective-permute-start | bytes 1572872 | tf_op jit(solution)/shard_map/ppermute | solution.py:23
  101.2 7.4 %collective-permute-start.20 = (bf16[64,4096]{1,0:T(8,128)(2,1)S(1)}, bf16[64,4096]{1,0:T(8,128)(2,1)S(1)}, u32[]{:S(2)}, u32[]{:S(2)}) collective-permute-start(bf16[64,4096]{1,0:T(8,128)(2,1)S(1)} %collective-permute-done.17.refs_12_.refs_0_.refs_4_), channel_id=1, source_target_pairs={{0,4},{4,0},{8,12},{12,8},{16,20},{20,16},{24,28},{28,24},{1,5},{5... | collective-permute-start | bytes 1572872 | tf_op jit(solution)/shard_map/ppermute | solution.py:23
  101.8 6.9 %collective-permute-start.21 = (bf16[64,4096]{1,0:T(8,128)(2,1)S(1)}, bf16[64,4096]{1,0:T(8,128)(2,1)S(1)}, u32[]{:S(2)}, u32[]{:S(2)}) collective-permute-start(bf16[64,4096]{1,0:T(8,128)(2,1)S(1)} %collective-permute-done.18.refs_13_.refs_1_.refs_6_), channel_id=1, source_target_pairs={{0,4},{4,0},{8,12},{12,8},{16,20},{20,16},{24,28},{28,24},{1,5},{5... | collective-permute-start | bytes 1572872 | tf_op jit(solution)/shard_map/ppermute | solution.py:23
  126.2 38.4 %collective-permute-start.28 = (bf16[384,2048]{1,0:T(8,128)(2,1)}, bf16[384,2048]{1,0:T(8,128)(2,1)S(1)}, u32[]{:S(2)}, u32[]{:S(2)}) collective-permute-start(bf16[384,2048]{1,0:T(8,128)(2,1)} %get-tuple-element.46), channel_id=1, source_target_pairs={{0,4},{4,0},{8,12},{12,8},{16,20},{20,16},{24,28},{28,24},{1,5},{5... | collective-permute-start | bytes 4718600 | tf_op jit(solution)/shard_map/ppermute | solution.py:23
  126.8 29.1 %collective-permute-start.26 = (bf16[384,1024]{1,0:T(8,128)(2,1)}, bf16[384,1024]{1,0:T(8,128)(2,1)S(1)}, u32[]{:S(2)}, u32[]{:S(2)}) collective-permute-start(bf16[384,1024]{1,0:T(8,128)(2,1)} %get-tuple-element.44), channel_id=1, source_target_pairs={{0,12},{4,8},{8,4},{12,0},{16,28},{20,24},{24,20},{28,16},{1,13},{... | collective-permute-start | bytes 2359304 | tf_op jit(solution)/shard_map/ppermute | solution.py:23
  127.6 28.3 %collective-permute-start.27 = (bf16[384,1024]{1,0:T(8,128)(2,1)}, bf16[384,1024]{1,0:T(8,128)(2,1)S(1)}, u32[]{:S(2)}, u32[]{:S(2)}) collective-permute-start(bf16[384,1024]{1,0:T(8,128)(2,1)} %get-tuple-element.45), channel_id=1, source_target_pairs={{0,20},{4,16},{8,28},{12,24},{16,4},{20,0},{24,12},{28,8},{1,21},{... | collective-permute-start | bytes 2359304 | tf_op jit(solution)/shard_map/ppermute | solution.py:23
  128.7 35.2 %collective-permute-start.29 = (bf16[384,1024]{1,0:T(8,128)(2,1)}, bf16[384,1024]{1,0:T(8,128)(2,1)}, u32[]{:S(2)}, u32[]{:S(2)}) collective-permute-start(bf16[384,1024]{1,0:T(8,128)(2,1)} %get-tuple-element.47), channel_id=1, source_target_pairs={{0,8},{4,12},{8,0},{12,4},{16,24},{20,28},{24,16},{28,20},{1,9},{5... | collective-permute-start | bytes 2359304 | tf_op jit(solution)/shard_map/ppermute | solution.py:23
  129.3 35.3 %collective-permute-start.30 = (bf16[384,1024]{1,0:T(8,128)(2,1)}, bf16[384,1024]{1,0:T(8,128)(2,1)}, u32[]{:S(2)}, u32[]{:S(2)}) collective-permute-start(bf16[384,1024]{1,0:T(8,128)(2,1)} %get-tuple-element.48), channel_id=1, source_target_pairs={{0,16},{4,20},{8,24},{12,28},{16,0},{20,4},{24,8},{28,12},{1,17},{... | collective-permute-start | bytes 2359304 | tf_op jit(solution)/shard_map/ppermute | solution.py:23
  165.2 10.9 %collective-permute-start.32 = (bf16[192,1024]{1,0:T(8,128)(2,1)S(1)}, bf16[192,1024]{1,0:T(8,128)(2,1)S(1)}, u32[]{:S(2)}, u32[]{:S(2)}) collective-permute-start(bf16[192,1024]{1,0:T(8,128)(2,1)S(1)} %get-tuple-element.49.refs_4_), channel_id=1, source_target_pairs={{0,8},{4,12},{8,0},{12,4},{16,24},{20,28},{24,16},{28,20},{1,9},{5... | collective-permute-start | bytes 1179656 | tf_op jit(solution)/shard_map/ppermute | solution.py:23
  166.6 10.5 %collective-permute-start.34 = (bf16[192,1024]{1,0:T(8,128)(2,1)S(1)}, bf16[192,1024]{1,0:T(8,128)(2,1)S(1)}, u32[]{:S(2)}, u32[]{:S(2)}) collective-permute-start(bf16[192,1024]{1,0:T(8,128)(2,1)S(1)} %get-tuple-element.49.refs_4_), channel_id=1, source_target_pairs={{0,16},{4,20},{8,24},{12,28},{16,0},{20,4},{24,8},{28,12},{1,17},{... | collective-permute-start | bytes 1179656 | tf_op jit(solution)/shard_map/ppermute | solution.py:23
  167.3 15.5 %collective-permute-start.45 = (bf16[192,1024]{1,0:T(8,128)(2,1)S(1)}, bf16[192,1024]{1,0:T(8,128)(2,1)S(1)}, u32[]{:S(2)}, u32[]{:S(2)}) collective-permute-start(bf16[192,1024]{1,0:T(8,128)(2,1)S(1)} %get-tuple-element.52), channel_id=1, source_target_pairs={{0,1},{1,0},{2,3},{3,2},{4,5},{5,4},{6,7},{7,6},{8,9},{9,8},{10,11... | collective-permute-start | bytes 1179656 | tf_op jit(solution)/shard_map/ppermute | solution.py:23
  167.7 29.1 %collective-permute-start.46 = (bf16[192,1024]{1,0:T(8,128)(2,1)S(1)}, bf16[192,1024]{1,0:T(8,128)(2,1)S(1)}, u32[]{:S(2)}, u32[]{:S(2)}) collective-permute-start(bf16[192,1024]{1,0:T(8,128)(2,1)S(1)} %get-tuple-element.53), channel_id=1, source_target_pairs={{0,2},{1,3},{2,0},{3,1},{4,6},{5,7},{6,4},{7,5},{8,10},{9,11},{10,... | collective-permute-start | bytes 1179656 | tf_op jit(solution)/shard_map/ppermute | solution.py:23
  170.3 33.7 %collective-permute-start.47 = (bf16[192,1024]{1,0:T(8,128)(2,1)S(1)}, bf16[192,1024]{1,0:T(8,128)(2,1)S(1)}, u32[]{:S(2)}, u32[]{:S(2)}) collective-permute-start(bf16[192,1024]{1,0:T(8,128)(2,1)S(1)} %get-tuple-element.54), channel_id=1, source_target_pairs={{0,3},{1,2},{2,1},{3,0},{4,7},{5,6},{6,5},{7,4},{8,11},{9,10},{10,... | collective-permute-start | bytes 1179656 | tf_op jit(solution)/shard_map/ppermute | solution.py:23
  177.3 26.8 %collective-permute-start.36 = (bf16[96,1024]{1,0:T(8,128)(2,1)S(1)}, bf16[96,1024]{1,0:T(8,128)(2,1)S(1)}, u32[]{:S(2)}, u32[]{:S(2)}) collective-permute-start(bf16[96,1024]{1,0:T(8,128)(2,1)S(1)} %get-tuple-element.50), channel_id=1, source_target_pairs={{0,16},{4,20},{8,24},{12,28},{16,0},{20,4},{24,8},{28,12},{1,17},{... | collective-permute-start | bytes 589832 | tf_op jit(solution)/shard_map/ppermute | solution.py:23
  178.0 26.1 %collective-permute-start.38 = (bf16[96,1024]{1,0:T(8,128)(2,1)S(1)}, bf16[96,1024]{1,0:T(8,128)(2,1)S(1)}, u32[]{:S(2)}, u32[]{:S(2)}) collective-permute-start(bf16[96,1024]{1,0:T(8,128)(2,1)S(1)} %get-tuple-element.51), channel_id=1, source_target_pairs={{0,8},{4,12},{8,0},{12,4},{16,24},{20,28},{24,16},{28,20},{1,9},{5... | collective-permute-start | bytes 589832 | tf_op jit(solution)/shard_map/ppermute | solution.py:23
  204.6 28.0 %collective-permute-start.49 = (bf16[576,1024]{1,0:T(8,128)(2,1)S(1)}, bf16[576,1024]{1,0:T(8,128)(2,1)S(1)}, u32[]{:S(2)}, u32[]{:S(2)}) collective-permute-start(bf16[576,1024]{1,0:T(8,128)(2,1)S(1)} %join.1.refs_4_), channel_id=1, source_target_pairs={{0,8},{4,12},{8,0},{12,4},{16,24},{20,28},{24,16},{28,20},{1,9},{5... | collective-permute-start | bytes 3538952 | tf_op jit(solution)/shard_map/ppermute | solution.py:23
  206.1 28.9 %collective-permute-start.51 = (bf16[576,1024]{1,0:T(8,128)(2,1)S(1)}, bf16[576,1024]{1,0:T(8,128)(2,1)S(1)}, u32[]{:S(2)}, u32[]{:S(2)}) collective-permute-start(bf16[576,1024]{1,0:T(8,128)(2,1)S(1)} %join.1.refs_4_), channel_id=1, source_target_pairs={{0,16},{4,20},{8,24},{12,28},{16,0},{20,4},{24,8},{28,12},{1,17},{... | collective-permute-start | bytes 3538952 | tf_op jit(solution)/shard_map/ppermute | solution.py:23
  206.8 2.0 collective-permute-start.37
  207.3 3.2 collective-permute-start.33
  208.5 2.0 collective-permute-start.35
  217.3 19.8 %collective-permute-start.41 = (bf16[192,384]{1,0:T(8,128)(2,1)S(1)}, bf16[192,384]{1,0:T(8,128)(2,1)S(1)}, u32[]{:S(2)}, u32[]{:S(2)}) collective-permute-start(bf16[192,384]{1,0:T(8,128)(2,1)S(1)} %hidden_units.2.refs_2_.refs_1_), channel_id=1, source_target_pairs={{0,8},{4,12},{8,0},{12,4},{16,24},{20,28},{24,16},{28,20},{1,9},{5... | collective-permute-start | bytes 442376 | tf_op jit(solution)/shard_map/ppermute | solution.py:23
  218.7 19.4 %collective-permute-start.43 = (bf16[192,384]{1,0:T(8,128)(2,1)S(1)}, bf16[192,384]{1,0:T(8,128)(2,1)S(1)}, u32[]{:S(2)}, u32[]{:S(2)}) collective-permute-start(bf16[192,384]{1,0:T(8,128)(2,1)S(1)} %hidden_units.2.refs_2_.refs_1_), channel_id=1, source_target_pairs={{0,16},{4,20},{8,24},{12,28},{16,0},{20,4},{24,8},{28,12},{1,17},{... | collective-permute-start | bytes 442376 | tf_op jit(solution)/shard_map/ppermute | solution.py:23
  219.4 28.7 %collective-permute-start.48 = (bf16[576,1024]{1,0:T(8,128)(2,1)S(1)}, bf16[576,1024]{1,0:T(8,128)(2,1)S(1)}, u32[]{:S(2)}, u32[]{:S(2)}) collective-permute-start(bf16[576,1024]{1,0:T(8,128)(2,1)S(1)} %join.1.refs_4_), channel_id=1, source_target_pairs={{0,4},{4,0},{8,12},{12,8},{16,20},{20,16},{24,28},{28,24},{1,5},{5... | collective-permute-start | bytes 3538952 | tf_op jit(solution)/shard_map/ppermute | solution.py:23
  235.1 12.5 %collective-permute-start.53 = (bf16[288,1024]{1,0:T(8,128)(2,1)S(1)}, bf16[288,1024]{1,0:T(8,128)(2,1)S(1)}, u32[]{:S(2)}, u32[]{:S(2)}) collective-permute-start(bf16[288,1024]{1,0:T(8,128)(2,1)S(1)} %get-tuple-element.55), channel_id=1, source_target_pairs={{0,16},{4,20},{8,24},{12,28},{16,0},{20,4},{24,8},{28,12},{1,17},{... | collective-permute-start | bytes 1769480 | tf_op jit(solution)/shard_map/ppermute | solution.py:23
  235.8 11.8 %collective-permute-start.55 = (bf16[288,1024]{1,0:T(8,128)(2,1)S(1)}, bf16[288,1024]{1,0:T(8,128)(2,1)S(1)}, u32[]{:S(2)}, u32[]{:S(2)}) collective-permute-start(bf16[288,1024]{1,0:T(8,128)(2,1)S(1)} %get-tuple-element.56), channel_id=1, source_target_pairs={{0,8},{4,12},{8,0},{12,4},{16,24},{20,28},{24,16},{28,20},{1,9},{5... | collective-permute-start | bytes 1769480 | tf_op jit(solution)/shard_map/ppermute | solution.py:23
  237.2 13.3 %collective-permute-start.50 = (bf16[576,1024]{1,0:T(8,128)(2,1)S(1)}, bf16[576,1024]{1,0:T(8,128)(2,1)S(1)}, u32[]{:S(2)}, u32[]{:S(2)}) collective-permute-start(bf16[576,1024]{1,0:T(8,128)(2,1)S(1)} %collective-permute-done.49.refs_0_.refs_6_), channel_id=1, source_target_pairs={{0,4},{4,0},{8,12},{12,8},{16,20},{20,16},{24,28},{28,24},{1,5},{5... | collective-permute-start | bytes 3538952 | tf_op jit(solution)/shard_map/ppermute | solution.py:23
  238.2 12.3 %collective-permute-start.52 = (bf16[576,1024]{1,0:T(8,128)(2,1)S(1)}, bf16[576,1024]{1,0:T(8,128)(2,1)S(1)}, u32[]{:S(2)}, u32[]{:S(2)}) collective-permute-start(bf16[576,1024]{1,0:T(8,128)(2,1)S(1)} %collective-permute-done.51.refs_1_.refs_8_), channel_id=1, source_target_pairs={{0,4},{4,0},{8,12},{12,8},{16,20},{20,16},{24,28},{28,24},{1,5},{5... | collective-permute-start | bytes 3538952 | tf_op jit(solution)/shard_map/ppermute | solution.py:23
  247.6 2.0 collective-permute-start.54
  247.6 2.8 collective-permute-start.56
  265.9 12.3 %collective-permute-start.58 = (bf16[576,384]{1,0:T(8,128)(2,1)S(1)}, bf16[576,384]{1,0:T(8,128)(2,1)S(1)}, u32[]{:S(2)}, u32[]{:S(2)}) collective-permute-start(bf16[576,384]{1,0:T(8,128)(2,1)S(1)} %hidden_units.3.refs_1_), channel_id=1, source_target_pairs={{0,8},{4,12},{8,0},{12,4},{16,24},{20,28},{24,16},{28,20},{1,9},{5... | collective-permute-start | bytes 1327112 | tf_op jit(solution)/shard_map/ppermute | solution.py:23
  266.6 11.9 %collective-permute-start.60 = (bf16[576,384]{1,0:T(8,128)(2,1)S(1)}, bf16[576,384]{1,0:T(8,128)(2,1)S(1)}, u32[]{:S(2)}, u32[]{:S(2)}) collective-permute-start(bf16[576,384]{1,0:T(8,128)(2,1)S(1)} %hidden_units.3.refs_1_), channel_id=1, source_target_pairs={{0,16},{4,20},{8,24},{12,28},{16,0},{20,4},{24,8},{28,12},{1,17},{... | collective-permute-start | bytes 1327112 | tf_op jit(solution)/shard_map/ppermute | solution.py:23
  267.9 10.7 %collective-permute-start.57 = (bf16[576,384]{1,0:T(8,128)(2,1)S(1)}, bf16[576,384]{1,0:T(8,128)(2,1)S(1)}, u32[]{:S(2)}, u32[]{:S(2)}) collective-permute-start(bf16[576,384]{1,0:T(8,128)(2,1)S(1)} %hidden_units.3.refs_1_), channel_id=1, source_target_pairs={{0,4},{4,0},{8,12},{12,8},{16,20},{20,16},{24,28},{28,24},{1,5},{5... | collective-permute-start | bytes 1327112 | tf_op jit(solution)/shard_map/ppermute | solution.py:23
  278.1 1.8 collective-permute-start.59
  278.5 2.1 collective-permute-start.61
  287.0 15.4 %collective-permute-start.64 = (bf16[576,512]{1,0:T(8,128)(2,1)S(1)}, bf16[576,512]{1,0:T(8,128)(2,1)S(1)}, u32[]{:S(2)}, u32[]{:S(2)}) collective-permute-start(bf16[576,512]{1,0:T(8,128)(2,1)S(1)} %get-tuple-element.61), channel_id=1, source_target_pairs={{0,16},{4,20},{8,24},{12,28},{16,0},{20,4},{24,8},{28,12},{1,17},{... | collective-permute-start | bytes 1769480 | tf_op jit(solution)/shard_map/ppermute | solution.py:23
  288.2 15.1 %collective-permute-start.65 = (bf16[576,512]{1,0:T(8,128)(2,1)S(1)}, bf16[576,512]{1,0:T(8,128)(2,1)S(1)}, u32[]{:S(2)}, u32[]{:S(2)}) collective-permute-start(bf16[576,512]{1,0:T(8,128)(2,1)S(1)} %get-tuple-element.62), channel_id=1, source_target_pairs={{0,8},{4,12},{8,0},{12,4},{16,24},{20,28},{24,16},{28,20},{1,9},{5... | collective-permute-start | bytes 1769480 | tf_op jit(solution)/shard_map/ppermute | solution.py:23
  289.1 18.3 %collective-permute-start.40 = (bf16[192,384]{1,0:T(8,128)(2,1)S(1)}, bf16[192,384]{1,0:T(8,128)(2,1)S(1)}, u32[]{:S(2)}, u32[]{:S(2)}) collective-permute-start(bf16[192,384]{1,0:T(8,128)(2,1)S(1)} %hidden_units.2.refs_2_.refs_1_), channel_id=1, source_target_pairs={{0,4},{4,0},{8,12},{12,8},{16,20},{20,16},{24,28},{28,24},{1,5},{5... | collective-permute-start | bytes 442376 | tf_op jit(solution)/shard_map/ppermute | solution.py:23
  289.1 18.8 %collective-permute-start.42 = (bf16[192,384]{1,0:T(8,128)(2,1)S(1)}, bf16[192,384]{1,0:T(8,128)(2,1)S(1)}, u32[]{:S(2)}, u32[]{:S(2)}) collective-permute-start(bf16[192,384]{1,0:T(8,128)(2,1)S(1)} %collective-permute-done.41.refs_14_.refs_3_), channel_id=1, source_target_pairs={{0,4},{4,0},{8,12},{12,8},{16,20},{20,16},{24,28},{28,24},{1,5},{5... | collective-permute-start | bytes 442376 | tf_op jit(solution)/shard_map/ppermute | solution.py:23
  289.6 18.3 %collective-permute-start.44 = (bf16[192,384]{1,0:T(8,128)(2,1)S(1)}, bf16[192,384]{1,0:T(8,128)(2,1)S(1)}, u32[]{:S(2)}, u32[]{:S(2)}) collective-permute-start(bf16[192,384]{1,0:T(8,128)(2,1)S(1)} %collective-permute-done.43.refs_15_.refs_5_), channel_id=1, source_target_pairs={{0,4},{4,0},{8,12},{12,8},{16,20},{20,16},{24,28},{28,24},{1,5},{5... | collective-permute-start | bytes 442376 | tf_op jit(solution)/shard_map/ppermute | solution.py:23
  304.4 17.1 %collective-permute-start.66 = (bf16[192,1024]{1,0:T(8,128)(2,1)}, bf16[192,1024]{1,0:T(8,128)(2,1)}, u32[]{:S(2)}, u32[]{:S(2)}) collective-permute-start(bf16[192,1024]{1,0:T(8,128)(2,1)} %get-tuple-element.63.refs_3_), channel_id=1, source_target_pairs={{0,1},{1,0},{2,3},{3,2},{4,5},{5,4},{6,7},{7,6},{8,9},{9,8},{10,11... | collective-permute-start | bytes 1179656 | tf_op jit(solution)/shard_map/ppermute | solution.py:23
  304.4 29.7 %collective-permute-start.67 = (bf16[192,1024]{1,0:T(8,128)(2,1)}, bf16[192,1024]{1,0:T(8,128)(2,1)}, u32[]{:S(2)}, u32[]{:S(2)}) collective-permute-start(bf16[192,1024]{1,0:T(8,128)(2,1)} %get-tuple-element.64.refs_4_), channel_id=1, source_target_pairs={{0,2},{1,3},{2,0},{3,1},{4,6},{5,7},{6,4},{7,5},{8,10},{9,11},{10,... | collective-permute-start | bytes 1179656 | tf_op jit(solution)/shard_map/ppermute | solution.py:23
  307.4 33.9 %collective-permute-start.68 = (bf16[192,1024]{1,0:T(8,128)(2,1)}, bf16[192,1024]{1,0:T(8,128)(2,1)}, u32[]{:S(2)}, u32[]{:S(2)}) collective-permute-start(bf16[192,1024]{1,0:T(8,128)(2,1)} %get-tuple-element.65.refs_5_), channel_id=1, source_target_pairs={{0,3},{1,2},{2,1},{3,0},{4,7},{5,6},{6,5},{7,4},{8,11},{9,10},{10,... | collective-permute-start | bytes 1179656 | tf_op jit(solution)/shard_map/ppermute | solution.py:23
  313.5 5.9 %collective-permute-start.62 = (bf16[192,512]{1,0:T(8,128)(2,1)}, bf16[192,512]{1,0:T(8,128)(2,1)S(1)}, u32[]{:S(2)}, u32[]{:S(2)}) collective-permute-start(bf16[192,512]{1,0:T(8,128)(2,1)} %get-tuple-element.59), channel_id=1, source_target_pairs={{0,16},{4,20},{8,24},{12,28},{16,0},{20,4},{24,8},{28,12},{1,17},{... | collective-permute-start | bytes 589832 | tf_op jit(solution)/shard_map/ppermute | solution.py:23
  314.5 5.9 %collective-permute-start.63 = (bf16[192,512]{1,0:T(8,128)(2,1)}, bf16[192,512]{1,0:T(8,128)(2,1)S(1)}, u32[]{:S(2)}, u32[]{:S(2)}) collective-permute-start(bf16[192,512]{1,0:T(8,128)(2,1)} %get-tuple-element.60), channel_id=1, source_target_pairs={{0,8},{4,12},{8,0},{12,4},{16,24},{20,28},{24,16},{28,20},{1,9},{5... | collective-permute-start | bytes 589832 | tf_op jit(solution)/shard_map/ppermute | solution.py:23
  (40 other events, 696.8 us)
Sparse Core Ops, SparseCore 0:
  98.9 25.2 reduce-scatter.2
  126.7 25.7 reduce-scatter.4

commit v9 on v8

--- a/solution.py
+++ b/solution.py
@@ -616,7 +616,7 @@
     )
 
 
-def cross_kernel(me, *refs):
+def cross_kernel(begin, me, *refs):
     units, (own, *sent), refs = refs[:6], refs[6:12], refs[12:]
     keep, give_a, give_b, held, sems = refs
     width = own.shape[0]
@@ -628,7 +628,11 @@
         for mask, unit in enumerate(units):
             column = (2, 3, 0, 1, 4, 5)[mask] * width
             copies.append(
-                pltpu.make_async_copy(unit, held.at[:, pl.ds(column, width)], sems.at[mask])
+                pltpu.make_async_copy(
+                    unit.at[pl.ds(begin, held.shape[0]), :],
+                    held.at[:, pl.ds(column, width)],
+                    sems.at[mask],
+                )
             )
         for copy in copies:
             copy.start()
@@ -650,10 +654,9 @@
                 out[...] = summed(2, [own, sent[0], sent[3], sent[4]])
 
 
-def cross_down(me, units, weights, own, after=()):
+def cross_down(me, units, begin, slots, weights, own, after=()):
     width = own.shape[0]
     half = weights[2].shape[1] // 2
-    slots = units[0].shape[0]
 
     def mine(j, me):
         return (0, (me[0] ^ (jnp.where(j == 1, 4, 0) + jnp.where(j == 3, 2, 0))) * 2 + j // 2)
@@ -662,7 +665,7 @@
     back = pl.BlockSpec((width, half), lambda j, me: (0, jnp.maximum(j - 2, 0)))
     given = pl.BlockSpec((slots, half), lambda j, me: (0, 0))
     return launch(
-        cross_kernel,
+        functools.partial(cross_kernel, begin),
         [me],
         [units[mask] for mask in range(6)] + [own] + [weights[mask] for mask in range(1, 6)],
         [ANY] * 6
@@ -825,7 +828,7 @@
             cuts = cut_columns(me, down_rows, width, [[(m, 0)] for m in masks], after)
         for mask, cut in zip(masks, cuts):
             down_parts[mask] = swap(cut, "ctx", mask)
-        return tuple(down_parts[mask] for mask in masks)
+        return cuts, tuple(down_parts[mask] for mask in masks)
 
 
     extra, left = [], norm_gain
@@ -875,11 +878,11 @@
     far = lambda parts: [part for mask, which, part in parts if which is not None][::2]
     scatter = lambda rows: lax.psum_scatter(rows, "exp", scatter_dimension=0, tiled=True)
     front = gather_parts(gated[0], 1, gated[1:])
-    late = send_columns([3, 5, 1, 2, 4] if crossing else list(range(1, ctx_count)), near(front))
+    cuts, late = send_columns([3, 5, 1, 2, 4] if crossing else list(range(1, ctx_count)), near(front))
     back = gather_parts(gated[1], 1, far(front))
     partial = project(me, front, out_proj, near(back))
     projected = [scatter(partial)]
-    partial = project(me, back, out_proj, [partial])
+    partial = project(me, back, out_proj, [partial, cuts[0]])
     projected.append(scatter(partial))
 
     block_rows = residual.shape[0]
@@ -922,16 +925,26 @@
             units = gather_parts(hidden)
         gathered_units.append(units)
     answers, order, before = {}, (), ()
-    for group, units in list(zip(groups, gathered_units))[::-1]:
+    if crossing:
+        far_masks = list(range(2, exp_count))
+        work = [
+            (gathered_units[1], capacity, far_masks),
+            (gathered_units[1], 0, [1]),
+            (gathered_units[0], 0, [0]),
+        ]
+    else:
+        work = [(gathered_units[1], 0, groups[1]), (gathered_units[0], 0, groups[0])]
+    for units, begin, masks in work:
         if crossing:
-            keep, first, second = cross_down(me, units, weights, down_rows, order)
+            slots = capacity * len(masks)
+            keep, first, second = cross_down(me, units, begin, slots, weights, down_rows, order)
             first, second = swap(first, "ctx", 4), swap(second, "ctx", 2)
-            before = settle(keep, first, second, len(group), before)
+            before = settle(keep, first, second, len(masks), before)
         else:
             keep = down(me, units, weights, down_rows, order)
-            before = jnp.split(keep, len(group))
-        order = [keep]
-        for mask, piece in zip(group, before):
+            before = jnp.split(keep, len(masks))
+        order = [keep] if order else list(before)
+        for mask, piece in zip(masks, before):
             answers[mask] = piece if mask == 0 else swap(piece, "exp", mask)
     block_out = combine(
         exp_me.astype(jnp.int32).reshape(1),

time: 352 us -> 352 us (level)
  waiting for transfers between devices: 179 us -> 174 us
    ppermute x68 -> x70, waiting for transfers between devices: 159 us -> 152 us  [swap(): lax.ppermute(array, axis, [(i, i ^ mask) for i in range(lax.axis_size(axi...]
    pallas_call x20 -> x22, Pallas kernels: 92.5 us -> 95.9 us  [launch(): pl.pallas_call(body, grid_spec=pltpu.PrefetchScalarGridSpec(num_scalar_pr...]
    ppermute x68 -> x70, starting transfers between devices: 44.9 us -> 47.3 us  [swap(): lax.ppermute(array, axis, [(i, i ^ mask) for i in range(lax.axis_size(axi...]
  transfers between devices with their start and end apart: 71 -> 73, of which waited for: 42 -> 42; matrix products, arithmetic and copies ran while one was open for 3% -> 3% of each run, Pallas kernels for 10% -> 10%
where the time goes in v9:
time: 352 us; the launch traced here: 351 us
  waiting for transfers between devices  174 us (49%)
  Pallas kernels  95.9 us (27%)
  starting transfers between devices  49.3 us (14%)
  between operations  14.7 us (4%)
  other arithmetic  8.89 us (3%)
  local copies, waits for them, and re-layouts  8.55 us (2%)
    ppermute x70, waiting for transfers between devices, swap(): lax.ppermute(array, axis, [(i, i ^ mask) for i in range(lax.axis_size(axi...  152 us
    pallas_call x22, Pallas kernels, launch(): pl.pallas_call(body, grid_spec=pltpu.PrefetchScalarGridSpec(num_scalar_pr...  95.9 us
    ppermute x70, starting transfers between devices, swap(): lax.ppermute(array, axis, [(i, i ^ mask) for i in range(lax.axis_size(axi...  47.3 us
    reduce_scatter x2, waiting for transfers between devices, shards(): lax.psum_scatter(rows, 'exp', scatter_dimension=0, tiled=True)  22 us
  transfers between devices with their start and end apart: 73, of which 42 were waited for; matrix products, arithmetic and copies ran while one was open for 3% of the time, Pallas kernels for 10%

profile of v9, /device:TPU:8, one launch (start us, length us, event | category | flops | bytes accessed | tf_op | source)
XLA Modules:
  0.0 351.4 jit_solution(5998433578824484097)
XLA Ops:
  8.1 1.7 collective-permute-start
  13.5 1.3 broadcast_in_dim.20.refs_8_.refs_6_
  14.8 13.9 %local_states.1 = (f32[128,4096]{1,0:T(8,128)}, f32[128,4096]{1,0:T(8,128)}, bf16[32,4096]{1,0:T(8,128)(2,1)}) custom-call(bf16[128,4096]{1,0:T(8,128)(2,1)} %refs_0_.1, f32[8,4096]{1,0:T(8,128)} %pad_convert_fusion.refs_1_, bf16[128,4096]{1,0:T(8,128)(2,1)} %refs_2_.2, f32[4,4096]{1,0:T(4,128)} %refs_3_.4, f32[1,4096]{1,0:T(1,128)} %bitcast.67, ...), custom_call_target="tpu_custom_call" | custom-call | flops 41943040 | bytes 6291456 | tf_op jit(solution)/shard_map/local_states/pallas_call | solution.py:95
  28.7 2.1 collective-permute-start.2
  30.8 1.5 collective-permute-start.4
  33.2 4.9 %collective-permute-done.2.refs_11_.refs_3_ = bf16[32,4096]{1,0:T(8,128)(2,1)S(1)} collective-permute-done((bf16[32,4096]{1,0:T(8,128)(2,1)}, bf16[32,4096]{1,0:T(8,128)(2,1)S(1)}, u32[]{:S(2)}, u32[]{:S(2)}) %collective-permute-start.2) | collective-permute-done | bytes 262176 | tf_op jit(solution)/shard_map/ppermute | solution.py:23
  38.3 6.7 %collective-permute-done.4.refs_13_.refs_5_ = bf16[32,4096]{1,0:T(8,128)(2,1)S(1)} collective-permute-done((bf16[32,4096]{1,0:T(8,128)(2,1)}, bf16[32,4096]{1,0:T(8,128)(2,1)S(1)}, u32[]{:S(2)}, u32[]{:S(2)}) %collective-permute-start.4) | collective-permute-done | bytes 262176 | tf_op jit(solution)/shard_map/ppermute | solution.py:23
  47.0 1.3 broadcast_in_dim.23.refs_7_
  48.3 9.1 %read_out.2 = (bf16[64,4096]{1,0:T(8,128)(2,1)}, f32[16,4096]{1,0:T(8,128)}) custom-call(s32[1]{0:T(128)} %bitcast.refs_0_, f32[128,4096]{1,0:T(8,128)} %get-tuple-element.36.refs_1_, f32[128,4096]{1,0:T(8,128)} %get-tuple-element.37.refs_2_, bf16[128,4096]{1,0:T(8,128)(2,1)} %refs_3_.6, f32[16,4096]{1,0:T(8,128)} %refs_4_.3, f32[1,4096]{1,0:T(1,128)} %bitcast.62, ...), custom_call_target="tpu_custom_call" | custom-call | flops 29360128 | bytes 3145728 | tf_op jit(solution)/shard_map/read_out/pallas_call | solution.py:95
  57.9 1.7 collective-permute-start.9
  59.6 8.4 %read_out.3 = (bf16[64,4096]{1,0:T(8,128)(2,1)}, f32[16,4096]{1,0:T(8,128)}) custom-call(s32[1]{0:T(128)} %bitcast.refs_0_, f32[128,4096]{1,0:T(8,128)} %get-tuple-element.36.refs_1_, f32[128,4096]{1,0:T(8,128)} %get-tuple-element.37.refs_2_, bf16[128,4096]{1,0:T(8,128)(2,1)} %refs_3_.6, f32[16,4096]{1,0:T(8,128)} %refs_4_.3, f32[1,4096]{1,0:T(1,128)} %bitcast.63, ...), custom_call_target="tpu_custom_call" | custom-call | flops 29360128 | bytes 3145728 | tf_op jit(solution)/shard_map/read_out/pallas_call | solution.py:95
  68.3 1.6 collective-permute-start.18
  70.0 2.5 collective-permute-done.11.refs_1_.refs_6_.refs_14_
  74.0 1.7 collective-permute-start.13
  76.2 7.9 %collective-permute-done.17.refs_12_.refs_0_.refs_4_ = bf16[64,4096]{1,0:T(8,128)(2,1)S(1)} collective-permute-done((bf16[64,4096]{1,0:T(8,128)(2,1)}, bf16[64,4096]{1,0:T(8,128)(2,1)S(1)}, u32[]{:S(2)}, u32[]{:S(2)}) %collective-permute-start.17) | collective-permute-done | bytes 524320 | tf_op jit(solution)/shard_map/ppermute | solution.py:23
  84.7 3.9 %collective-permute-done.13.refs_8_.refs_2_ = bf16[64,2048]{1,0:T(8,128)(2,1)S(1)} collective-permute-done((bf16[64,2048]{1,0:T(8,128)(2,1)S(1)}, bf16[64,2048]{1,0:T(8,128)(2,1)S(1)}, u32[]{:S(2)}, u32[]{:S(2)}) %collective-permute-start.13) | collective-permute-done | bytes 262176 | tf_op jit(solution)/shard_map/ppermute | solution.py:23
  90.5 8.3 %project.2.refs_12_ = bf16[512,1024]{1,0:T(8,128)(2,1)} custom-call(s32[1]{0:T(128)} %bitcast.refs_0_, bf16[4096,1024]{1,0:T(8,128)(2,1)} %refs_1_.3, bf16[64,4096]{1,0:T(8,128)(2,1)S(1)} %copy-done.30, bf16[64,4096]{1,0:T(8,128)(2,1)S(1)} %collective-permute-done.8.refs_3_, bf16[64,4096]{1,0:T(8,128)(2,1)S(1)} %collective-permute-done.9.refs_0_.refs_4_.refs_13_, ...), custom_call_target="tpu_custom_call" | custom-call | flops 4294967296 | bytes 13631488 | tf_op jit(solution)/shard_map/project/pallas_call | solution.py:95
  99.1 1.4 collective-permute-start.22
  101.8 5.7 %collective-permute-done.22.refs_8_ = bf16[64,2048]{1,0:T(8,128)(2,1)S(1)} collective-permute-done((bf16[64,2048]{1,0:T(8,128)(2,1)S(1)}, bf16[64,2048]{1,0:T(8,128)(2,1)S(1)}, u32[]{:S(2)}, u32[]{:S(2)}) %collective-permute-start.22) | collective-permute-done | bytes 262176 | tf_op jit(solution)/shard_map/ppermute | solution.py:23
  107.5 1.1 collective-permute-done.24.refs_10_
  108.6 5.5 %cut_columns.1 = (bf16[384,1024]{1,0:T(8,128)(2,1)}, bf16[384,1024]{1,0:T(8,128)(2,1)}, bf16[384,2048]{1,0:T(8,128)(2,1)}, bf16[384,1024]{1,0:T(8,128)(2,1)}, bf16[384,1024]{1,0:T(8,128)(2,1)}) custom-call(s32[1]{0:T(128)} %bitcast.refs_0_, bf16[384,8192]{1,0:T(8,128)(2,1)} %bitcast.37, bf16[384,8192]{1,0:T(8,128)(2,1)} %bitcast.38, ...), custom_call_target="tpu_custom_call" | custom-call | bytes 9437184 | tf_op jit(solution)/shard_map/cut_columns/pallas_call | solution.py:95
  114.2 8.4 %project.3 = bf16[512,1024]{1,0:T(8,128)(2,1)} custom-call(s32[1]{0:T(128)} %bitcast.refs_0_, bf16[4096,1024]{1,0:T(8,128)(2,1)} %refs_1_.3, bf16[64,4096]{1,0:T(8,128)(2,1)S(1)} %copy-done.27, bf16[64,4096]{1,0:T(8,128)(2,1)S(1)} %collective-permute-done.19.refs_3_, bf16[64,4096]{1,0:T(8,128)(2,1)S(1)} %collective-permute-done.17.refs_12_.refs_0_.refs_4_, ...), custom_call_target="tpu_custom_call" | custom-call | flops 4294967296 | bytes 13631488 | tf_op jit(solution)/shard_map/project/pallas_call | solution.py:95
  126.2 1.4 collective-permute-start.27
  128.2 1.4 collective-permute-start.30
  130.5 22.0 %reduce-scatter.5.cloned.1.call-done = bf16[128,1024]{1,0:T(8,128)(2,1)} async-done(((bf16[512,1024]{1,0:T(8,128)(2,1)}), bf16[128,1024]{1,0:T(8,128)(2,1)}) %reduce-scatter.5.cloned.1.call-update) | async-done | bytes 262160 | tf_op jit(solution)/shard_map/reduce_scatter | solution.py:879
  152.5 1.1 pad_maximum_fusion
  153.7 2.3 multiply_convert_fusion
  155.9 6.9 %collective-permute-done.29.refs_8_.refs_9_ = bf16[384,1024]{1,0:T(8,128)(2,1)} collective-permute-done((bf16[384,1024]{1,0:T(8,128)(2,1)}, bf16[384,1024]{1,0:T(8,128)(2,1)}, u32[]{:S(2)}, u32[]{:S(2)}) %collective-permute-start.29) | collective-permute-done | bytes 786464 | tf_op jit(solution)/shard_map/ppermute | solution.py:23
  163.9 1.3 collective-permute-start.32
  166.4 2.6 collective-permute-start.46
  169.4 5.2 %collective-permute-done.32.refs_0_.refs_6_ = bf16[192,1024]{1,0:T(8,128)(2,1)S(1)} collective-permute-done((bf16[192,1024]{1,0:T(8,128)(2,1)S(1)}, bf16[192,1024]{1,0:T(8,128)(2,1)S(1)}, u32[]{:S(2)}, u32[]{:S(2)}) %collective-permute-start.32) | collective-permute-done | bytes 393248 | tf_op jit(solution)/shard_map/ppermute | solution.py:23
  176.5 1.1 collective-permute-start.38
  177.7 3.6 %collective-permute-done.45.refs_0_ = bf16[192,1024]{1,0:T(8,128)(2,1)S(1)} collective-permute-done((bf16[192,1024]{1,0:T(8,128)(2,1)S(1)}, bf16[192,1024]{1,0:T(8,128)(2,1)S(1)}, u32[]{:S(2)}, u32[]{:S(2)}) %collective-permute-start.45) | collective-permute-done | bytes 393248 | tf_op jit(solution)/shard_map/ppermute | solution.py:23
  181.3 14.1 %collective-permute-done.46.refs_1_ = bf16[192,1024]{1,0:T(8,128)(2,1)S(1)} collective-permute-done((bf16[192,1024]{1,0:T(8,128)(2,1)S(1)}, bf16[192,1024]{1,0:T(8,128)(2,1)S(1)}, u32[]{:S(2)}, u32[]{:S(2)}) %collective-permute-start.46) | collective-permute-done | bytes 393248 | tf_op jit(solution)/shard_map/ppermute | solution.py:23
  195.4 7.1 %collective-permute-done.47.refs_2_ = bf16[192,1024]{1,0:T(8,128)(2,1)S(1)} collective-permute-done((bf16[192,1024]{1,0:T(8,128)(2,1)S(1)}, bf16[192,1024]{1,0:T(8,128)(2,1)S(1)}, u32[]{:S(2)}, u32[]{:S(2)}) %collective-permute-start.47) | collective-permute-done | bytes 393248 | tf_op jit(solution)/shard_map/ppermute | solution.py:23
  203.2 1.2 collective-permute-start.49
  205.8 1.2 collective-permute-done.31.refs_5_
  207.7 1.4 collective-permute-done.39.refs_13_
  209.1 6.8 %hidden_units.2.refs_2_.refs_1_ = bf16[192,384]{1,0:T(8,128)(2,1)S(1)} custom-call(s32[1]{0:T(128)} %bitcast.refs_0_, f32[8,1,1024]{2,1,0:T(1,128)S(1)} %inverse_gains.1.refs_1_, bf16[8192,384]{1,0:T(8,128)(2,1)S(1)} %bitcast.57, bf16[8192,384]{1,0:T(8,128)(2,1)} %bitcast.58, bf16[192,1024]{1,0:T(8,128)(2,1)S(1)} %get-tuple-element.51.refs_4_, ...), custom_call_target="tpu_custom_call" | custom-call | flops 2415919104 | bytes 15728640 | tf_op jit(solution)/shard_map/hidden_units/pallas_call | solution.py:95
  215.9 1.1 collective-permute-start.41
  217.9 13.2 %collective-permute-done.49.refs_0_.refs_6_ = bf16[576,1024]{1,0:T(8,128)(2,1)S(1)} collective-permute-done((bf16[576,1024]{1,0:T(8,128)(2,1)S(1)}, bf16[576,1024]{1,0:T(8,128)(2,1)S(1)}, u32[]{:S(2)}, u32[]{:S(2)}) %collective-permute-start.49) | collective-permute-done | bytes 1179680 | tf_op jit(solution)/shard_map/ppermute | solution.py:23
  231.1 2.1 collective-permute-done.51.refs_1_.refs_8_
  234.4 1.1 collective-permute-start.55
  236.4 9.1 %collective-permute-done.53.refs_10_ = bf16[288,1024]{1,0:T(8,128)(2,1)S(1)} collective-permute-done((bf16[288,1024]{1,0:T(8,128)(2,1)S(1)}, bf16[288,1024]{1,0:T(8,128)(2,1)S(1)}, u32[]{:S(2)}, u32[]{:S(2)}) %collective-permute-start.53) | collective-permute-done | bytes 589856 | tf_op jit(solution)/shard_map/ppermute | solution.py:23
  246.1 1.5 collective-permute-done.54.refs_11_
  248.4 15.3 %hidden_units.3.refs_1_ = bf16[576,384]{1,0:T(8,128)(2,1)S(1)} custom-call(s32[1]{0:T(128)} %bitcast.refs_0_, f32[8,1,1024]{2,1,0:T(1,128)S(1)} %inverse_gains.1.refs_1_, bf16[8192,384]{1,0:T(8,128)(2,1)} %bitcast.54, bf16[8192,384]{1,0:T(8,128)(2,1)} %bitcast.59, bf16[576,1024]{1,0:T(8,128)(2,1)S(1)} %join.1.refs_4_, ...), custom_call_target="tpu_custom_call" | custom-call | flops 7247757312 | bytes 22020096 | tf_op jit(solution)/shard_map/hidden_units/pallas_call | solution.py:95
  263.7 1.1 collective-permute-start.58
  265.7 10.2 %collective-permute-done.58.refs_3_ = bf16[576,384]{1,0:T(8,128)(2,1)S(1)} collective-permute-done((bf16[576,384]{1,0:T(8,128)(2,1)S(1)}, bf16[576,384]{1,0:T(8,128)(2,1)S(1)}, u32[]{:S(2)}, u32[]{:S(2)}) %collective-permute-start.58) | collective-permute-done | bytes 442400 | tf_op jit(solution)/shard_map/ppermute | solution.py:23
  276.7 1.0 collective-permute-done.59.refs_4_
  278.5 5.3 %cross_down.3 = (bf16[384,1024]{1,0:T(8,128)(2,1)S(1)}, bf16[384,512]{1,0:T(8,128)(2,1)S(1)}, bf16[384,512]{1,0:T(8,128)(2,1)S(1)}) custom-call(s32[1]{0:T(128)} %bitcast.refs_0_, bf16[576,384]{1,0:T(8,128)(2,1)S(1)} %hidden_units.3.refs_1_, bf16[576,384]{1,0:T(8,128)(2,1)S(1)} %collective-permute-done.57.refs_2_, ...), custom_call_target="tpu_custom_call" | custom-call | flops 4831838208 | bytes 9437184 | tf_op jit(solution)/shard_map/cross_down/pallas_call | solution.py:95
  284.8 1.1 collective-permute-start.63
  285.9 9.1 %collective-permute-done.62.refs_1_ = bf16[384,512]{1,0:T(8,128)(2,1)S(1)} collective-permute-done((bf16[384,512]{1,0:T(8,128)(2,1)S(1)}, bf16[384,512]{1,0:T(8,128)(2,1)S(1)}, u32[]{:S(2)}, u32[]{:S(2)}) %collective-permute-start.62) | collective-permute-done | bytes 393248 | tf_op jit(solution)/shard_map/ppermute | solution.py:23
  296.6 4.6 %cross_down.4 = (bf16[192,1024]{1,0:T(8,128)(2,1)S(1)}, bf16[192,512]{1,0:T(8,128)(2,1)S(1)}, bf16[192,512]{1,0:T(8,128)(2,1)S(1)}) custom-call(s32[1]{0:T(128)} %bitcast.refs_0_, bf16[576,384]{1,0:T(8,128)(2,1)S(1)} %hidden_units.3.refs_1_, bf16[576,384]{1,0:T(8,128)(2,1)S(1)} %collective-permute-done.57.refs_2_, ...), custom_call_target="tpu_custom_call" | custom-call | flops 2415919104 | bytes 9437184 | tf_op jit(solution)/shard_map/cross_down/pallas_call | solution.py:95
  301.3 1.1 collective-permute-start.66
  303.9 3.2 collective-permute-done.66.refs_1_
  308.1 1.6 collective-permute-start.70
  309.8 1.9 collective-permute-start.68
  311.8 4.9 %cross_down.5 = (bf16[192,1024]{1,0:T(8,128)(2,1)S(1)}, bf16[192,512]{1,0:T(8,128)(2,1)}, bf16[192,512]{1,0:T(8,128)(2,1)}) custom-call(s32[1]{0:T(128)} %bitcast.refs_0_, bf16[192,384]{1,0:T(8,128)(2,1)S(1)} %hidden_units.2.refs_2_.refs_1_, bf16[192,384]{1,0:T(8,128)(2,1)S(1)} %collective-permute-done.40.refs_2_, ...), custom_call_target="tpu_custom_call" | custom-call | flops 2415919104 | bytes 9437184 | tf_op jit(solution)/shard_map/cross_down/pallas_call | solution.py:95
  317.4 1.1 collective-permute-start.64
  319.9 3.5 collective-permute-done.64.refs_1_
  323.4 1.1 collective-permute-done.65.refs_2_
  325.5 8.1 %collective-permute-done.69.refs_10_ = bf16[192,1024]{1,0:T(8,128)(2,1)} collective-permute-done((bf16[192,1024]{1,0:T(8,128)(2,1)}, bf16[192,1024]{1,0:T(8,128)(2,1)}, u32[]{:S(2)}, u32[]{:S(2)}) %collective-permute-start.69) | collective-permute-done | bytes 393248 | tf_op jit(solution)/shard_map/ppermute | solution.py:23
  333.6 8.1 %collective-permute-done.70.refs_11_ = bf16[192,1024]{1,0:T(8,128)(2,1)} collective-permute-done((bf16[192,1024]{1,0:T(8,128)(2,1)}, bf16[192,1024]{1,0:T(8,128)(2,1)}, u32[]{:S(2)}, u32[]{:S(2)}) %collective-permute-start.70) | collective-permute-done | bytes 393248 | tf_op jit(solution)/shard_map/ppermute | solution.py:23
  341.8 2.8 combine.1
  (228 shorter events, 41.9 us)
Async XLA Ops:
  7.2 123.3 %reduce-scatter.3.cloned.1.call-start = ((), (), s32[]{:S(2)}) async-start(), calls=%async_computation.2 | async-start | bytes 1310720 | tf_op jit(solution)/shard_map/reduce_scatter | solution.py:879
  8.1 3.9 %collective-permute-start = (bf16[3,4096]{1,0:T(4,128)(2,1)S(1)}, bf16[3,4096]{1,0:T(4,128)(2,1)S(1)}, u32[]{:S(2)}, u32[]{:S(2)}) collective-permute-start(bf16[3,4096]{1,0:T(4,128)(2,1)S(1)} %slice.31), channel_id=1, source_target_pairs={{0,4},{4,8},{8,12},{12,16},{16,20},{20,24},{24,28},{1,5},{5,9},{9,... | collective-permute-start | bytes 73736 | tf_op jit(solution)/shard_map/ppermute | solution.py:19
  28.7 9.4 %collective-permute-start.2 = (bf16[32,4096]{1,0:T(8,128)(2,1)}, bf16[32,4096]{1,0:T(8,128)(2,1)S(1)}, u32[]{:S(2)}, u32[]{:S(2)}) collective-permute-start(bf16[32,4096]{1,0:T(8,128)(2,1)} %get-tuple-element.38.refs_9_.refs_1_), channel_id=1, source_target_pairs={{0,8},{4,12},{8,0},{12,4},{16,24},{20,28},{24,16},{28,20},{1,9},{5... | collective-permute-start | bytes 786440 | tf_op jit(solution)/shard_map/ppermute | solution.py:23
  30.8 14.2 %collective-permute-start.4 = (bf16[32,4096]{1,0:T(8,128)(2,1)}, bf16[32,4096]{1,0:T(8,128)(2,1)S(1)}, u32[]{:S(2)}, u32[]{:S(2)}) collective-permute-start(bf16[32,4096]{1,0:T(8,128)(2,1)} %get-tuple-element.38.refs_9_.refs_1_), channel_id=1, source_target_pairs={{0,16},{4,20},{8,24},{12,28},{16,0},{20,4},{24,8},{28,12},{1,17},{... | collective-permute-start | bytes 786440 | tf_op jit(solution)/shard_map/ppermute | solution.py:23
  32.3 12.7 %collective-permute-start.6 = (bf16[32,4096]{1,0:T(8,128)(2,1)}, bf16[32,4096]{1,0:T(8,128)(2,1)S(1)}, u32[]{:S(2)}, u32[]{:S(2)}) collective-permute-start(bf16[32,4096]{1,0:T(8,128)(2,1)} %get-tuple-element.38.refs_9_.refs_1_), channel_id=1, source_target_pairs={{0,24},{4,28},{8,16},{12,20},{16,8},{20,12},{24,0},{28,4},{1,25},{... | collective-permute-start | bytes 786440 | tf_op jit(solution)/shard_map/ppermute | solution.py:23
  33.2 12.6 %collective-permute-start.1 = (bf16[32,4096]{1,0:T(8,128)(2,1)}, bf16[32,4096]{1,0:T(8,128)(2,1)S(1)}, u32[]{:S(2)}, u32[]{:S(2)}) collective-permute-start(bf16[32,4096]{1,0:T(8,128)(2,1)} %get-tuple-element.38.refs_9_.refs_1_), channel_id=1, source_target_pairs={{0,4},{4,0},{8,12},{12,8},{16,20},{20,16},{24,28},{28,24},{1,5},{5... | collective-permute-start | bytes 786440 | tf_op jit(solution)/shard_map/ppermute | solution.py:23
  38.1 7.6 %collective-permute-start.3 = (bf16[32,4096]{1,0:T(8,128)(2,1)S(1)}, bf16[32,4096]{1,0:T(8,128)(2,1)S(1)}, u32[]{:S(2)}, u32[]{:S(2)}) collective-permute-start(bf16[32,4096]{1,0:T(8,128)(2,1)S(1)} %collective-permute-done.2.refs_11_.refs_3_), channel_id=1, source_target_pairs={{0,4},{4,0},{8,12},{12,8},{16,20},{20,16},{24,28},{28,24},{1,5},{5... | collective-permute-start | bytes 786440 | tf_op jit(solution)/shard_map/ppermute | solution.py:23
  57.5 15.0 %collective-permute-start.11 = (bf16[64,4096]{1,0:T(8,128)(2,1)}, bf16[64,4096]{1,0:T(8,128)(2,1)S(1)}, u32[]{:S(2)}, u32[]{:S(2)}) collective-permute-start(bf16[64,4096]{1,0:T(8,128)(2,1)} %get-tuple-element.39.refs_2_), channel_id=1, source_target_pairs={{0,16},{4,20},{8,24},{12,28},{16,0},{20,4},{24,8},{28,12},{1,17},{... | collective-permute-start | bytes 1572872 | tf_op jit(solution)/shard_map/ppermute | solution.py:23
  57.9 15.0 %collective-permute-start.9 = (bf16[64,4096]{1,0:T(8,128)(2,1)}, bf16[64,4096]{1,0:T(8,128)(2,1)S(1)}, u32[]{:S(2)}, u32[]{:S(2)}) collective-permute-start(bf16[64,4096]{1,0:T(8,128)(2,1)} %get-tuple-element.39.refs_2_), channel_id=1, source_target_pairs={{0,8},{4,12},{8,0},{12,4},{16,24},{20,28},{24,16},{28,20},{1,9},{5... | collective-permute-start | bytes 1572872 | tf_op jit(solution)/shard_map/ppermute | solution.py:23
  67.9 16.2 %collective-permute-start.17 = (bf16[64,4096]{1,0:T(8,128)(2,1)}, bf16[64,4096]{1,0:T(8,128)(2,1)S(1)}, u32[]{:S(2)}, u32[]{:S(2)}) collective-permute-start(bf16[64,4096]{1,0:T(8,128)(2,1)} %get-tuple-element.41.refs_2_), channel_id=1, source_target_pairs={{0,8},{4,12},{8,0},{12,4},{16,24},{20,28},{24,16},{28,20},{1,9},{5... | collective-permute-start | bytes 1572872 | tf_op jit(solution)/shard_map/ppermute | solution.py:23
  68.3 15.8 %collective-permute-start.18 = (bf16[64,4096]{1,0:T(8,128)(2,1)}, bf16[64,4096]{1,0:T(8,128)(2,1)S(1)}, u32[]{:S(2)}, u32[]{:S(2)}) collective-permute-start(bf16[64,4096]{1,0:T(8,128)(2,1)} %get-tuple-element.41.refs_2_), channel_id=1, source_target_pairs={{0,16},{4,20},{8,24},{12,28},{16,0},{20,4},{24,8},{28,12},{1,17},{... | collective-permute-start | bytes 1572872 | tf_op jit(solution)/shard_map/ppermute | solution.py:23
  70.0 19.1 %collective-permute-start.8 = (bf16[64,4096]{1,0:T(8,128)(2,1)S(1)}, bf16[64,4096]{1,0:T(8,128)(2,1)S(1)}, u32[]{:S(2)}, u32[]{:S(2)}) collective-permute-start(bf16[64,4096]{1,0:T(8,128)(2,1)S(1)} %copy-done.30), channel_id=1, source_target_pairs={{0,4},{4,0},{8,12},{12,8},{16,20},{20,16},{24,28},{28,24},{1,5},{5... | collective-permute-start | bytes 1572872 | tf_op jit(solution)/shard_map/ppermute | solution.py:23
  74.0 14.5 %collective-permute-start.13 = (bf16[64,2048]{1,0:T(8,128)(2,1)S(1)}, bf16[64,2048]{1,0:T(8,128)(2,1)S(1)}, u32[]{:S(2)}, u32[]{:S(2)}) collective-permute-start(bf16[64,2048]{1,0:T(8,128)(2,1)S(1)} %get-tuple-element.42), channel_id=1, source_target_pairs={{0,16},{4,20},{8,24},{12,28},{16,0},{20,4},{24,8},{28,12},{1,17},{... | collective-permute-start | bytes 786440 | tf_op jit(solution)/shard_map/ppermute | solution.py:23
  75.7 13.0 %collective-permute-start.15 = (bf16[64,2048]{1,0:T(8,128)(2,1)S(1)}, bf16[64,2048]{1,0:T(8,128)(2,1)S(1)}, u32[]{:S(2)}, u32[]{:S(2)}) collective-permute-start(bf16[64,2048]{1,0:T(8,128)(2,1)S(1)} %get-tuple-element.43), channel_id=1, source_target_pairs={{0,8},{4,12},{8,0},{12,4},{16,24},{20,28},{24,16},{28,20},{1,9},{5... | collective-permute-start | bytes 786440 | tf_op jit(solution)/shard_map/ppermute | solution.py:23
  84.2 6.3 %collective-permute-start.10 = (bf16[64,4096]{1,0:T(8,128)(2,1)S(1)}, bf16[64,4096]{1,0:T(8,128)(2,1)S(1)}, u32[]{:S(2)}, u32[]{:S(2)}) collective-permute-start(bf16[64,4096]{1,0:T(8,128)(2,1)S(1)} %collective-permute-done.9.refs_0_.refs_4_.refs_13_), channel_id=1, source_target_pairs={{0,4},{4,0},{8,12},{12,8},{16,20},{20,16},{24,28},{28,24},{1,5},{5... | collective-permute-start | bytes 1572872 | tf_op jit(solution)/shard_map/ppermute | solution.py:23
  84.2 6.3 %collective-permute-start.12 = (bf16[64,4096]{1,0:T(8,128)(2,1)S(1)}, bf16[64,4096]{1,0:T(8,128)(2,1)S(1)}, u32[]{:S(2)}, u32[]{:S(2)}) collective-permute-start(bf16[64,4096]{1,0:T(8,128)(2,1)S(1)} %collective-permute-done.11.refs_1_.refs_6_.refs_14_), channel_id=1, source_target_pairs={{0,4},{4,0},{8,12},{12,8},{16,20},{20,16},{24,28},{28,24},{1,5},{5... | collective-permute-start | bytes 1572872 | tf_op jit(solution)/shard_map/ppermute | solution.py:23
  98.8 53.7 %reduce-scatter.5.cloned.1.call-start = ((), (), s32[]{:S(2)}) async-start(), calls=%async_computation.3 | async-start | bytes 1310720 | tf_op jit(solution)/shard_map/reduce_scatter | solution.py:879
  99.1 8.4 %collective-permute-start.22 = (bf16[64,2048]{1,0:T(8,128)(2,1)S(1)}, bf16[64,2048]{1,0:T(8,128)(2,1)S(1)}, u32[]{:S(2)}, u32[]{:S(2)}) collective-permute-start(bf16[64,2048]{1,0:T(8,128)(2,1)S(1)} %get-tuple-element.44), channel_id=1, source_target_pairs={{0,16},{4,20},{8,24},{12,28},{16,0},{20,4},{24,8},{28,12},{1,17},{... | collective-permute-start | bytes 786440 | tf_op jit(solution)/shard_map/ppermute | solution.py:23
  100.6 8.1 %collective-permute-start.24 = (bf16[64,2048]{1,0:T(8,128)(2,1)S(1)}, bf16[64,2048]{1,0:T(8,128)(2,1)S(1)}, u32[]{:S(2)}, u32[]{:S(2)}) collective-permute-start(bf16[64,2048]{1,0:T(8,128)(2,1)S(1)} %get-tuple-element.45), channel_id=1, source_target_pairs={{0,8},{4,12},{8,0},{12,4},{16,24},{20,28},{24,16},{28,20},{1,9},{5... | collective-permute-start | bytes 786440 | tf_op jit(solution)/shard_map/ppermute | solution.py:23
  101.3 12.9 %collective-permute-start.19 = (bf16[64,4096]{1,0:T(8,128)(2,1)S(1)}, bf16[64,4096]{1,0:T(8,128)(2,1)S(1)}, u32[]{:S(2)}, u32[]{:S(2)}) collective-permute-start(bf16[64,4096]{1,0:T(8,128)(2,1)S(1)} %copy-done.27), channel_id=1, source_target_pairs={{0,4},{4,0},{8,12},{12,8},{16,20},{20,16},{24,28},{28,24},{1,5},{5... | collective-permute-start | bytes 1572872 | tf_op jit(solution)/shard_map/ppermute | solution.py:23
  101.3 12.9 %collective-permute-start.20 = (bf16[64,4096]{1,0:T(8,128)(2,1)S(1)}, bf16[64,4096]{1,0:T(8,128)(2,1)S(1)}, u32[]{:S(2)}, u32[]{:S(2)}) collective-permute-start(bf16[64,4096]{1,0:T(8,128)(2,1)S(1)} %collective-permute-done.17.refs_12_.refs_0_.refs_4_), channel_id=1, source_target_pairs={{0,4},{4,0},{8,12},{12,8},{16,20},{20,16},{24,28},{28,24},{1,5},{5... | collective-permute-start | bytes 1572872 | tf_op jit(solution)/shard_map/ppermute | solution.py:23
  101.8 12.4 %collective-permute-start.21 = (bf16[64,4096]{1,0:T(8,128)(2,1)S(1)}, bf16[64,4096]{1,0:T(8,128)(2,1)S(1)}, u32[]{:S(2)}, u32[]{:S(2)}) collective-permute-start(bf16[64,4096]{1,0:T(8,128)(2,1)S(1)} %collective-permute-done.18.refs_13_.refs_1_.refs_6_), channel_id=1, source_target_pairs={{0,4},{4,0},{8,12},{12,8},{16,20},{20,16},{24,28},{28,24},{1,5},{5... | collective-permute-start | bytes 1572872 | tf_op jit(solution)/shard_map/ppermute | solution.py:23
  107.5 6.7 %collective-permute-start.23 = (bf16[64,2048]{1,0:T(8,128)(2,1)S(1)}, bf16[64,2048]{1,0:T(8,128)(2,1)S(1)}, u32[]{:S(2)}, u32[]{:S(2)}) collective-permute-start(bf16[64,2048]{1,0:T(8,128)(2,1)S(1)} %collective-permute-done.22.refs_8_), channel_id=1, source_target_pairs={{0,4},{4,0},{8,12},{12,8},{16,20},{20,16},{24,28},{28,24},{1,5},{5... | collective-permute-start | bytes 786440 | tf_op jit(solution)/shard_map/ppermute | solution.py:23
  108.6 5.6 %collective-permute-start.25 = (bf16[64,2048]{1,0:T(8,128)(2,1)S(1)}, bf16[64,2048]{1,0:T(8,128)(2,1)S(1)}, u32[]{:S(2)}, u32[]{:S(2)}) collective-permute-start(bf16[64,2048]{1,0:T(8,128)(2,1)S(1)} %collective-permute-done.24.refs_10_), channel_id=1, source_target_pairs={{0,4},{4,0},{8,12},{12,8},{16,20},{20,16},{24,28},{28,24},{1,5},{5... | collective-permute-start | bytes 786440 | tf_op jit(solution)/shard_map/ppermute | solution.py:23
  124.8 38.5 %collective-permute-start.28 = (bf16[384,2048]{1,0:T(8,128)(2,1)}, bf16[384,2048]{1,0:T(8,128)(2,1)S(1)}, u32[]{:S(2)}, u32[]{:S(2)}) collective-permute-start(bf16[384,2048]{1,0:T(8,128)(2,1)} %get-tuple-element.48), channel_id=1, source_target_pairs={{0,4},{4,0},{8,12},{12,8},{16,20},{20,16},{24,28},{28,24},{1,5},{5... | collective-permute-start | bytes 4718600 | tf_op jit(solution)/shard_map/ppermute | solution.py:23
  125.7 30.2 %collective-permute-start.26 = (bf16[384,1024]{1,0:T(8,128)(2,1)}, bf16[384,1024]{1,0:T(8,128)(2,1)S(1)}, u32[]{:S(2)}, u32[]{:S(2)}) collective-permute-start(bf16[384,1024]{1,0:T(8,128)(2,1)} %get-tuple-element.46.refs_13_), channel_id=1, source_target_pairs={{0,12},{4,8},{8,4},{12,0},{16,28},{20,24},{24,20},{28,16},{1,13},{... | collective-permute-start | bytes 2359304 | tf_op jit(solution)/shard_map/ppermute | solution.py:23
  126.2 29.7 %collective-permute-start.27 = (bf16[384,1024]{1,0:T(8,128)(2,1)}, bf16[384,1024]{1,0:T(8,128)(2,1)S(1)}, u32[]{:S(2)}, u32[]{:S(2)}) collective-permute-start(bf16[384,1024]{1,0:T(8,128)(2,1)} %get-tuple-element.47), channel_id=1, source_target_pairs={{0,20},{4,16},{8,28},{12,24},{16,4},{20,0},{24,12},{28,8},{1,21},{... | collective-permute-start | bytes 2359304 | tf_op jit(solution)/shard_map/ppermute | solution.py:23
  127.6 35.2 %collective-permute-start.29 = (bf16[384,1024]{1,0:T(8,128)(2,1)}, bf16[384,1024]{1,0:T(8,128)(2,1)}, u32[]{:S(2)}, u32[]{:S(2)}) collective-permute-start(bf16[384,1024]{1,0:T(8,128)(2,1)} %get-tuple-element.49), channel_id=1, source_target_pairs={{0,8},{4,12},{8,0},{12,4},{16,24},{20,28},{24,16},{28,20},{1,9},{5... | collective-permute-start | bytes 2359304 | tf_op jit(solution)/shard_map/ppermute | solution.py:23
  128.2 35.1 %collective-permute-start.30 = (bf16[384,1024]{1,0:T(8,128)(2,1)}, bf16[384,1024]{1,0:T(8,128)(2,1)}, u32[]{:S(2)}, u32[]{:S(2)}) collective-permute-start(bf16[384,1024]{1,0:T(8,128)(2,1)} %get-tuple-element.50), channel_id=1, source_target_pairs={{0,16},{4,20},{8,24},{12,28},{16,0},{20,4},{24,8},{28,12},{1,17},{... | collective-permute-start | bytes 2359304 | tf_op jit(solution)/shard_map/ppermute | solution.py:23
  163.9 10.7 %collective-permute-start.32 = (bf16[192,1024]{1,0:T(8,128)(2,1)S(1)}, bf16[192,1024]{1,0:T(8,128)(2,1)S(1)}, u32[]{:S(2)}, u32[]{:S(2)}) collective-permute-start(bf16[192,1024]{1,0:T(8,128)(2,1)S(1)} %get-tuple-element.51.refs_4_), channel_id=1, source_target_pairs={{0,8},{4,12},{8,0},{12,4},{16,24},{20,28},{24,16},{28,20},{1,9},{5... | collective-permute-start | bytes 1179656 | tf_op jit(solution)/shard_map/ppermute | solution.py:23
  165.2 10.2 %collective-permute-start.34 = (bf16[192,1024]{1,0:T(8,128)(2,1)S(1)}, bf16[192,1024]{1,0:T(8,128)(2,1)S(1)}, u32[]{:S(2)}, u32[]{:S(2)}) collective-permute-start(bf16[192,1024]{1,0:T(8,128)(2,1)S(1)} %get-tuple-element.51.refs_4_), channel_id=1, source_target_pairs={{0,16},{4,20},{8,24},{12,28},{16,0},{20,4},{24,8},{28,12},{1,17},{... | collective-permute-start | bytes 1179656 | tf_op jit(solution)/shard_map/ppermute | solution.py:23
  166.0 15.3 %collective-permute-start.45 = (bf16[192,1024]{1,0:T(8,128)(2,1)S(1)}, bf16[192,1024]{1,0:T(8,128)(2,1)S(1)}, u32[]{:S(2)}, u32[]{:S(2)}) collective-permute-start(bf16[192,1024]{1,0:T(8,128)(2,1)S(1)} %get-tuple-element.54), channel_id=1, source_target_pairs={{0,1},{1,0},{2,3},{3,2},{4,5},{5,4},{6,7},{7,6},{8,9},{9,8},{10,11... | collective-permute-start | bytes 1179656 | tf_op jit(solution)/shard_map/ppermute | solution.py:23
  166.4 29.0 %collective-permute-start.46 = (bf16[192,1024]{1,0:T(8,128)(2,1)S(1)}, bf16[192,1024]{1,0:T(8,128)(2,1)S(1)}, u32[]{:S(2)}, u32[]{:S(2)}) collective-permute-start(bf16[192,1024]{1,0:T(8,128)(2,1)S(1)} %get-tuple-element.55), channel_id=1, source_target_pairs={{0,2},{1,3},{2,0},{3,1},{4,6},{5,7},{6,4},{7,5},{8,10},{9,11},{10,... | collective-permute-start | bytes 1179656 | tf_op jit(solution)/shard_map/ppermute | solution.py:23
  169.0 33.6 %collective-permute-start.47 = (bf16[192,1024]{1,0:T(8,128)(2,1)S(1)}, bf16[192,1024]{1,0:T(8,128)(2,1)S(1)}, u32[]{:S(2)}, u32[]{:S(2)}) collective-permute-start(bf16[192,1024]{1,0:T(8,128)(2,1)S(1)} %get-tuple-element.56), channel_id=1, source_target_pairs={{0,3},{1,2},{2,1},{3,0},{4,7},{5,6},{6,5},{7,4},{8,11},{9,10},{10,... | collective-permute-start | bytes 1179656 | tf_op jit(solution)/shard_map/ppermute | solution.py:23
  175.5 27.0 %collective-permute-start.36 = (bf16[96,1024]{1,0:T(8,128)(2,1)S(1)}, bf16[96,1024]{1,0:T(8,128)(2,1)S(1)}, u32[]{:S(2)}, u32[]{:S(2)}) collective-permute-start(bf16[96,1024]{1,0:T(8,128)(2,1)S(1)} %get-tuple-element.52), channel_id=1, source_target_pairs={{0,16},{4,20},{8,24},{12,28},{16,0},{20,4},{24,8},{28,12},{1,17},{... | collective-permute-start | bytes 589832 | tf_op jit(solution)/shard_map/ppermute | solution.py:23
  176.5 26.1 %collective-permute-start.38 = (bf16[96,1024]{1,0:T(8,128)(2,1)S(1)}, bf16[96,1024]{1,0:T(8,128)(2,1)S(1)}, u32[]{:S(2)}, u32[]{:S(2)}) collective-permute-start(bf16[96,1024]{1,0:T(8,128)(2,1)S(1)} %get-tuple-element.53), channel_id=1, source_target_pairs={{0,8},{4,12},{8,0},{12,4},{16,24},{20,28},{24,16},{28,20},{1,9},{5... | collective-permute-start | bytes 589832 | tf_op jit(solution)/shard_map/ppermute | solution.py:23
  203.2 28.0 %collective-permute-start.49 = (bf16[576,1024]{1,0:T(8,128)(2,1)S(1)}, bf16[576,1024]{1,0:T(8,128)(2,1)S(1)}, u32[]{:S(2)}, u32[]{:S(2)}) collective-permute-start(bf16[576,1024]{1,0:T(8,128)(2,1)S(1)} %join.1.refs_4_), channel_id=1, source_target_pairs={{0,8},{4,12},{8,0},{12,4},{16,24},{20,28},{24,16},{28,20},{1,9},{5... | collective-permute-start | bytes 3538952 | tf_op jit(solution)/shard_map/ppermute | solution.py:23
  204.4 28.9 %collective-permute-start.51 = (bf16[576,1024]{1,0:T(8,128)(2,1)S(1)}, bf16[576,1024]{1,0:T(8,128)(2,1)S(1)}, u32[]{:S(2)}, u32[]{:S(2)}) collective-permute-start(bf16[576,1024]{1,0:T(8,128)(2,1)S(1)} %join.1.refs_4_), channel_id=1, source_target_pairs={{0,16},{4,20},{8,24},{12,28},{16,0},{20,4},{24,8},{28,12},{1,17},{... | collective-permute-start | bytes 3538952 | tf_op jit(solution)/shard_map/ppermute | solution.py:23
  205.8 3.2 collective-permute-start.33
  207.0 2.0 collective-permute-start.35
  215.9 19.6 %collective-permute-start.41 = (bf16[192,384]{1,0:T(8,128)(2,1)S(1)}, bf16[192,384]{1,0:T(8,128)(2,1)S(1)}, u32[]{:S(2)}, u32[]{:S(2)}) collective-permute-start(bf16[192,384]{1,0:T(8,128)(2,1)S(1)} %hidden_units.2.refs_2_.refs_1_), channel_id=1, source_target_pairs={{0,8},{4,12},{8,0},{12,4},{16,24},{20,28},{24,16},{28,20},{1,9},{5... | collective-permute-start | bytes 442376 | tf_op jit(solution)/shard_map/ppermute | solution.py:23
  217.0 19.4 %collective-permute-start.43 = (bf16[192,384]{1,0:T(8,128)(2,1)S(1)}, bf16[192,384]{1,0:T(8,128)(2,1)S(1)}, u32[]{:S(2)}, u32[]{:S(2)}) collective-permute-start(bf16[192,384]{1,0:T(8,128)(2,1)S(1)} %hidden_units.2.refs_2_.refs_1_), channel_id=1, source_target_pairs={{0,16},{4,20},{8,24},{12,28},{16,0},{20,4},{24,8},{28,12},{1,17},{... | collective-permute-start | bytes 442376 | tf_op jit(solution)/shard_map/ppermute | solution.py:23
  217.9 28.1 %collective-permute-start.48 = (bf16[576,1024]{1,0:T(8,128)(2,1)S(1)}, bf16[576,1024]{1,0:T(8,128)(2,1)S(1)}, u32[]{:S(2)}, u32[]{:S(2)}) collective-permute-start(bf16[576,1024]{1,0:T(8,128)(2,1)S(1)} %join.1.refs_4_), channel_id=1, source_target_pairs={{0,4},{4,0},{8,12},{12,8},{16,20},{20,16},{24,28},{28,24},{1,5},{5... | collective-permute-start | bytes 3538952 | tf_op jit(solution)/shard_map/ppermute | solution.py:23
  233.4 12.2 %collective-permute-start.53 = (bf16[288,1024]{1,0:T(8,128)(2,1)S(1)}, bf16[288,1024]{1,0:T(8,128)(2,1)S(1)}, u32[]{:S(2)}, u32[]{:S(2)}) collective-permute-start(bf16[288,1024]{1,0:T(8,128)(2,1)S(1)} %get-tuple-element.57), channel_id=1, source_target_pairs={{0,16},{4,20},{8,24},{12,28},{16,0},{20,4},{24,8},{28,12},{1,17},{... | collective-permute-start | bytes 1769480 | tf_op jit(solution)/shard_map/ppermute | solution.py:23
  234.4 11.2 %collective-permute-start.55 = (bf16[288,1024]{1,0:T(8,128)(2,1)S(1)}, bf16[288,1024]{1,0:T(8,128)(2,1)S(1)}, u32[]{:S(2)}, u32[]{:S(2)}) collective-permute-start(bf16[288,1024]{1,0:T(8,128)(2,1)S(1)} %get-tuple-element.58), channel_id=1, source_target_pairs={{0,8},{4,12},{8,0},{12,4},{16,24},{20,28},{24,16},{28,20},{1,9},{5... | collective-permute-start | bytes 1769480 | tf_op jit(solution)/shard_map/ppermute | solution.py:23
  235.4 13.0 %collective-permute-start.50 = (bf16[576,1024]{1,0:T(8,128)(2,1)S(1)}, bf16[576,1024]{1,0:T(8,128)(2,1)S(1)}, u32[]{:S(2)}, u32[]{:S(2)}) collective-permute-start(bf16[576,1024]{1,0:T(8,128)(2,1)S(1)} %collective-permute-done.49.refs_0_.refs_6_), channel_id=1, source_target_pairs={{0,4},{4,0},{8,12},{12,8},{16,20},{20,16},{24,28},{28,24},{1,5},{5... | collective-permute-start | bytes 3538952 | tf_op jit(solution)/shard_map/ppermute | solution.py:23
  236.4 12.0 %collective-permute-start.52 = (bf16[576,1024]{1,0:T(8,128)(2,1)S(1)}, bf16[576,1024]{1,0:T(8,128)(2,1)S(1)}, u32[]{:S(2)}, u32[]{:S(2)}) collective-permute-start(bf16[576,1024]{1,0:T(8,128)(2,1)S(1)} %collective-permute-done.51.refs_1_.refs_8_), channel_id=1, source_target_pairs={{0,4},{4,0},{8,12},{12,8},{16,20},{20,16},{24,28},{28,24},{1,5},{5... | collective-permute-start | bytes 3538952 | tf_op jit(solution)/shard_map/ppermute | solution.py:23
  245.5 2.0 collective-permute-start.54
  245.5 2.8 collective-permute-start.56
  263.7 12.3 %collective-permute-start.58 = (bf16[576,384]{1,0:T(8,128)(2,1)S(1)}, bf16[576,384]{1,0:T(8,128)(2,1)S(1)}, u32[]{:S(2)}, u32[]{:S(2)}) collective-permute-start(bf16[576,384]{1,0:T(8,128)(2,1)S(1)} %hidden_units.3.refs_1_), channel_id=1, source_target_pairs={{0,8},{4,12},{8,0},{12,4},{16,24},{20,28},{24,16},{28,20},{1,9},{5... | collective-permute-start | bytes 1327112 | tf_op jit(solution)/shard_map/ppermute | solution.py:23
  264.8 11.9 %collective-permute-start.60 = (bf16[576,384]{1,0:T(8,128)(2,1)S(1)}, bf16[576,384]{1,0:T(8,128)(2,1)S(1)}, u32[]{:S(2)}, u32[]{:S(2)}) collective-permute-start(bf16[576,384]{1,0:T(8,128)(2,1)S(1)} %hidden_units.3.refs_1_), channel_id=1, source_target_pairs={{0,16},{4,20},{8,24},{12,28},{16,0},{20,4},{24,8},{28,12},{1,17},{... | collective-permute-start | bytes 1327112 | tf_op jit(solution)/shard_map/ppermute | solution.py:23
  265.7 11.0 %collective-permute-start.57 = (bf16[576,384]{1,0:T(8,128)(2,1)S(1)}, bf16[576,384]{1,0:T(8,128)(2,1)S(1)}, u32[]{:S(2)}, u32[]{:S(2)}) collective-permute-start(bf16[576,384]{1,0:T(8,128)(2,1)S(1)} %hidden_units.3.refs_1_), channel_id=1, source_target_pairs={{0,4},{4,0},{8,12},{12,8},{16,20},{20,16},{24,28},{28,24},{1,5},{5... | collective-permute-start | bytes 1327112 | tf_op jit(solution)/shard_map/ppermute | solution.py:23
  283.8 11.2 %collective-permute-start.62 = (bf16[384,512]{1,0:T(8,128)(2,1)S(1)}, bf16[384,512]{1,0:T(8,128)(2,1)S(1)}, u32[]{:S(2)}, u32[]{:S(2)}) collective-permute-start(bf16[384,512]{1,0:T(8,128)(2,1)S(1)} %get-tuple-element.60), channel_id=1, source_target_pairs={{0,16},{4,20},{8,24},{12,28},{16,0},{20,4},{24,8},{28,12},{1,17},{... | collective-permute-start | bytes 1179656 | tf_op jit(solution)/shard_map/ppermute | solution.py:23
  284.8 10.9 %collective-permute-start.63 = (bf16[384,512]{1,0:T(8,128)(2,1)S(1)}, bf16[384,512]{1,0:T(8,128)(2,1)S(1)}, u32[]{:S(2)}, u32[]{:S(2)}) collective-permute-start(bf16[384,512]{1,0:T(8,128)(2,1)S(1)} %get-tuple-element.61), channel_id=1, source_target_pairs={{0,8},{4,12},{8,0},{12,4},{16,24},{20,28},{24,16},{28,20},{1,9},{5... | collective-permute-start | bytes 1179656 | tf_op jit(solution)/shard_map/ppermute | solution.py:23
  301.3 5.9 %collective-permute-start.66 = (bf16[192,512]{1,0:T(8,128)(2,1)S(1)}, bf16[192,512]{1,0:T(8,128)(2,1)S(1)}, u32[]{:S(2)}, u32[]{:S(2)}) collective-permute-start(bf16[192,512]{1,0:T(8,128)(2,1)S(1)} %get-tuple-element.68), channel_id=1, source_target_pairs={{0,16},{4,20},{8,24},{12,28},{16,0},{20,4},{24,8},{28,12},{1,17},{... | collective-permute-start | bytes 589832 | tf_op jit(solution)/shard_map/ppermute | solution.py:23
  302.4 5.7 %collective-permute-start.67 = (bf16[192,512]{1,0:T(8,128)(2,1)S(1)}, bf16[192,512]{1,0:T(8,128)(2,1)S(1)}, u32[]{:S(2)}, u32[]{:S(2)}) collective-permute-start(bf16[192,512]{1,0:T(8,128)(2,1)S(1)} %get-tuple-element.69), channel_id=1, source_target_pairs={{0,8},{4,12},{8,0},{12,4},{16,24},{20,28},{24,16},{28,20},{1,9},{5... | collective-permute-start | bytes 589832 | tf_op jit(solution)/shard_map/ppermute | solution.py:23
  303.4 6.3 %collective-permute-start.40 = (bf16[192,384]{1,0:T(8,128)(2,1)S(1)}, bf16[192,384]{1,0:T(8,128)(2,1)S(1)}, u32[]{:S(2)}, u32[]{:S(2)}) collective-permute-start(bf16[192,384]{1,0:T(8,128)(2,1)S(1)} %hidden_units.2.refs_2_.refs_1_), channel_id=1, source_target_pairs={{0,4},{4,0},{8,12},{12,8},{16,20},{20,16},{24,28},{28,24},{1,5},{5... | collective-permute-start | bytes 442376 | tf_op jit(solution)/shard_map/ppermute | solution.py:23
  303.4 8.3 %collective-permute-start.42 = (bf16[192,384]{1,0:T(8,128)(2,1)S(1)}, bf16[192,384]{1,0:T(8,128)(2,1)S(1)}, u32[]{:S(2)}, u32[]{:S(2)}) collective-permute-start(bf16[192,384]{1,0:T(8,128)(2,1)S(1)} %collective-permute-done.41.refs_14_.refs_3_), channel_id=1, source_target_pairs={{0,4},{4,0},{8,12},{12,8},{16,20},{20,16},{24,28},{28,24},{1,5},{5... | collective-permute-start | bytes 442376 | tf_op jit(solution)/shard_map/ppermute | solution.py:23
  303.9 7.8 %collective-permute-start.44 = (bf16[192,384]{1,0:T(8,128)(2,1)S(1)}, bf16[192,384]{1,0:T(8,128)(2,1)S(1)}, u32[]{:S(2)}, u32[]{:S(2)}) collective-permute-start(bf16[192,384]{1,0:T(8,128)(2,1)S(1)} %collective-permute-done.43.refs_15_.refs_5_), channel_id=1, source_target_pairs={{0,4},{4,0},{8,12},{12,8},{16,20},{20,16},{24,28},{28,24},{1,5},{5... | collective-permute-start | bytes 442376 | tf_op jit(solution)/shard_map/ppermute | solution.py:23
  307.1 26.5 %collective-permute-start.69 = (bf16[192,1024]{1,0:T(8,128)(2,1)}, bf16[192,1024]{1,0:T(8,128)(2,1)}, u32[]{:S(2)}, u32[]{:S(2)}) collective-permute-start(bf16[192,1024]{1,0:T(8,128)(2,1)} %get-tuple-element.62.refs_13_.refs_3_), channel_id=1, source_target_pairs={{0,2},{1,3},{2,0},{3,1},{4,6},{5,7},{6,4},{7,5},{8,10},{9,11},{10,... | collective-permute-start | bytes 1179656 | tf_op jit(solution)/shard_map/ppermute | solution.py:23
  308.1 33.6 %collective-permute-start.70 = (bf16[192,1024]{1,0:T(8,128)(2,1)}, bf16[192,1024]{1,0:T(8,128)(2,1)}, u32[]{:S(2)}, u32[]{:S(2)}) collective-permute-start(bf16[192,1024]{1,0:T(8,128)(2,1)} %get-tuple-element.63.refs_14_.refs_4_), channel_id=1, source_target_pairs={{0,3},{1,2},{2,1},{3,0},{4,7},{5,6},{6,5},{7,4},{8,11},{9,10},{10,... | collective-permute-start | bytes 1179656 | tf_op jit(solution)/shard_map/ppermute | solution.py:23
  309.8 31.9 %collective-permute-start.68 = (bf16[192,1024]{1,0:T(8,128)(2,1)S(1)}, bf16[192,1024]{1,0:T(8,128)(2,1)}, u32[]{:S(2)}, u32[]{:S(2)}) collective-permute-start(bf16[192,1024]{1,0:T(8,128)(2,1)S(1)} %settle.4.refs_3_), channel_id=1, source_target_pairs={{0,1},{1,0},{2,3},{3,2},{4,5},{5,4},{6,7},{7,6},{8,9},{9,8},{10,11... | collective-permute-start | bytes 1179656 | tf_op jit(solution)/shard_map/ppermute | solution.py:23
  317.4 5.9 %collective-permute-start.64 = (bf16[192,512]{1,0:T(8,128)(2,1)}, bf16[192,512]{1,0:T(8,128)(2,1)S(1)}, u32[]{:S(2)}, u32[]{:S(2)}) collective-permute-start(bf16[192,512]{1,0:T(8,128)(2,1)} %get-tuple-element.66), channel_id=1, source_target_pairs={{0,16},{4,20},{8,24},{12,28},{16,0},{20,4},{24,8},{28,12},{1,17},{... | collective-permute-start | bytes 589832 | tf_op jit(solution)/shard_map/ppermute | solution.py:23
  318.6 5.9 %collective-permute-start.65 = (bf16[192,512]{1,0:T(8,128)(2,1)}, bf16[192,512]{1,0:T(8,128)(2,1)S(1)}, u32[]{:S(2)}, u32[]{:S(2)}) collective-permute-start(bf16[192,512]{1,0:T(8,128)(2,1)} %get-tuple-element.67), channel_id=1, source_target_pairs={{0,8},{4,12},{8,0},{12,4},{16,24},{20,28},{24,16},{28,20},{1,9},{5... | collective-permute-start | bytes 589832 | tf_op jit(solution)/shard_map/ppermute | solution.py:23
  (48 other events, 810.0 us)
Sparse Core Ops, SparseCore 0:
  99.0 25.2 reduce-scatter.2
  126.7 25.7 reduce-scatter.4
